TPU v7x, 32 devices: a whole 2x2x4 slice. The times are simulated.
32 devices in a mesh: dp: 4 (over x, core), ctx: 2 (over y), tensor: 4 (over z).
Axes of the slice: x: 2, y: 2, z: 4, core: 2. Of those that a mesh axis runs over, the one named last changes fastest.
Arguments:
- tokens: bfloat16 [5120, 2304], P(('dp', 'ctx')), may hold values from -6 to 6
- segment: int32 [5120], P('dp'), may hold values from 0 to 2, as said below
- position: int32 [5120], P('dp'), may hold values from 0 to 1151, as said below
- gain_attn: float32 [2304], P('dp'), may hold values from 0.5 to 1.5
- w_query: float32 [2304, 2304], P('dp', 'tensor'), may hold values from -0.1875 to 0.1875
- w_key: float32 [2304, 2304], P('dp', 'tensor'), may hold values from -0.1875 to 0.1875
- w_value: float32 [2304, 2304], P('dp', 'tensor'), may hold values from -0.125 to 0.125
- w_out: float32 [2304, 2304], P('tensor', 'dp'), may hold values from -2 to 2
- gain_ffn: float32 [2304], P('dp'), may hold values from 0.5 to 1.5
- w_gate: float32 [2304, 5760], P('dp', 'tensor'), may hold values from -0.125 to 0.125
- w_up: float32 [2304, 5760], P('dp', 'tensor'), may hold values from -0.125 to 0.125
- w_down: float32 [5760, 2304], P('tensor', 'dp'), may hold values from -0.625 to 0.625
- cotangent: bfloat16 [5120, 2304], P(('dp', 'ctx')), may hold values from -6 to 6
Outputs:
- output: float32 [5120, 2304], P(('dp', 'ctx'))
- grad_tokens: float32 [5120, 2304], P(('dp', 'ctx'))
- grad_gain_attn: float32 [2304], P('dp')
- grad_w_query: float32 [2304, 2304], P('dp', 'tensor')
- grad_w_key: float32 [2304, 2304], P('dp', 'tensor')
- grad_w_value: float32 [2304, 2304], P('dp', 'tensor')
- grad_w_out: float32 [2304, 2304], P('tensor', 'dp')
- grad_gain_ffn: float32 [2304], P('dp')
- grad_w_gate: float32 [2304, 5760], P('dp', 'tensor')
- grad_w_up: float32 [2304, 5760], P('dp', 'tensor')
- grad_w_down: float32 [5760, 2304], P('tensor', 'dp')
Inputs may be any that keep to these rules, and one draw needn't show every extreme that they name: Within each group of 1280 consecutive tokens the prompt (segment 0, 1024 tokens) and each continuation 1 to 2 (128 tokens each) fill one contiguous run, in an order drawn from the seed. `position`: positions count up from 0 along the prompt and from 1024 along each continuation.
All inputs are finite; a program needn't handle non-finite values.
Results may differ from a plain program's by a relative error of at most 0.025.
Values may be sent and summed in bfloat16 or wider, within the bound.
No kernel may reach another device: no remote copies, remote signals or barrier semaphores. Data moves between devices by JAX's collectives and lax.ppermute only.
A program may use at most 256 MiB of HBM per device.

v0:
```python
import math

import jax
import jax.numpy as jnp
from jax import lax
from jax.sharding import PartitionSpec as P

HEAD = 64


norm_eps = 1e-05
branch_scale = 1.4 / math.sqrt(40.0)


def rope_tables(positions):
    freq = 10000.0 ** (-(jnp.arange(HEAD // 2, dtype=jnp.float32) * 2.0 / HEAD))
    angle = positions.astype(jnp.float32)[:, None] * freq[None, :]
    return (jnp.cos(angle), jnp.sin(angle))


def rotate(field, cosine, sine, sign):
    heads = field.reshape(field.shape[0], -1, HEAD)
    half = HEAD // 2
    first = heads[:, :, :half]
    second = heads[:, :, half:]
    cos_b = cosine[:, None, :]
    sin_b = sine[:, None, :] * sign
    turned = jnp.concatenate(
        [first * cos_b - second * sin_b, second * cos_b + first * sin_b], axis=-1
    )
    return turned.reshape(field.shape)


def allowed_pairs(q_seg, q_pos, k_seg, k_pos):
    same = (k_seg[None, :] == q_seg[:, None]) | (k_seg[None, :] == 0)
    return same & (k_pos[None, :] <= q_pos[:, None])


def per_device(
    tokens,
    segment,
    position,
    gain_attn,
    w_query,
    w_key,
    w_value,
    w_out,
    gain_ffn,
    w_gate,
    w_up,
    w_down,
    cotangent,
):
    bf = jnp.bfloat16
    f32 = jnp.float32
    g_attn, wq_b, wk_b, wv_b, wo_b, g_ffn, wg_b, wu_b, wd_b = (
        lax.all_gather(gain_attn.astype(bf), "dp", axis=0, tiled=True),
        lax.all_gather(w_query.astype(bf), "dp", axis=0, tiled=True),
        lax.all_gather(w_key.astype(bf), "dp", axis=0, tiled=True),
        lax.all_gather(w_value.astype(bf), "dp", axis=0, tiled=True),
        lax.all_gather(w_out.astype(bf), "dp", axis=1, tiled=True),
        lax.all_gather(gain_ffn.astype(bf), "dp", axis=0, tiled=True),
        lax.all_gather(w_gate.astype(bf), "dp", axis=0, tiled=True),
        lax.all_gather(w_up.astype(bf), "dp", axis=0, tiled=True),
        lax.all_gather(w_down.astype(bf), "dp", axis=1, tiled=True),
    )
    rows = tokens.shape[0]
    group = segment.shape[0]
    offset = lax.axis_index("ctx") * rows
    my_seg = lax.dynamic_slice_in_dim(segment, offset, rows)
    my_pos = lax.dynamic_slice_in_dim(position, offset, rows)
    cosine, sine = rope_tables(my_pos)
    sm_scale = HEAD ** (-0.5)
    heads_dev = wq_b.shape[1] // HEAD
    inputs = tokens.astype(f32)
    scale1 = lax.rsqrt(jnp.mean(inputs * inputs, axis=-1, keepdims=True) + norm_eps)
    gain1 = g_attn.astype(f32)
    normed1 = (inputs * scale1 * gain1).astype(bf)
    q_pre = jnp.dot(normed1, wq_b, preferred_element_type=f32)
    k_pre = jnp.dot(normed1, wk_b, preferred_element_type=f32)
    values = jnp.dot(normed1, wv_b, preferred_element_type=f32).astype(bf)
    query = rotate(q_pre, cosine, sine, 1.0).astype(bf)
    keys = rotate(k_pre, cosine, sine, 1.0).astype(bf)
    query3 = query.reshape(rows, heads_dev, HEAD)
    best = jnp.full((heads_dev, rows), -1e30, f32)
    total = jnp.zeros((heads_dev, rows), f32)
    accum = jnp.zeros((rows, heads_dev, HEAD), f32)
    key_rows = lax.all_gather(keys, "ctx", axis=0, tiled=True)
    value_rows = lax.all_gather(values, "ctx", axis=0, tiled=True)
    count = key_rows.shape[0]
    step = min(count, 512)
    for first in range(0, count, step):
        size = min(step, count - first)
        key_blk = key_rows[first : first + size].reshape(size, heads_dev, HEAD)
        val_blk = value_rows[first : first + size].reshape(size, heads_dev, HEAD)
        k_seg = lax.dynamic_slice_in_dim(segment, first, size)
        k_pos = lax.dynamic_slice_in_dim(position, first, size)
        allowed = allowed_pairs(my_seg, my_pos, k_seg, k_pos)[None, :, :]
        score = jnp.einsum("qhd,khd->hqk", query3, key_blk, preferred_element_type=f32) * sm_scale
        score = jnp.where(allowed, score, -1e30)
        fresh = jnp.maximum(best, jnp.max(score, axis=-1))
        weight = jnp.where(allowed, jnp.exp(score - fresh[:, :, None]), 0.0)
        decay = jnp.exp(best - fresh)
        total = total * decay + jnp.sum(weight, axis=-1)
        accum = accum * decay.T[:, :, None] + jnp.einsum(
            "hqk,khd->qhd", weight.astype(bf), val_blk, preferred_element_type=f32
        )
        best = fresh
    best, total, accum = (best, total, accum)
    log_total = best + jnp.log(total)
    attn_out = (accum / total.T[:, :, None]).reshape(rows, heads_dev * HEAD).astype(bf)
    mixed = lax.psum(
        jnp.dot(attn_out, wo_b, preferred_element_type=f32).astype(jnp.bfloat16), "tensor"
    ).astype(jnp.float32)
    hidden_in = inputs + branch_scale * mixed
    scale2 = lax.rsqrt(jnp.mean(hidden_in * hidden_in, axis=-1, keepdims=True) + norm_eps)
    gain2 = g_ffn.astype(f32)
    normed2 = (hidden_in * scale2 * gain2).astype(bf)
    gate = jnp.dot(normed2, wg_b, preferred_element_type=f32)
    up_val = jnp.dot(normed2, wu_b, preferred_element_type=f32)
    sigma = jax.nn.sigmoid(gate)
    active = gate * sigma
    hidden = (active * up_val).astype(bf)
    ffn_out = lax.psum(
        jnp.dot(hidden, wd_b, preferred_element_type=f32).astype(jnp.bfloat16), "tensor"
    ).astype(jnp.float32)
    output = hidden_in + branch_scale * ffn_out
    g_attn, wq_b, wk_b, wv_b, wo_b, g_ffn, wg_b, wu_b, wd_b = (
        lax.all_gather(gain_attn.astype(bf), "dp", axis=0, tiled=True),
        lax.all_gather(w_query.astype(bf), "dp", axis=0, tiled=True),
        lax.all_gather(w_key.astype(bf), "dp", axis=0, tiled=True),
        lax.all_gather(w_value.astype(bf), "dp", axis=0, tiled=True),
        lax.all_gather(w_out.astype(bf), "dp", axis=1, tiled=True),
        lax.all_gather(gain_ffn.astype(bf), "dp", axis=0, tiled=True),
        lax.all_gather(w_gate.astype(bf), "dp", axis=0, tiled=True),
        lax.all_gather(w_up.astype(bf), "dp", axis=0, tiled=True),
        lax.all_gather(w_down.astype(bf), "dp", axis=1, tiled=True),
    )
    grad_out = cotangent.astype(f32)
    grad_ffn = (branch_scale * grad_out).astype(bf)
    grad_wd = jnp.einsum("rf,rd->fd", hidden, grad_ffn, preferred_element_type=f32)
    grad_hidden = jnp.einsum("rd,fd->rf", grad_ffn, wd_b, preferred_element_type=f32)
    grad_gate = (grad_hidden * up_val * sigma * (1.0 + gate * (1.0 - sigma))).astype(bf)
    grad_up = (grad_hidden * active).astype(bf)
    grad_wg = jnp.einsum("rd,rf->df", normed2, grad_gate, preferred_element_type=f32)
    grad_wu = jnp.einsum("rd,rf->df", normed2, grad_up, preferred_element_type=f32)
    partial2 = jnp.einsum("rf,df->rd", grad_gate, wg_b, preferred_element_type=f32) + jnp.einsum(
        "rf,df->rd", grad_up, wu_b, preferred_element_type=f32
    )
    grad_norm2 = lax.psum(partial2.astype(jnp.bfloat16), "tensor").astype(jnp.float32)
    grad_g2 = jnp.sum(grad_norm2 * hidden_in * scale2, axis=0)
    grad_h = (
        grad_out
        + scale2 * gain2 * grad_norm2
        - hidden_in * scale2**3 * jnp.mean(hidden_in * gain2 * grad_norm2, axis=-1, keepdims=True)
    )
    grad_mixed = (branch_scale * grad_h).astype(bf)
    grad_wo = jnp.einsum("rk,rd->kd", attn_out, grad_mixed, preferred_element_type=f32)
    grad_attn = jnp.einsum("rd,kd->rk", grad_mixed, wo_b, preferred_element_type=f32).astype(bf)
    grad_attn3 = grad_attn.reshape(rows, heads_dev, HEAD)
    delta = jnp.sum(
        grad_attn3.astype(f32) * attn_out.reshape(rows, heads_dev, HEAD).astype(f32), axis=-1
    ).T
    grad_q = jnp.zeros((rows, heads_dev, HEAD), f32)
    grad_k_all = jnp.zeros((group, heads_dev, HEAD), f32)
    grad_v_all = jnp.zeros((group, heads_dev, HEAD), f32)
    key_rows = lax.all_gather(keys, "ctx", axis=0, tiled=True)
    value_rows = lax.all_gather(values, "ctx", axis=0, tiled=True)
    count = key_rows.shape[0]
    step = min(count, 512)
    for first in range(0, count, step):
        size = min(step, count - first)
        key_blk = key_rows[first : first + size].reshape(size, heads_dev, HEAD)
        val_blk = value_rows[first : first + size].reshape(size, heads_dev, HEAD)
        k_seg = lax.dynamic_slice_in_dim(segment, first, size)
        k_pos = lax.dynamic_slice_in_dim(position, first, size)
        allowed = allowed_pairs(my_seg, my_pos, k_seg, k_pos)[None, :, :]
        score = jnp.einsum("qhd,khd->hqk", query3, key_blk, preferred_element_type=f32) * sm_scale
        prob = jnp.where(allowed, jnp.exp(score - log_total[:, :, None]), 0.0)
        grad_v_blk = jnp.einsum(
            "hqk,qhd->khd", prob.astype(bf), grad_attn3, preferred_element_type=f32
        )
        grad_prob = jnp.einsum("qhd,khd->hqk", grad_attn3, val_blk, preferred_element_type=f32)
        grad_score = (prob * (grad_prob - delta[:, :, None])).astype(bf)
        grad_q = grad_q + sm_scale * jnp.einsum(
            "hqk,khd->qhd", grad_score, key_blk, preferred_element_type=f32
        )
        grad_k_blk = sm_scale * jnp.einsum(
            "hqk,qhd->khd", grad_score, query3, preferred_element_type=f32
        )
        grad_k_all = lax.dynamic_update_slice_in_dim(grad_k_all, grad_k_blk, first, 0)
        grad_v_all = lax.dynamic_update_slice_in_dim(grad_v_all, grad_v_blk, first, 0)
    grad_q, grad_k_all, grad_v_all = (grad_q, grad_k_all, grad_v_all)
    grad_k, grad_v = (
        lax.psum_scatter(
            grad_k_all.astype(jnp.bfloat16), "ctx", scatter_dimension=0, tiled=True
        ).astype(jnp.float32),
        lax.psum_scatter(
            grad_v_all.astype(jnp.bfloat16), "ctx", scatter_dimension=0, tiled=True
        ).astype(jnp.float32),
    )
    grad_qp = rotate(grad_q.reshape(rows, heads_dev * HEAD), cosine, sine, -1.0).astype(bf)
    grad_kp = rotate(grad_k.reshape(rows, heads_dev * HEAD), cosine, sine, -1.0).astype(bf)
    grad_vp = grad_v.reshape(rows, heads_dev * HEAD).astype(bf)
    grad_wq = jnp.einsum("rd,rk->dk", normed1, grad_qp, preferred_element_type=f32)
    grad_wk = jnp.einsum("rd,rk->dk", normed1, grad_kp, preferred_element_type=f32)
    grad_wv = jnp.einsum("rd,rk->dk", normed1, grad_vp, preferred_element_type=f32)
    partial1 = (
        jnp.einsum("rk,dk->rd", grad_qp, wq_b, preferred_element_type=f32)
        + jnp.einsum("rk,dk->rd", grad_kp, wk_b, preferred_element_type=f32)
        + jnp.einsum("rk,dk->rd", grad_vp, wv_b, preferred_element_type=f32)
    )
    grad_norm1 = lax.psum(partial1.astype(jnp.bfloat16), "tensor").astype(jnp.float32)
    grad_g1 = jnp.sum(grad_norm1 * inputs * scale1, axis=0)
    grad_in = (
        grad_h
        + scale1 * gain1 * grad_norm1
        - inputs * scale1**3 * jnp.mean(inputs * gain1 * grad_norm1, axis=-1, keepdims=True)
    )
    part_g1, part_wq, part_wk, part_wv, part_wo, part_g2, part_wg, part_wu, part_wd = (
        lax.psum_scatter(
            grad_g1.astype(jnp.bfloat16), ("dp", "ctx"), scatter_dimension=0, tiled=True
        ).astype(jnp.float32),
        lax.psum_scatter(
            grad_wq.astype(jnp.bfloat16), ("dp", "ctx"), scatter_dimension=0, tiled=True
        ).astype(jnp.float32),
        lax.psum_scatter(
            grad_wk.astype(jnp.bfloat16), ("dp", "ctx"), scatter_dimension=0, tiled=True
        ).astype(jnp.float32),
        lax.psum_scatter(
            grad_wv.astype(jnp.bfloat16), ("dp", "ctx"), scatter_dimension=0, tiled=True
        ).astype(jnp.float32),
        lax.psum_scatter(
            grad_wo.astype(jnp.bfloat16), ("dp", "ctx"), scatter_dimension=1, tiled=True
        ).astype(jnp.float32),
        lax.psum_scatter(
            grad_g2.astype(jnp.bfloat16), ("dp", "ctx"), scatter_dimension=0, tiled=True
        ).astype(jnp.float32),
        lax.psum_scatter(
            grad_wg.astype(jnp.bfloat16), ("dp", "ctx"), scatter_dimension=0, tiled=True
        ).astype(jnp.float32),
        lax.psum_scatter(
            grad_wu.astype(jnp.bfloat16), ("dp", "ctx"), scatter_dimension=0, tiled=True
        ).astype(jnp.float32),
        lax.psum_scatter(
            grad_wd.astype(jnp.bfloat16), ("dp", "ctx"), scatter_dimension=1, tiled=True
        ).astype(jnp.float32),
    )
    sum_g1, sum_wq, sum_wk, sum_wv, sum_wo, sum_g2, sum_wg, sum_wu, sum_wd = (
        lax.all_gather(part_g1.astype(jnp.bfloat16), "ctx", axis=0, tiled=True).astype(
            part_g1.dtype
        ),
        lax.all_gather(part_wq.astype(jnp.bfloat16), "ctx", axis=0, tiled=True).astype(
            part_wq.dtype
        ),
        lax.all_gather(part_wk.astype(jnp.bfloat16), "ctx", axis=0, tiled=True).astype(
            part_wk.dtype
        ),
        lax.all_gather(part_wv.astype(jnp.bfloat16), "ctx", axis=0, tiled=True).astype(
            part_wv.dtype
        ),
        lax.all_gather(part_wo.astype(jnp.bfloat16), "ctx", axis=1, tiled=True).astype(
            part_wo.dtype
        ),
        lax.all_gather(part_g2.astype(jnp.bfloat16), "ctx", axis=0, tiled=True).astype(
            part_g2.dtype
        ),
        lax.all_gather(part_wg.astype(jnp.bfloat16), "ctx", axis=0, tiled=True).astype(
            part_wg.dtype
        ),
        lax.all_gather(part_wu.astype(jnp.bfloat16), "ctx", axis=0, tiled=True).astype(
            part_wu.dtype
        ),
        lax.all_gather(part_wd.astype(jnp.bfloat16), "ctx", axis=1, tiled=True).astype(
            part_wd.dtype
        ),
    )
    return (output, grad_in, sum_g1, sum_wq, sum_wk, sum_wv, sum_wo, sum_g2, sum_wg, sum_wu, sum_wd)


def solution(mesh):
    return jax.shard_map(
        per_device,
        mesh=mesh,
        in_specs=(
            P(("dp", "ctx"), None),
            P("dp"),
            P("dp"),
            P("dp"),
            P("dp", "tensor"),
            P("dp", "tensor"),
            P("dp", "tensor"),
            P("tensor", "dp"),
            P("dp"),
            P("dp", "tensor"),
            P("dp", "tensor"),
            P("tensor", "dp"),
            P(("dp", "ctx"), None),
        ),
        out_specs=(
            P(("dp", "ctx"), None),
            P(("dp", "ctx"), None),
            P("dp"),
            P("dp", "tensor"),
            P("dp", "tensor"),
            P("dp", "tensor"),
            P("tensor", "dp"),
            P("dp"),
            P("dp", "tensor"),
            P("dp", "tensor"),
            P("tensor", "dp"),
        ),
        check_vma=False,
    )
```

profile of v0, /device:TPU:26, one launch (start us, length us, event | category | flops | bytes accessed | tf_op | source)
XLA Modules:
  0.0 1463.9 jit_solution(15009026914571021302)
XLA Ops:
  16.4 10.7 all-reduce.10
  29.5 8.5 all-gather.13.cloned.1.call-done
  38.0 5.3 fusion.106
  43.3 24.2 %all-gather.15.cloned.1.call-done = bf16[2304,576]{1,0:T(8,128)(2,1)} async-done(((bf16[576,576]{1,0:T(8,128)(2,1)}), bf16[2304,576]{1,0:T(8,128)(2,1)}) %all-gather.15.cloned.1.call-update) | async-done | bytes 2654224 | tf_op jit(solution)/shard_map/all_gather | solution.py:59
  74.2 22.9 %all-gather.19.cloned.1.call-done = bf16[2304,576]{1,0:T(8,128)(2,1)} async-done(((bf16[576,576]{1,0:T(8,128)(2,1)}), bf16[2304,576]{1,0:T(8,128)(2,1)}) %all-gather.19.cloned.1.call-update) | async-done | bytes 2654224 | tf_op jit(solution)/shard_map/all_gather | solution.py:60
  107.2 19.0 %all-gather.17.cloned.1.call-done = bf16[1280,576]{0,1:T(8,128)(2,1)} async-done(((bf16[640,576]{0,1:T(8,128)(2,1)}), bf16[1280,576]{0,1:T(8,128)(2,1)}) %all-gather.17.cloned.1.call-update) | async-done | bytes 1474576 | tf_op jit(solution)/shard_map/all_gather | solution.py:88
  141.4 6.6 fusion.2
  148.0 6.3 all-gather.21.cloned.1.call-done
  160.5 6.3 fusion.38
  173.0 6.6 fusion.46
  182.8 6.2 convolution_convert_fusion.8
  199.8 103.0 %all-reduce.16.cloned.1.call-done = bf16[640,2304]{1,0:T(8,128)(2,1)} async-done(((bf16[640,2304]{1,0:T(8,128)(2,1)}), bf16[640,2304]{1,0:T(8,128)(2,1)}) %all-reduce.16.cloned.1.call-update) | async-done | bytes 2949136 | tf_op jit(solution)/shard_map/psum | solution.py:112
  309.2 46.8 %all-gather.25.cloned.1.call-done = bf16[2304,1440]{1,0:T(8,128)(2,1)} async-done(((bf16[576,1440]{1,0:T(8,128)(2,1)}), bf16[2304,1440]{1,0:T(8,128)(2,1)}) %all-gather.25.cloned.1.call-update) | async-done | bytes 6635536 | tf_op jit(solution)/shard_map/all_gather | solution.py:63
  356.0 11.1 fusion.116
  367.1 42.0 %all-gather.27.cloned.1.call-done = bf16[2304,1440]{1,0:T(8,128)(2,1)} async-done(((bf16[576,1440]{1,0:T(8,128)(2,1)}), bf16[2304,1440]{1,0:T(8,128)(2,1)}) %all-gather.27.cloned.1.call-update) | async-done | bytes 6635536 | tf_op jit(solution)/shard_map/all_gather | solution.py:64
  409.1 11.5 fusion.117
  420.6 40.8 %all-gather.29.cloned.1.call-done = bf16[1440,2304]{0,1:T(8,128)(2,1)} async-done(((bf16[1440,576]{0,1:T(8,128)(2,1)}), bf16[1440,2304]{0,1:T(8,128)(2,1)}) %all-gather.29.cloned.1.call-update) | async-done | bytes 6635536 | tf_op jit(solution)/shard_map/all_gather | solution.py:65
  461.5 14.8 %multiply_convert_fusion.5 = (bf16[640,1440]{0,1:T(8,128)(2,1)S(1)}, bf16[640,1440]{0,1:T(8,128)(2,1)}, bf16[640,1440]{0,1:T(8,128)(2,1)}) fusion(f32[640,1440]{0,1:T(8,128)} %fusion.116, f32[640,1440]{0,1:T(8,128)} %fusion.117, bf16[1440,2304]{0,1:T(8,128)(2,1)} %all-gather.29.cloned.1.call-done, bf16[640,2304]{1,0:T(8,128)(2,1)} %param.25), kind=kOutput, calls=%fused_computation.71 | convolution fusion | flops 4264980480 | bytes 22487040 | tf_op jit(solution)/shard_map/rd,fd->rf/dot_general | solution.py:142
  476.2 11.9 fusion.118
  488.2 8.6 add_convert_fusion.1
  498.4 112.2 %all-reduce.18.cloned.1.call-done = bf16[640,2304]{1,0:T(8,128)(2,1)} async-done(((bf16[640,2304]{1,0:T(8,128)(2,1)}), bf16[640,2304]{1,0:T(8,128)(2,1)}) %all-reduce.18.cloned.1.call-update) | async-done | bytes 2949136 | tf_op jit(solution)/shard_map/psum | solution.py:150
  610.6 5.1 fusion.10
  618.6 6.4 convolution_convert_fusion.9
  645.0 8.6 multiply_convert_fusion.1
  656.2 6.7 multiply_convert_fusion
  675.8 9.7 convolution_convert_fusion.2
  685.6 9.8 convolution_convert_fusion.1
  695.4 9.7 convolution_convert_fusion
  705.3 7.4 convolution_convert_fusion.3
  712.9 5.5 convolution_convert_fusion.4
  747.4 24.9 %reduce-scatter.22.cloned.1.call-done = bf16[288,1440]{1,0:T(8,128)(2,1)} async-done(((bf16[2304,1440]{1,0:T(8,128)(2,1)}), bf16[288,1440]{1,0:T(8,128)(2,1)}) %reduce-scatter.22.cloned.1.call-update) | async-done | bytes 829456 | tf_op jit(solution)/shard_map/reduce_scatter | solution.py:239
  772.4 69.2 %reduce-scatter.24.cloned.1.call-done = bf16[288,1440]{1,0:T(8,128)(2,1)} async-done(((bf16[2304,1440]{1,0:T(8,128)(2,1)}), bf16[288,1440]{1,0:T(8,128)(2,1)}) %reduce-scatter.24.cloned.1.call-update) | async-done | bytes 829456 | tf_op jit(solution)/shard_map/reduce_scatter | solution.py:242
  841.9 10.0 convolution_convert_fusion.7
  851.9 58.6 %reduce-scatter.26.cloned.1.call-done = bf16[1440,288]{0,1:T(8,128)(2,1)} async-done(((bf16[1440,2304]{0,1:T(8,128)(2,1)}), bf16[1440,288]{0,1:T(8,128)(2,1)}) %reduce-scatter.26.cloned.1.call-update) | async-done | bytes 829456 | tf_op jit(solution)/shard_map/reduce_scatter | solution.py:245
  925.3 34.1 %reduce-scatter.20.cloned.1.call-done = bf16[576,288]{0,1:T(8,128)(2,1)} async-done(((bf16[576,2304]{0,1:T(8,128)(2,1)}), bf16[576,288]{0,1:T(8,128)(2,1)}) %reduce-scatter.20.cloned.1.call-update) | async-done | bytes 331792 | tf_op jit(solution)/shard_map/reduce_scatter | solution.py:233
  959.5 11.8 all_gather.84
  973.9 35.1 %reduce-scatter.18.cloned.1.call-done = bf16[288,576]{1,0:T(8,128)(2,1)} async-done(((bf16[2304,576]{1,0:T(8,128)(2,1)}), bf16[288,576]{1,0:T(8,128)(2,1)}) %reduce-scatter.18.cloned.1.call-update) | async-done | bytes 331792 | tf_op jit(solution)/shard_map/reduce_scatter | solution.py:230
  1009.0 11.2 all_gather.83
  1021.4 37.2 %reduce-scatter.16.cloned.1.call-done = bf16[288,576]{1,0:T(8,128)(2,1)} async-done(((bf16[2304,576]{1,0:T(8,128)(2,1)}), bf16[288,576]{1,0:T(8,128)(2,1)}) %reduce-scatter.16.cloned.1.call-update) | async-done | bytes 331792 | tf_op jit(solution)/shard_map/reduce_scatter | solution.py:227
  1058.6 11.5 all_gather.82
  1071.3 36.8 %reduce-scatter.14.cloned.1.call-done = bf16[288,576]{1,0:T(8,128)(2,1)} async-done(((bf16[2304,576]{1,0:T(8,128)(2,1)}), bf16[288,576]{1,0:T(8,128)(2,1)}) %reduce-scatter.14.cloned.1.call-update) | async-done | bytes 331792 | tf_op jit(solution)/shard_map/reduce_scatter | solution.py:224
  1108.2 11.2 all_gather.81
  1120.6 18.7 %all-gather.31.cloned.1.call-done = bf16[576,1440]{1,0:T(8,128)(2,1)} async-done(((bf16[288,1440]{1,0:T(8,128)(2,1)}), bf16[576,1440]{1,0:T(8,128)(2,1)}) %all-gather.31.cloned.1.call-update) | async-done | bytes 1658896 | tf_op jit(solution)/shard_map/all_gather | solution.py:268
  1143.0 27.3 %all-gather.33.cloned.1.call-done = bf16[576,1440]{1,0:T(8,128)(2,1)} async-done(((bf16[288,1440]{1,0:T(8,128)(2,1)}), bf16[576,1440]{1,0:T(8,128)(2,1)}) %all-gather.33.cloned.1.call-update) | async-done | bytes 1658896 | tf_op jit(solution)/shard_map/all_gather | solution.py:271
  1174.1 27.3 %all-gather.35.cloned.1.call-done = bf16[1440,576]{0,1:T(8,128)(2,1)} async-done(((bf16[1440,288]{0,1:T(8,128)(2,1)}), bf16[1440,576]{0,1:T(8,128)(2,1)}) %all-gather.35.cloned.1.call-update) | async-done | bytes 1658896 | tf_op jit(solution)/shard_map/all_gather | solution.py:274
  1205.2 207.7 %all-reduce.20.cloned.1.call-done = (bf16[640,2304]{1,0:T(8,128)(2,1)}, bf16[640,2304]{1,0:T(8,128)(2,1)}) async-done(((bf16[640,2304]{1,0:T(8,128)(2,1)}, bf16[640,2304]{1,0:T(8,128)(2,1)}), (bf16[640,2304]{1,0:T(8,128)(2,1)}, bf16[640,2304]{1,0:T(8,128)(2,1)})) %all-reduce.20.cloned.1.call-update) | async-done | bytes 5898256 | tf_op jit(solution)/shard_map/psum | solution.py:124
  1416.7 23.8 %all-reduce.8 = (bf16[2304]{0:T(1024)(128)(2,1)S(1)}, bf16[2304]{0:T(1024)(128)(2,1)S(1)}) all-reduce(bf16[2304]{0:T(1024)(128)(2,1)S(1)} %get-tuple-element.35, bf16[2304]{0:T(1024)(128)(2,1)S(1)} %copy-done.64), channel_id=4, replica_groups=mesh['dp'=4,'ctx'=2,'tensor'=4] {'dp','ctx'}, use_global_device_ids=true, to_apply=%region_18.19.clone | all-reduce | flops 4608 | bytes 18432
  1447.2 9.4 fusion.12
  (325 shorter events, 185.6 us)
Async XLA Ops:
  7.2 19.9 %copy-start.67 = (s32[1280]{0:T(1024)S(1)}, s32[1280]{0:T(1024)}, u32[]{:S(2)}) copy-start(s32[1280]{0:T(1024)} %param.15) | copy-start | bytes 15364
  7.2 20.0 %copy-start = (bf16[640,2304]{1,0:T(8,128)(2,1)S(1)}, bf16[640,2304]{1,0:T(8,128)(2,1)}, u32[]{:S(2)}) copy-start(bf16[640,2304]{1,0:T(8,128)(2,1)} %param.13) | copy-start | bytes 8847364
  7.2 30.7 %all-gather.13.cloned.1.call-start = ((), (), s32[]{:S(2)}) async-start(), calls=%async_computation.9 | async-start | bytes 3686400 | tf_op jit(solution)/shard_map/all_gather | solution.py:58
  9.8 57.8 %all-gather.15.cloned.1.call-start = ((), (), s32[]{:S(2)}) async-start(), calls=%async_computation.10 | async-start | bytes 3686400 | tf_op jit(solution)/shard_map/all_gather | solution.py:59
  12.2 85.0 %all-gather.19.cloned.1.call-start = ((), (), s32[]{:S(2)}) async-start(), calls=%async_computation.12 | async-start | bytes 3686400 | tf_op jit(solution)/shard_map/all_gather | solution.py:60
  14.6 111.6 %all-gather.17.cloned.1.call-start = ((), (), s32[]{:S(2)}) async-start(), calls=%async_computation.11 | async-start | bytes 2211840 | tf_op jit(solution)/shard_map/all_gather | solution.py:88
  27.1 70.1 %copy-start.58 = (f32[2304]{0:T(1024)}, f32[2304]{0:T(1024)S(1)}, u32[]{:S(2)}) copy-start(f32[2304]{0:T(1024)S(1)} %convert_element_type.242) | copy-start | bytes 27652
  28.4 68.7 %copy-start.62 = (f32[640]{0:T(1024)}, f32[640]{0:T(1024)S(1)}, u32[]{:S(2)}) copy-start(f32[640]{0:T(1024)S(1)} %get-tuple-element.87) | copy-start | bytes 7684
  29.4 42.5 %copy-start.38 = (f32[640,32]{0,1:T(8,128)}, f32[640,32]{0,1:T(8,128)S(1)}, u32[]{:S(2)}) copy-start(f32[640,32]{0,1:T(8,128)S(1)} %get-tuple-element.85) | copy-start | bytes 245764
  74.1 31.0 %copy-start.65 = (s32[1280]{0:T(1024)S(1)}, s32[1280]{0:T(1024)}, u32[]{:S(2)}) copy-start(s32[1280]{0:T(1024)} %param.14) | copy-start | bytes 15364
  74.1 31.1 %slice-start.9 = ((s32[1280]{0:T(1024)}), s32[256]{0:T(256)S(1)}, s32[]{:S(2)}) async-start(s32[1280]{0:T(1024)} %param.14), calls=%async_computation.42 | async-start | bytes 2048 | tf_op jit(solution)/shard_map/dynamic_slice | solution.py:96
  74.2 31.1 %slice-start.10 = ((s32[1280]{0:T(1024)}), s32[256]{0:T(256)S(1)}, s32[]{:S(2)}) async-start(s32[1280]{0:T(1024)} %param.15), calls=%async_computation.43 | async-start | bytes 2048 | tf_op jit(solution)/shard_map/dynamic_slice | solution.py:97
  74.2 80.1 %all-gather.21.cloned.1.call-start = ((), (), s32[]{:S(2)}) async-start(), calls=%async_computation.13 | async-start | bytes 2211840 | tf_op jit(solution)/shard_map/all_gather | solution.py:89
  102.3 80.5 %all-gather.23.cloned.1.call-start = ((), (), s32[]{:S(2)}) async-start(), calls=%async_computation.14 | async-start | bytes 3686400 | tf_op jit(solution)/shard_map/all_gather | solution.py:61
  104.9 197.9 %all-reduce.16.cloned.1.call-start = ((), (), s32[]{:S(2)}) async-start(), calls=%async_computation.15 | async-start | bytes 5898240 | tf_op jit(solution)/shard_map/psum | solution.py:112
  131.1 9.6 copy-start.5
  155.4 11.3 copy-start.52
  160.4 12.6 copy-start.40
  160.4 12.6 copy-start.42
  160.5 12.5 slice-start.3
  189.0 167.0 %all-gather.25.cloned.1.call-start = ((), (), s32[]{:S(2)}) async-start(), calls=%async_computation.16 | async-start | bytes 8847360 | tf_op jit(solution)/shard_map/all_gather | solution.py:63
  192.5 216.6 %all-gather.27.cloned.1.call-start = ((), (), s32[]{:S(2)}) async-start(), calls=%async_computation.17 | async-start | bytes 8847360 | tf_op jit(solution)/shard_map/all_gather | solution.py:64
  196.0 265.5 %all-gather.29.cloned.1.call-start = ((), (), s32[]{:S(2)}) async-start(), calls=%async_computation.18 | async-start | bytes 8847360 | tf_op jit(solution)/shard_map/all_gather | solution.py:65
  199.6 411.0 %all-reduce.18.cloned.1.call-start = ((), (), s32[]{:S(2)}) async-start(), calls=%async_computation.19 | async-start | bytes 5898240 | tf_op jit(solution)/shard_map/psum | solution.py:150
  461.5 26.7 %slice-start.11 = ((s8[7077888]{0:T(1024)(128)(4,1)}), s8[2883584]{0:T(1024)(128)(4,1)S(1)}, s32[]{:S(2)}) async-start(s8[7077888]{0:T(1024)(128)(4,1)} %bitcast.205), calls=%async_computation.44 | async-start | bytes 5767168
  476.2 11.9 copy-start.74
  476.2 11.9 slice-start.12
  496.8 216.1 %reduce-scatter.30.cloned.1.call-start = ((), (), s32[]{:S(2)}) async-start(), calls=%async_computation.31 | async-start | bytes 2457600 | tf_op jit(solution)/shard_map/convert_element_type | solution.py:204
  615.9 10.2 slice-start.6
  616.0 10.2 slice-start.7
  618.6 14.4 slice-start
  618.6 14.4 slice-start.1
  644.7 84.6 %reduce-scatter.28.cloned.1.call-start = ((), (), s32[]{:S(2)}) async-start(), calls=%async_computation.30 | async-start | bytes 2457600
  645.0 8.6 copy-start.10
  653.6 9.3 copy-start.6
  675.4 96.9 %reduce-scatter.22.cloned.1.call-start = ((), (), s32[]{:S(2)}) async-start(), calls=%async_computation.24 | async-start | bytes 7962624 | tf_op jit(solution)/shard_map/reduce_scatter | solution.py:239
  685.5 156.0 %reduce-scatter.24.cloned.1.call-start = ((), (), s32[]{:S(2)}) async-start(), calls=%async_computation.26 | async-start | bytes 7962624 | tf_op jit(solution)/shard_map/reduce_scatter | solution.py:242
  695.4 215.1 %reduce-scatter.26.cloned.1.call-start = ((), (), s32[]{:S(2)}) async-start(), calls=%async_computation.28 | async-start | bytes 7962624 | tf_op jit(solution)/shard_map/reduce_scatter | solution.py:245
  705.2 254.2 %reduce-scatter.20.cloned.1.call-start = ((), (), s32[]{:S(2)}) async-start(), calls=%async_computation.23 | async-start | bytes 3317760 | tf_op jit(solution)/shard_map/reduce_scatter | solution.py:233
  712.7 296.3 %reduce-scatter.18.cloned.1.call-start = ((), (), s32[]{:S(2)}) async-start(), calls=%async_computation.22 | async-start | bytes 3317760 | tf_op jit(solution)/shard_map/reduce_scatter | solution.py:230
  718.5 340.1 %reduce-scatter.16.cloned.1.call-start = ((), (), s32[]{:S(2)}) async-start(), calls=%async_computation.21 | async-start | bytes 3317760 | tf_op jit(solution)/shard_map/reduce_scatter | solution.py:227
  741.0 367.2 %reduce-scatter.14.cloned.1.call-start = ((), (), s32[]{:S(2)}) async-start(), calls=%async_computation.20 | async-start | bytes 3317760 | tf_op jit(solution)/shard_map/reduce_scatter | solution.py:224
  747.4 391.9 %all-gather.31.cloned.1.call-start = ((), (), s32[]{:S(2)}) async-start(), calls=%async_computation.25 | async-start | bytes 2654208 | tf_op jit(solution)/shard_map/all_gather | solution.py:268
  772.3 398.0 %all-gather.33.cloned.1.call-start = ((), (), s32[]{:S(2)}) async-start(), calls=%async_computation.27 | async-start | bytes 2654208 | tf_op jit(solution)/shard_map/all_gather | solution.py:271
  841.6 359.8 %all-gather.35.cloned.1.call-start = ((), (), s32[]{:S(2)}) async-start(), calls=%async_computation.29 | async-start | bytes 2654208 | tf_op jit(solution)/shard_map/all_gather | solution.py:274
  910.5 502.4 %all-reduce.20.cloned.1.call-start = ((), (), s32[]{:S(2)}) async-start(), calls=%async_computation.32 | async-start | bytes 11796480 | tf_op jit(solution)/shard_map/psum | solution.py:124
  1174.1 242.6 %copy-start.64 = (bf16[2304]{0:T(1024)(128)(2,1)S(1)}, bf16[2304]{0:T(1024)(128)(2,1)}, u32[]{:S(2)}) copy-start(bf16[2304]{0:T(1024)(128)(2,1)} %get-tuple-element.33) | copy-start | bytes 13828
  1174.1 273.1 %copy-start.66 = (f32[640]{0:T(1024)S(1)}, f32[640]{0:T(1024)}, u32[]{:S(2)}) copy-start(f32[640]{0:T(1024)} %get-tuple-element.86) | copy-start | bytes 7684
  (64 other events, 290.7 us)
Sparse Core Ops, SparseCore 0:
  10.2 27.7 all-gather.12
  40.1 27.4 all-gather.14
  69.7 27.4 all-gather.18
  99.1 27.0 all-gather.16
  128.1 26.1 all-gather.20
  156.3 26.4 all-gather.22
  189.1 113.6 all-reduce.15
  305.0 50.9 all-gather.24
  358.2 50.8 all-gather.26
  410.6 50.8 all-gather.28
  496.9 113.6 all-reduce.17
  644.9 27.8 reduce-scatter.29
  675.7 27.7 reduce-scatter.27
  706.9 65.3 reduce-scatter.21
  776.1 65.4 reduce-scatter.23
  845.0 65.4 reduce-scatter.25
  914.1 45.2 reduce-scatter.19
  963.7 45.2 reduce-scatter.17
  1013.3 45.2 reduce-scatter.15
  1062.9 45.2 reduce-scatter.13
  1109.8 29.4 all-gather.30
  1140.9 29.4 all-gather.32
  1172.0 29.4 all-gather.34
  1204.4 208.4 all-reduce.19
where the time goes:
time: 1480 us; the launch traced here: 1460 us
  waiting for transfers between devices  1010 us (68%)
  matrix products  235 us (16%)
  other arithmetic  86.6 us (6%)
  blocking collectives  85.2 us (6%)
  local copies, waits for them, and re-layouts  30.5 us (2%)
  between operations  18 us (1%)
    psum x1, waiting for transfers between devices, per_device(): lax.psum(jnp.dot(hidden, wd_b, preferred_element_type=f32).astype(jnp.bfl...  208 us
    psum x1, waiting for transfers between devices, per_device(): lax.psum(partial2.astype(jnp.bfloat16), 'tensor').astype(jnp.float32)  112 us
    psum x1, waiting for transfers between devices, per_device(): lax.psum(jnp.dot(attn_out, wo_b, preferred_element_type=f32).astype(jnp.b...  103 us
    reduce_scatter x1, waiting for transfers between devices, per_device(): lax.psum_scatter(grad_wu.astype(jnp.bfloat16), ('dp', 'ctx'), scatter_dim...  69.2 us
    reduce_scatter x1, waiting for transfers between devices, per_device(): lax.psum_scatter(grad_wd.astype(jnp.bfloat16), ('dp', 'ctx'), scatter_dim...  58.6 us
    all_gather x1, waiting for transfers between devices, per_device(): lax.all_gather(w_gate.astype(bf), 'dp', axis=0, tiled=True)  46.8 us
    all_gather x1, waiting for transfers between devices, per_device(): lax.all_gather(w_up.astype(bf), 'dp', axis=0, tiled=True)  42 us
    all_gather x1, waiting for transfers between devices, per_device(): lax.all_gather(w_down.astype(bf), 'dp', axis=1, tiled=True)  40.8 us
  transfers between devices with their start and end apart: 24, of which 22 were waited for; matrix products, arithmetic and copies ran while one was open for 17% of the time, Pallas kernels for 0%

commit v1 on v0

v1 whole, which is shorter than its diff:
```python
import functools
import math

import jax
import jax.numpy as jnp
from jax import lax
from jax.experimental import pallas as pl
from jax.experimental.pallas import tpu as pltpu
from jax.sharding import PartitionSpec as P

HEAD = 64
LANES = 128
NEG = -1e30
norm_eps = 1e-05
branch_scale = 1.4 / math.sqrt(40.0)
bf = jnp.bfloat16
f32 = jnp.float32
MB = 1 << 20


def rope_tables(positions):
    freq = 10000.0 ** (-(jnp.arange(HEAD // 2, dtype=f32) * 2.0 / HEAD))
    angle = positions.astype(f32)[:, None] * freq[None, :]
    cosine, sine = jnp.cos(angle), jnp.sin(angle)
    cos_t = jnp.concatenate([cosine] * 4, axis=1)
    sin_t = jnp.concatenate([-sine, sine, -sine, sine], axis=1)
    return cos_t, sin_t


def rope_block(u, cos_t, sin_t, sign):
    lane = lax.broadcasted_iota(jnp.int32, u.shape, 1)
    low = (lane % HEAD) < HEAD // 2
    partner = jnp.where(low, pltpu.roll(u, LANES - HEAD // 2, 1), pltpu.roll(u, HEAD // 2, 1))
    return u * cos_t + sign * (partner * sin_t)


def dot(a, b, dims=((1,), (0,))):
    return lax.dot_general(a, b, (dims, ((), ())), preferred_element_type=f32)


def proj_kernel(rotary, n_ref, w_ref, cos_ref, sin_ref, o_ref, y_ref):
    feats = o_ref.shape[1]
    y_ref[:, :feats] = dot(n_ref[...], w_ref[...])
    for first in range(0, feats, LANES):
        size = min(LANES, feats - first)
        y = y_ref[:, first : first + LANES]
        if rotary:
            y = rope_block(y, cos_ref[...], sin_ref[...], 1.0)
        o_ref[:, first : first + size] = y[:, :size].astype(bf)


def project(normed, weight, cos_t, sin_t, rotary):
    rows, depth = normed.shape
    feats = weight.shape[1]
    padded = -(-feats // LANES) * LANES
    vm = pl.BlockSpec(memory_space=pltpu.VMEM)
    return pl.pallas_call(
        functools.partial(proj_kernel, rotary),
        out_shape=jax.ShapeDtypeStruct((rows, feats), bf),
        in_specs=[vm] * 4,
        out_specs=vm,
        scratch_shapes=[pltpu.VMEM((rows, padded), f32)],
        compiler_params=pltpu.CompilerParams(vmem_limit_bytes=40 * MB),
        cost_estimate=pl.CostEstimate(
            flops=2 * rows * depth * feats, bytes_accessed=2 * (rows * depth + depth * feats + rows * feats), transcendentals=0
        ),
    )(normed, weight, cos_t, sin_t)


def fill_bias(qseg_ref, qpos_ref, kseg_ref, kpos_ref, bias_ref):
    kseg = kseg_ref[...]
    allowed = ((kseg == qseg_ref[...]) | (kseg == 0)) & (kpos_ref[...] <= qpos_ref[...])
    bias_ref[...] = jnp.where(allowed, 0.0, NEG)


def attn_fwd_kernel(parts, feats, *refs):
    qseg, qpos = refs[:2]
    kseg, kpos = refs[2 : 2 + parts], refs[2 + parts : 2 + 2 * parts]
    rest = refs[2 + 2 * parts :]
    q_ref = rest[0]
    k_refs, v_refs = rest[1 : 1 + parts], rest[1 + parts : 1 + 2 * parts]
    o_ref, lse_ref = rest[1 + 2 * parts : 3 + 2 * parts]
    bias = rest[3 + 2 * parts : 3 + 3 * parts]
    ot_ref = rest[3 + 3 * parts]
    blk = pl.program_id(0)

    @pl.when(blk == 0)
    def _():
        for i in range(parts):
            fill_bias(qseg, qpos, kseg[i], kpos[i], bias[i])

    left = feats - blk * LANES

    def one(sub):
        lane = lax.broadcasted_iota(jnp.int32, (1, LANES), 1)
        mine = (lane >= sub * HEAD) & (lane < (sub + 1) * HEAD)
        valid = lane < left
        q = jnp.where(mine, q_ref[...] * 0.125, 0.0).astype(bf)
        scores = []
        best = None
        for i in range(parts):
            k = jnp.where(valid, k_refs[i][...], 0.0).astype(bf)
            s = dot(k, q, ((1,), (1,))) + bias[i][...]
            scores.append(s)
            top = jnp.max(s, axis=0, keepdims=True)
            best = top if best is None else jnp.maximum(best, top)
        total, acc = None, None
        for i in range(parts):
            p = jnp.exp(scores[i] - best)
            t = jnp.sum(p, axis=0, keepdims=True)
            v = jnp.where(valid, v_refs[i][...], 0.0).astype(bf)
            a = dot(v, p.astype(bf), ((0,), (0,)))
            total = t if total is None else total + t
            acc = a if acc is None else acc + a
        ot_ref[sub * HEAD : (sub + 1) * HEAD, :] = acc[sub * HEAD : (sub + 1) * HEAD, :] / total
        lse_ref[0, sub : sub + 1, :] = best + jnp.log(total)

    for sub in range(LANES // HEAD):
        pl.when(sub * HEAD < left)(functools.partial(one, sub))
    o_ref[...] = ot_ref[...].T.astype(bf)


def attn_specs(rows, key_rows, feats):
    blocks = -(-feats // LANES)
    row = pl.BlockSpec((1, rows), lambda h: (0, 0))
    cols = [pl.BlockSpec((n, 1), lambda h: (0, 0)) for n in key_rows]
    q = pl.BlockSpec((rows, LANES), lambda h: (0, h))
    ks = [pl.BlockSpec((n, LANES), lambda h: (0, h)) for n in key_rows]
    lse = pl.BlockSpec((1, 8, rows), lambda h: (h, 0, 0))
    return blocks, row, cols, q, ks, lse


def attention_fwd(q, keys, values, q_meta, k_metas):
    rows, feats = q.shape
    parts = len(keys)
    key_rows = [k.shape[0] for k in keys]
    count = sum(key_rows)
    blocks, row, cols, qs, ks, lse = attn_specs(rows, key_rows, feats)
    return pl.pallas_call(
        functools.partial(attn_fwd_kernel, parts, feats),
        grid=(blocks,),
        out_shape=(
            jax.ShapeDtypeStruct((rows, feats), bf),
            jax.ShapeDtypeStruct((blocks, 8, rows), f32),
        ),
        in_specs=[row, row] + cols + cols + [qs] + ks + ks,
        out_specs=(qs, lse),
        scratch_shapes=[pltpu.VMEM((n, rows), f32) for n in key_rows] + [pltpu.VMEM((LANES, rows), f32)],
        compiler_params=pltpu.CompilerParams(vmem_limit_bytes=56 * MB),
        cost_estimate=pl.CostEstimate(
            flops=16 * rows * count * feats, bytes_accessed=4 * (rows + count) * feats, transcendentals=rows * count * feats // HEAD
        ),
    )(
        q_meta[0][None, :], q_meta[1][None, :],
        *[m[0][:, None] for m in k_metas], *[m[1][:, None] for m in k_metas],
        q, *keys, *values,
    )


def attn_bwd_kernel(parts, feats, *refs):
    qseg, qpos, qcos, qsin = refs[:4]
    refs = refs[4:]
    take = lambda n: (refs[:n], refs[n:])
    kseg, refs = take(parts)
    kpos, refs = take(parts)
    kcos, refs = take(parts)
    ksin, refs = take(parts)
    (q_ref, att_ref, do_ref, lse_ref), refs = take(4)
    k_refs, refs = take(parts)
    v_refs, refs = take(parts)
    (dq_ref,), refs = take(1)
    dk_refs, refs = take(parts)
    dv_refs, refs = take(parts)
    bias, refs = take(parts)
    dqt_ref, refs = refs[0], refs[1:]
    dka, refs = take(parts)
    dva, refs = take(parts)
    blk = pl.program_id(0)

    @pl.when(blk == 0)
    def _():
        for i in range(parts):
            fill_bias(qseg, qpos, kseg[i], kpos[i], bias[i])

    left = feats - blk * LANES
    valid = lax.broadcasted_iota(jnp.int32, (1, LANES), 1) < left
    prod = jnp.where(valid, do_ref[...].astype(f32) * att_ref[...].astype(f32), 0.0).T

    def one(sub):
        lane = lax.broadcasted_iota(jnp.int32, (1, LANES), 1)
        mine = (lane >= sub * HEAD) & (lane < (sub + 1) * HEAD)
        q = jnp.where(mine, q_ref[...] * 0.125, 0.0).astype(bf)
        do = jnp.where(mine, do_ref[...], 0.0).astype(bf)
        lse = lse_ref[0, sub : sub + 1, :]
        delta = jnp.sum(prod[sub * HEAD : (sub + 1) * HEAD, :], axis=0, keepdims=True)
        dqt = None
        for i in range(parts):
            k = jnp.where(valid, k_refs[i][...], 0.0).astype(bf)
            v = jnp.where(valid, v_refs[i][...], 0.0).astype(bf)
            p = jnp.exp(dot(k, q, ((1,), (1,))) + bias[i][...] - lse)
            dp = dot(v, do, ((1,), (1,)))
            ds = (p * (dp - delta)).astype(bf)
            dv = dot(p.astype(bf), do)
            dk = dot(ds, q)
            if sub == 0:
                dva[i][...] = dv
                dka[i][...] = dk
            else:
                dva[i][...] += dv
                dka[i][...] += dk
            d = dot(k, ds, ((0,), (0,)))
            dqt = d if dqt is None else dqt + d
        dqt_ref[sub * HEAD : (sub + 1) * HEAD, :] = dqt[sub * HEAD : (sub + 1) * HEAD, :] * 0.125

    for sub in range(LANES // HEAD):
        pl.when(sub * HEAD < left)(functools.partial(one, sub))
    dq_ref[...] = rope_block(dqt_ref[...].T, qcos[...], qsin[...], -1.0).astype(bf)
    for i in range(parts):
        dk_refs[i][...] = rope_block(dka[i][...], kcos[i][...], ksin[i][...], -1.0).astype(bf)
        dv_refs[i][...] = dva[i][...].astype(bf)


def attention_bwd(q, att, grad_att, lse, keys, values, q_meta, k_metas):
    rows, feats = q.shape
    parts = len(keys)
    key_rows = [k.shape[0] for k in keys]
    count = sum(key_rows)
    blocks, row, cols, qs, ks, lses = attn_specs(rows, key_rows, feats)
    tab = pl.BlockSpec((rows, LANES), lambda h: (0, 0))
    tabs = [pl.BlockSpec((n, LANES), lambda h: (0, 0)) for n in key_rows]
    out = pl.pallas_call(
        functools.partial(attn_bwd_kernel, parts, feats),
        grid=(blocks,),
        out_shape=(jax.ShapeDtypeStruct((rows, feats), bf),)
        + tuple(jax.ShapeDtypeStruct((n, feats), bf) for n in key_rows) * 2,
        in_specs=[row, row, tab, tab] + cols + cols + tabs + tabs + [qs, qs, qs, lses] + ks + ks,
        out_specs=(qs,) + tuple(ks) + tuple(ks),
        scratch_shapes=[pltpu.VMEM((n, rows), f32) for n in key_rows]
        + [pltpu.VMEM((LANES, rows), f32)]
        + [pltpu.VMEM((n, LANES), f32) for n in key_rows] * 2,
        compiler_params=pltpu.CompilerParams(vmem_limit_bytes=56 * MB),
        cost_estimate=pl.CostEstimate(
            flops=40 * rows * count * feats, bytes_accessed=10 * (rows + count) * feats, transcendentals=rows * count * feats // HEAD
        ),
    )(
        q_meta[0][None, :], q_meta[1][None, :], q_meta[2], q_meta[3],
        *[m[0][:, None] for m in k_metas], *[m[1][:, None] for m in k_metas],
        *[m[2] for m in k_metas], *[m[3] for m in k_metas],
        q, att, grad_att, lse, *keys, *values,
    )
    return out[0], out[1 : 1 + parts], out[1 + parts :]


def swap(n, bit):
    return [(i, i ^ bit) for i in range(n)]


def power_of_two(n):
    return n & (n - 1) == 0


def sum_all(value, sizes):
    for axis, n in sizes:
        if power_of_two(n):
            bit = 1
            while bit < n:
                value = value + lax.ppermute(value, axis, swap(n, bit))
                bit *= 2
        else:
            value = lax.psum(value, axis)
    return value


def line_scatter(chunk, n, me, axis):
    ahead, behind = None, None
    for step in range(n - 1):
        fore = chunk(jnp.clip(me + (n - 1 - step), 0, n - 1))
        back = chunk(jnp.clip(me - (n - 1 - step), 0, n - 1))
        if step > 0:
            fore, back = fore + ahead.astype(f32), back + behind.astype(f32)
        ahead = lax.ppermute(fore.astype(bf), axis, [(i, i + 1) for i in range(step + 1)])
        behind = lax.ppermute(back.astype(bf), axis, [(i, i - 1) for i in range(n - 1 - step, n)])
    own = chunk(me)
    if n == 1:
        return own
    return own + ahead.astype(f32) + behind.astype(f32)


def line_gather(own, n, me, axis):
    rows = own.shape[0]
    ahead, behind, fores, backs = own, own, [], []
    for step in range(n - 1):
        ahead = lax.ppermute(ahead, axis, [(i, i + 1) for i in range(step, n - 1)])
        behind = lax.ppermute(behind, axis, [(i, i - 1) for i in range(1, n - step)])
        fores.append(ahead)
        backs.append(behind)
    out = jnp.concatenate([own] * n, axis=0)
    for step in range(n - 1):
        out = lax.dynamic_update_slice_in_dim(out, fores[step] + backs[n - 2 - step], ((me + n - 1 - step) % n) * rows, 0)
    return out


def gather_weight(shard, n, me):
    if n != 4:
        return lax.all_gather(shard, "dp", axis=0, tiled=True)
    rows = shard.shape[0]
    far = lax.ppermute(shard, "dp", swap(4, 2))
    near = lax.ppermute(shard, "dp", swap(4, 1))
    cross = lax.ppermute(far, "dp", swap(4, 1))
    out = jnp.concatenate([shard] * n, axis=0)
    for bit, part in ((1, near), (2, far), (3, cross)):
        out = lax.dynamic_update_slice_in_dim(out, part, (me ^ bit) * rows, 0)
    return out


def relative_rows(array, n, me):
    rows = array.shape[0] // n
    return [lax.dynamic_slice_in_dim(array, (me ^ j) * rows, rows, 0) for j in range(n)]


def reduce_weight(left_t, right, n, me, n_ctx):
    if n == 4:
        b0, b1, b2, b3 = [dot(part, right).astype(bf) for part in left_t]
        r1 = lax.ppermute(b1, "dp", swap(4, 1))
        r3 = lax.ppermute(b3, "dp", swap(4, 1))
        a0 = b0.astype(f32) + r1.astype(f32)
        a2 = (b2.astype(f32) + r3.astype(f32)).astype(bf)
        total = a0 + lax.ppermute(a2, "dp", swap(4, 2)).astype(f32)
    else:
        total = lax.psum_scatter(dot(left_t, right).astype(bf), "dp", scatter_dimension=0, tiled=True).astype(f32)
    total = lax.optimization_barrier(total.astype(bf))
    if n_ctx == 2:
        return total.astype(f32) + lax.ppermute(total, "ctx", swap(2, 1)).astype(f32)
    return lax.psum(total, "ctx").astype(f32)


def per_device(
    n_dp, n_ctx, n_tp,
    tokens, segment, position, gain_attn, w_query, w_key, w_value, w_out, gain_ffn, w_gate, w_up, w_down, cotangent,
):
    dp, ctx, me = lax.axis_index("dp"), lax.axis_index("ctx"), lax.axis_index("tensor")
    rows = tokens.shape[0]
    piece = rows // n_tp
    mine = functools.partial(lax.dynamic_slice_in_dim, start_index=me * piece, slice_size=piece, axis=0)

    wk, wv, wq, wo, wg, wu, wd = [
        gather_weight(w, n_dp, dp)
        for w in (
            w_key.astype(bf), w_value.astype(bf), w_query.astype(bf), w_out.astype(bf).T,
            w_gate.astype(bf), w_up.astype(bf), w_down.T.astype(bf),
        )
    ]
    gains = lax.all_gather(jnp.stack([gain_attn, gain_ffn]).astype(bf), "dp", axis=1, tiled=True).astype(f32)
    gain1, gain2 = gains[0], gains[1]

    def meta(start, size):
        seg = lax.dynamic_slice_in_dim(segment, start, size)
        pos = lax.dynamic_slice_in_dim(position, start, size)
        return (seg, pos) + rope_tables(pos)

    q_meta = meta(ctx * rows, rows)
    cos_t, sin_t = q_meta[2:]
    inputs = tokens.astype(f32)
    scale1 = lax.rsqrt(jnp.mean(inputs * inputs, axis=-1, keepdims=True) + norm_eps)
    normed1 = (inputs * scale1 * gain1).astype(bf)
    keys = project(normed1, wk, cos_t, sin_t, True)
    values = project(normed1, wv, cos_t, sin_t, False)
    query = project(normed1, wq, cos_t, sin_t, True)
    if n_ctx == 2:
        trade = lambda a: lax.ppermute(a, "ctx", swap(2, 1))
        keys_all, values_all = [keys, trade(keys)], [values, trade(values)]
        k_metas = [q_meta, meta((1 - ctx) * rows, rows)]
    else:
        spread = lambda a: [lax.all_gather(a, "ctx", axis=0, tiled=True)]
        keys_all, values_all = spread(keys), spread(values)
        k_metas = [meta(0, segment.shape[0])]

    att, lse = attention_fwd(query, keys_all, values_all, q_meta, k_metas)

    def chunk_of(array):
        return lambda i: lax.dynamic_slice_in_dim(array, i * piece, piece, 0).astype(f32)

    mixed = line_scatter(chunk_of(dot(att, wo, ((1,), (1,)))), n_tp, me, "tensor")
    hidden_in = mine(inputs) + branch_scale * mixed
    scale2 = lax.rsqrt(jnp.mean(hidden_in * hidden_in, axis=-1, keepdims=True) + norm_eps)
    normed2 = line_gather((hidden_in * scale2 * gain2).astype(bf), n_tp, me, "tensor")

    grad_out = cotangent.astype(f32)
    grad_ffn = (branch_scale * grad_out).astype(bf)
    grad_hidden = dot(grad_ffn, wd)
    gate = dot(normed2, wg)
    up_val = dot(normed2, wu)
    sigma = jax.nn.sigmoid(gate)
    active = gate * sigma
    hidden = (active * up_val).astype(bf)
    grad_gate = (grad_hidden * up_val * sigma * (1.0 + gate * (1.0 - sigma))).astype(bf)
    grad_up = (grad_hidden * active).astype(bf)
    partial2 = dot(grad_gate, wg, ((1,), (1,))) + dot(grad_up, wu, ((1,), (1,)))
    grad_norm2 = line_scatter(chunk_of(partial2), n_tp, me, "tensor")
    part_g2 = jnp.sum(grad_norm2 * hidden_in * scale2, axis=0)
    grad_h = (
        mine(grad_out)
        + scale2 * gain2 * grad_norm2
        - hidden_in * scale2**3 * jnp.mean(hidden_in * gain2 * grad_norm2, axis=-1, keepdims=True)
    )
    grad_mixed = line_gather((branch_scale * grad_h).astype(bf), n_tp, me, "tensor")

    ffn_part = line_scatter(chunk_of(dot(hidden, wd, ((1,), (1,)))), n_tp, me, "tensor")
    output = hidden_in + branch_scale * ffn_part
    output = line_gather(lax.optimization_barrier(output.astype(bf)), n_tp, me, "tensor").astype(f32)

    grad_att = dot(grad_mixed, wo).astype(bf)
    grad_q, grad_ks, grad_vs = attention_bwd(query, att, grad_att, lse, keys_all, values_all, q_meta, k_metas)
    if n_ctx == 2:
        merge = lambda pair: (pair[0].astype(f32) + trade(pair[1]).astype(f32)).astype(bf)
    else:
        merge = lambda whole: lax.psum_scatter(whole[0], "ctx", scatter_dimension=0, tiled=True)
    grad_k, grad_v = merge(grad_ks), merge(grad_vs)

    partial1 = (
        dot(grad_q, wq, ((1,), (1,))) + dot(grad_k, wk, ((1,), (1,))) + dot(grad_v, wv, ((1,), (1,)))
    )
    grad_norm1 = line_scatter(chunk_of(partial1), n_tp, me, "tensor")
    my_in, my_scale = mine(inputs), mine(scale1)
    part_g1 = jnp.sum(grad_norm1 * my_in * my_scale, axis=0)
    grad_in = (
        grad_h
        + my_scale * gain1 * grad_norm1
        - my_in * my_scale**3 * jnp.mean(my_in * gain1 * grad_norm1, axis=-1, keepdims=True)
    )
    grad_in = line_gather(lax.optimization_barrier(grad_in.astype(bf)), n_tp, me, "tensor").astype(f32)
    gain_sum = sum_all(jnp.stack([part_g1, part_g2]), (("tensor", n_tp), ("ctx", n_ctx), ("dp", n_dp)))
    shard = gain_attn.shape[0]
    gain_sum = lax.dynamic_slice_in_dim(gain_sum, dp * shard, shard, 1)

    order = (lambda a: relative_rows(a.T, n_dp, dp)) if n_dp == 4 else (lambda a: a.T)
    n1_t, n2_t = order(normed1), order(normed2)
    da_t, df_t = order(grad_mixed), order(grad_ffn)
    reduce = lambda left, right: reduce_weight(left, right, n_dp, dp, n_ctx)
    sum_wd = reduce(df_t, hidden).T
    sum_wg = reduce(n2_t, grad_gate)
    sum_wu = reduce(n2_t, grad_up)
    sum_wo = reduce(da_t, att).T
    sum_wq = reduce(n1_t, grad_q)
    sum_wk = reduce(n1_t, grad_k)
    sum_wv = reduce(n1_t, grad_v)
    return (output, grad_in, gain_sum[0], sum_wq, sum_wk, sum_wv, sum_wo, gain_sum[1], sum_wg, sum_wu, sum_wd)


def solution(mesh):
    rows, col, row = P(("dp", "ctx"), None), P("dp", "tensor"), P("tensor", "dp")
    sizes = (mesh.shape["dp"], mesh.shape["ctx"], mesh.shape["tensor"])
    return jax.shard_map(
        functools.partial(per_device, *sizes),
        mesh=mesh,
        in_specs=(rows, P("dp"), P("dp"), P("dp"), col, col, col, row, P("dp"), col, col, row, rows),
        out_specs=(rows, rows, P("dp"), col, col, col, row, P("dp"), col, col, row),
        check_vma=False,
    )
```

time: 1480 us -> 1020 us (0.69)
  waiting for transfers between devices: 1010 us -> 337 us
  starting transfers between devices: 2.38 us -> 174 us
  matrix products: 235 us -> 157 us
  local copies, waits for them, and re-layouts: 30.5 us -> 108 us
  Pallas kernels: 0 us -> 58.6 us
  other arithmetic: 86.6 us -> 135 us
  blocking collectives: 85.2 us -> 38.8 us
  between operations: 18 us -> 2.72 us
    psum x3 -> x0, waiting for transfers between devices: 423 us -> none  [the longest x1 208 us: per_device(): lax.psum(jnp.dot(hidden, wd_b, preferred_element_type=f32).astype(jnp.bfl...]
    ppermute x0 -> x106, waiting for transfers between devices: none -> 337 us  [the longest x12 103 us: line_gather(): ahead = lax.ppermute(ahead, axis, [(i, i + 1) for i in range(step, n - 1)])]
    reduce_scatter x7 -> x0, waiting for transfers between devices: 296 us -> none  [the longest x1 69.2 us: per_device(): lax.psum_scatter(grad_wu.astype(jnp.bfloat16), ('dp', 'ctx'), scatter_dim...]
    all_gather x12 -> x0, waiting for transfers between devices: 287 us -> none  [the longest x1 46.8 us: per_device(): lax.all_gather(w_gate.astype(bf), 'dp', axis=0, tiled=True)]
    ppermute x0 -> x106, starting transfers between devices: none -> 174 us  [the longest x12 90.9 us: line_scatter(): lax.ppermute(back.astype(bf), axis, [(i, i - 1) for i in range(n - 1 - st...]
    dot_general x39, matrix products: 235 us -> 157 us  [dot(): return lax.dot_general(a, b, (dims, ((), ())), preferred_element_type=f32)]
    pallas_call x0 -> x5, Pallas kernels: none -> 58.6 us  [the longest x1 29.6 us: attention_bwd(): pl.pallas_call(functools.partial(attn_bwd_kernel, parts, feats), grid=(bl...]
    dynamic_update_slice x2 -> x21, local copies, waits for them, and re-layouts: 2.4 us -> 60.4 us  [gather_weight(): out = lax.dynamic_update_slice_in_dim(out, part, (me ^ bit) * rows, 0)]
  transfers between devices with their start and end apart: 24 -> 106, of which waited for: 22 -> 30; matrix products, arithmetic and copies ran while one was open for 17% -> 31% of each run, Pallas kernels for 0% -> 6%
where the time goes in v1:
time: 1020 us; the launch traced here: 1010 us
  waiting for transfers between devices  337 us (33%)
  starting transfers between devices  174 us (17%)
  matrix products  157 us (15%)
  other arithmetic  135 us (13%)
  local copies, waits for them, and re-layouts  108 us (11%)
  Pallas kernels  58.6 us (6%)
  blocking collectives  38.8 us (4%)
    dot_general x39, matrix products, dot(): return lax.dot_general(a, b, (dims, ((), ())), preferred_element_type=f32)  157 us
    ppermute x12, waiting for transfers between devices, line_gather(): ahead = lax.ppermute(ahead, axis, [(i, i + 1) for i in range(step, n - 1)])  103 us
    ppermute x12, starting transfers between devices, line_scatter(): lax.ppermute(back.astype(bf), axis, [(i, i - 1) for i in range(n - 1 - st...  90.9 us
    ppermute x7, waiting for transfers between devices, reduce_weight(): total = a0 + lax.ppermute(a2, 'dp', swap(4, 2)).astype(f32)  77.4 us
    ppermute x12, waiting for transfers between devices, line_scatter(): lax.ppermute(back.astype(bf), axis, [(i, i - 1) for i in range(n - 1 - st...  76.7 us
    dynamic_update_slice x21, local copies, waits for them, and re-layouts, gather_weight(): out = lax.dynamic_update_slice_in_dim(out, part, (me ^ bit) * rows, 0)  60.4 us
    all_gather x1, blocking collectives, per_device(): lax.all_gather(jnp.stack([gain_attn, gain_ffn]).astype(bf), 'dp', axis=1,...  38.8 us
    pallas_call x1, Pallas kernels, attention_bwd(): pl.pallas_call(functools.partial(attn_bwd_kernel, parts, feats), grid=(bl...  29.6 us
  transfers between devices with their start and end apart: 106, of which 30 were waited for; matrix products, arithmetic and copies ran while one was open for 31% of the time, Pallas kernels for 6%

profile of v1, /device:TPU:26, one launch (start us, length us, event | category | flops | bytes accessed | tf_op | source)
XLA Modules:
  0.0 1010.5 jit_solution(10175440331946624071)
XLA Ops:
  16.1 38.8 %all-gather = bf16[4,576,2]{1,2,0:T(2,128)(2,1)S(1)} all-gather(bf16[1,576,2]{1,2,0:T(2,128)(2,1)S(1)} %maximum_bitcast_fusion), channel_id=1, replica_groups=mesh['dp'=4,'ctx'=2,'tensor'=4] {'dp'}, dimensions={0}, use_global_device_ids=true | all-gather | bytes 11520 | tf_op jit(solution)/shard_map/all_gather | solution.py:353
  59.1 7.2 pad_maximum_fusion.2
  88.8 6.7 collective-permute-done.12
  124.7 6.0 concatenate.50
  135.8 8.3 dynamic_update_slice.108
  144.1 8.1 dynamic_update_slice.109
  157.3 9.1 dynamic_update_slice.110
  179.8 18.9 %shard_map.215 = (bf16[640,576]{1,0:T(8,128)(2,1)}, f32[5,8,640]{2,1,0:T(8,128)}) custom-call(s32[1,640]{1,0:T(1,128)} %broadcast_in_dim.12.refs_0_, s32[1,640]{1,0:T(1,128)} %broadcast_in_dim.13.refs_1_, s32[640,1]{1,0:T(8,128)} %broadcast_in_dim.18.refs_2_.refs_4_, s32[640,1]{1,0:T(8,128)} %broadcast_in_dim.19.refs_3_.refs_5_, ...), custom_call_target="tpu_custom_call" | custom-call | flops 7549747200 | bytes 4423680 | tf_op jit(solution)/shard_map/pallas_call | solution.py:139
  217.2 11.2 %collective-permute-done.17 = bf16[160,2304]{1,0:T(8,128)(2,1)} collective-permute-done((bf16[160,2304]{1,0:T(8,128)(2,1)}, bf16[160,2304]{1,0:T(8,128)(2,1)}, u32[]{:S(2)}, u32[]{:S(2)}) %collective-permute-start.17) | collective-permute-done | bytes 737312 | tf_op jit(solution)/shard_map/ppermute | solution.py:282
  232.4 19.3 %collective-permute-start.18 = (bf16[160,2304]{1,0:T(8,128)(2,1)}, bf16[160,2304]{1,0:T(8,128)(2,1)}, u32[]{:S(2)}, u32[]{:S(2)}) collective-permute-start(bf16[160,2304]{1,0:T(8,128)(2,1)} %get-tuple-element.113), channel_id=1, source_target_pairs={{2,1},{3,2},{6,5},{7,6},{10,9},{11,10},{14,13},{15,14},{18,17},{19... | collective-permute-start | bytes 2211848 | tf_op jit(solution)/shard_map/ppermute | solution.py:282
  257.6 4.9 convert_element_type.551
  285.2 21.5 %collective-permute-done.27 = bf16[576,1440]{1,0:T(8,128)(2,1)S(1)} collective-permute-done((bf16[576,1440]{1,0:T(8,128)(2,1)}, bf16[576,1440]{1,0:T(8,128)(2,1)S(1)}, u32[]{:S(2)}, u32[]{:S(2)}) %collective-permute-start.27) | collective-permute-done | bytes 1658912 | tf_op jit(solution)/shard_map/ppermute | solution.py:307
  320.0 10.1 %collective-permute-done.21 = bf16[160,2304]{1,0:T(8,128)(2,1)S(1)} collective-permute-done((bf16[160,2304]{1,0:T(8,128)(2,1)S(1)}, bf16[160,2304]{1,0:T(8,128)(2,1)S(1)}, u32[]{:S(2)}, u32[]{:S(2)}) %collective-permute-start.21) | collective-permute-done | bytes 737312 | tf_op jit(solution)/shard_map/ppermute | solution.py:294
  331.7 10.3 %fusion.61 = f32[640,1440]{0,1:T(8,128)} fusion(bf16[2304,1440]{1,0:T(8,128)(2,1)} %constant_dynamic-update-slice_fusion, bf16[640,2304]{1,0:T(8,128)(2,1)S(1)} %copy-done.18), kind=kOutput, calls=%fused_computation.225 | convolution fusion | flops 4251156480 | bytes 13271040 | tf_op jit(solution)/shard_map/dot_general | solution.py:38
  345.9 17.8 %collective-permute-done.24 = bf16[160,2304]{1,0:T(8,128)(2,1)S(1)} collective-permute-done((bf16[160,2304]{1,0:T(8,128)(2,1)S(1)}, bf16[160,2304]{1,0:T(8,128)(2,1)S(1)}, u32[]{:S(2)}, u32[]{:S(2)}) %collective-permute-start.24) | collective-permute-done | bytes 737312 | tf_op jit(solution)/shard_map/ppermute | solution.py:293
  366.7 15.8 %collective-permute-done.25 = bf16[160,2304]{1,0:T(8,128)(2,1)S(1)} collective-permute-done((bf16[160,2304]{1,0:T(8,128)(2,1)S(1)}, bf16[160,2304]{1,0:T(8,128)(2,1)S(1)}, u32[]{:S(2)}, u32[]{:S(2)}) %collective-permute-start.25) | collective-permute-done | bytes 737312 | tf_op jit(solution)/shard_map/ppermute | solution.py:293
  382.8 7.4 fusion.66
  390.2 14.8 %multiply_convert_fusion.3 = (bf16[640,1440]{0,1:T(8,128)(2,1)S(1)}, bf16[640,1440]{0,1:T(8,128)(2,1)}, bf16[640,1440]{0,1:T(8,128)(2,1)}) fusion(f32[640,1440]{0,1:T(8,128)} %fusion.61, f32[640,1440]{0,1:T(8,128)} %fusion.66, bf16[640,2304]{1,0:T(8,128)(2,1)S(1)} %add_dynamic-update-slice_fusion.9, bf16[2304,1440]{1,0:T(8,128)(2,1)} %constant_dynamic-update-slice_fusion.6), kind=kOutput, calls=%fused_computation.9 | convolution fusion | flops 4260556800 | bytes 22487040 | tf_op jit(solution)/shard_map/dot_general | solution.py:38
  415.6 7.4 fusion.68
  438.5 9.5 convolution_add_fusion
  450.6 7.2 fusion.67
  459.6 5.0 convolution_convert_fusion
  475.3 11.5 %collective-permute-done.38 = bf16[160,2304]{1,0:T(8,128)(2,1)S(1)} collective-permute-done((bf16[160,2304]{1,0:T(8,128)(2,1)S(1)}, bf16[160,2304]{1,0:T(8,128)(2,1)S(1)}, u32[]{:S(2)}, u32[]{:S(2)}) %collective-permute-start.38) | collective-permute-done | bytes 737312 | tf_op jit(solution)/shard_map/ppermute | solution.py:282
  486.8 17.8 %collective-permute-start.51 = (bf16[160,2304]{1,0:T(8,128)(2,1)S(1)}, bf16[160,2304]{1,0:T(8,128)(2,1)S(1)}, u32[]{:S(2)}, u32[]{:S(2)}) collective-permute-start(bf16[160,2304]{1,0:T(8,128)(2,1)S(1)} %get-tuple-element.105), channel_id=1, source_target_pairs={{2,1},{3,2},{6,5},{7,6},{10,9},{11,10},{14,13},{15,14},{18,17},{19... | collective-permute-start | bytes 2211848 | tf_op jit(solution)/shard_map/ppermute | solution.py:282
  514.4 7.1 collective-permute-done.51
  523.1 9.6 collective-permute-done.39
  541.9 5.0 add_convert_fusion.1
  546.9 7.1 collective-permute-done.52
  555.7 8.1 collective-permute-done.40
  567.7 11.5 %collective-permute-done.96 = bf16[576,1440]{1,0:T(8,128)(2,1)} collective-permute-done((bf16[576,1440]{1,0:T(8,128)(2,1)}, bf16[576,1440]{1,0:T(8,128)(2,1)}, u32[]{:S(2)}, u32[]{:S(2)}) %collective-permute-start.96) | collective-permute-done | bytes 1658912 | tf_op jit(solution)/shard_map/ppermute | solution.py:328
  589.2 27.9 %collective-permute-done.100 = bf16[576,1440]{1,0:T(8,128)(2,1)S(1)} collective-permute-done((bf16[576,1440]{1,0:T(8,128)(2,1)}, bf16[576,1440]{1,0:T(8,128)(2,1)S(1)}, u32[]{:S(2)}, u32[]{:S(2)}) %collective-permute-start.100) | collective-permute-done | bytes 1658912 | tf_op jit(solution)/shard_map/ppermute | solution.py:328
  618.3 29.7 %collective-permute-done.104 = bf16[576,1440]{1,0:T(8,128)(2,1)S(1)} collective-permute-done((bf16[576,1440]{1,0:T(8,128)(2,1)}, bf16[576,1440]{1,0:T(8,128)(2,1)S(1)}, u32[]{:S(2)}, u32[]{:S(2)}) %collective-permute-start.104) | collective-permute-done | bytes 1658912 | tf_op jit(solution)/shard_map/ppermute | solution.py:328
  665.3 18.0 %collective-permute-done.45 = bf16[160,2304]{1,0:T(8,128)(2,1)} collective-permute-done((bf16[160,2304]{1,0:T(8,128)(2,1)S(1)}, bf16[160,2304]{1,0:T(8,128)(2,1)}, u32[]{:S(2)}, u32[]{:S(2)}) %collective-permute-start.45) | collective-permute-done | bytes 737312 | tf_op jit(solution)/shard_map/ppermute | solution.py:293
  686.1 16.5 %collective-permute-done.57 = bf16[160,2304]{1,0:T(8,128)(2,1)S(1)} collective-permute-done((bf16[160,2304]{1,0:T(8,128)(2,1)S(1)}, bf16[160,2304]{1,0:T(8,128)(2,1)S(1)}, u32[]{:S(2)}, u32[]{:S(2)}) %collective-permute-start.57) | collective-permute-done | bytes 737312 | tf_op jit(solution)/shard_map/ppermute | solution.py:293
  707.4 16.1 %collective-permute-done.105 = bf16[576,1440]{1,0:T(8,128)(2,1)S(1)} collective-permute-done((bf16[576,1440]{1,0:T(8,128)(2,1)S(1)}, bf16[576,1440]{1,0:T(8,128)(2,1)S(1)}, u32[]{:S(2)}, u32[]{:S(2)}) %collective-permute-start.105) | collective-permute-done | bytes 1658912 | tf_op jit(solution)/shard_map/ppermute | solution.py:333
  733.5 29.6 %shard_map.216 = (bf16[640,576]{1,0:T(8,128)(2,1)}, bf16[640,576]{1,0:T(8,128)(2,1)}, bf16[640,576]{1,0:T(8,128)(2,1)}, bf16[640,576]{1,0:T(8,128)(2,1)}, bf16[640,576]{1,0:T(8,128)(2,1)}) custom-call(s32[1,640]{1,0:T(1,128)} %broadcast_in_dim.12.refs_0_, s32[1,640]{1,0:T(1,128)} %broadcast_in_dim.13.refs_1_, f32[640,128]{1,0:T(8,128)} %copy-done.5, ...), custom_call_target="tpu_custom_call" | custom-call | flops 18874368000 | bytes 11059200 | tf_op jit(solution)/shard_map/pallas_call | solution.py:231
  775.8 5.1 fusion.69
  807.5 6.5 collective-permute-done.59
  823.9 5.0 fusion.70
  832.8 7.7 add_add_fusion
  863.6 8.3 collective-permute-done.92
  871.9 11.4 %collective-permute-start.65 = (bf16[160,2304]{1,0:T(8,128)(2,1)S(1)}, bf16[160,2304]{1,0:T(8,128)(2,1)S(1)}, u32[]{:S(2)}, u32[]{:S(2)}) collective-permute-start(bf16[160,2304]{1,0:T(8,128)(2,1)S(1)} %get-tuple-element.101), channel_id=1, source_target_pairs={{2,1},{3,2},{6,5},{7,6},{10,9},{11,10},{14,13},{15,14},{18,17},{19... | collective-permute-start | bytes 2211848 | tf_op jit(solution)/shard_map/ppermute | solution.py:282
  887.7 11.6 %collective-permute-done.65 = bf16[160,2304]{1,0:T(8,128)(2,1)S(1)} collective-permute-done((bf16[160,2304]{1,0:T(8,128)(2,1)S(1)}, bf16[160,2304]{1,0:T(8,128)(2,1)S(1)}, u32[]{:S(2)}, u32[]{:S(2)}) %collective-permute-start.65) | collective-permute-done | bytes 737312 | tf_op jit(solution)/shard_map/ppermute | solution.py:282
  903.1 13.5 %collective-permute-start.66 = (bf16[160,2304]{1,0:T(8,128)(2,1)}, bf16[160,2304]{1,0:T(8,128)(2,1)S(1)}, u32[]{:S(2)}, u32[]{:S(2)}) collective-permute-start(bf16[160,2304]{1,0:T(8,128)(2,1)} %add_convert_fusion.16), channel_id=1, source_target_pairs={{1,0},{2,1},{3,2},{5,4},{6,5},{7,6},{9,8},{10,9},{11,10},{13,12},{... | collective-permute-start | bytes 2211848 | tf_op jit(solution)/shard_map/ppermute | solution.py:282
  924.8 7.8 collective-permute-done.66
  948.3 8.5 collective-permute-done.68
  972.9 13.8 %collective-permute-done.71 = bf16[160,2304]{1,0:T(8,128)(2,1)S(1)} collective-permute-done((bf16[160,2304]{1,0:T(8,128)(2,1)S(1)}, bf16[160,2304]{1,0:T(8,128)(2,1)S(1)}, u32[]{:S(2)}, u32[]{:S(2)}) %collective-permute-start.71) | collective-permute-done | bytes 737312 | tf_op jit(solution)/shard_map/ppermute | solution.py:293
  988.4 18.5 %collective-permute-done.72 = bf16[160,2304]{1,0:T(8,128)(2,1)S(1)} collective-permute-done((bf16[160,2304]{1,0:T(8,128)(2,1)S(1)}, bf16[160,2304]{1,0:T(8,128)(2,1)S(1)}, u32[]{:S(2)}, u32[]{:S(2)}) %collective-permute-start.72) | collective-permute-done | bytes 737312 | tf_op jit(solution)/shard_map/ppermute | solution.py:293
  (511 shorter events, 409.1 us)
Async XLA Ops:
  3.1 73.4 %collective-permute-start.3 = (bf16[576,576]{1,0:T(8,128)(2,1)}, bf16[576,576]{1,0:T(8,128)(2,1)}, u32[]{:S(2)}, u32[]{:S(2)}) collective-permute-start(bf16[576,576]{1,0:T(8,128)(2,1)} %convert_element_type.516), channel_id=1, source_target_pairs={{0,8},{8,0},{16,24},{24,16},{1,9},{9,1},{17,25},{25,17},{2,10},{10... | collective-permute-start | bytes 1990664 | tf_op jit(solution)/shard_map/ppermute | solution.py:308
  3.1 74.0 %collective-permute-start.4 = (bf16[576,576]{1,0:T(8,128)(2,1)}, bf16[576,576]{1,0:T(8,128)(2,1)}, u32[]{:S(2)}, u32[]{:S(2)}) collective-permute-start(bf16[576,576]{1,0:T(8,128)(2,1)} %convert_element_type.516), channel_id=1, source_target_pairs={{0,16},{8,24},{16,0},{24,8},{1,17},{9,25},{17,1},{25,9},{2,18},{10... | collective-permute-start | bytes 1990664 | tf_op jit(solution)/shard_map/ppermute | solution.py:307
  4.6 79.4 %collective-permute-start.7 = (bf16[576,576]{1,0:T(8,128)(2,1)}, bf16[576,576]{1,0:T(8,128)(2,1)}, u32[]{:S(2)}, u32[]{:S(2)}) collective-permute-start(bf16[576,576]{1,0:T(8,128)(2,1)} %convert_element_type.517), channel_id=1, source_target_pairs={{0,8},{8,0},{16,24},{24,16},{1,9},{9,1},{17,25},{25,17},{2,10},{10... | collective-permute-start | bytes 1990664 | tf_op jit(solution)/shard_map/ppermute | solution.py:308
  4.8 74.5 %collective-permute-start.8 = (bf16[576,576]{1,0:T(8,128)(2,1)}, bf16[576,576]{1,0:T(8,128)(2,1)}, u32[]{:S(2)}, u32[]{:S(2)}) collective-permute-start(bf16[576,576]{1,0:T(8,128)(2,1)} %convert_element_type.517), channel_id=1, source_target_pairs={{0,16},{8,24},{16,0},{24,8},{1,17},{9,25},{17,1},{25,9},{2,18},{10... | collective-permute-start | bytes 1990664 | tf_op jit(solution)/shard_map/ppermute | solution.py:307
  7.3 81.0 %collective-permute-start.1 = (bf16[576,576]{1,0:T(8,128)(2,1)}, bf16[576,576]{1,0:T(8,128)(2,1)}, u32[]{:S(2)}, u32[]{:S(2)}) collective-permute-start(bf16[576,576]{1,0:T(8,128)(2,1)} %convert_element_type.514), channel_id=1, source_target_pairs={{0,16},{8,24},{16,0},{24,8},{1,17},{9,25},{17,1},{25,9},{2,18},{10... | collective-permute-start | bytes 1990664 | tf_op jit(solution)/shard_map/ppermute | solution.py:307
  84.0 33.1 %collective-permute-start.11 = (bf16[576,576]{0,1:T(8,128)(2,1)}, bf16[576,576]{0,1:T(8,128)(2,1)}, u32[]{:S(2)}, u32[]{:S(2)}) collective-permute-start(bf16[576,576]{0,1:T(8,128)(2,1)} %convert_bitcast_fusion.1), channel_id=1, source_target_pairs={{0,8},{8,0},{16,24},{24,16},{1,9},{9,1},{17,25},{25,17},{2,10},{10... | collective-permute-start | bytes 1990664 | tf_op jit(solution)/shard_map/ppermute | solution.py:308
  88.3 63.9 %collective-permute-start = (bf16[576,576]{1,0:T(8,128)(2,1)}, bf16[576,576]{1,0:T(8,128)(2,1)}, u32[]{:S(2)}, u32[]{:S(2)}) collective-permute-start(bf16[576,576]{1,0:T(8,128)(2,1)} %convert_element_type.514), channel_id=1, source_target_pairs={{0,8},{8,0},{16,24},{24,16},{1,9},{9,1},{17,25},{25,17},{2,10},{10... | collective-permute-start | bytes 1990664 | tf_op jit(solution)/shard_map/ppermute | solution.py:308
  95.6 70.9 %collective-permute-start.2 = (bf16[576,576]{1,0:T(8,128)(2,1)}, bf16[576,576]{1,0:T(8,128)(2,1)}, u32[]{:S(2)}, u32[]{:S(2)}) collective-permute-start(bf16[576,576]{1,0:T(8,128)(2,1)} %collective-permute-done.1), channel_id=1, source_target_pairs={{0,8},{8,0},{16,24},{24,16},{1,9},{9,1},{17,25},{25,17},{2,10},{10... | collective-permute-start | bytes 1990664 | tf_op jit(solution)/shard_map/ppermute | solution.py:309
  95.6 60.8 %collective-permute-start.13 = (bf16[576,576]{0,1:T(8,128)(2,1)}, bf16[576,576]{0,1:T(8,128)(2,1)}, u32[]{:S(2)}, u32[]{:S(2)}) collective-permute-start(bf16[576,576]{0,1:T(8,128)(2,1)} %collective-permute-done.12), channel_id=1, source_target_pairs={{0,8},{8,0},{16,24},{24,16},{1,9},{9,1},{17,25},{25,17},{2,10},{10... | collective-permute-start | bytes 1990664 | tf_op jit(solution)/shard_map/ppermute | solution.py:309
  105.0 70.2 %collective-permute-start.6 = (bf16[640,576]{0,1:T(8,128)(2,1)}, bf16[640,576]{0,1:T(8,128)(2,1)}, u32[]{:S(2)}, u32[]{:S(2)}) collective-permute-start(bf16[640,576]{0,1:T(8,128)(2,1)} %copy.70), channel_id=1, source_target_pairs={{0,4},{4,0},{1,5},{5,1},{2,6},{6,2},{3,7},{7,3},{8,12},{12,8},{9,1... | collective-permute-start | bytes 2211848 | tf_op jit(solution)/shard_map/ppermute | solution.py:370
  117.1 60.4 %collective-permute-start.10 = (bf16[640,576]{0,1:T(8,128)(2,1)}, bf16[640,576]{0,1:T(8,128)(2,1)}, u32[]{:S(2)}, u32[]{:S(2)}) collective-permute-start(bf16[640,576]{0,1:T(8,128)(2,1)} %copy.71), channel_id=1, source_target_pairs={{0,4},{4,0},{1,5},{5,1},{2,6},{6,2},{3,7},{7,3},{8,12},{12,8},{9,1... | collective-permute-start | bytes 2211848 | tf_op jit(solution)/shard_map/ppermute | solution.py:370
  152.2 113.1 %collective-permute-start.32 = (bf16[576,1440]{1,0:T(8,128)(2,1)}, bf16[576,1440]{1,0:T(8,128)(2,1)}, u32[]{:S(2)}, u32[]{:S(2)}) collective-permute-start(bf16[576,1440]{1,0:T(8,128)(2,1)} %convert_bitcast_fusion), channel_id=1, source_target_pairs={{0,8},{8,0},{16,24},{24,16},{1,9},{9,1},{17,25},{25,17},{2,10},{10... | collective-permute-start | bytes 4976648 | tf_op jit(solution)/shard_map/ppermute | solution.py:308
  156.4 115.3 %collective-permute-start.33 = (bf16[576,1440]{1,0:T(8,128)(2,1)}, bf16[576,1440]{1,0:T(8,128)(2,1)}, u32[]{:S(2)}, u32[]{:S(2)}) collective-permute-start(bf16[576,1440]{1,0:T(8,128)(2,1)} %convert_bitcast_fusion), channel_id=1, source_target_pairs={{0,16},{8,24},{16,0},{24,8},{1,17},{9,25},{17,1},{25,9},{2,18},{10... | collective-permute-start | bytes 4976648 | tf_op jit(solution)/shard_map/ppermute | solution.py:307
  166.5 112.6 %collective-permute-start.29 = (bf16[576,1440]{1,0:T(8,128)(2,1)}, bf16[576,1440]{1,0:T(8,128)(2,1)}, u32[]{:S(2)}, u32[]{:S(2)}) collective-permute-start(bf16[576,1440]{1,0:T(8,128)(2,1)} %copy-done.20), channel_id=1, source_target_pairs={{0,8},{8,0},{16,24},{24,16},{1,9},{9,1},{17,25},{25,17},{2,10},{10... | collective-permute-start | bytes 4976648 | tf_op jit(solution)/shard_map/ppermute | solution.py:308
  228.4 53.6 %collective-permute-start.30 = (bf16[576,1440]{1,0:T(8,128)(2,1)}, bf16[576,1440]{1,0:T(8,128)(2,1)}, u32[]{:S(2)}, u32[]{:S(2)}) collective-permute-start(bf16[576,1440]{1,0:T(8,128)(2,1)} %copy-done.20), channel_id=1, source_target_pairs={{0,16},{8,24},{16,0},{24,8},{1,17},{9,25},{17,1},{25,9},{2,18},{10... | collective-permute-start | bytes 4976648 | tf_op jit(solution)/shard_map/ppermute | solution.py:307
  232.4 36.1 %collective-permute-start.18 = (bf16[160,2304]{1,0:T(8,128)(2,1)}, bf16[160,2304]{1,0:T(8,128)(2,1)}, u32[]{:S(2)}, u32[]{:S(2)}) collective-permute-start(bf16[160,2304]{1,0:T(8,128)(2,1)} %get-tuple-element.113), channel_id=1, source_target_pairs={{2,1},{3,2},{6,5},{7,6},{10,9},{11,10},{14,13},{15,14},{18,17},{19... | collective-permute-start | bytes 2211848 | tf_op jit(solution)/shard_map/ppermute | solution.py:282
  265.3 41.5 %collective-permute-start.27 = (bf16[576,1440]{1,0:T(8,128)(2,1)}, bf16[576,1440]{1,0:T(8,128)(2,1)S(1)}, u32[]{:S(2)}, u32[]{:S(2)}) collective-permute-start(bf16[576,1440]{1,0:T(8,128)(2,1)} %convert_element_type.532), channel_id=1, source_target_pairs={{0,16},{8,24},{16,0},{24,8},{1,17},{9,25},{17,1},{25,9},{2,18},{10... | collective-permute-start | bytes 4976648 | tf_op jit(solution)/shard_map/ppermute | solution.py:307
  268.5 38.3 %collective-permute-start.16 = (bf16[160,2304]{1,0:T(8,128)(2,1)S(1)}, bf16[160,2304]{1,0:T(8,128)(2,1)S(1)}, u32[]{:S(2)}, u32[]{:S(2)}) collective-permute-start(bf16[160,2304]{1,0:T(8,128)(2,1)S(1)} %copy-done.39), channel_id=1, source_target_pairs={{0,1},{1,2},{2,3},{4,5},{5,6},{6,7},{8,9},{9,10},{10,11},{12,13},{... | collective-permute-start | bytes 2211848 | tf_op jit(solution)/shard_map/ppermute | solution.py:281
  271.7 35.6 %collective-permute-start.19 = (bf16[160,2304]{1,0:T(8,128)(2,1)S(1)}, bf16[160,2304]{1,0:T(8,128)(2,1)S(1)}, u32[]{:S(2)}, u32[]{:S(2)}) collective-permute-start(bf16[160,2304]{1,0:T(8,128)(2,1)S(1)} %add_convert_fusion.29), channel_id=1, source_target_pairs={{1,0},{2,1},{3,2},{5,4},{6,5},{7,6},{9,8},{10,9},{11,10},{13,12},{... | collective-permute-start | bytes 2211848 | tf_op jit(solution)/shard_map/ppermute | solution.py:282
  279.1 35.2 %collective-permute-start.26 = (bf16[576,1440]{1,0:T(8,128)(2,1)S(1)}, bf16[576,1440]{1,0:T(8,128)(2,1)S(1)}, u32[]{:S(2)}, u32[]{:S(2)}) collective-permute-start(bf16[576,1440]{1,0:T(8,128)(2,1)S(1)} %copy-done.22), channel_id=1, source_target_pairs={{0,8},{8,0},{16,24},{24,16},{1,9},{9,1},{17,25},{25,17},{2,10},{10... | collective-permute-start | bytes 4976648 | tf_op jit(solution)/shard_map/ppermute | solution.py:308
  282.0 35.0 %collective-permute-start.34 = (bf16[576,1440]{1,0:T(8,128)(2,1)}, bf16[576,1440]{1,0:T(8,128)(2,1)S(1)}, u32[]{:S(2)}, u32[]{:S(2)}) collective-permute-start(bf16[576,1440]{1,0:T(8,128)(2,1)} %collective-permute-done.33), channel_id=1, source_target_pairs={{0,8},{8,0},{16,24},{24,16},{1,9},{9,1},{17,25},{25,17},{2,10},{10... | collective-permute-start | bytes 4976648 | tf_op jit(solution)/shard_map/ppermute | solution.py:309
  306.8 37.2 %collective-permute-start.31 = (bf16[576,1440]{1,0:T(8,128)(2,1)}, bf16[576,1440]{1,0:T(8,128)(2,1)S(1)}, u32[]{:S(2)}, u32[]{:S(2)}) collective-permute-start(bf16[576,1440]{1,0:T(8,128)(2,1)} %collective-permute-done.30), channel_id=1, source_target_pairs={{0,8},{8,0},{16,24},{24,16},{1,9},{9,1},{17,25},{25,17},{2,10},{10... | collective-permute-start | bytes 4976648 | tf_op jit(solution)/shard_map/ppermute | solution.py:309
  306.8 37.5 %collective-permute-start.28 = (bf16[576,1440]{1,0:T(8,128)(2,1)S(1)}, bf16[576,1440]{1,0:T(8,128)(2,1)S(1)}, u32[]{:S(2)}, u32[]{:S(2)}) collective-permute-start(bf16[576,1440]{1,0:T(8,128)(2,1)S(1)} %collective-permute-done.27), channel_id=1, source_target_pairs={{0,8},{8,0},{16,24},{24,16},{1,9},{9,1},{17,25},{25,17},{2,10},{10... | collective-permute-start | bytes 4976648 | tf_op jit(solution)/shard_map/ppermute | solution.py:309
  473.4 81.3 %collective-permute-start.94 = (bf16[576,1440]{1,0:T(8,128)(2,1)}, bf16[576,1440]{1,0:T(8,128)(2,1)S(1)}, u32[]{:S(2)}, u32[]{:S(2)}) collective-permute-start(bf16[576,1440]{1,0:T(8,128)(2,1)} %convolution_convert_fusion.10), channel_id=1, source_target_pairs={{0,8},{8,0},{16,24},{24,16},{1,9},{9,1},{17,25},{25,17},{2,10},{10... | collective-permute-start | bytes 4976648 | tf_op jit(solution)/shard_map/ppermute | solution.py:324
  474.1 34.1 %collective-permute-start.99 = (bf16[576,1440]{1,0:T(8,128)(2,1)S(1)}, bf16[576,1440]{1,0:T(8,128)(2,1)S(1)}, u32[]{:S(2)}, u32[]{:S(2)}) collective-permute-start(bf16[576,1440]{1,0:T(8,128)(2,1)S(1)} %copy-done.62), channel_id=1, source_target_pairs={{0,8},{8,0},{16,24},{24,16},{1,9},{9,1},{17,25},{25,17},{2,10},{10... | collective-permute-start | bytes 4976648 | tf_op jit(solution)/shard_map/ppermute | solution.py:325
  486.8 50.5 %collective-permute-start.103 = (bf16[576,1440]{1,0:T(8,128)(2,1)}, bf16[576,1440]{1,0:T(8,128)(2,1)}, u32[]{:S(2)}, u32[]{:S(2)}) collective-permute-start(bf16[576,1440]{1,0:T(8,128)(2,1)} %convolution_convert_fusion), channel_id=1, source_target_pairs={{0,8},{8,0},{16,24},{24,16},{1,9},{9,1},{17,25},{25,17},{2,10},{10... | collective-permute-start | bytes 4976648 | tf_op jit(solution)/shard_map/ppermute | solution.py:325
  486.8 34.7 %collective-permute-start.51 = (bf16[160,2304]{1,0:T(8,128)(2,1)S(1)}, bf16[160,2304]{1,0:T(8,128)(2,1)S(1)}, u32[]{:S(2)}, u32[]{:S(2)}) collective-permute-start(bf16[160,2304]{1,0:T(8,128)(2,1)S(1)} %get-tuple-element.105), channel_id=1, source_target_pairs={{2,1},{3,2},{6,5},{7,6},{10,9},{11,10},{14,13},{15,14},{18,17},{19... | collective-permute-start | bytes 2211848 | tf_op jit(solution)/shard_map/ppermute | solution.py:282
  505.1 32.6 %collective-permute-start.49 = (bf16[160,2304]{1,0:T(8,128)(2,1)S(1)}, bf16[160,2304]{1,0:T(8,128)(2,1)S(1)}, u32[]{:S(2)}, u32[]{:S(2)}) collective-permute-start(bf16[160,2304]{1,0:T(8,128)(2,1)S(1)} %get-tuple-element.104), channel_id=1, source_target_pairs={{0,1},{1,2},{2,3},{4,5},{5,6},{6,7},{8,9},{9,10},{10,11},{12,13},{... | collective-permute-start | bytes 2211848 | tf_op jit(solution)/shard_map/ppermute | solution.py:281
  521.5 33.8 %collective-permute-start.37 = (bf16[160,2304]{1,0:T(8,128)(2,1)S(1)}, bf16[160,2304]{1,0:T(8,128)(2,1)S(1)}, u32[]{:S(2)}, u32[]{:S(2)}) collective-permute-start(bf16[160,2304]{1,0:T(8,128)(2,1)S(1)} %get-tuple-element.108), channel_id=1, source_target_pairs={{0,1},{1,2},{2,3},{4,5},{5,6},{6,7},{8,9},{9,10},{10,11},{12,13},{... | collective-permute-start | bytes 2211848 | tf_op jit(solution)/shard_map/ppermute | solution.py:281
  537.3 41.9 %collective-permute-start.96 = (bf16[576,1440]{1,0:T(8,128)(2,1)}, bf16[576,1440]{1,0:T(8,128)(2,1)}, u32[]{:S(2)}, u32[]{:S(2)}) collective-permute-start(bf16[576,1440]{1,0:T(8,128)(2,1)} %add_convert_fusion.5), channel_id=1, source_target_pairs={{0,16},{8,24},{16,0},{24,8},{1,17},{9,25},{17,1},{25,9},{2,18},{10... | collective-permute-start | bytes 4976648 | tf_op jit(solution)/shard_map/ppermute | solution.py:328
  555.3 61.7 %collective-permute-start.100 = (bf16[576,1440]{1,0:T(8,128)(2,1)}, bf16[576,1440]{1,0:T(8,128)(2,1)S(1)}, u32[]{:S(2)}, u32[]{:S(2)}) collective-permute-start(bf16[576,1440]{1,0:T(8,128)(2,1)} %add_convert_fusion.3), channel_id=1, source_target_pairs={{0,16},{8,24},{16,0},{24,8},{1,17},{9,25},{17,1},{25,9},{2,18},{10... | collective-permute-start | bytes 4976648 | tf_op jit(solution)/shard_map/ppermute | solution.py:328
  563.7 84.2 %collective-permute-start.104 = (bf16[576,1440]{1,0:T(8,128)(2,1)}, bf16[576,1440]{1,0:T(8,128)(2,1)S(1)}, u32[]{:S(2)}, u32[]{:S(2)}) collective-permute-start(bf16[576,1440]{1,0:T(8,128)(2,1)} %add_convert_fusion.1), channel_id=1, source_target_pairs={{0,16},{8,24},{16,0},{24,8},{1,17},{9,25},{17,1},{25,9},{2,18},{10... | collective-permute-start | bytes 4976648 | tf_op jit(solution)/shard_map/ppermute | solution.py:328
  579.2 71.3 %collective-permute-start.42 = (bf16[160,2304]{1,0:T(8,128)(2,1)S(1)}, bf16[160,2304]{1,0:T(8,128)(2,1)S(1)}, u32[]{:S(2)}, u32[]{:S(2)}) collective-permute-start(bf16[160,2304]{1,0:T(8,128)(2,1)S(1)} %get-tuple-element.116), channel_id=1, source_target_pairs={{1,0},{2,1},{3,2},{5,4},{6,5},{7,6},{9,8},{10,9},{11,10},{13,12},{... | collective-permute-start | bytes 2211848 | tf_op jit(solution)/shard_map/ppermute | solution.py:294
  584.6 68.2 %collective-permute-start.41 = (bf16[160,2304]{1,0:T(8,128)(2,1)S(1)}, bf16[160,2304]{1,0:T(8,128)(2,1)S(1)}, u32[]{:S(2)}, u32[]{:S(2)}) collective-permute-start(bf16[160,2304]{1,0:T(8,128)(2,1)S(1)} %get-tuple-element.116), channel_id=1, source_target_pairs={{0,1},{1,2},{2,3},{4,5},{5,6},{6,7},{8,9},{9,10},{10,11},{12,13},{... | collective-permute-start | bytes 2211848 | tf_op jit(solution)/shard_map/ppermute | solution.py:293
  585.9 75.5 %collective-permute-start.97 = (bf16[576,1440]{1,0:T(8,128)(2,1)S(1)}, bf16[576,1440]{1,0:T(8,128)(2,1)S(1)}, u32[]{:S(2)}, u32[]{:S(2)}) collective-permute-start(bf16[576,1440]{1,0:T(8,128)(2,1)S(1)} %add_convert_fusion.4), channel_id=1, source_target_pairs={{0,4},{4,0},{1,5},{5,1},{2,6},{6,2},{3,7},{7,3},{8,12},{12,8},{9,1... | collective-permute-start | bytes 4976648 | tf_op jit(solution)/shard_map/ppermute | solution.py:333
  617.0 38.0 %collective-permute-start.53 = (bf16[160,2304]{1,0:T(8,128)(2,1)S(1)}, bf16[160,2304]{1,0:T(8,128)(2,1)S(1)}, u32[]{:S(2)}, u32[]{:S(2)}) collective-permute-start(bf16[160,2304]{1,0:T(8,128)(2,1)S(1)} %get-tuple-element.88), channel_id=1, source_target_pairs={{0,1},{1,2},{2,3},{4,5},{5,6},{6,7},{8,9},{9,10},{10,11},{12,13},{... | collective-permute-start | bytes 2211848 | tf_op jit(solution)/shard_map/ppermute | solution.py:293
  652.8 50.6 %collective-permute-start.101 = (bf16[576,1440]{1,0:T(8,128)(2,1)S(1)}, bf16[576,1440]{1,0:T(8,128)(2,1)S(1)}, u32[]{:S(2)}, u32[]{:S(2)}) collective-permute-start(bf16[576,1440]{1,0:T(8,128)(2,1)S(1)} %add_convert_fusion.2), channel_id=1, source_target_pairs={{0,4},{4,0},{1,5},{5,1},{2,6},{6,2},{3,7},{7,3},{8,12},{12,8},{9,1... | collective-permute-start | bytes 4976648 | tf_op jit(solution)/shard_map/ppermute | solution.py:333
  655.0 68.4 %collective-permute-start.105 = (bf16[576,1440]{1,0:T(8,128)(2,1)S(1)}, bf16[576,1440]{1,0:T(8,128)(2,1)S(1)}, u32[]{:S(2)}, u32[]{:S(2)}) collective-permute-start(bf16[576,1440]{1,0:T(8,128)(2,1)S(1)} %add_convert_fusion), channel_id=1, source_target_pairs={{0,4},{4,0},{1,5},{5,1},{2,6},{6,2},{3,7},{7,3},{8,12},{12,8},{9,1... | collective-permute-start | bytes 4976648 | tf_op jit(solution)/shard_map/ppermute | solution.py:333
  661.4 41.2 %collective-permute-start.57 = (bf16[160,2304]{1,0:T(8,128)(2,1)S(1)}, bf16[160,2304]{1,0:T(8,128)(2,1)S(1)}, u32[]{:S(2)}, u32[]{:S(2)}) collective-permute-start(bf16[160,2304]{1,0:T(8,128)(2,1)S(1)} %collective-permute-done.53), channel_id=1, source_target_pairs={{1,2},{2,3},{5,6},{6,7},{9,10},{10,11},{13,14},{14,15},{17,18},{18... | collective-permute-start | bytes 2211848 | tf_op jit(solution)/shard_map/ppermute | solution.py:293
  683.3 97.6 %collective-permute-start.44 = (bf16[160,2304]{1,0:T(8,128)(2,1)}, bf16[160,2304]{1,0:T(8,128)(2,1)}, u32[]{:S(2)}, u32[]{:S(2)}) collective-permute-start(bf16[160,2304]{1,0:T(8,128)(2,1)} %collective-permute-done.43), channel_id=1, source_target_pairs={{1,0},{5,4},{9,8},{13,12},{17,16},{21,20},{25,24},{29,28}} | collective-permute-start | bytes 2211848 | tf_op jit(solution)/shard_map/ppermute | solution.py:294
  684.9 99.0 %collective-permute-start.46 = (bf16[160,2304]{1,0:T(8,128)(2,1)}, bf16[160,2304]{1,0:T(8,128)(2,1)}, u32[]{:S(2)}, u32[]{:S(2)}) collective-permute-start(bf16[160,2304]{1,0:T(8,128)(2,1)} %collective-permute-done.45), channel_id=1, source_target_pairs={{2,3},{6,7},{10,11},{14,15},{18,19},{22,23},{26,27},{30,31}} | collective-permute-start | bytes 2211848 | tf_op jit(solution)/shard_map/ppermute | solution.py:293
  798.7 55.9 %collective-permute-start.78 = (bf16[576,576]{1,0:T(8,128)(2,1)}, bf16[576,576]{1,0:T(8,128)(2,1)}, u32[]{:S(2)}, u32[]{:S(2)}) collective-permute-start(bf16[576,576]{1,0:T(8,128)(2,1)} %convolution_convert_fusion.26), channel_id=1, source_target_pairs={{0,8},{8,0},{16,24},{24,16},{1,9},{9,1},{17,25},{25,17},{2,10},{10... | collective-permute-start | bytes 1990664 | tf_op jit(solution)/shard_map/ppermute | solution.py:324
  802.3 59.7 %collective-permute-start.90 = (bf16[576,576]{1,0:T(8,128)(2,1)}, bf16[576,576]{1,0:T(8,128)(2,1)}, u32[]{:S(2)}, u32[]{:S(2)}) collective-permute-start(bf16[576,576]{1,0:T(8,128)(2,1)} %convolution_convert_fusion.14), channel_id=1, source_target_pairs={{0,8},{8,0},{16,24},{24,16},{1,9},{9,1},{17,25},{25,17},{2,10},{10... | collective-permute-start | bytes 1990664 | tf_op jit(solution)/shard_map/ppermute | solution.py:324
  805.0 50.0 %collective-permute-start.80 = (bf16[576,576]{1,0:T(8,128)(2,1)}, bf16[576,576]{1,0:T(8,128)(2,1)}, u32[]{:S(2)}, u32[]{:S(2)}) collective-permute-start(bf16[576,576]{1,0:T(8,128)(2,1)} %add_convert_fusion.15), channel_id=1, source_target_pairs={{0,16},{8,24},{16,0},{24,8},{1,17},{9,25},{17,1},{25,9},{2,18},{10... | collective-permute-start | bytes 1990664 | tf_op jit(solution)/shard_map/ppermute | solution.py:328
  860.3 60.9 %collective-permute-start.82 = (bf16[576,576]{1,0:T(8,128)(2,1)}, bf16[576,576]{1,0:T(8,128)(2,1)}, u32[]{:S(2)}, u32[]{:S(2)}) collective-permute-start(bf16[576,576]{1,0:T(8,128)(2,1)} %convolution_convert_fusion.22), channel_id=1, source_target_pairs={{0,8},{8,0},{16,24},{24,16},{1,9},{9,1},{17,25},{25,17},{2,10},{10... | collective-permute-start | bytes 1990664 | tf_op jit(solution)/shard_map/ppermute | solution.py:324
  862.1 56.4 %collective-permute-start.81 = (bf16[576,576]{1,0:T(8,128)(2,1)}, bf16[576,576]{1,0:T(8,128)(2,1)}, u32[]{:S(2)}, u32[]{:S(2)}) collective-permute-start(bf16[576,576]{1,0:T(8,128)(2,1)} %add_convert_fusion.14), channel_id=1, source_target_pairs={{0,4},{4,0},{1,5},{5,1},{2,6},{6,2},{3,7},{7,3},{8,12},{12,8},{9,1... | collective-permute-start | bytes 1990664 | tf_op jit(solution)/shard_map/ppermute | solution.py:333
  886.4 35.2 %collective-permute-start.84 = (bf16[576,576]{1,0:T(8,128)(2,1)}, bf16[576,576]{1,0:T(8,128)(2,1)}, u32[]{:S(2)}, u32[]{:S(2)}) collective-permute-start(bf16[576,576]{1,0:T(8,128)(2,1)} %add_convert_fusion.13), channel_id=1, source_target_pairs={{0,16},{8,24},{16,0},{24,8},{1,17},{9,25},{17,1},{25,9},{2,18},{10... | collective-permute-start | bytes 1990664 | tf_op jit(solution)/shard_map/ppermute | solution.py:328
  923.2 36.0 %collective-permute-start.85 = (bf16[576,576]{1,0:T(8,128)(2,1)S(1)}, bf16[576,576]{1,0:T(8,128)(2,1)S(1)}, u32[]{:S(2)}, u32[]{:S(2)}) collective-permute-start(bf16[576,576]{1,0:T(8,128)(2,1)S(1)} %add_convert_fusion.12), channel_id=1, source_target_pairs={{0,4},{4,0},{1,5},{5,1},{2,6},{6,2},{3,7},{7,3},{8,12},{12,8},{9,1... | collective-permute-start | bytes 1990664 | tf_op jit(solution)/shard_map/ppermute | solution.py:333
  (134 other events, 1946.6 us)

commit v2 on v1

v2 whole, which is shorter than its diff:
```python
import functools
import math

import jax
import jax.numpy as jnp
from jax import lax
from jax.experimental import pallas as pl
from jax.experimental.pallas import tpu as pltpu
from jax.sharding import PartitionSpec as P

HEAD = 64
LANES = 128
NEG = -1e30
norm_eps = 1e-05
branch_scale = 1.4 / math.sqrt(40.0)
bf = jnp.bfloat16
f32 = jnp.float32
MB = 1 << 20


def rope_tables(positions):
    freq = 10000.0 ** (-(jnp.arange(HEAD // 2, dtype=f32) * 2.0 / HEAD))
    angle = positions.astype(f32)[:, None] * freq[None, :]
    cosine, sine = jnp.cos(angle), jnp.sin(angle)
    cos_t = jnp.concatenate([cosine] * 4, axis=1)
    sin_t = jnp.concatenate([-sine, sine, -sine, sine], axis=1)
    return cos_t, sin_t


def rope_block(u, cos_t, sin_t, sign):
    lane = lax.broadcasted_iota(jnp.int32, u.shape, 1)
    low = (lane % HEAD) < HEAD // 2
    partner = jnp.where(low, pltpu.roll(u, LANES - HEAD // 2, 1), pltpu.roll(u, HEAD // 2, 1))
    return u * cos_t + sign * (partner * sin_t)


def dot(a, b, dims=((1,), (0,))):
    return lax.dot_general(a, b, (dims, ((), ())), preferred_element_type=f32)


def up_to(n, unit):
    return -(-n // unit) * unit


COST = pl.CostEstimate(flops=1024, bytes_accessed=1024, transcendentals=0)


def fetch(offs_ref, shards, scratch, sems, width):
    copies = []
    for b in range(scratch.shape[1] // width):
        row = []
        for j, ref in enumerate(shards):
            rows = min(ref.shape[0], scratch.shape[0] // min(len(shards), 4))
            first = pl.multiple_of(offs_ref[j], 16)
            copy = pltpu.make_async_copy(
                ref.at[pl.ds(0, rows), pl.ds(b * width, width)],
                scratch.at[pl.ds(first, rows), pl.ds(b * width, width)],
                sems.at[b, j],
            )
            copy.start()
            row.append(copy)
        copies.append(row)
    return copies


def wait_all(copies):
    for copy in copies:
        copy.wait()


HBM = pl.BlockSpec(memory_space=pltpu.HBM)
VM = pl.BlockSpec(memory_space=pltpu.VMEM)
SM = pl.BlockSpec(memory_space=pltpu.SMEM)


def params(mbytes):
    return pltpu.CompilerParams(vmem_limit_bytes=mbytes * MB)


def proj_kernel(ns, rotary, offs, n_ref, cos_ref, sin_ref, *rest):
    shards, (o_ref, w_ref, sems) = rest[:ns], rest[ns:]
    copies = fetch(offs, shards, w_ref, sems, w_ref.shape[1])
    wait_all(copies[0])
    y = dot(n_ref[...], w_ref[...])
    for first in range(0, o_ref.shape[1], LANES):
        u = y[:, first : first + LANES]
        if rotary:
            u = rope_block(u, cos_ref[...], sin_ref[...], 1.0)
        o_ref[:, first : first + LANES] = u.astype(bf)


def project(normed, weight, cos_t, sin_t, rotary):
    offs, shards = weight
    rows, depth = normed.shape
    feats = shards[0].shape[1]
    ns = len(shards)
    return pl.pallas_call(
        functools.partial(proj_kernel, ns, rotary),
        out_shape=jax.ShapeDtypeStruct((rows, feats), bf),
        in_specs=[SM, VM, VM, VM] + [HBM] * ns,
        out_specs=VM,
        scratch_shapes=[pltpu.VMEM((depth, feats), bf), pltpu.SemaphoreType.DMA((1, ns))],
        compiler_params=params(16),
        cost_estimate=COST,
    )(offs, normed, cos_t, sin_t, *shards)


def wide_kernel(ns, nt, width, offs, a_ref, *rest):
    shards, (o_ref, w_ref, sems) = rest[:ns], rest[ns:]
    if nt:
        for row in fetch(offs, shards, w_ref, sems, w_ref.shape[1]):
            wait_all(row)
        for first in range(0, o_ref.shape[1], width):
            part = slice(first, first + width)
            o_ref[:, part] = dot(a_ref[...], w_ref[part, :], ((1,), (1,))).astype(o_ref.dtype)
    else:
        for b, row in enumerate(fetch(offs, shards, w_ref, sems, width)):
            wait_all(row)
            part = slice(b * width, (b + 1) * width)
            o_ref[:, part] = dot(a_ref[...], w_ref[:, part]).astype(o_ref.dtype)


def wide_matmul(a, weight, nt, dtype, width=256):
    offs, shards = weight
    rows = a.shape[0]
    ns = len(shards)
    depth, feats = sum(s.shape[0] for s in shards), shards[0].shape[1]
    if feats % width and not nt:
        width = feats
    return pl.pallas_call(
        functools.partial(wide_kernel, ns, nt, width),
        out_shape=jax.ShapeDtypeStruct((rows, depth if nt else feats), dtype),
        in_specs=[SM, VM] + [HBM] * ns,
        out_specs=VM,
        scratch_shapes=[pltpu.VMEM((depth, feats), bf), pltpu.SemaphoreType.DMA((feats // width, ns))],
        compiler_params=params(20),
        cost_estimate=COST,
    )(offs, a, *shards)


def qkv_back_kernel(ns, offs, x_ref, scale_ref, *rest):
    grads, rest = rest[:3], rest[3:]
    shards, (o_ref, gain_ref, w_ref, sems) = rest[: 3 * ns], rest[3 * ns :]
    rows = [fetch(offs, shards[i * ns : (i + 1) * ns], w_ref.at[i], sems.at[i], w_ref.shape[2])[0] for i in range(3)]
    for row in rows:
        wait_all(row)
    width = 256
    for first in range(0, o_ref.shape[1], width):
        part = slice(first, first + width)
        total = None
        for i in range(3):
            y = dot(grads[i][...], w_ref[i, part, :], ((1,), (1,)))
            total = y if total is None else total + y
        o_ref[:, part] = total.astype(bf)
        gain_ref[:, part] = jnp.sum(total * (x_ref[:, part].astype(f32) * scale_ref[...]), axis=0, keepdims=True)


def qkv_back(grads, weights, tokens, scale):
    offs = weights[0][0]
    shards = [s for w in weights for s in w[1]]
    ns = len(weights[0][1])
    rows, feats = grads[0].shape
    depth = sum(s.shape[0] for s in weights[2][1])
    return pl.pallas_call(
        functools.partial(qkv_back_kernel, ns),
        out_shape=(jax.ShapeDtypeStruct((rows, depth), bf), jax.ShapeDtypeStruct((1, depth), f32)),
        in_specs=[SM] + [VM] * 5 + [HBM] * (3 * ns),
        out_specs=(VM, VM),
        scratch_shapes=[pltpu.VMEM((3, depth, feats), bf), pltpu.SemaphoreType.DMA((3, 1, ns))],
        compiler_params=params(28),
        cost_estimate=COST,
    )(offs, tokens, scale, *grads, *shards)


def ffn_kernel(ns, width, offs, n_hbm, dh_hbm, *rest):
    g_shards, u_shards, rest = rest[:ns], rest[ns : 2 * ns], rest[2 * ns :]
    outs, dn_hbm, rest = rest[:3], rest[3], rest[4:]
    n_ref, dh_ref, wg, wu, mids, dn_ref, w_sems, in_sems, out_sems = rest
    hidden, depth = dh_ref.shape[1], n_ref.shape[1]
    blocks = [slice(f, min(f + width, hidden)) for f in range(0, hidden, width)]
    span = lambda part: pl.ds(part.start, part.stop - part.start)

    def load(b):
        part = span(blocks[b])
        copies = [pltpu.make_async_copy(dh_hbm.at[:, part], dh_ref.at[:, part], in_sems.at[b + 1])]
        for i, (shards, scratch) in enumerate(((g_shards, wg), (u_shards, wu))):
            for j, ref in enumerate(shards):
                first = pl.multiple_of(offs[j], 16)
                there = scratch.at[pl.ds(first, ref.shape[0]), part]
                copies.append(pltpu.make_async_copy(ref.at[:, part], there, w_sems.at[i, b, j]))
        for copy in copies:
            copy.start()
        return copies

    first = pltpu.make_async_copy(n_hbm, n_ref, in_sems.at[0])
    first.start()
    loads = [load(0)]
    first.wait()
    stores = []
    for b, part in enumerate(blocks):
        wait_all(loads[b])
        if b + 1 < len(blocks):
            loads.append(load(b + 1))
        gate = dot(n_ref[...], wg[:, part])
        up = dot(n_ref[...], wu[:, part])
        sigma = jax.nn.sigmoid(gate)
        active = gate * sigma
        dh = dh_ref[:, part]
        mids[0, :, part] = (active * up).astype(bf)
        mids[1, :, part] = (dh * up * sigma * (1.0 + gate * (1.0 - sigma))).astype(bf)
        mids[2, :, part] = (dh * active).astype(bf)
        for i in range(3):
            copy = pltpu.make_async_copy(mids.at[i, :, span(part)], outs[i].at[:, span(part)], out_sems.at[i, b])
            copy.start()
            stores.append(copy)
    for b, f in enumerate(range(0, depth, 768)):
        part = slice(f, f + 768)
        total = dot(mids[1], wg[part, :], ((1,), (1,))) + dot(mids[2], wu[part, :], ((1,), (1,)))
        dn_ref[:, part] = total.astype(bf)
        copy = pltpu.make_async_copy(dn_ref.at[:, span(part)], dn_hbm.at[:, span(part)], out_sems.at[3, b])
        copy.start()
        stores.append(copy)
    wait_all(stores)


def ffn(normed, grad_hidden, w_gate, w_up, width=512):
    offs, g_shards = w_gate
    ns = len(g_shards)
    rows, depth = normed.shape
    hidden = g_shards[0].shape[1]
    blocks = -(-hidden // width)
    mid = jax.ShapeDtypeStruct((rows, hidden), bf)
    return pl.pallas_call(
        functools.partial(ffn_kernel, ns, width),
        out_shape=(mid, mid, mid, jax.ShapeDtypeStruct((rows, depth), bf)),
        in_specs=[SM] + [HBM] * (2 + 2 * ns),
        out_specs=(HBM,) * 4,
        scratch_shapes=[
            pltpu.VMEM((rows, depth), bf),
            pltpu.VMEM((rows, hidden), f32),
            pltpu.VMEM((depth, hidden), bf),
            pltpu.VMEM((depth, hidden), bf),
            pltpu.VMEM((3, rows, hidden), bf),
            pltpu.VMEM((rows, depth), bf),
            pltpu.SemaphoreType.DMA((2, blocks, ns)),
            pltpu.SemaphoreType.DMA((blocks + 1,)),
            pltpu.SemaphoreType.DMA((4, max(blocks, depth // 768))),
        ],
        compiler_params=params(60),
        cost_estimate=COST,
    )(offs, normed, grad_hidden, *g_shards, *w_up[1])


def mix_kernel(spans, me_ref, offs, att_ref, x_ref, gain_ref, *rest):
    ns = len(spans)
    shards, (n_ref, own_ref, wo_hbm, w_ref, h_ref, sems) = rest[:ns], rest[ns:]
    copies = []
    for j, (ref, (z0, z1)) in enumerate(zip(shards, spans)):
        rows = pl.ds(pl.multiple_of(offs[j], 16), ref.shape[1])
        copies.append(pltpu.make_async_copy(ref, w_ref.at[z0:z1, rows, :], sems.at[j]))
        copies[-1].start()
    wait_all(copies)
    keep = pltpu.make_async_copy(w_ref.at[me_ref[0]], wo_hbm, sems.at[ns])
    keep.start()
    depth = h_ref.shape[1]
    width = 768
    for f in range(0, depth, width):
        part = slice(f, f + width)
        total = None
        for z in range(att_ref.shape[0]):
            y = dot(att_ref[z], w_ref[z, part, :], ((1,), (1,)))
            total = y if total is None else total + y
        h_ref[:, part] = x_ref[:, part].astype(f32) + branch_scale * total
    step = min(128, h_ref.shape[0])
    for f in range(0, h_ref.shape[0], step):
        part = slice(f, f + step)
        h = h_ref[part, :]
        scale = lax.rsqrt(jnp.mean(h * h, axis=-1, keepdims=True) + norm_eps)
        n_ref[part, :] = (h * scale * gain_ref[...]).astype(bf)
    piece = own_ref.shape[0]
    own_ref[...] = h_ref[pl.ds(pl.multiple_of(me_ref[0] * piece, 8), piece), :]
    keep.wait()


def mix(att, tokens, gain, offs, pieces, me):
    n, rows, feats = att.shape
    depth = tokens.shape[1]
    spans, shards = [p[0] for p in pieces], [p[1] for p in pieces]
    return pl.pallas_call(
        functools.partial(mix_kernel, spans),
        out_shape=(
            jax.ShapeDtypeStruct((rows, depth), bf),
            jax.ShapeDtypeStruct((rows // n, depth), f32),
            jax.ShapeDtypeStruct((depth, feats), bf),
        ),
        in_specs=[SM, SM, VM, VM, VM] + [HBM] * len(shards),
        out_specs=(VM, VM, HBM),
        scratch_shapes=[
            pltpu.VMEM((n, depth, feats), bf),
            pltpu.VMEM((rows, depth), f32),
            pltpu.SemaphoreType.DMA((len(shards) + 1,)),
        ],
        compiler_params=params(56),
        cost_estimate=COST,
    )(me[None], offs, att, tokens, gain[None, :], *shards)


def grad_kernel(offs, a_ref, b_ref, keep_ref, send_ref, at_ref):
    at_ref[...] = a_ref[...].T
    block = keep_ref.shape[0] // 2
    for j in range(4):
        left = at_ref[pl.ds(pl.multiple_of(offs[j], 16), block), :]
        ref = send_ref if j % 2 else keep_ref
        ref[(j // 2) * block : (j // 2 + 1) * block, :] = dot(left, b_ref[...]).astype(bf)


def weight_grad(a, b, offs):
    rows, depth = a.shape
    feats = b.shape[1]
    half = jax.ShapeDtypeStruct((depth // 2, feats), bf)
    return pl.pallas_call(
        grad_kernel,
        out_shape=(half, half),
        in_specs=[SM, VM, VM],
        out_specs=(VM, VM),
        scratch_shapes=[pltpu.VMEM((depth, rows), bf)],
        compiler_params=params(20),
        cost_estimate=COST,
    )(offs, a, b)


def fill_bias(qseg_ref, qpos_ref, kseg_ref, kpos_ref, bias_ref):
    kseg = kseg_ref[...]
    allowed = ((kseg == qseg_ref[...]) | (kseg == 0)) & (kpos_ref[...] <= qpos_ref[...])
    bias_ref[...] = jnp.where(allowed, 0.0, NEG)


def attn_fwd_kernel(parts, heads, *refs):
    qseg, qpos = refs[:2]
    kseg, kpos = refs[2 : 2 + parts], refs[2 + parts : 2 + 2 * parts]
    rest = refs[2 + 2 * parts :]
    q_ref = rest[0]
    k_refs, v_refs = rest[1 : 1 + parts], rest[1 + parts : 1 + 2 * parts]
    o_ref, lse_ref = rest[1 + 2 * parts : 3 + 2 * parts]
    bias = rest[3 + 2 * parts : 3 + 3 * parts]
    ot_ref = rest[3 + 3 * parts]
    blk = pl.program_id(0)

    @pl.when(blk == 0)
    def _():
        for i in range(parts):
            fill_bias(qseg, qpos, kseg[i], kpos[i], bias[i])

    ot_ref[...] = jnp.zeros_like(ot_ref)
    lse_ref[...] = jnp.zeros_like(lse_ref)

    def one(sub):
        lane = lax.broadcasted_iota(jnp.int32, (1, LANES), 1)
        mine = (lane >= sub * HEAD) & (lane < (sub + 1) * HEAD)
        q = jnp.where(mine, q_ref[...] * 0.125, 0.0).astype(bf)
        scores = []
        best = None
        for i in range(parts):
            k = k_refs[i][...]
            s = dot(k, q, ((1,), (1,))) + bias[i][...]
            scores.append(s)
            top = jnp.max(s, axis=0, keepdims=True)
            best = top if best is None else jnp.maximum(best, top)
        total, acc = None, None
        for i in range(parts):
            p = jnp.exp(scores[i] - best)
            t = jnp.sum(p, axis=0, keepdims=True)
            v = v_refs[i][...]
            a = dot(v, p.astype(bf), ((0,), (0,)))
            total = t if total is None else total + t
            acc = a if acc is None else acc + a
        ot_ref[sub * HEAD : (sub + 1) * HEAD, :] = acc[sub * HEAD : (sub + 1) * HEAD, :] / total
        lse_ref[0, sub : sub + 1, :] = best + jnp.log(total)

    for sub in range(LANES // HEAD):
        pl.when(blk * (LANES // HEAD) + sub < heads)(functools.partial(one, sub))
    o_ref[...] = ot_ref[...].T.astype(bf)


def attn_specs(rows, key_rows, feats):
    blocks = -(-feats // LANES)
    row = pl.BlockSpec((1, rows), lambda h: (0, 0))
    cols = [pl.BlockSpec((n, 1), lambda h: (0, 0)) for n in key_rows]
    q = pl.BlockSpec((rows, LANES), lambda h: (0, h))
    ks = [pl.BlockSpec((n, LANES), lambda h: (0, h)) for n in key_rows]
    lse = pl.BlockSpec((1, 8, rows), lambda h: (h, 0, 0))
    return blocks, row, cols, q, ks, lse


def attention_fwd(q, keys, values, q_meta, k_metas, heads):
    rows, feats = q.shape
    parts = len(keys)
    key_rows = [k.shape[0] for k in keys]
    count = sum(key_rows)
    blocks, row, cols, qs, ks, lse = attn_specs(rows, key_rows, feats)
    return pl.pallas_call(
        functools.partial(attn_fwd_kernel, parts, heads),
        grid=(blocks,),
        out_shape=(
            jax.ShapeDtypeStruct((rows, feats), bf),
            jax.ShapeDtypeStruct((blocks, 8, rows), f32),
        ),
        in_specs=[row, row] + cols + cols + [qs] + ks + ks,
        out_specs=(qs, lse),
        scratch_shapes=[pltpu.VMEM((n, rows), f32) for n in key_rows] + [pltpu.VMEM((LANES, rows), f32)],
        compiler_params=pltpu.CompilerParams(vmem_limit_bytes=28 * MB),
        cost_estimate=COST,
    )(
        q_meta[0][None, :], q_meta[1][None, :],
        *[m[0][:, None] for m in k_metas], *[m[1][:, None] for m in k_metas],
        q, *keys, *values,
    )


def attn_bwd_kernel(parts, heads, *refs):
    qseg, qpos, qcos, qsin = refs[:4]
    refs = refs[4:]
    take = lambda n: (refs[:n], refs[n:])
    kseg, refs = take(parts)
    kpos, refs = take(parts)
    kcos, refs = take(parts)
    ksin, refs = take(parts)
    (q_ref, att_ref, do_ref, lse_ref), refs = take(4)
    k_refs, refs = take(parts)
    v_refs, refs = take(parts)
    (dq_ref,), refs = take(1)
    dk_refs, refs = take(parts)
    dv_refs, refs = take(parts)
    bias, refs = take(parts)
    dqt_ref, refs = refs[0], refs[1:]
    dka, refs = take(parts)
    dva, refs = take(parts)
    blk = pl.program_id(0)

    @pl.when(blk == 0)
    def _():
        for i in range(parts):
            fill_bias(qseg, qpos, kseg[i], kpos[i], bias[i])

    prod = (do_ref[...].astype(f32) * att_ref[...].astype(f32)).T
    dqt_ref[...] = jnp.zeros_like(dqt_ref)

    def one(sub):
        lane = lax.broadcasted_iota(jnp.int32, (1, LANES), 1)
        mine = (lane >= sub * HEAD) & (lane < (sub + 1) * HEAD)
        q = jnp.where(mine, q_ref[...] * 0.125, 0.0).astype(bf)
        do = jnp.where(mine, do_ref[...], 0.0).astype(bf)
        lse = lse_ref[0, sub : sub + 1, :]
        delta = jnp.sum(prod[sub * HEAD : (sub + 1) * HEAD, :], axis=0, keepdims=True)
        dqt = None
        for i in range(parts):
            k = k_refs[i][...]
            v = v_refs[i][...]
            p = jnp.exp(dot(k, q, ((1,), (1,))) + bias[i][...] - lse)
            dp = dot(v, do, ((1,), (1,)))
            ds = (p * (dp - delta)).astype(bf)
            dv = dot(p.astype(bf), do)
            dk = dot(ds, q)
            if sub == 0:
                dva[i][...] = dv
                dka[i][...] = dk
            else:
                dva[i][...] += dv
                dka[i][...] += dk
            d = dot(k, ds, ((0,), (0,)))
            dqt = d if dqt is None else dqt + d
        dqt_ref[sub * HEAD : (sub + 1) * HEAD, :] = dqt[sub * HEAD : (sub + 1) * HEAD, :] * 0.125

    for sub in range(LANES // HEAD):
        pl.when(blk * (LANES // HEAD) + sub < heads)(functools.partial(one, sub))
    dq_ref[...] = rope_block(dqt_ref[...].T, qcos[...], qsin[...], -1.0).astype(bf)
    for i in range(parts):
        dk_refs[i][...] = rope_block(dka[i][...], kcos[i][...], ksin[i][...], -1.0).astype(bf)
        dv_refs[i][...] = dva[i][...].astype(bf)


def attention_bwd(q, att, grad_att, lse, keys, values, q_meta, k_metas, heads):
    rows, feats = q.shape
    parts = len(keys)
    key_rows = [k.shape[0] for k in keys]
    count = sum(key_rows)
    blocks, row, cols, qs, ks, lses = attn_specs(rows, key_rows, feats)
    tab = pl.BlockSpec((rows, LANES), lambda h: (0, 0))
    tabs = [pl.BlockSpec((n, LANES), lambda h: (0, 0)) for n in key_rows]
    out = pl.pallas_call(
        functools.partial(attn_bwd_kernel, parts, heads),
        grid=(blocks,),
        out_shape=(jax.ShapeDtypeStruct((rows, feats), bf),)
        + tuple(jax.ShapeDtypeStruct((n, feats), bf) for n in key_rows) * 2,
        in_specs=[row, row, tab, tab] + cols + cols + tabs + tabs + [qs, qs, qs, lses] + ks + ks,
        out_specs=(qs,) + tuple(ks) + tuple(ks),
        scratch_shapes=[pltpu.VMEM((n, rows), f32) for n in key_rows]
        + [pltpu.VMEM((LANES, rows), f32)]
        + [pltpu.VMEM((n, LANES), f32) for n in key_rows] * 2,
        compiler_params=pltpu.CompilerParams(vmem_limit_bytes=40 * MB),
        cost_estimate=COST,
    )(
        q_meta[0][None, :], q_meta[1][None, :], q_meta[2], q_meta[3],
        *[m[0][:, None] for m in k_metas], *[m[1][:, None] for m in k_metas],
        *[m[2] for m in k_metas], *[m[3] for m in k_metas],
        q, att, grad_att, lse, *keys, *values,
    )
    return out[0], out[1 : 1 + parts], out[1 + parts :]


def swap(n, bit):
    return [(i, i ^ bit) for i in range(n)]


def power_of_two(n):
    return n & (n - 1) == 0


def sum_all(value, sizes):
    for axis, n in sizes:
        if power_of_two(n):
            bit = 1
            while bit < n:
                value = value + lax.ppermute(value, axis, swap(n, bit))
                bit *= 2
        else:
            value = lax.psum(value, axis)
    return value


def after(value, *others):
    return lax.optimization_barrier((value,) + others)[0]


def scatter_sum(array):
    return lax.psum_scatter(array, "tensor", scatter_dimension=0, tiled=True).astype(f32)


def gather_rows(array):
    return lax.all_gather(array, "tensor", axis=0, tiled=True)


def gather_weight(shard, n, offs, late=()):
    if n != 4:
        return offs, [lax.all_gather(shard, "dp", axis=0, tiled=True)]
    far = after(lax.ppermute(shard, "dp", swap(4, 2)), *late)
    near = lax.ppermute(shard, "dp", swap(4, 1))
    cross = lax.ppermute(far, "dp", swap(4, 1))
    return offs, [shard, near, far, cross]


def lockstep(items, waits):
    firsts, seconds, before = [], [], ()
    for step in range(len(items) + 1):
        now = []
        if step in waits:
            before += waits[step](firsts, seconds)
        if step > 0:
            seconds.append(lax.ppermute(after(firsts[-1], *before), "ctx", swap(2, 1)))
            now.append(seconds[-1])
        if step < len(items):
            firsts.append(lax.ppermute(after(items[step], *before), "dp", swap(4, 2)))
            now.append(firsts[-1])
        before = tuple(now)
    return firsts, seconds


def two_halves(shard, n, n_ctx, ctx, first, second, offs):
    half = shard.shape[1] // 2
    cross = lambda a: lax.ppermute(a, "dp", swap(4, 1))
    out = []
    for place, piece in ((ctx * half, first), ((1 - ctx) * half, second)):
        out += [(offs[2] + place, piece), (offs[3] + place, cross(piece))]
    return out


class WeightGrad:
    def __init__(self, n, n_ctx, offs):
        self.n, self.n_ctx, self.offs = n, n_ctx, offs

    def start(self, left, right):
        if self.n == 4:
            self.keep, send = weight_grad(left, right, self.offs)
            self.got = lax.ppermute(send, "dp", swap(4, 1))
            block = send.shape[0] // 2
            self.far = (self.keep[block:].astype(f32) + self.got[block:].astype(f32)).astype(bf)
        else:
            self.far = self.whole = dot(left, right, ((0,), (0,))).astype(bf)
        return self

    def along_x(self, *late):
        if self.n == 4:
            block = self.far.shape[0]
            other = after(lax.ppermute(self.far, "dp", swap(4, 2)), *late).astype(f32)
            total = self.keep[:block].astype(f32) + self.got[:block].astype(f32) + other
        else:
            total = lax.psum_scatter(self.whole, "dp", scatter_dimension=0, tiled=True).astype(f32)
        self.total = lax.optimization_barrier(total.astype(bf))
        return self.total

    def along_y(self, *late):
        if self.n_ctx == 2:
            self.other = lax.ppermute(after(self.total, *late), "ctx", swap(2, 1))
        else:
            self.other = lax.psum(self.total, "ctx")
        return self.other

    def finish(self, size, *before):
        other = after(self.other, *before).astype(f32)
        out = self.total.astype(f32) + other if self.n_ctx == 2 else other
        return out[:, :size]


def per_device(
    n_dp, n_ctx, n_tp,
    tokens, segment, position, gain_attn, w_query, w_key, w_value, w_out, gain_ffn, w_gate, w_up, w_down, cotangent,
):
    dp, ctx, me = lax.axis_index("dp"), lax.axis_index("ctx"), lax.axis_index("tensor")
    rows = tokens.shape[0]
    piece = rows // n_tp
    shard = gain_attn.shape[0]
    feats, hidden_dev = w_query.shape[1], w_gate.shape[1]
    feats_pad, hidden_pad = up_to(feats, LANES), up_to(hidden_dev, 256)
    mine = functools.partial(lax.dynamic_slice_in_dim, start_index=me * piece, slice_size=piece, axis=0)
    offs = jnp.stack([(dp ^ j) * shard for j in range(4)]) if n_dp == 4 else jnp.zeros((4,), jnp.int32)

    def padded(w, width, *before):
        return after(jnp.pad(w.astype(bf), ((0, 0), (0, width - w.shape[1]))), *before)

    wo_all = lax.all_gather(padded(w_out.T, feats_pad), "tensor", axis=0, tiled=False)
    wk_b = jnp.pad(w_key.astype(bf), ((0, 16), (0, feats_pad - feats)))
    gain_rows = jnp.pad(jnp.stack([gain_attn, gain_ffn]).astype(bf), ((0, 0), (0, feats_pad - shard)))
    wk_b = lax.dynamic_update_slice(wk_b, gain_rows, (shard, 0))
    _, wk_ext = gather_weight(wk_b, n_dp, offs)
    if n_dp == 4:
        own = jnp.stack([w[shard : shard + 2, :shard] for w in wk_ext])
        gains = jnp.zeros((2, n_dp * shard), f32)
        for j in range(4):
            gains = lax.dynamic_update_slice(gains, own[j].astype(f32), (0, offs[j]))
        wk = (offs, wk_ext)
    else:
        ext = wk_ext[0].reshape(n_dp, shard + 16, feats_pad)
        gains = ext[:, shard : shard + 2, :shard].transpose(1, 0, 2).reshape(2, n_dp * shard).astype(f32)
        wk = (offs, [ext[:, :shard].reshape(n_dp * shard, feats_pad)])
    gain1, gain2 = gains[0], gains[1]
    def meta(start, size):
        seg = lax.dynamic_slice_in_dim(segment, start, size)
        pos = lax.dynamic_slice_in_dim(position, start, size)
        return (seg, pos) + rope_tables(pos)

    q_meta = meta(ctx * rows, rows)
    cos_t, sin_t = q_meta[2:]
    inputs = tokens.astype(f32)
    scale1 = lax.rsqrt(jnp.mean(inputs * inputs, axis=-1, keepdims=True) + norm_eps)
    normed1 = (inputs * scale1 * gain1).astype(bf)
    far = lambda w: w[1][2 if n_dp == 4 else 0]
    keys = project(normed1, wk, cos_t, sin_t, True)
    wv = gather_weight(padded(w_value, feats_pad, far(wk)), n_dp, offs, (keys,))
    values = project(normed1, wv, cos_t, sin_t, False)
    if n_ctx == 2:
        trade = lambda a: lax.ppermute(a, "ctx", swap(2, 1))
        keys_all, values_all = [keys, trade(keys)], [values, trade(values)]
        k_metas = [q_meta, meta((1 - ctx) * rows, rows)]
        early = (values, keys_all[1])
    else:
        spread = lambda a: [lax.all_gather(a, "ctx", axis=0, tiled=True)]
        keys_all, values_all = spread(keys), spread(values)
        k_metas = [meta(0, segment.shape[0])]
        early = (values,)
    wq = gather_weight(padded(w_query, feats_pad, far(wv)), n_dp, offs, early)
    wide = [padded(w, hidden_pad) for w in (w_down.T, w_gate, w_up)]
    grad_ffn = (branch_scale * cotangent.astype(f32)).astype(bf)
    if n_dp == 4 and n_ctx == 2:
        half = shard // 2
        near = lambda a: lax.ppermute(a, "dp", swap(4, 1))
        cut = lambda a: lax.dynamic_slice_in_dim(a, ctx * half, half, a.ndim - 2)
        mid = n_tp // 2
        items = [cut(wide[0]), cut(wo_all[:mid]), cut(wo_all[mid:]), cut(wide[1]), cut(wide[2])]
        items[0] = after(items[0], far(wq))
        query = project(normed1, wq, cos_t, sin_t, True)
        early = []

        def shards_of(own, first, second):
            got = two_halves(own[None], n_dp, n_ctx, ctx, first, second, offs)
            places, pieces = zip((offs[0], own), (offs[1], near(own)), *got)
            return jnp.stack(places), list(pieces)

        def attend(firsts, seconds):
            early.append(attention_fwd(after(query, *wide), keys_all, values_all, q_meta, k_metas, feats // HEAD))
            return (early[0][0],)

        def work_ahead(firsts, seconds):
            wd = shards_of(wide[0], firsts[0], seconds[0])
            early.extend((wd, wide_matmul(after(grad_ffn, firsts[2]), wd, False, f32)))
            return (early[2],)

        waits = {1: lambda f, s: (query, values_all[1]), 2: attend, 4: work_ahead}
        firsts, seconds = lockstep(items, waits)
        att, lse = early.pop(0)
        wd, grad_hidden = early
        wg = shards_of(wide[1], firsts[3], seconds[3])
        places, wo_pieces = [offs[0], offs[1]], [((0, n_tp), wo_all), ((0, n_tp), near(wo_all))]
        for k, span in ((1, (0, mid)), (2, (mid, n_tp))):
            for place, piece in two_halves(wo_all, n_dp, n_ctx, ctx, firsts[k], seconds[k], offs):
                places.append(place)
                wo_pieces.append((span, piece))
        places = jnp.stack(places)
        late = (firsts[4], seconds[3])
    else:
        wd, wg, wu = [gather_weight(w, n_dp, offs) for w in wide]
        places, wo_pieces = offs[:1] * 0, [((0, n_tp), lax.all_gather(wo_all, "dp", axis=1, tiled=True))]
        late = ()
        query = project(normed1, wq, cos_t, sin_t, True)
        att, lse = attention_fwd(query, keys_all, values_all, q_meta, k_metas, feats // HEAD)
        grad_hidden = wide_matmul(grad_ffn, wd, False, f32)
    att_all = after(lax.all_gather(att, "tensor", axis=0, tiled=False), *late)
    my_in, my_scale = mine(tokens).astype(f32), mine(scale1)
    normed2, hidden_in, wo_dev = mix(att_all, tokens, gain2, places, wo_pieces, me)
    wo = (jnp.zeros((1,), jnp.int32), [wo_dev])
    if n_dp == 4 and n_ctx == 2:
        wu = shards_of(wide[2], firsts[4], after(seconds[4], normed2))
    scale2 = lax.rsqrt(jnp.mean(hidden_in * hidden_in, axis=-1, keepdims=True) + norm_eps)

    hidden, grad_gate, grad_up, partial2 = ffn(normed2, grad_hidden, wg, wu)
    make = lambda: WeightGrad(n_dp, n_ctx, offs)
    grad_d = make().start(grad_ffn, hidden)
    ffn_part = wide_matmul(hidden, wd, True, bf)
    grad_g = make().start(after(normed2, grad_d.far), grad_gate)
    grad_norm2 = after(scatter_sum(partial2), grad_d.along_x(), ffn_part, grad_g.far)
    part_g2 = jnp.sum(grad_norm2 * hidden_in * scale2, axis=0)
    grad_h = (
        mine(cotangent).astype(f32)
        + scale2 * gain2 * grad_norm2
        - hidden_in * scale2**3 * jnp.mean(hidden_in * gain2 * grad_norm2, axis=-1, keepdims=True)
    )
    local_mixed = (branch_scale * grad_h).astype(bf)
    grad_mixed = gather_rows(local_mixed)

    grad_u = make().start(after(normed2, local_mixed), grad_up)
    grad_mixed = after(grad_mixed, grad_d.along_y(), grad_g.along_x(), grad_u.far)
    ffn_part = scatter_sum(after(ffn_part, grad_mixed))

    grad_att = wide_matmul(grad_mixed, wo, False, bf)
    back = lambda k, v, m: attention_bwd(query, att, grad_att, lse, k, v, q_meta, m, feats // HEAD)
    if n_ctx == 2:
        grad_q1, grad_k1, grad_v1 = back(keys_all[1:], values_all[1:], k_metas[1:])
        grad_att = after(grad_att, grad_q1, grad_g.along_y(), grad_u.along_x())
        grad_q0, grad_k0, grad_v0 = back(keys_all[:1], values_all[:1], k_metas[:1])
        grad_q = (grad_q0.astype(f32) + grad_q1.astype(f32)).astype(bf)
        grad_ks, grad_vs = grad_k0 + grad_k1, grad_v0 + grad_v1
    else:
        grad_g.along_y(), grad_u.along_x()
        grad_q, grad_ks, grad_vs = back(keys_all, values_all, k_metas)
    if n_ctx == 2:
        merge = lambda pair: (pair[0].astype(f32) + trade(pair[1]).astype(f32)).astype(bf)
    else:
        merge = lambda whole: lax.psum_scatter(whole[0], "ctx", scatter_dimension=0, tiled=True)
    grad_k, grad_v = merge(grad_ks), merge(grad_vs)

    grad_o = make().start(grad_mixed, att)
    grad_q = after(grad_q, grad_o.far)
    partial1, part_g1 = qkv_back((grad_q, grad_k, grad_v), (wq, wk, wv), tokens, scale1)
    output = hidden_in + branch_scale * after(ffn_part, grad_q)
    output = gather_rows(lax.optimization_barrier(output.astype(bf)))
    grads_a = [make().start(normed1, g) for g in (grad_q, grad_k, grad_v)]
    grad_norm1 = after(scatter_sum(after(partial1, output)), grad_o.along_x(), *[g.along_x() for g in grads_a[:2]])
    gain_sum = jnp.concatenate([part_g1, part_g2[None, :]])
    gain_sum = sum_all(gain_sum, (("dp", n_dp), ("ctx", n_ctx), ("tensor", n_tp)))
    grad_norm1 = after(grad_norm1, gain_sum)
    grad_in = (
        grad_h
        + my_scale * gain1 * grad_norm1
        - my_in * my_scale**3 * jnp.mean(my_in * gain1 * grad_norm1, axis=-1, keepdims=True)
    )
    local_in = lax.optimization_barrier(grad_in.astype(bf))
    grad_in = gather_rows(local_in).astype(f32)
    gain_sum = lax.dynamic_slice_in_dim(gain_sum, dp * shard, shard, 1)

    grad_u.along_y(grad_k, grad_v)
    grad_o.along_y(grad_k, grad_v)
    grads_a[2].along_x(local_in)
    for g in grads_a:
        g.along_y()
    sum_wd = grad_d.finish(hidden_dev, local_in).T
    sum_wg, sum_wu = grad_g.finish(hidden_dev, local_in), grad_u.finish(hidden_dev, local_in)
    sum_wo = grad_o.finish(feats, local_in).T
    sum_wq, sum_wk, sum_wv = [g.finish(feats, local_in) for g in grads_a]
    return (output.astype(f32), grad_in, gain_sum[0], sum_wq, sum_wk, sum_wv, sum_wo, gain_sum[1], sum_wg, sum_wu, sum_wd)


def solution(mesh):
    rows, col, row = P(("dp", "ctx"), None), P("dp", "tensor"), P("tensor", "dp")
    sizes = (mesh.shape["dp"], mesh.shape["ctx"], mesh.shape["tensor"])
    return jax.shard_map(
        functools.partial(per_device, *sizes),
        mesh=mesh,
        in_specs=(rows, P("dp"), P("dp"), P("dp"), col, col, col, row, P("dp"), col, col, row, rows),
        out_specs=(rows, rows, P("dp"), col, col, col, row, P("dp"), col, col, row),
        check_vma=False,
    )
```

time: 1020 us -> 688 us (0.67)
  matrix products: 157 us -> 0 us
  starting transfers between devices: 174 us -> 39.9 us
  Pallas kernels: 58.6 us -> 191 us
  waiting for transfers between devices: 337 us -> 272 us
  local copies, waits for them, and re-layouts: 108 us -> 60.2 us
  other arithmetic: 135 us -> 95.8 us
  blocking collectives: 38.8 us -> 0 us
  between operations: 2.72 us -> 15.6 us
    dot_general x39 -> x0, matrix products: 157 us -> none  [dot(): return lax.dot_general(a, b, (dims, ((), ())), preferred_element_type=f32)]
    pallas_call x5 -> x19, Pallas kernels: 58.6 us -> 191 us  [the longest x7 42.1 us: weight_grad(): pl.pallas_call(grad_kernel, out_shape=(half, half), in_specs=[SM, VM, VM]...]
    ppermute x83 -> x48, starting transfers between devices: 159 us -> 28.8 us  [the longest x7 9.42 us: along_y(): self.other = lax.ppermute(after(self.total, *late), 'ctx', swap(2, 1))]
    ppermute x83 -> x48, waiting for transfers between devices: 326 us -> 212 us  [the longest x7 109 us: along_x(): other = after(lax.ppermute(self.far, 'dp', swap(4, 2)), *late).astype(f32)]
    dynamic_update_slice x21 -> x5, local copies, waits for them, and re-layouts: 60.4 us -> 1.5 us  [the longest x4 0.92 us: per_device(): gains = lax.dynamic_update_slice(gains, own[j].astype(f32), (0, offs[j]))]
    all_gather x1 -> x0, blocking collectives: 38.8 us -> none  [per_device(): lax.all_gather(jnp.stack([gain_attn, gain_ffn]).astype(bf), 'dp', axis=1,...]
    ppermute x4, waiting for transfers between devices: 6.56 us -> 41.1 us  [per_device(): trade = lambda a: lax.ppermute(a, 'ctx', swap(2, 1))]
    concatenate x10 -> x1, other arithmetic: 29.9 us -> 0.02 us  [per_device(): gain_sum = jnp.concatenate([part_g1, part_g2[None, :]])]
  transfers between devices with their start and end apart: 106 -> 71, of which waited for: 30 -> 34; matrix products, arithmetic and copies ran while one was open for 31% -> 15% of each run, Pallas kernels for 6% -> 23%
where the time goes in v2:
time: 688 us; the launch traced here: 675 us
  waiting for transfers between devices  272 us (40%)
  Pallas kernels  191 us (28%)
  other arithmetic  95.8 us (14%)
  local copies, waits for them, and re-layouts  60.2 us (9%)
  starting transfers between devices  39.9 us (6%)
  between operations  15.6 us (2%)
    ppermute x7, waiting for transfers between devices, along_x(): other = after(lax.ppermute(self.far, 'dp', swap(4, 2)), *late).astype(f32)  109 us
    pallas_call x7, Pallas kernels, weight_grad(): pl.pallas_call(grad_kernel, out_shape=(half, half), in_specs=[SM, VM, VM]...  42.1 us
    ppermute x4, waiting for transfers between devices, per_device(): trade = lambda a: lax.ppermute(a, 'ctx', swap(2, 1))  41.1 us
    unnamed x186, local copies, waits for them, and re-layouts  37.8 us
    pallas_call x2, Pallas kernels, attention_bwd(): pl.pallas_call(functools.partial(attn_bwd_kernel, parts, heads), grid=(bl...  33.6 us
    ppermute x7, waiting for transfers between devices, along_y(): self.other = lax.ppermute(after(self.total, *late), 'ctx', swap(2, 1))  32.1 us
    pallas_call x1, Pallas kernels, ffn(): pl.pallas_call(functools.partial(ffn_kernel, ns, width), out_shape=(mid,...  27.6 us
    pallas_call x3, Pallas kernels, wide_matmul(): pl.pallas_call(functools.partial(wide_kernel, ns, nt, width), out_shape=j...  24.1 us
  transfers between devices with their start and end apart: 71, of which 34 were waited for; matrix products, arithmetic and copies ran while one was open for 15% of the time, Pallas kernels for 23%

profile of v2, /device:TPU:26, one launch (start us, length us, event | category | flops | bytes accessed | tf_op | source)
XLA Modules:
  0.0 674.9 jit_solution(4230735867865781865)
XLA Ops:
  13.8 3.6 fusion.9
  23.7 7.6 %collective-permute-done.1.rest_2_.rest_9_ = bf16[592,640]{1,0:T(8,128)(2,1)} collective-permute-done((bf16[592,640]{1,0:T(8,128)(2,1)}, bf16[592,640]{1,0:T(8,128)(2,1)}, u32[]{:S(2)}, u32[]{:S(2)}) %collective-permute-start.1) | collective-permute-done | bytes 757792 | tf_op jit(solution)/shard_map/ppermute | solution.py:546
  38.6 6.2 shard_map.212.refs_7_.refs_12_
  46.3 4.4 collective-permute-done.3.rest_2_.rest_13_
  54.1 4.8 shard_map.213.refs_9_.refs_13_
  59.0 11.0 %collective-permute-done.5.rest_2_.rest_5_ = bf16[576,640]{1,0:T(8,128)(2,1)} collective-permute-done((bf16[576,640]{1,0:T(8,128)(2,1)}, bf16[576,640]{1,0:T(8,128)(2,1)}, u32[]{:S(2)}, u32[]{:S(2)}) %collective-permute-start.5) | collective-permute-done | bytes 737312 | tf_op jit(solution)/shard_map/ppermute | solution.py:546
  76.5 4.9 shard_map.214.refs_6_.refs_8_
  82.4 7.7 %collective-permute-done.10.refs_10_.refs_13_ = bf16[640,640]{1,0:T(8,128)(2,1)S(1)} collective-permute-done((bf16[640,640]{1,0:T(8,128)(2,1)S(1)}, bf16[640,640]{1,0:T(8,128)(2,1)S(1)}, u32[]{:S(2)}, u32[]{:S(2)}) %collective-permute-start.10) | collective-permute-done | bytes 819232 | tf_op jit(solution)/shard_map/ppermute | solution.py:661
  103.9 17.4 %shard_map.215 = (bf16[640,640]{1,0:T(8,128)(2,1)S(1)}, f32[5,8,640]{2,1,0:T(8,128)S(1)}) custom-call(s32[1,640]{1,0:T(1,128)S(1)} %broadcast_in_dim.19.refs_0_, s32[1,640]{1,0:T(1,128)S(1)} %broadcast_in_dim.20.refs_1_, s32[640,1]{1,0:T(8,128)S(1)} %broadcast_in_dim.52.refs_2_.refs_4_, s32[640,1]{1,0:T(8,128)S(1)} %broadcast_in_dim.53.refs_3_.refs_4_, ...), custom_call_target="tpu_custom_call" | custom-call | flops 1024 | bytes 1024 | tf_op jit(solution)/shard_map/pallas_call | solution.py:401
  127.9 12.5 %collective-permute-done.14.rest_6_ = bf16[2,288,640]{2,1,0:T(8,128)(2,1)} collective-permute-done((bf16[2,288,640]{2,1,0:T(8,128)(2,1)S(1)}, bf16[2,288,640]{2,1,0:T(8,128)(2,1)}, u32[]{:S(2)}, u32[]{:S(2)}) %collective-permute-start.14) | collective-permute-done | bytes 737312 | tf_op jit(solution)/shard_map/ppermute | solution.py:562
  147.0 12.1 %shard_map.216.dh_hbm = f32[640,1536]{1,0:T(8,128)S(1)} custom-call(s32[6]{0:T(128)S(1)} %stack.71.offs, bf16[640,2304]{1,0:T(8,128)(2,1)S(1)} %copy-done.5, bf16[576,1536]{1,0:T(8,128)(2,1)} %pad.32.rest_0_, bf16[576,1536]{1,0:T(8,128)(2,1)} %collective-permute-done.18.rest_1_, bf16[288,1536]{1,0:T(8,128)(2,1)} %collective-permute-done.11.rest_2_, ...), custom_call_target="tpu_custom_call" | custom-call | flops 1024 | bytes 1024 | tf_op jit(solution)/shard_map/pallas_call | solution.py:130
  165.5 17.6 %collective-permute-done.22.rest_4_ = bf16[288,1536]{1,0:T(8,128)(2,1)S(1)} collective-permute-done((bf16[288,1536]{1,0:T(8,128)(2,1)}, bf16[288,1536]{1,0:T(8,128)(2,1)S(1)}, u32[]{:S(2)}, u32[]{:S(2)}) %collective-permute-start.22) | collective-permute-done | bytes 884768 | tf_op jit(solution)/shard_map/ppermute | solution.py:559
  191.8 19.7 %shard_map.217 = (bf16[640,2304]{1,0:T(8,128)(2,1)}, f32[160,2304]{1,0:T(8,128)}, bf16[2304,640]{1,0:T(8,128)(2,1)}) custom-call(s32[1]{0:T(128)} %bitcast.me_ref, s32[10]{0:T(128)} %stack.64.offs, bf16[4,640,640]{2,1,0:T(8,128)(2,1)} %bitcast.26, bf16[640,2304]{1,0:T(8,128)(2,1)} %x_ref.3, f32[1,2304]{1,0:T(1,128)} %get-tuple-element.211.gain_ref, ...), custom_call_target="tpu_custom_call" | custom-call | flops 1024 | bytes 1024 | tf_op jit(solution)/shard_map/pallas_call | solution.py:289
  215.6 27.6 %shard_map.218 = (bf16[640,1536]{1,0:T(8,128)(2,1)}, bf16[640,1536]{1,0:T(8,128)(2,1)}, bf16[640,1536]{1,0:T(8,128)(2,1)}, bf16[640,2304]{1,0:T(8,128)(2,1)}) custom-call(s32[6]{0:T(128)} %copy-done.63, bf16[640,2304]{1,0:T(8,128)(2,1)} %get-tuple-element.111.n_hbm.a_ref, f32[640,1536]{1,0:T(8,128)} %copy-done.10, bf16[576,1536]{1,0:T(8,128)(2,1)} %pad.33.rest_0_, ...), custom_call_target="tpu_custom_call" | custom-call | flops 1024 | bytes 1024 | tf_op jit(solution)/shard_map/pallas_call | solution.py:233
  246.5 8.8 %shard_map.220 = (bf16[1152,1536]{1,0:T(8,128)(2,1)S(1)}, bf16[1152,1536]{1,0:T(8,128)(2,1)}) custom-call(s32[4]{0:T(128)S(1)} %pad_add_fusion.offs, bf16[640,2304]{1,0:T(8,128)(2,1)S(1)} %copy-done.6, bf16[640,1536]{1,0:T(8,128)(2,1)S(1)} %copy-done.19), custom_call_target="tpu_custom_call" | custom-call | flops 1024 | bytes 1024 | tf_op jit(solution)/shard_map/pallas_call | solution.py:321
  257.7 5.9 collective-permute-done.35
  263.7 4.3 add_convert_fusion.5
  267.9 8.9 %shard_map.221 = (bf16[1152,1536]{1,0:T(8,128)(2,1)S(1)}, bf16[1152,1536]{1,0:T(8,128)(2,1)}) custom-call(s32[4]{0:T(128)S(1)} %pad_add_fusion.offs, bf16[640,2304]{1,0:T(8,128)(2,1)S(1)} %copy-done.3, bf16[640,1536]{1,0:T(8,128)(2,1)S(1)} %copy-done.56), custom_call_target="tpu_custom_call" | custom-call | flops 1024 | bytes 1024 | tf_op jit(solution)/shard_map/pallas_call | solution.py:321
  282.9 8.7 %shard_map.219 = bf16[640,2304]{1,0:T(8,128)(2,1)S(1)} custom-call(s32[6]{0:T(128)S(1)} %copy-done.64, bf16[640,1536]{1,0:T(8,128)(2,1)S(1)} %copy-done.20, bf16[576,1536]{1,0:T(8,128)(2,1)} %pad.32.rest_0_, bf16[576,1536]{1,0:T(8,128)(2,1)} %collective-permute-done.18.rest_1_, bf16[288,1536]{1,0:T(8,128)(2,1)} %collective-permute-done.11.rest_2_, ...), custom_call_target="tpu_custom_call" | custom-call | flops 1024 | bytes 1024 | tf_op jit(solution)/shard_map/pallas_call | solution.py:130
  293.2 26.7 %collective-permute-done.36 = bf16[576,1536]{1,0:T(8,128)(2,1)} collective-permute-done((bf16[576,1536]{1,0:T(8,128)(2,1)}, bf16[576,1536]{1,0:T(8,128)(2,1)}, u32[]{:S(2)}, u32[]{:S(2)}) %collective-permute-start.36) | collective-permute-done | bytes 1769504 | tf_op jit(solution)/shard_map/ppermute | solution.py:594
  319.9 4.4 add_convert_fusion.4
  325.6 3.8 add_convert_fusion.3
  336.6 7.0 %shard_map.222 = (bf16[1152,1536]{1,0:T(8,128)(2,1)S(1)}, bf16[1152,1536]{1,0:T(8,128)(2,1)S(1)}) custom-call(s32[4]{0:T(128)S(1)} %pad_add_fusion.offs, bf16[640,2304]{1,0:T(8,128)(2,1)S(1)} %copy-done.4, bf16[640,1536]{1,0:T(8,128)(2,1)S(1)} %copy-done.55), custom_call_target="tpu_custom_call" | custom-call | flops 1024 | bytes 1024 | tf_op jit(solution)/shard_map/pallas_call | solution.py:321
  345.8 39.1 %collective-permute-done.39 = bf16[576,1536]{1,0:T(8,128)(2,1)S(1)} collective-permute-done((bf16[576,1536]{1,0:T(8,128)(2,1)}, bf16[576,1536]{1,0:T(8,128)(2,1)S(1)}, u32[]{:S(2)}, u32[]{:S(2)}) %collective-permute-start.39) | collective-permute-done | bytes 1769504 | tf_op jit(solution)/shard_map/ppermute | solution.py:594
  384.9 3.4 add_convert_fusion.2
  396.8 4.1 shard_map.226
  405.0 16.8 %shard_map.224 = (bf16[640,640]{1,0:T(8,128)(2,1)S(1)}, bf16[640,640]{1,0:T(8,128)(2,1)S(1)}, bf16[640,640]{1,0:T(8,128)(2,1)S(1)}) custom-call(s32[1,640]{1,0:T(1,128)S(1)} %broadcast_in_dim.19.refs_0_, s32[1,640]{1,0:T(1,128)S(1)} %broadcast_in_dim.20.refs_1_, f32[640,128]{1,0:T(8,128)S(1)} %pad_maximum_fusion.cos_ref.refs_2_.refs_6_, ...), custom_call_target="tpu_custom_call" | custom-call | flops 1024 | bytes 1024 | tf_op jit(solution)/shard_map/pallas_call | solution.py:490
  422.7 9.9 %collective-permute-done.42 = bf16[576,1536]{1,0:T(8,128)(2,1)} collective-permute-done((bf16[576,1536]{1,0:T(8,128)(2,1)}, bf16[576,1536]{1,0:T(8,128)(2,1)}, u32[]{:S(2)}, u32[]{:S(2)}) %collective-permute-start.42) | collective-permute-done | bytes 1769504 | tf_op jit(solution)/shard_map/ppermute | solution.py:594
  432.6 3.4 add_convert_fusion
  436.0 16.9 %shard_map.225 = (bf16[640,640]{1,0:T(8,128)(2,1)S(1)}, bf16[640,640]{1,0:T(8,128)(2,1)S(1)}, bf16[640,640]{1,0:T(8,128)(2,1)S(1)}) custom-call(s32[1,640]{1,0:T(1,128)S(1)} %broadcast_in_dim.19.refs_0_, s32[1,640]{1,0:T(1,128)S(1)} %broadcast_in_dim.20.refs_1_, f32[640,128]{1,0:T(8,128)S(1)} %pad_maximum_fusion.cos_ref.refs_2_.refs_6_, ...), custom_call_target="tpu_custom_call" | custom-call | flops 1024 | bytes 1024 | tf_op jit(solution)/shard_map/pallas_call | solution.py:490
  462.9 19.2 %collective-permute-done.45 = bf16[640,640]{1,0:T(8,128)(2,1)S(1)} collective-permute-done((bf16[640,640]{1,0:T(8,128)(2,1)}, bf16[640,640]{1,0:T(8,128)(2,1)S(1)}, u32[]{:S(2)}, u32[]{:S(2)}) %collective-permute-start.45) | collective-permute-done | bytes 819232 | tf_op jit(solution)/shard_map/ppermute | solution.py:661
  483.7 14.2 %collective-permute-done.44 = bf16[640,640]{1,0:T(8,128)(2,1)S(1)} collective-permute-done((bf16[640,640]{1,0:T(8,128)(2,1)}, bf16[640,640]{1,0:T(8,128)(2,1)S(1)}, u32[]{:S(2)}, u32[]{:S(2)}) %collective-permute-start.44) | collective-permute-done | bytes 819232 | tf_op jit(solution)/shard_map/ppermute | solution.py:661
  501.5 10.9 %shard_map.227 = (bf16[640,2304]{1,0:T(8,128)(2,1)S(1)}, f32[1,2304]{1,0:T(1,128)S(1)}) custom-call(s32[4]{0:T(128)S(1)} %pad_add_fusion.offs, bf16[640,2304]{1,0:T(8,128)(2,1)S(1)} %copy-done.1, f32[640,1]{1,0:T(8,128)S(1)} %rsqrt.19.scale_ref, bf16[640,640]{1,0:T(8,128)(2,1)S(1)} %copy-done.23, bf16[640,640]{1,0:T(8,128)(2,1)S(1)} %add_convert_fusion.7.rest_1_.b_ref, ...), custom_call_target="tpu_custom_call" | custom-call | flops 1024 | bytes 1024 | tf_op jit(solution)/shard_map/pallas_call | solution.py:164
  514.9 4.7 all-gather.10.cloned.1.call-done
  521.0 4.1 shard_map.229
  525.8 4.1 shard_map.228
  530.4 3.4 collective-permute-done.52
  546.0 5.2 shard_map.230
  552.7 6.2 collective-permute-done.46
  562.6 12.0 %collective-permute-done.50 = bf16[576,640]{1,0:T(8,128)(2,1)S(1)} collective-permute-done((bf16[576,640]{1,0:T(8,128)(2,1)S(1)}, bf16[576,640]{1,0:T(8,128)(2,1)S(1)}, u32[]{:S(2)}, u32[]{:S(2)}) %collective-permute-start.50) | collective-permute-done | bytes 737312 | tf_op jit(solution)/shard_map/ppermute | solution.py:594
  575.8 12.3 %collective-permute-done.48 = bf16[576,640]{1,0:T(8,128)(2,1)S(1)} collective-permute-done((bf16[576,640]{1,0:T(8,128)(2,1)S(1)}, bf16[576,640]{1,0:T(8,128)(2,1)S(1)}, u32[]{:S(2)}, u32[]{:S(2)}) %collective-permute-start.48) | collective-permute-done | bytes 737312 | tf_op jit(solution)/shard_map/ppermute | solution.py:594
  601.6 7.3 %collective-permute-done.61 = bf16[576,640]{1,0:T(8,128)(2,1)} collective-permute-done((bf16[576,640]{1,0:T(8,128)(2,1)}, bf16[576,640]{1,0:T(8,128)(2,1)}, u32[]{:S(2)}, u32[]{:S(2)}) %collective-permute-start.61) | collective-permute-done | bytes 737312 | tf_op jit(solution)/shard_map/ppermute | solution.py:603
  615.7 9.0 %collective-permute-done.57 = bf16[576,640]{1,0:T(8,128)(2,1)} collective-permute-done((bf16[576,640]{1,0:T(8,128)(2,1)}, bf16[576,640]{1,0:T(8,128)(2,1)}, u32[]{:S(2)}, u32[]{:S(2)}) %collective-permute-start.57) | collective-permute-done | bytes 737312 | tf_op jit(solution)/shard_map/ppermute | solution.py:603
  624.6 15.8 %collective-permute-done.56 = bf16[576,640]{1,0:T(8,128)(2,1)} collective-permute-done((bf16[576,640]{1,0:T(8,128)(2,1)}, bf16[576,640]{1,0:T(8,128)(2,1)}, u32[]{:S(2)}, u32[]{:S(2)}) %collective-permute-start.56) | collective-permute-done | bytes 737312 | tf_op jit(solution)/shard_map/ppermute | solution.py:603
  644.5 3.8 add_bitcast_fusion
  648.2 4.4 convert_add_fusion
  656.6 3.8 convert_add_fusion.1
  663.0 4.9 convert_element_type.395
  (410 shorter events, 185.0 us)
Async XLA Ops:
  7.2 85.7 %all-gather.16.cloned.1.call-start = ((), (), s32[]{:S(2)}) async-start(), calls=%async_computation.10 | async-start | bytes 3686400 | tf_op jit(solution)/shard_map/all_gather | solution.py:630
  11.7 20.3 %collective-permute-start = (bf16[592,640]{1,0:T(8,128)(2,1)}, bf16[592,640]{1,0:T(8,128)(2,1)}, u32[]{:S(2)}, u32[]{:S(2)}) collective-permute-start(bf16[592,640]{1,0:T(8,128)(2,1)} %pad_dynamic-update-slice_fusion.rest_0_.rest_7_), channel_id=1, source_target_pairs={{0,8},{8,0},{16,24},{24,16},{1,9},{9,1},{17,25},{25,17},{2,10},{10... | collective-permute-start | bytes 2273288 | tf_op jit(solution)/shard_map/ppermute | solution.py:547
  11.7 19.7 %collective-permute-start.1 = (bf16[592,640]{1,0:T(8,128)(2,1)}, bf16[592,640]{1,0:T(8,128)(2,1)}, u32[]{:S(2)}, u32[]{:S(2)}) collective-permute-start(bf16[592,640]{1,0:T(8,128)(2,1)} %pad_dynamic-update-slice_fusion.rest_0_.rest_7_), channel_id=1, source_target_pairs={{0,16},{8,24},{16,0},{24,8},{1,17},{9,25},{17,1},{25,9},{2,18},{10... | collective-permute-start | bytes 2273288 | tf_op jit(solution)/shard_map/ppermute | solution.py:546
  13.6 175.3 %all-gather.14.cloned.1.call-start = ((), (), s32[]{:S(2)}) async-start(), calls=%async_computation.9 | async-start | bytes 4096000 | tf_op jit(solution)/shard_map/all_gather | solution.py:716
  31.5 19.2 %collective-permute-start.3 = (bf16[576,640]{1,0:T(8,128)(2,1)}, bf16[576,640]{1,0:T(8,128)(2,1)}, u32[]{:S(2)}, u32[]{:S(2)}) collective-permute-start(bf16[576,640]{1,0:T(8,128)(2,1)} %pad.31.rest_0_.rest_11_), channel_id=1, source_target_pairs={{0,16},{8,24},{16,0},{24,8},{1,17},{9,25},{17,1},{25,9},{2,18},{10... | collective-permute-start | bytes 2211848 | tf_op jit(solution)/shard_map/ppermute | solution.py:546
  44.7 25.2 %collective-permute-start.8 = (bf16[640,640]{1,0:T(8,128)(2,1)}, bf16[640,640]{1,0:T(8,128)(2,1)}, u32[]{:S(2)}, u32[]{:S(2)}) collective-permute-start(bf16[640,640]{1,0:T(8,128)(2,1)} %shard_map.212.refs_7_.refs_12_), channel_id=1, source_target_pairs={{0,4},{4,0},{1,5},{5,1},{2,6},{6,2},{3,7},{7,3},{8,12},{12,8},{9,1... | collective-permute-start | bytes 2457608 | tf_op jit(solution)/shard_map/ppermute | solution.py:661
  50.7 19.2 %collective-permute-start.5 = (bf16[576,640]{1,0:T(8,128)(2,1)}, bf16[576,640]{1,0:T(8,128)(2,1)}, u32[]{:S(2)}, u32[]{:S(2)}) collective-permute-start(bf16[576,640]{1,0:T(8,128)(2,1)} %pad.30.rest_0_.rest_3_), channel_id=1, source_target_pairs={{0,16},{8,24},{16,0},{24,8},{1,17},{9,25},{17,1},{25,9},{2,18},{10... | collective-permute-start | bytes 2211848 | tf_op jit(solution)/shard_map/ppermute | solution.py:546
  69.9 21.4 %collective-permute-start.11 = (bf16[288,1536]{1,0:T(8,128)(2,1)S(1)}, bf16[288,1536]{1,0:T(8,128)(2,1)}, u32[]{:S(2)}, u32[]{:S(2)}) collective-permute-start(bf16[288,1536]{1,0:T(8,128)(2,1)S(1)} %constant_dynamic-slice_fusion.2), channel_id=1, source_target_pairs={{0,16},{8,24},{16,0},{24,8},{1,17},{9,25},{17,1},{25,9},{2,18},{10... | collective-permute-start | bytes 2654216 | tf_op jit(solution)/shard_map/ppermute | solution.py:562
  70.5 19.6 %collective-permute-start.10 = (bf16[640,640]{1,0:T(8,128)(2,1)S(1)}, bf16[640,640]{1,0:T(8,128)(2,1)S(1)}, u32[]{:S(2)}, u32[]{:S(2)}) collective-permute-start(bf16[640,640]{1,0:T(8,128)(2,1)S(1)} %shard_map.213.refs_9_.refs_13_), channel_id=1, source_target_pairs={{0,4},{4,0},{1,5},{5,1},{2,6},{6,2},{3,7},{7,3},{8,12},{12,8},{9,1... | collective-permute-start | bytes 2457608 | tf_op jit(solution)/shard_map/ppermute | solution.py:661
  72.5 69.9 %collective-permute-start.18 = (bf16[576,1536]{1,0:T(8,128)(2,1)}, bf16[576,1536]{1,0:T(8,128)(2,1)}, u32[]{:S(2)}, u32[]{:S(2)}) collective-permute-start(bf16[576,1536]{1,0:T(8,128)(2,1)} %pad.32.rest_0_), channel_id=1, source_target_pairs={{0,8},{8,0},{16,24},{24,16},{1,9},{9,1},{17,25},{25,17},{2,10},{10... | collective-permute-start | bytes 5308424 | tf_op jit(solution)/shard_map/ppermute | solution.py:675
  91.3 32.5 %collective-permute-start.12 = (bf16[288,1536]{1,0:T(8,128)(2,1)}, bf16[288,1536]{1,0:T(8,128)(2,1)}, u32[]{:S(2)}, u32[]{:S(2)}) collective-permute-start(bf16[288,1536]{1,0:T(8,128)(2,1)} %collective-permute-done.11.rest_2_), channel_id=1, source_target_pairs={{0,4},{4,0},{1,5},{5,1},{2,6},{6,2},{3,7},{7,3},{8,12},{12,8},{9,1... | collective-permute-start | bytes 2654216 | tf_op jit(solution)/shard_map/ppermute | solution.py:559
  97.1 26.7 %collective-permute-start.13 = (bf16[2,288,640]{2,1,0:T(8,128)(2,1)}, bf16[2,288,640]{2,1,0:T(8,128)(2,1)}, u32[]{:S(2)}, u32[]{:S(2)}) collective-permute-start(bf16[2,288,640]{2,1,0:T(8,128)(2,1)} %constant_dynamic-slice_fusion.1), channel_id=1, source_target_pairs={{0,16},{8,24},{16,0},{24,8},{1,17},{9,25},{17,1},{25,9},{2,18},{10... | collective-permute-start | bytes 2211848 | tf_op jit(solution)/shard_map/ppermute | solution.py:562
  122.2 202.1 %reduce-scatter.4.cloned.1.call-start = ((), (), s32[]{:S(2)}) async-start(), calls=%async_computation.3 | async-start | bytes 3686400 | tf_op jit(solution)/shard_map/reduce_scatter | solution.py:536
  141.5 20.2 %collective-permute-start.17 = (bf16[288,1536]{1,0:T(8,128)(2,1)}, bf16[288,1536]{1,0:T(8,128)(2,1)}, u32[]{:S(2)}, u32[]{:S(2)}) collective-permute-start(bf16[288,1536]{1,0:T(8,128)(2,1)} %constant_dynamic-slice_fusion), channel_id=1, source_target_pairs={{0,16},{8,24},{16,0},{24,8},{1,17},{9,25},{17,1},{25,9},{2,18},{10... | collective-permute-start | bytes 2654216 | tf_op jit(solution)/shard_map/ppermute | solution.py:562
  142.4 46.5 %collective-permute-start.23 = (bf16[4,576,640]{2,1,0:T(8,128)(2,1)}, bf16[4,576,640]{2,1,0:T(8,128)(2,1)}, u32[]{:S(2)}, u32[]{:S(2)}) collective-permute-start(bf16[4,576,640]{2,1,0:T(8,128)(2,1)} %bitcast.14.rest_0_), channel_id=1, source_target_pairs={{0,8},{8,0},{16,24},{24,16},{1,9},{9,1},{17,25},{25,17},{2,10},{10... | collective-permute-start | bytes 8847368 | tf_op jit(solution)/shard_map/ppermute | solution.py:675
  142.4 19.2 %collective-permute-start.16 = (bf16[2,288,640]{2,1,0:T(8,128)(2,1)}, bf16[2,288,640]{2,1,0:T(8,128)(2,1)}, u32[]{:S(2)}, u32[]{:S(2)}) collective-permute-start(bf16[2,288,640]{2,1,0:T(8,128)(2,1)} %collective-permute-done.14.rest_6_), channel_id=1, source_target_pairs={{0,4},{4,0},{1,5},{5,1},{2,6},{6,2},{3,7},{7,3},{8,12},{12,8},{9,1... | collective-permute-start | bytes 2211848 | tf_op jit(solution)/shard_map/ppermute | solution.py:559
  161.7 21.5 %collective-permute-start.22 = (bf16[288,1536]{1,0:T(8,128)(2,1)}, bf16[288,1536]{1,0:T(8,128)(2,1)S(1)}, u32[]{:S(2)}, u32[]{:S(2)}) collective-permute-start(bf16[288,1536]{1,0:T(8,128)(2,1)} %collective-permute-done.17.rest_2_), channel_id=1, source_target_pairs={{0,4},{4,0},{1,5},{5,1},{2,6},{6,2},{3,7},{7,3},{8,12},{12,8},{9,1... | collective-permute-start | bytes 2654216 | tf_op jit(solution)/shard_map/ppermute | solution.py:559
  163.8 21.7 %collective-permute-start.21 = (bf16[288,1536]{1,0:T(8,128)(2,1)S(1)}, bf16[288,1536]{1,0:T(8,128)(2,1)}, u32[]{:S(2)}, u32[]{:S(2)}) collective-permute-start(bf16[288,1536]{1,0:T(8,128)(2,1)S(1)} %constant_dynamic-slice_fusion.4), channel_id=1, source_target_pairs={{0,16},{8,24},{16,0},{24,8},{1,17},{9,25},{17,1},{25,9},{2,18},{10... | collective-permute-start | bytes 2654216 | tf_op jit(solution)/shard_map/ppermute | solution.py:562
  165.0 46.9 %collective-permute-start.28 = (bf16[576,1536]{1,0:T(8,128)(2,1)}, bf16[576,1536]{1,0:T(8,128)(2,1)}, u32[]{:S(2)}, u32[]{:S(2)}) collective-permute-start(bf16[576,1536]{1,0:T(8,128)(2,1)} %pad.33.rest_0_), channel_id=1, source_target_pairs={{0,8},{8,0},{16,24},{24,16},{1,9},{9,1},{17,25},{25,17},{2,10},{10... | collective-permute-start | bytes 5308424 | tf_op jit(solution)/shard_map/ppermute | solution.py:675
  165.0 20.5 %collective-permute-start.24 = (bf16[2,288,640]{2,1,0:T(8,128)(2,1)}, bf16[2,288,640]{2,1,0:T(8,128)(2,1)}, u32[]{:S(2)}, u32[]{:S(2)}) collective-permute-start(bf16[2,288,640]{2,1,0:T(8,128)(2,1)} %collective-permute-done.13.rest_2_), channel_id=1, source_target_pairs={{0,8},{8,0},{16,24},{24,16},{1,9},{9,1},{17,25},{25,17},{2,10},{10... | collective-permute-start | bytes 2211848 | tf_op jit(solution)/shard_map/ppermute | solution.py:570
  185.5 25.9 %collective-permute-start.33 = (bf16[288,1536]{1,0:T(8,128)(2,1)}, bf16[288,1536]{1,0:T(8,128)(2,1)}, u32[]{:S(2)}, u32[]{:S(2)}) collective-permute-start(bf16[288,1536]{1,0:T(8,128)(2,1)} %collective-permute-done.21.rest_8_), channel_id=1, source_target_pairs={{0,4},{4,0},{1,5},{5,1},{2,6},{6,2},{3,7},{7,3},{8,12},{12,8},{9,1... | collective-permute-start | bytes 2654216 | tf_op jit(solution)/shard_map/ppermute | solution.py:559
  186.2 25.9 %collective-permute-start.31 = (bf16[576,1536]{1,0:T(8,128)(2,1)}, bf16[576,1536]{1,0:T(8,128)(2,1)}, u32[]{:S(2)}, u32[]{:S(2)}) collective-permute-start(bf16[576,1536]{1,0:T(8,128)(2,1)} %pad.34.rest_6_), channel_id=1, source_target_pairs={{0,8},{8,0},{16,24},{24,16},{1,9},{9,1},{17,25},{25,17},{2,10},{10... | collective-permute-start | bytes 5308424 | tf_op jit(solution)/shard_map/ppermute | solution.py:675
  188.9 23.2 %collective-permute-start.29 = (bf16[288,1536]{1,0:T(8,128)(2,1)}, bf16[288,1536]{1,0:T(8,128)(2,1)}, u32[]{:S(2)}, u32[]{:S(2)}) collective-permute-start(bf16[288,1536]{1,0:T(8,128)(2,1)} %collective-permute-done.17.rest_2_), channel_id=1, source_target_pairs={{0,8},{8,0},{16,24},{24,16},{1,9},{9,1},{17,25},{25,17},{2,10},{10... | collective-permute-start | bytes 2654216 | tf_op jit(solution)/shard_map/ppermute | solution.py:570
  191.7 20.4 %collective-permute-start.30 = (bf16[288,1536]{1,0:T(8,128)(2,1)}, bf16[288,1536]{1,0:T(8,128)(2,1)}, u32[]{:S(2)}, u32[]{:S(2)}) collective-permute-start(bf16[288,1536]{1,0:T(8,128)(2,1)} %copy-done.88), channel_id=1, source_target_pairs={{0,8},{8,0},{16,24},{24,16},{1,9},{9,1},{17,25},{25,17},{2,10},{10... | collective-permute-start | bytes 2654216 | tf_op jit(solution)/shard_map/ppermute | solution.py:570
  257.5 134.1 %all-gather.8.cloned.1.call-start = ((), (), s32[]{:S(2)}) async-start(), calls=%async_computation.4 | async-start | bytes 3686400 | tf_op jit(solution)/shard_map/all_gather | solution.py:540
  278.6 47.0 %collective-permute-start.37 = (bf16[1152,1536]{1,0:T(8,128)(2,1)}, bf16[1152,1536]{1,0:T(8,128)(2,1)}, u32[]{:S(2)}, u32[]{:S(2)}) collective-permute-start(bf16[1152,1536]{1,0:T(8,128)(2,1)} %get-tuple-element.109), channel_id=1, source_target_pairs={{0,8},{8,0},{16,24},{24,16},{1,9},{9,1},{17,25},{25,17},{2,10},{10... | collective-permute-start | bytes 10616840 | tf_op jit(solution)/shard_map/ppermute | solution.py:584
  278.9 41.1 %collective-permute-start.36 = (bf16[576,1536]{1,0:T(8,128)(2,1)}, bf16[576,1536]{1,0:T(8,128)(2,1)}, u32[]{:S(2)}, u32[]{:S(2)}) collective-permute-start(bf16[576,1536]{1,0:T(8,128)(2,1)} %add_convert_fusion.5), channel_id=1, source_target_pairs={{0,16},{8,24},{16,0},{24,8},{1,17},{9,25},{17,1},{25,9},{2,18},{10... | collective-permute-start | bytes 5308424 | tf_op jit(solution)/shard_map/ppermute | solution.py:594
  332.9 125.1 %reduce-scatter.6.cloned.1.call-start = ((), (), s32[]{:S(2)}) async-start(), calls=%async_computation.5 | async-start | bytes 3686400 | tf_op jit(solution)/shard_map/reduce_scatter | solution.py:536
  343.6 44.7 %collective-permute-start.40 = (bf16[1152,1536]{1,0:T(8,128)(2,1)S(1)}, bf16[1152,1536]{1,0:T(8,128)(2,1)S(1)}, u32[]{:S(2)}, u32[]{:S(2)}) collective-permute-start(bf16[1152,1536]{1,0:T(8,128)(2,1)S(1)} %get-tuple-element.114), channel_id=1, source_target_pairs={{0,8},{8,0},{16,24},{24,16},{1,9},{9,1},{17,25},{25,17},{2,10},{10... | collective-permute-start | bytes 10616840 | tf_op jit(solution)/shard_map/ppermute | solution.py:584
  343.6 41.2 %collective-permute-start.39 = (bf16[576,1536]{1,0:T(8,128)(2,1)}, bf16[576,1536]{1,0:T(8,128)(2,1)S(1)}, u32[]{:S(2)}, u32[]{:S(2)}) collective-permute-start(bf16[576,1536]{1,0:T(8,128)(2,1)} %add_convert_fusion.3), channel_id=1, source_target_pairs={{0,16},{8,24},{16,0},{24,8},{1,17},{9,25},{17,1},{25,9},{2,18},{10... | collective-permute-start | bytes 5308424 | tf_op jit(solution)/shard_map/ppermute | solution.py:594
  344.6 46.1 %collective-permute-start.38 = (bf16[576,1536]{1,0:T(8,128)(2,1)}, bf16[576,1536]{1,0:T(8,128)(2,1)}, u32[]{:S(2)}, u32[]{:S(2)}) collective-permute-start(bf16[576,1536]{1,0:T(8,128)(2,1)} %add_convert_fusion.4), channel_id=1, source_target_pairs={{0,4},{4,0},{1,5},{5,1},{2,6},{6,2},{3,7},{7,3},{8,12},{12,8},{9,1... | collective-permute-start | bytes 5308424 | tf_op jit(solution)/shard_map/ppermute | solution.py:603
  391.6 128.0 %all-gather.10.cloned.1.call-start = ((), (), s32[]{:S(2)}) async-start(), calls=%async_computation.6 | async-start | bytes 3686400 | tf_op jit(solution)/shard_map/all_gather | solution.py:540
  391.7 40.9 %collective-permute-start.42 = (bf16[576,1536]{1,0:T(8,128)(2,1)}, bf16[576,1536]{1,0:T(8,128)(2,1)}, u32[]{:S(2)}, u32[]{:S(2)}) collective-permute-start(bf16[576,1536]{1,0:T(8,128)(2,1)} %add_convert_fusion.1), channel_id=1, source_target_pairs={{0,16},{8,24},{16,0},{24,8},{1,17},{9,25},{17,1},{25,9},{2,18},{10... | collective-permute-start | bytes 5308424 | tf_op jit(solution)/shard_map/ppermute | solution.py:594
  392.1 43.9 %collective-permute-start.41 = (bf16[576,1536]{1,0:T(8,128)(2,1)}, bf16[576,1536]{1,0:T(8,128)(2,1)S(1)}, u32[]{:S(2)}, u32[]{:S(2)}) collective-permute-start(bf16[576,1536]{1,0:T(8,128)(2,1)} %add_convert_fusion.2), channel_id=1, source_target_pairs={{0,4},{4,0},{1,5},{5,1},{2,6},{6,2},{3,7},{7,3},{8,12},{12,8},{9,1... | collective-permute-start | bytes 5308424 | tf_op jit(solution)/shard_map/ppermute | solution.py:603
  400.9 54.9 %collective-permute-start.43 = (bf16[1152,640]{1,0:T(8,128)(2,1)S(1)}, bf16[1152,640]{1,0:T(8,128)(2,1)}, u32[]{:S(2)}, u32[]{:S(2)}) collective-permute-start(bf16[1152,640]{1,0:T(8,128)(2,1)S(1)} %get-tuple-element.123), channel_id=1, source_target_pairs={{0,8},{8,0},{16,24},{24,16},{1,9},{9,1},{17,25},{25,17},{2,10},{10... | collective-permute-start | bytes 4423688 | tf_op jit(solution)/shard_map/ppermute | solution.py:584
  460.6 128.6 %reduce-scatter.8.cloned.1.call-start = ((), (), s32[]{:S(2)}) async-start(), calls=%async_computation.7 | async-start | bytes 3686400 | tf_op jit(solution)/shard_map/reduce_scatter | solution.py:536
  460.7 21.5 %collective-permute-start.45 = (bf16[640,640]{1,0:T(8,128)(2,1)}, bf16[640,640]{1,0:T(8,128)(2,1)S(1)}, u32[]{:S(2)}, u32[]{:S(2)}) collective-permute-start(bf16[640,640]{1,0:T(8,128)(2,1)} %copy-done.66), channel_id=1, source_target_pairs={{0,4},{4,0},{1,5},{5,1},{2,6},{6,2},{3,7},{7,3},{8,12},{12,8},{9,1... | collective-permute-start | bytes 2457608 | tf_op jit(solution)/shard_map/ppermute | solution.py:661
  462.2 35.7 %collective-permute-start.44 = (bf16[640,640]{1,0:T(8,128)(2,1)}, bf16[640,640]{1,0:T(8,128)(2,1)S(1)}, u32[]{:S(2)}, u32[]{:S(2)}) collective-permute-start(bf16[640,640]{1,0:T(8,128)(2,1)} %copy-done.65), channel_id=1, source_target_pairs={{0,4},{4,0},{1,5},{5,1},{2,6},{6,2},{3,7},{7,3},{8,12},{12,8},{9,1... | collective-permute-start | bytes 2457608 | tf_op jit(solution)/shard_map/ppermute | solution.py:661
  519.6 143.3 %all-gather.12.cloned.1.call-start = ((), (), s32[]{:S(2)}) async-start(), calls=%async_computation.8 | async-start | bytes 3686400 | tf_op jit(solution)/shard_map/all_gather | solution.py:540
  539.4 19.4 %collective-permute-start.46 = (bf16[576,640]{1,0:T(8,128)(2,1)S(1)}, bf16[576,640]{1,0:T(8,128)(2,1)S(1)}, u32[]{:S(2)}, u32[]{:S(2)}) collective-permute-start(bf16[576,640]{1,0:T(8,128)(2,1)S(1)} %copy-done.89), channel_id=1, source_target_pairs={{0,16},{8,24},{16,0},{24,8},{1,17},{9,25},{17,1},{25,9},{2,18},{10... | collective-permute-start | bytes 2211848 | tf_op jit(solution)/shard_map/ppermute | solution.py:594
  543.6 31.0 %collective-permute-start.50 = (bf16[576,640]{1,0:T(8,128)(2,1)S(1)}, bf16[576,640]{1,0:T(8,128)(2,1)S(1)}, u32[]{:S(2)}, u32[]{:S(2)}) collective-permute-start(bf16[576,640]{1,0:T(8,128)(2,1)S(1)} %add_convert_fusion.12), channel_id=1, source_target_pairs={{0,16},{8,24},{16,0},{24,8},{1,17},{9,25},{17,1},{25,9},{2,18},{10... | collective-permute-start | bytes 2211848 | tf_op jit(solution)/shard_map/ppermute | solution.py:594
  544.4 43.8 %collective-permute-start.48 = (bf16[576,640]{1,0:T(8,128)(2,1)S(1)}, bf16[576,640]{1,0:T(8,128)(2,1)S(1)}, u32[]{:S(2)}, u32[]{:S(2)}) collective-permute-start(bf16[576,640]{1,0:T(8,128)(2,1)S(1)} %add_convert_fusion.14), channel_id=1, source_target_pairs={{0,16},{8,24},{16,0},{24,8},{1,17},{9,25},{17,1},{25,9},{2,18},{10... | collective-permute-start | bytes 2211848 | tf_op jit(solution)/shard_map/ppermute | solution.py:594
  551.2 50.4 %collective-permute-start.62 = (bf16[576,1536]{1,0:T(8,128)(2,1)}, bf16[576,1536]{1,0:T(8,128)(2,1)}, u32[]{:S(2)}, u32[]{:S(2)}) collective-permute-start(bf16[576,1536]{1,0:T(8,128)(2,1)} %add_convert_fusion), channel_id=1, source_target_pairs={{0,4},{4,0},{1,5},{5,1},{2,6},{6,2},{3,7},{7,3},{8,12},{12,8},{9,1... | collective-permute-start | bytes 5308424 | tf_op jit(solution)/shard_map/ppermute | solution.py:603
  552.7 39.9 %collective-permute-start.58 = (bf16[1152,640]{1,0:T(8,128)(2,1)}, bf16[1152,640]{1,0:T(8,128)(2,1)}, u32[]{:S(2)}, u32[]{:S(2)}) collective-permute-start(bf16[1152,640]{1,0:T(8,128)(2,1)} %get-tuple-element.142), channel_id=1, source_target_pairs={{0,8},{8,0},{16,24},{24,16},{1,9},{9,1},{17,25},{25,17},{2,10},{10... | collective-permute-start | bytes 4423688 | tf_op jit(solution)/shard_map/ppermute | solution.py:584
  561.1 47.7 %collective-permute-start.61 = (bf16[576,640]{1,0:T(8,128)(2,1)}, bf16[576,640]{1,0:T(8,128)(2,1)}, u32[]{:S(2)}, u32[]{:S(2)}) collective-permute-start(bf16[576,640]{1,0:T(8,128)(2,1)} %add_convert_fusion.15), channel_id=1, source_target_pairs={{0,4},{4,0},{1,5},{5,1},{2,6},{6,2},{3,7},{7,3},{8,12},{12,8},{9,1... | collective-permute-start | bytes 2211848 | tf_op jit(solution)/shard_map/ppermute | solution.py:603
  595.6 29.0 %collective-permute-start.57 = (bf16[576,640]{1,0:T(8,128)(2,1)}, bf16[576,640]{1,0:T(8,128)(2,1)}, u32[]{:S(2)}, u32[]{:S(2)}) collective-permute-start(bf16[576,640]{1,0:T(8,128)(2,1)} %add_convert_fusion.11), channel_id=1, source_target_pairs={{0,4},{4,0},{1,5},{5,1},{2,6},{6,2},{3,7},{7,3},{8,12},{12,8},{9,1... | collective-permute-start | bytes 2211848 | tf_op jit(solution)/shard_map/ppermute | solution.py:603
  597.1 43.3 %collective-permute-start.56 = (bf16[576,640]{1,0:T(8,128)(2,1)}, bf16[576,640]{1,0:T(8,128)(2,1)}, u32[]{:S(2)}, u32[]{:S(2)}) collective-permute-start(bf16[576,640]{1,0:T(8,128)(2,1)} %add_convert_fusion.13), channel_id=1, source_target_pairs={{0,4},{4,0},{1,5},{5,1},{2,6},{6,2},{3,7},{7,3},{8,12},{12,8},{9,1... | collective-permute-start | bytes 2211848 | tf_op jit(solution)/shard_map/ppermute | solution.py:603
  614.2 46.2 %collective-permute-start.60 = (bf16[576,640]{1,0:T(8,128)(2,1)}, bf16[576,640]{1,0:T(8,128)(2,1)}, u32[]{:S(2)}, u32[]{:S(2)}) collective-permute-start(bf16[576,640]{1,0:T(8,128)(2,1)} %add_convert_fusion.9), channel_id=1, source_target_pairs={{0,4},{4,0},{1,5},{5,1},{2,6},{6,2},{3,7},{7,3},{8,12},{12,8},{9,1... | collective-permute-start | bytes 2211848 | tf_op jit(solution)/shard_map/ppermute | solution.py:603
  (115 other events, 923.0 us)
Sparse Core Ops, SparseCore 0:
  13.7 58.8 all-gather.15
  122.4 63.2 all-gather.13
  257.6 56.5 reduce-scatter.3
  333.0 58.5 all-gather.7
  394.4 57.0 reduce-scatter.5
  460.8 58.8 all-gather.9
  522.5 57.8 reduce-scatter.7
  592.6 58.8 all-gather.11

commit v3 on v2

--- a/solution.py
+++ b/solution.py
@@ -329,6 +329,30 @@
     )(offs, a, b)
 
 
+def add_kernel(*refs):
+    total = refs[0][...].astype(f32)
+    for ref in refs[1:-1]:
+        total = total + ref[...].astype(f32)
+    refs[-1][...] = total.astype(bf)
+
+
+def add_halves(pairs, others, half):
+    rows, cols = pairs[0].shape[0] // 2, pairs[0].shape[1]
+    steps = 4 if rows % 64 == 0 else 1
+    block = (rows // steps, cols)
+    picked = pl.BlockSpec(block, lambda i: (i + half * steps, 0))
+    plain = pl.BlockSpec(block, lambda i: (i, 0))
+    return pl.pallas_call(
+        add_kernel,
+        grid=(steps,),
+        out_shape=jax.ShapeDtypeStruct((rows, cols), bf),
+        in_specs=[picked] * len(pairs) + [plain] * len(others),
+        out_specs=plain,
+        compiler_params=params(16),
+        cost_estimate=COST,
+    )(*pairs, *others)
+
+
 def fill_bias(qseg_ref, qpos_ref, kseg_ref, kpos_ref, bias_ref):
     kseg = kseg_ref[...]
     allowed = ((kseg == qseg_ref[...]) | (kseg == 0)) & (kpos_ref[...] <= qpos_ref[...])
@@ -542,11 +566,13 @@
 
 def gather_weight(shard, n, offs, late=()):
     if n != 4:
-        return offs, [lax.all_gather(shard, "dp", axis=0, tiled=True)]
-    far = after(lax.ppermute(shard, "dp", swap(4, 2)), *late)
+        whole = lax.all_gather(shard, "dp", axis=0, tiled=True)
+        return offs, [whole], whole
+    raw = lax.ppermute(shard, "dp", swap(4, 2))
+    far = after(raw, *late)
     near = lax.ppermute(shard, "dp", swap(4, 1))
     cross = lax.ppermute(far, "dp", swap(4, 1))
-    return offs, [shard, near, far, cross]
+    return offs, [shard, near, far, cross], raw
 
 
 def lockstep(items, waits):
@@ -581,22 +607,30 @@
     def start(self, left, right):
         if self.n == 4:
             self.keep, send = weight_grad(left, right, self.offs)
+            self.first = send
             self.got = lax.ppermute(send, "dp", swap(4, 1))
-            block = send.shape[0] // 2
-            self.far = (self.keep[block:].astype(f32) + self.got[block:].astype(f32)).astype(bf)
+            self.far = add_halves((self.keep, self.got), (), 1)
         else:
-            self.far = self.whole = dot(left, right, ((0,), (0,))).astype(bf)
+            self.first = self.far = self.whole = dot(left, right, ((0,), (0,))).astype(bf)
         return self
 
+    def start_x(self):
+        if self.n == 4:
+            self.raw = lax.ppermute(self.far, "dp", swap(4, 2))
+        else:
+            self.raw = lax.psum_scatter(self.whole, "dp", scatter_dimension=0, tiled=True)
+        return self.raw
+
+    def finish_x(self, *late):
+        other = after(self.raw, *late)
+        if self.n == 4:
+            other = add_halves((self.keep, self.got), (other,), 0)
+        self.total = lax.optimization_barrier(other)
+        return self.total
+
     def along_x(self, *late):
-        if self.n == 4:
-            block = self.far.shape[0]
-            other = after(lax.ppermute(self.far, "dp", swap(4, 2)), *late).astype(f32)
-            total = self.keep[:block].astype(f32) + self.got[:block].astype(f32) + other
-        else:
-            total = lax.psum_scatter(self.whole, "dp", scatter_dimension=0, tiled=True).astype(f32)
-        self.total = lax.optimization_barrier(total.astype(bf))
-        return self.total
+        self.start_x()
+        return self.finish_x(*late)
 
     def along_y(self, *late):
         if self.n_ctx == 2:
@@ -624,14 +658,15 @@
     mine = functools.partial(lax.dynamic_slice_in_dim, start_index=me * piece, slice_size=piece, axis=0)
     offs = jnp.stack([(dp ^ j) * shard for j in range(4)]) if n_dp == 4 else jnp.zeros((4,), jnp.int32)
 
-    def padded(w, width, *before):
-        return after(jnp.pad(w.astype(bf), ((0, 0), (0, width - w.shape[1]))), *before)
+    def padded(w, width):
+        return jnp.pad(w.astype(bf), ((0, 0), (0, width - w.shape[1])))
 
     wo_all = lax.all_gather(padded(w_out.T, feats_pad), "tensor", axis=0, tiled=False)
     wk_b = jnp.pad(w_key.astype(bf), ((0, 16), (0, feats_pad - feats)))
     gain_rows = jnp.pad(jnp.stack([gain_attn, gain_ffn]).astype(bf), ((0, 0), (0, feats_pad - shard)))
     wk_b = lax.dynamic_update_slice(wk_b, gain_rows, (shard, 0))
-    _, wk_ext = gather_weight(wk_b, n_dp, offs)
+    v_cast, q_cast = padded(w_value, feats_pad), padded(w_query, feats_pad)
+    _, wk_ext, raw_k = gather_weight(wk_b, n_dp, offs, (v_cast, q_cast))
     if n_dp == 4:
         own = jnp.stack([w[shard : shard + 2, :shard] for w in wk_ext])
         gains = jnp.zeros((2, n_dp * shard), f32)
@@ -653,30 +688,31 @@
     inputs = tokens.astype(f32)
     scale1 = lax.rsqrt(jnp.mean(inputs * inputs, axis=-1, keepdims=True) + norm_eps)
     normed1 = (inputs * scale1 * gain1).astype(bf)
-    far = lambda w: w[1][2 if n_dp == 4 else 0]
     keys = project(normed1, wk, cos_t, sin_t, True)
-    wv = gather_weight(padded(w_value, feats_pad, far(wk)), n_dp, offs, (keys,))
+    *wv, raw_v = gather_weight(after(v_cast, raw_k), n_dp, offs, (keys,))
     values = project(normed1, wv, cos_t, sin_t, False)
     if n_ctx == 2:
         trade = lambda a: lax.ppermute(a, "ctx", swap(2, 1))
-        keys_all, values_all = [keys, trade(keys)], [values, trade(values)]
+        keys_all = [keys, trade(keys)]
+        values_all = [values, trade(after(values, keys_all[1]))]
         k_metas = [q_meta, meta((1 - ctx) * rows, rows)]
-        early = (values, keys_all[1])
+        early = (values_all[1],)
     else:
         spread = lambda a: [lax.all_gather(a, "ctx", axis=0, tiled=True)]
         keys_all, values_all = spread(keys), spread(values)
         k_metas = [meta(0, segment.shape[0])]
         early = (values,)
-    wq = gather_weight(padded(w_query, feats_pad, far(wv)), n_dp, offs, early)
     wide = [padded(w, hidden_pad) for w in (w_down.T, w_gate, w_up)]
+    half, mid = shard // 2, n_tp // 2
+    items = []
+    if n_dp == 4 and n_ctx == 2:
+        cut = lambda a: lax.dynamic_slice_in_dim(a, ctx * half, half, a.ndim - 2)
+        items = [cut(wide[0]), cut(wo_all[:mid]), cut(wo_all[mid:]), cut(wide[1]), cut(wide[2])]
+    *wq, raw_q = gather_weight(after(q_cast, wv[1][-2] if n_dp == 4 else raw_v), n_dp, offs, early + tuple(wide))
     grad_ffn = (branch_scale * cotangent.astype(f32)).astype(bf)
     if n_dp == 4 and n_ctx == 2:
-        half = shard // 2
         near = lambda a: lax.ppermute(a, "dp", swap(4, 1))
-        cut = lambda a: lax.dynamic_slice_in_dim(a, ctx * half, half, a.ndim - 2)
-        mid = n_tp // 2
-        items = [cut(wide[0]), cut(wo_all[:mid]), cut(wo_all[mid:]), cut(wide[1]), cut(wide[2])]
-        items[0] = after(items[0], far(wq))
+        items[0] = after(items[0], raw_q)
         query = project(normed1, wq, cos_t, sin_t, True)
         early = []
 
@@ -686,7 +722,7 @@
             return jnp.stack(places), list(pieces)
 
         def attend(firsts, seconds):
-            early.append(attention_fwd(after(query, *wide), keys_all, values_all, q_meta, k_metas, feats // HEAD))
+            early.append(attention_fwd(query, keys_all, values_all, q_meta, k_metas, feats // HEAD))
             return (early[0][0],)
 
         def work_ahead(firsts, seconds):
@@ -701,13 +737,13 @@
         wg = shards_of(wide[1], firsts[3], seconds[3])
         places, wo_pieces = [offs[0], offs[1]], [((0, n_tp), wo_all), ((0, n_tp), near(wo_all))]
         for k, span in ((1, (0, mid)), (2, (mid, n_tp))):
-            for place, piece in two_halves(wo_all, n_dp, n_ctx, ctx, firsts[k], seconds[k], offs):
+            for place, got in two_halves(wo_all, n_dp, n_ctx, ctx, firsts[k], seconds[k], offs):
                 places.append(place)
-                wo_pieces.append((span, piece))
+                wo_pieces.append((span, got))
         places = jnp.stack(places)
         late = (firsts[4], seconds[3])
     else:
-        wd, wg, wu = [gather_weight(w, n_dp, offs) for w in wide]
+        wd, wg, wu = [gather_weight(w, n_dp, offs)[:2] for w in wide]
         places, wo_pieces = offs[:1] * 0, [((0, n_tp), lax.all_gather(wo_all, "dp", axis=1, tiled=True))]
         late = ()
         query = project(normed1, wq, cos_t, sin_t, True)
@@ -715,6 +751,7 @@
         grad_hidden = wide_matmul(grad_ffn, wd, False, f32)
     att_all = after(lax.all_gather(att, "tensor", axis=0, tiled=False), *late)
     my_in, my_scale = mine(tokens).astype(f32), mine(scale1)
+    att_all = after(att_all, *[t for m in k_metas for t in m[2:]])
     normed2, hidden_in, wo_dev = mix(att_all, tokens, gain2, places, wo_pieces, me)
     wo = (jnp.zeros((1,), jnp.int32), [wo_dev])
     if n_dp == 4 and n_ctx == 2:
@@ -725,8 +762,10 @@
     make = lambda: WeightGrad(n_dp, n_ctx, offs)
     grad_d = make().start(grad_ffn, hidden)
     ffn_part = wide_matmul(hidden, wd, True, bf)
-    grad_g = make().start(after(normed2, grad_d.far), grad_gate)
-    grad_norm2 = after(scatter_sum(partial2), grad_d.along_x(), ffn_part, grad_g.far)
+    grad_g = make().start(after(normed2, grad_d.far, ffn_part), grad_gate)
+    grad_norm2 = scatter_sum(partial2)
+    grad_d.along_x(grad_norm2)
+    grad_norm2 = after(grad_norm2, grad_d.raw, ffn_part, grad_g.first)
     part_g2 = jnp.sum(grad_norm2 * hidden_in * scale2, axis=0)
     grad_h = (
         mine(cotangent).astype(f32)
@@ -744,7 +783,7 @@
     back = lambda k, v, m: attention_bwd(query, att, grad_att, lse, k, v, q_meta, m, feats // HEAD)
     if n_ctx == 2:
         grad_q1, grad_k1, grad_v1 = back(keys_all[1:], values_all[1:], k_metas[1:])
-        grad_att = after(grad_att, grad_q1, grad_g.along_y(), grad_u.along_x())
+        grad_att = after(grad_att, grad_q1, grad_g.along_y(), grad_u.along_x(grad_q1))
         grad_q0, grad_k0, grad_v0 = back(keys_all[:1], values_all[:1], k_metas[:1])
         grad_q = (grad_q0.astype(f32) + grad_q1.astype(f32)).astype(bf)
         grad_ks, grad_vs = grad_k0 + grad_k1, grad_v0 + grad_v1
@@ -758,27 +797,29 @@
     grad_k, grad_v = merge(grad_ks), merge(grad_vs)
 
     grad_o = make().start(grad_mixed, att)
-    grad_q = after(grad_q, grad_o.far)
+    worked = (grad_q, grad_k)
+    grad_q = after(grad_q, grad_o.along_x())
+    grad_u.along_y(grad_k, grad_v)
     partial1, part_g1 = qkv_back((grad_q, grad_k, grad_v), (wq, wk, wv), tokens, scale1)
-    output = hidden_in + branch_scale * after(ffn_part, grad_q)
+    output = hidden_in + branch_scale * after(ffn_part, *worked)
     output = gather_rows(lax.optimization_barrier(output.astype(bf)))
     grads_a = [make().start(normed1, g) for g in (grad_q, grad_k, grad_v)]
-    grad_norm1 = after(scatter_sum(after(partial1, output)), grad_o.along_x(), *[g.along_x() for g in grads_a[:2]])
-    gain_sum = jnp.concatenate([part_g1, part_g2[None, :]])
-    gain_sum = sum_all(gain_sum, (("dp", n_dp), ("ctx", n_ctx), ("tensor", n_tp)))
-    grad_norm1 = after(grad_norm1, gain_sum)
+    gain_sum = sum_all(jnp.concatenate([part_g1, part_g2[None, :]]), (("ctx", n_ctx), ("dp", n_dp)))
+    totals = [g.along_x() for g in grads_a[:2]]
+    grad_u.other = after(grad_u.other, *totals)
+    grad_norm1 = after(scatter_sum(after(partial1, output, gain_sum)), *totals, grads_a[2].start_x(), grad_u.other)
+    grad_o.along_y()
     grad_in = (
         grad_h
         + my_scale * gain1 * grad_norm1
         - my_in * my_scale**3 * jnp.mean(my_in * gain1 * grad_norm1, axis=-1, keepdims=True)
     )
     local_in = lax.optimization_barrier(grad_in.astype(bf))
+    grads_a[2].finish_x(local_in)
     grad_in = gather_rows(local_in).astype(f32)
+    gain_sum = sum_all(after(gain_sum, local_in), (("tensor", n_tp),))
     gain_sum = lax.dynamic_slice_in_dim(gain_sum, dp * shard, shard, 1)
 
-    grad_u.along_y(grad_k, grad_v)
-    grad_o.along_y(grad_k, grad_v)
-    grads_a[2].along_x(local_in)
     for g in grads_a:
         g.along_y()
     sum_wd = grad_d.finish(hidden_dev, local_in).T

time: 688 us -> 657 us (0.955)
  the two profiles are of different devices: /device:TPU:26 before, /device:TPU:0 now
where the time goes in v3:
time: 657 us; the launch traced here: 647 us
  waiting for transfers between devices  241 us (37%)
  Pallas kernels  207 us (32%)
  local copies, waits for them, and re-layouts  69.3 us (11%)
  other arithmetic  66.5 us (10%)
  starting transfers between devices  47.3 us (7%)
  between operations  15.7 us (2%)
    ppermute x7, waiting for transfers between devices, start_x(): self.raw = lax.ppermute(self.far, 'dp', swap(4, 2))  99.6 us
    unnamed x214, local copies, waits for them, and re-layouts  49.4 us
    pallas_call x7, Pallas kernels, weight_grad(): pl.pallas_call(grad_kernel, out_shape=(half, half), in_specs=[SM, VM, VM]...  39.1 us
    ppermute x7, waiting for transfers between devices, along_y(): self.other = lax.ppermute(after(self.total, *late), 'ctx', swap(2, 1))  38.2 us
    pallas_call x2, Pallas kernels, attention_bwd(): pl.pallas_call(functools.partial(attn_bwd_kernel, parts, heads), grid=(bl...  33.6 us
    pallas_call x1, Pallas kernels, ffn(): pl.pallas_call(functools.partial(ffn_kernel, ns, width), out_shape=(mid,...  27.5 us
    pallas_call x3, Pallas kernels, wide_matmul(): pl.pallas_call(functools.partial(wide_kernel, ns, nt, width), out_shape=j...  23.6 us
    ppermute x5, waiting for transfers between devices, lockstep(): seconds.append(lax.ppermute(after(firsts[-1], *before), 'ctx', swap(2, 1)))  20.4 us
  transfers between devices with their start and end apart: 71, of which 39 were waited for; matrix products, arithmetic and copies ran while one was open for 11% of the time, Pallas kernels for 28%

profile of v3, /device:TPU:0, one launch (start us, length us, event | category | flops | bytes accessed | tf_op | source)
XLA Modules:
  0.0 647.1 jit_solution(4651352199631808195)
XLA Ops:
  16.2 3.6 fusion.9
  26.3 6.4 collective-permute-done.1.rest_2_.rest_9_
  40.9 5.9 shard_map.212.refs_7_.refs_12_
  48.4 3.6 collective-permute-done.3.rest_2_.rest_13_
  55.5 5.1 shard_map.213.refs_9_.refs_13_
  60.6 6.8 %collective-permute-done.8.refs_8_.refs_12_ = bf16[640,640]{1,0:T(8,128)(2,1)} collective-permute-done((bf16[640,640]{1,0:T(8,128)(2,1)}, bf16[640,640]{1,0:T(8,128)(2,1)}, u32[]{:S(2)}, u32[]{:S(2)}) %collective-permute-start.8) | collective-permute-done | bytes 819232 | tf_op jit(solution)/shard_map/ppermute | solution.py:695
  80.2 6.5 %collective-permute-done.9.refs_10_.refs_13_ = bf16[640,640]{1,0:T(8,128)(2,1)S(1)} collective-permute-done((bf16[640,640]{1,0:T(8,128)(2,1)S(1)}, bf16[640,640]{1,0:T(8,128)(2,1)S(1)}, u32[]{:S(2)}, u32[]{:S(2)}) %collective-permute-start.9) | collective-permute-done | bytes 819232 | tf_op jit(solution)/shard_map/ppermute | solution.py:695
  89.9 5.0 shard_map.214.refs_6_.refs_8_
  97.4 3.2 fusion.14
  102.9 17.4 %shard_map.215 = (bf16[640,640]{1,0:T(8,128)(2,1)S(1)}, f32[5,8,640]{2,1,0:T(8,128)S(1)}) custom-call(s32[1,640]{1,0:T(1,128)S(1)} %broadcast_in_dim.19.refs_0_, s32[1,640]{1,0:T(1,128)S(1)} %broadcast_in_dim.20.refs_1_, s32[640,1]{1,0:T(8,128)S(1)} %broadcast_in_dim.52.refs_2_.refs_4_, s32[640,1]{1,0:T(8,128)S(1)} %broadcast_in_dim.53.refs_3_.refs_4_, ...), custom_call_target="tpu_custom_call" | custom-call | flops 1024 | bytes 1024 | tf_op jit(solution)/shard_map/pallas_call | solution.py:425
  127.7 13.6 %collective-permute-done.14.rest_6_ = bf16[2,288,640]{2,1,0:T(8,128)(2,1)} collective-permute-done((bf16[2,288,640]{2,1,0:T(8,128)(2,1)S(1)}, bf16[2,288,640]{2,1,0:T(8,128)(2,1)}, u32[]{:S(2)}, u32[]{:S(2)}) %collective-permute-start.14) | collective-permute-done | bytes 737312 | tf_op jit(solution)/shard_map/ppermute | solution.py:588
  147.7 12.2 %shard_map.216.dh_hbm = f32[640,1536]{1,0:T(8,128)S(1)} custom-call(s32[6]{0:T(128)S(1)} %stack.71.offs, bf16[640,2304]{1,0:T(8,128)(2,1)S(1)} %copy-done.4, bf16[576,1536]{1,0:T(8,128)(2,1)} %pad.32.rest_0_, bf16[576,1536]{1,0:T(8,128)(2,1)} %collective-permute-done.18.rest_1_, bf16[288,1536]{1,0:T(8,128)(2,1)} %collective-permute-done.11.rest_2_, ...), custom_call_target="tpu_custom_call" | custom-call | flops 1024 | bytes 1024 | tf_op jit(solution)/shard_map/pallas_call | solution.py:130
  165.4 18.5 %collective-permute-done.22.rest_4_ = bf16[288,1536]{1,0:T(8,128)(2,1)S(1)} collective-permute-done((bf16[288,1536]{1,0:T(8,128)(2,1)}, bf16[288,1536]{1,0:T(8,128)(2,1)S(1)}, u32[]{:S(2)}, u32[]{:S(2)}) %collective-permute-start.22) | collective-permute-done | bytes 884768 | tf_op jit(solution)/shard_map/ppermute | solution.py:585
  194.0 19.6 %shard_map.217 = (bf16[640,2304]{1,0:T(8,128)(2,1)}, f32[160,2304]{1,0:T(8,128)}, bf16[2304,640]{1,0:T(8,128)(2,1)}) custom-call(s32[1]{0:T(128)} %bitcast.me_ref, s32[10]{0:T(128)} %stack.64.offs, bf16[4,640,640]{2,1,0:T(8,128)(2,1)} %bitcast.26, bf16[640,2304]{1,0:T(8,128)(2,1)} %x_ref.3, f32[1,2304]{1,0:T(1,128)} %get-tuple-element.219.gain_ref, ...), custom_call_target="tpu_custom_call" | custom-call | flops 1024 | bytes 1024 | tf_op jit(solution)/shard_map/pallas_call | solution.py:289
  217.7 27.5 %shard_map.218 = (bf16[640,1536]{1,0:T(8,128)(2,1)}, bf16[640,1536]{1,0:T(8,128)(2,1)}, bf16[640,1536]{1,0:T(8,128)(2,1)}, bf16[640,2304]{1,0:T(8,128)(2,1)}) custom-call(s32[6]{0:T(128)} %copy-done.85, bf16[640,2304]{1,0:T(8,128)(2,1)} %get-tuple-element.118.n_hbm.a_ref, f32[640,1536]{1,0:T(8,128)} %copy-done.10, bf16[576,1536]{1,0:T(8,128)(2,1)} %pad.33.rest_0_, ...), custom_call_target="tpu_custom_call" | custom-call | flops 1024 | bytes 1024 | tf_op jit(solution)/shard_map/pallas_call | solution.py:233
  248.7 7.0 %shard_map.220 = (bf16[1152,1536]{1,0:T(8,128)(2,1)S(1)}, bf16[1152,1536]{1,0:T(8,128)(2,1)S(1)}) custom-call(s32[4]{0:T(128)S(1)} %pad_add_fusion.offs, bf16[640,2304]{1,0:T(8,128)(2,1)S(1)} %copy-done.5, bf16[640,1536]{1,0:T(8,128)(2,1)S(1)} %copy-done.30), custom_call_target="tpu_custom_call" | custom-call | flops 1024 | bytes 1024 | tf_op jit(solution)/shard_map/pallas_call | solution.py:321
  256.2 5.9 collective-permute-done.35.refs_1_
  268.9 8.6 %shard_map.219 = bf16[640,2304]{1,0:T(8,128)(2,1)S(1)} custom-call(s32[6]{0:T(128)S(1)} %copy-done.86, bf16[640,1536]{1,0:T(8,128)(2,1)S(1)} %copy-done.31, bf16[576,1536]{1,0:T(8,128)(2,1)} %pad.32.rest_0_, bf16[576,1536]{1,0:T(8,128)(2,1)} %collective-permute-done.18.rest_1_, bf16[288,1536]{1,0:T(8,128)(2,1)} %collective-permute-done.11.rest_2_, ...), custom_call_target="tpu_custom_call" | custom-call | flops 1024 | bytes 1024 | tf_op jit(solution)/shard_map/pallas_call | solution.py:130
  282.6 8.8 %shard_map.222 = (bf16[1152,1536]{1,0:T(8,128)(2,1)S(1)}, bf16[1152,1536]{1,0:T(8,128)(2,1)}) custom-call(s32[4]{0:T(128)S(1)} %pad_add_fusion.offs, bf16[640,2304]{1,0:T(8,128)(2,1)S(1)} %copy-done.2, bf16[640,1536]{1,0:T(8,128)(2,1)S(1)} %copy-done.77), custom_call_target="tpu_custom_call" | custom-call | flops 1024 | bytes 1024 | tf_op jit(solution)/shard_map/pallas_call | solution.py:321
  293.2 10.4 %reduce-scatter.4.cloned.1.call-done = bf16[160,2304]{1,0:T(8,128)(2,1)} async-done(((bf16[640,2304]{1,0:T(8,128)(2,1)}), bf16[160,2304]{1,0:T(8,128)(2,1)}) %reduce-scatter.4.cloned.1.call-update) | async-done | bytes 737296 | tf_op jit(solution)/shard_map/reduce_scatter | solution.py:560
  306.1 3.0 multiply_convert_fusion.1
  312.8 7.0 %shard_map.226 = (bf16[1152,1536]{1,0:T(8,128)(2,1)S(1)}, bf16[1152,1536]{1,0:T(8,128)(2,1)S(1)}) custom-call(s32[4]{0:T(128)S(1)} %pad_add_fusion.offs, bf16[640,2304]{1,0:T(8,128)(2,1)S(1)} %copy-done.3, bf16[640,1536]{1,0:T(8,128)(2,1)S(1)} %copy-done.76), custom_call_target="tpu_custom_call" | custom-call | flops 1024 | bytes 1024 | tf_op jit(solution)/shard_map/pallas_call | solution.py:321
  319.9 4.0 shard_map.224
  329.3 35.1 %collective-permute-done.39.refs_2_ = bf16[576,1536]{1,0:T(8,128)(2,1)S(1)} collective-permute-done((bf16[576,1536]{1,0:T(8,128)(2,1)S(1)}, bf16[576,1536]{1,0:T(8,128)(2,1)S(1)}, u32[]{:S(2)}, u32[]{:S(2)}) %collective-permute-start.39) | collective-permute-done | bytes 1769504 | tf_op jit(solution)/shard_map/ppermute | solution.py:619
  377.2 2.7 shard_map.228.refs_10_
  382.9 16.8 %shard_map.229 = (bf16[640,640]{1,0:T(8,128)(2,1)S(1)}, bf16[640,640]{1,0:T(8,128)(2,1)S(1)}, bf16[640,640]{1,0:T(8,128)(2,1)S(1)}) custom-call(s32[1,640]{1,0:T(1,128)S(1)} %broadcast_in_dim.19.refs_0_, s32[1,640]{1,0:T(1,128)S(1)} %broadcast_in_dim.20.refs_1_, f32[640,128]{1,0:T(8,128)S(1)} %pad_maximum_fusion.cos_ref.refs_2_.refs_6_, ...), custom_call_target="tpu_custom_call" | custom-call | flops 1024 | bytes 1024 | tf_op jit(solution)/shard_map/pallas_call | solution.py:514
  400.4 10.6 %collective-permute-done.42.refs_2_ = bf16[576,1536]{1,0:T(8,128)(2,1)S(1)} collective-permute-done((bf16[576,1536]{1,0:T(8,128)(2,1)}, bf16[576,1536]{1,0:T(8,128)(2,1)S(1)}, u32[]{:S(2)}, u32[]{:S(2)}) %collective-permute-start.42) | collective-permute-done | bytes 1769504 | tf_op jit(solution)/shard_map/ppermute | solution.py:619
  413.9 16.8 %shard_map.231 = (bf16[640,640]{1,0:T(8,128)(2,1)S(1)}, bf16[640,640]{1,0:T(8,128)(2,1)S(1)}, bf16[640,640]{1,0:T(8,128)(2,1)S(1)}) custom-call(s32[1,640]{1,0:T(1,128)S(1)} %broadcast_in_dim.19.refs_0_, s32[1,640]{1,0:T(1,128)S(1)} %broadcast_in_dim.20.refs_1_, f32[640,128]{1,0:T(8,128)S(1)} %pad_maximum_fusion.cos_ref.refs_2_.refs_6_, ...), custom_call_target="tpu_custom_call" | custom-call | flops 1024 | bytes 1024 | tf_op jit(solution)/shard_map/pallas_call | solution.py:514
  439.7 4.1 shard_map.232
  448.3 17.8 %collective-permute-done.45.refs_2_ = bf16[576,640]{1,0:T(8,128)(2,1)S(1)} collective-permute-done((bf16[576,640]{1,0:T(8,128)(2,1)S(1)}, bf16[576,640]{1,0:T(8,128)(2,1)S(1)}, u32[]{:S(2)}, u32[]{:S(2)}) %collective-permute-start.45) | collective-permute-done | bytes 737312 | tf_op jit(solution)/shard_map/ppermute | solution.py:619
  469.6 11.5 %shard_map.235 = (bf16[640,2304]{1,0:T(8,128)(2,1)S(1)}, f32[1,2304]{1,0:T(1,128)S(1)}) custom-call(s32[4]{0:T(128)S(1)} %pad_add_fusion.offs, bf16[640,2304]{1,0:T(8,128)(2,1)S(1)} %copy-done.1, f32[640,1]{1,0:T(8,128)S(1)} %rsqrt.19.scale_ref, bf16[640,640]{1,0:T(8,128)(2,1)S(1)} %copy-done.32, bf16[640,640]{1,0:T(8,128)(2,1)S(1)} %copy-done.34, ...), custom_call_target="tpu_custom_call" | custom-call | flops 1024 | bytes 1024 | tf_op jit(solution)/shard_map/pallas_call | solution.py:164
  488.5 3.1 collective-permute-done.49
  491.7 5.4 all-gather.10.cloned.1.call-done
  498.7 4.1 shard_map.239
  502.9 4.1 shard_map.236
  507.6 4.1 shard_map.242
  518.8 14.3 %collective-permute-done.53.refs_2_ = bf16[576,640]{1,0:T(8,128)(2,1)S(1)} collective-permute-done((bf16[576,640]{1,0:T(8,128)(2,1)S(1)}, bf16[576,640]{1,0:T(8,128)(2,1)S(1)}, u32[]{:S(2)}, u32[]{:S(2)}) %collective-permute-start.53) | collective-permute-done | bytes 737312 | tf_op jit(solution)/shard_map/ppermute | solution.py:619
  534.7 14.2 %collective-permute-done.51.refs_2_ = bf16[576,640]{1,0:T(8,128)(2,1)S(1)} collective-permute-done((bf16[576,640]{1,0:T(8,128)(2,1)S(1)}, bf16[576,640]{1,0:T(8,128)(2,1)S(1)}, u32[]{:S(2)}, u32[]{:S(2)}) %collective-permute-start.51) | collective-permute-done | bytes 737312 | tf_op jit(solution)/shard_map/ppermute | solution.py:619
  552.9 3.0 reduce-scatter.8.cloned.1.call-done
  557.1 6.8 %collective-permute-done.55.refs_2_ = bf16[576,640]{1,0:T(8,128)(2,1)S(1)} collective-permute-done((bf16[576,640]{1,0:T(8,128)(2,1)S(1)}, bf16[576,640]{1,0:T(8,128)(2,1)S(1)}, u32[]{:S(2)}, u32[]{:S(2)}) %collective-permute-start.55) | collective-permute-done | bytes 737312 | tf_op jit(solution)/shard_map/ppermute | solution.py:619
  565.6 2.9 fusion.5
  571.2 4.9 convert_element_type.199
  576.1 3.9 add_bitcast_fusion
  580.1 3.9 convert_add_fusion
  589.1 15.0 %collective-permute-done.60 = bf16[576,640]{1,0:T(8,128)(2,1)S(1)} collective-permute-done((bf16[576,640]{1,0:T(8,128)(2,1)}, bf16[576,640]{1,0:T(8,128)(2,1)S(1)}, u32[]{:S(2)}, u32[]{:S(2)}) %collective-permute-start.60) | collective-permute-done | bytes 737312 | tf_op jit(solution)/shard_map/ppermute | solution.py:637
  607.7 12.2 %collective-permute-done.59 = bf16[576,640]{1,0:T(8,128)(2,1)S(1)} collective-permute-done((bf16[576,640]{1,0:T(8,128)(2,1)}, bf16[576,640]{1,0:T(8,128)(2,1)S(1)}, u32[]{:S(2)}, u32[]{:S(2)}) %collective-permute-start.59) | collective-permute-done | bytes 737312 | tf_op jit(solution)/shard_map/ppermute | solution.py:637
  626.8 7.2 %collective-permute-done.61 = bf16[576,640]{1,0:T(8,128)(2,1)S(1)} collective-permute-done((bf16[576,640]{1,0:T(8,128)(2,1)S(1)}, bf16[576,640]{1,0:T(8,128)(2,1)S(1)}, u32[]{:S(2)}, u32[]{:S(2)}) %collective-permute-start.61) | collective-permute-done | bytes 737312 | tf_op jit(solution)/shard_map/ppermute | solution.py:637
  635.2 4.9 convert_element_type.206
  (438 shorter events, 192.6 us)
Async XLA Ops:
  7.2 90.2 %all-gather.16.cloned.1.call-start = ((), (), s32[]{:S(2)}) async-start(), calls=%async_computation.10 | async-start | bytes 3686400 | tf_op jit(solution)/shard_map/all_gather | solution.py:664
  11.8 22.7 %collective-permute-start = (bf16[592,640]{1,0:T(8,128)(2,1)}, bf16[592,640]{1,0:T(8,128)(2,1)}, u32[]{:S(2)}, u32[]{:S(2)}) collective-permute-start(bf16[592,640]{1,0:T(8,128)(2,1)} %pad_dynamic-update-slice_fusion.rest_0_.rest_7_), channel_id=1, source_target_pairs={{0,8},{8,0},{16,24},{24,16},{1,9},{9,1},{17,25},{25,17},{2,10},{10... | collective-permute-start | bytes 2273288 | tf_op jit(solution)/shard_map/ppermute | solution.py:573
  12.2 20.4 %collective-permute-start.1 = (bf16[592,640]{1,0:T(8,128)(2,1)}, bf16[592,640]{1,0:T(8,128)(2,1)}, u32[]{:S(2)}, u32[]{:S(2)}) collective-permute-start(bf16[592,640]{1,0:T(8,128)(2,1)} %pad_dynamic-update-slice_fusion.rest_0_.rest_7_), channel_id=1, source_target_pairs={{0,16},{8,24},{16,0},{24,8},{1,17},{9,25},{17,1},{25,9},{2,18},{10... | collective-permute-start | bytes 2273288 | tf_op jit(solution)/shard_map/ppermute | solution.py:571
  16.0 177.4 %all-gather.14.cloned.1.call-start = ((), (), s32[]{:S(2)}) async-start(), calls=%async_computation.9 | async-start | bytes 4096000 | tf_op jit(solution)/shard_map/all_gather | solution.py:752
  32.7 19.2 %collective-permute-start.3 = (bf16[576,640]{1,0:T(8,128)(2,1)}, bf16[576,640]{1,0:T(8,128)(2,1)}, u32[]{:S(2)}, u32[]{:S(2)}) collective-permute-start(bf16[576,640]{1,0:T(8,128)(2,1)} %pad.30.rest_0_.rest_11_), channel_id=1, source_target_pairs={{0,16},{8,24},{16,0},{24,8},{1,17},{9,25},{17,1},{25,9},{2,18},{10... | collective-permute-start | bytes 2211848 | tf_op jit(solution)/shard_map/ppermute | solution.py:571
  46.8 20.6 %collective-permute-start.8 = (bf16[640,640]{1,0:T(8,128)(2,1)}, bf16[640,640]{1,0:T(8,128)(2,1)}, u32[]{:S(2)}, u32[]{:S(2)}) collective-permute-start(bf16[640,640]{1,0:T(8,128)(2,1)} %shard_map.212.refs_7_.refs_12_), channel_id=1, source_target_pairs={{0,4},{4,0},{1,5},{5,1},{2,6},{6,2},{3,7},{7,3},{8,12},{12,8},{9,1... | collective-permute-start | bytes 2457608 | tf_op jit(solution)/shard_map/ppermute | solution.py:695
  51.9 19.1 %collective-permute-start.5 = (bf16[576,640]{1,0:T(8,128)(2,1)}, bf16[576,640]{1,0:T(8,128)(2,1)S(1)}, u32[]{:S(2)}, u32[]{:S(2)}) collective-permute-start(bf16[576,640]{1,0:T(8,128)(2,1)} %pad.31.rest_0_.rest_3_), channel_id=1, source_target_pairs={{0,16},{8,24},{16,0},{24,8},{1,17},{9,25},{17,1},{25,9},{2,18},{10... | collective-permute-start | bytes 2211848 | tf_op jit(solution)/shard_map/ppermute | solution.py:571
  67.3 19.3 %collective-permute-start.9 = (bf16[640,640]{1,0:T(8,128)(2,1)S(1)}, bf16[640,640]{1,0:T(8,128)(2,1)S(1)}, u32[]{:S(2)}, u32[]{:S(2)}) collective-permute-start(bf16[640,640]{1,0:T(8,128)(2,1)S(1)} %shard_map.213.refs_9_.refs_13_), channel_id=1, source_target_pairs={{0,4},{4,0},{1,5},{5,1},{2,6},{6,2},{3,7},{7,3},{8,12},{12,8},{9,1... | collective-permute-start | bytes 2457608 | tf_op jit(solution)/shard_map/ppermute | solution.py:695
  71.0 24.8 %collective-permute-start.11 = (bf16[288,1536]{1,0:T(8,128)(2,1)S(1)}, bf16[288,1536]{1,0:T(8,128)(2,1)}, u32[]{:S(2)}, u32[]{:S(2)}) collective-permute-start(bf16[288,1536]{1,0:T(8,128)(2,1)S(1)} %constant_dynamic-slice_fusion.2), channel_id=1, source_target_pairs={{0,16},{8,24},{16,0},{24,8},{1,17},{9,25},{17,1},{25,9},{2,18},{10... | collective-permute-start | bytes 2654216 | tf_op jit(solution)/shard_map/ppermute | solution.py:588
  86.7 56.5 %collective-permute-start.18 = (bf16[576,1536]{1,0:T(8,128)(2,1)}, bf16[576,1536]{1,0:T(8,128)(2,1)}, u32[]{:S(2)}, u32[]{:S(2)}) collective-permute-start(bf16[576,1536]{1,0:T(8,128)(2,1)} %pad.32.rest_0_), channel_id=1, source_target_pairs={{0,8},{8,0},{16,24},{24,16},{1,9},{9,1},{17,25},{25,17},{2,10},{10... | collective-permute-start | bytes 5308424 | tf_op jit(solution)/shard_map/ppermute | solution.py:714
  95.9 27.3 %collective-permute-start.12 = (bf16[288,1536]{1,0:T(8,128)(2,1)}, bf16[288,1536]{1,0:T(8,128)(2,1)}, u32[]{:S(2)}, u32[]{:S(2)}) collective-permute-start(bf16[288,1536]{1,0:T(8,128)(2,1)} %collective-permute-done.11.rest_2_), channel_id=1, source_target_pairs={{0,4},{4,0},{1,5},{5,1},{2,6},{6,2},{3,7},{7,3},{8,12},{12,8},{9,1... | collective-permute-start | bytes 2654216 | tf_op jit(solution)/shard_map/ppermute | solution.py:585
  101.5 21.6 %collective-permute-start.13 = (bf16[2,288,640]{2,1,0:T(8,128)(2,1)}, bf16[2,288,640]{2,1,0:T(8,128)(2,1)}, u32[]{:S(2)}, u32[]{:S(2)}) collective-permute-start(bf16[2,288,640]{2,1,0:T(8,128)(2,1)} %constant_dynamic-slice_fusion.1), channel_id=1, source_target_pairs={{0,16},{8,24},{16,0},{24,8},{1,17},{9,25},{17,1},{25,9},{2,18},{10... | collective-permute-start | bytes 2211848 | tf_op jit(solution)/shard_map/ppermute | solution.py:588
  121.2 182.3 %reduce-scatter.4.cloned.1.call-start = ((), (), s32[]{:S(2)}) async-start(), calls=%async_computation.3 | async-start | bytes 3686400 | tf_op jit(solution)/shard_map/reduce_scatter | solution.py:560
  127.2 18.6 %collective-permute-start.19 = (bf16[288,1536]{1,0:T(8,128)(2,1)}, bf16[288,1536]{1,0:T(8,128)(2,1)}, u32[]{:S(2)}, u32[]{:S(2)}) collective-permute-start(bf16[288,1536]{1,0:T(8,128)(2,1)} %collective-permute-done.11.rest_2_), channel_id=1, source_target_pairs={{0,8},{8,0},{16,24},{24,16},{1,9},{9,1},{17,25},{25,17},{2,10},{10... | collective-permute-start | bytes 2654216 | tf_op jit(solution)/shard_map/ppermute | solution.py:596
  127.2 18.6 %collective-permute-start.20 = (bf16[288,1536]{1,0:T(8,128)(2,1)}, bf16[288,1536]{1,0:T(8,128)(2,1)}, u32[]{:S(2)}, u32[]{:S(2)}) collective-permute-start(bf16[288,1536]{1,0:T(8,128)(2,1)} %collective-permute-done.12.rest_4_), channel_id=1, source_target_pairs={{0,8},{8,0},{16,24},{24,16},{1,9},{9,1},{17,25},{25,17},{2,10},{10... | collective-permute-start | bytes 2654216 | tf_op jit(solution)/shard_map/ppermute | solution.py:596
  142.5 20.3 %collective-permute-start.17 = (bf16[288,1536]{1,0:T(8,128)(2,1)}, bf16[288,1536]{1,0:T(8,128)(2,1)}, u32[]{:S(2)}, u32[]{:S(2)}) collective-permute-start(bf16[288,1536]{1,0:T(8,128)(2,1)} %constant_dynamic-slice_fusion), channel_id=1, source_target_pairs={{0,16},{8,24},{16,0},{24,8},{1,17},{9,25},{17,1},{25,9},{2,18},{10... | collective-permute-start | bytes 2654216 | tf_op jit(solution)/shard_map/ppermute | solution.py:588
  143.2 50.2 %collective-permute-start.23 = (bf16[4,576,640]{2,1,0:T(8,128)(2,1)}, bf16[4,576,640]{2,1,0:T(8,128)(2,1)}, u32[]{:S(2)}, u32[]{:S(2)}) collective-permute-start(bf16[4,576,640]{2,1,0:T(8,128)(2,1)} %bitcast.14.rest_0_), channel_id=1, source_target_pairs={{0,8},{8,0},{16,24},{24,16},{1,9},{9,1},{17,25},{25,17},{2,10},{10... | collective-permute-start | bytes 8847368 | tf_op jit(solution)/shard_map/ppermute | solution.py:714
  143.2 19.2 %collective-permute-start.16 = (bf16[2,288,640]{2,1,0:T(8,128)(2,1)}, bf16[2,288,640]{2,1,0:T(8,128)(2,1)}, u32[]{:S(2)}, u32[]{:S(2)}) collective-permute-start(bf16[2,288,640]{2,1,0:T(8,128)(2,1)} %collective-permute-done.14.rest_6_), channel_id=1, source_target_pairs={{0,4},{4,0},{1,5},{5,1},{2,6},{6,2},{3,7},{7,3},{8,12},{12,8},{9,1... | collective-permute-start | bytes 2211848 | tf_op jit(solution)/shard_map/ppermute | solution.py:585
  162.8 21.2 %collective-permute-start.22 = (bf16[288,1536]{1,0:T(8,128)(2,1)}, bf16[288,1536]{1,0:T(8,128)(2,1)S(1)}, u32[]{:S(2)}, u32[]{:S(2)}) collective-permute-start(bf16[288,1536]{1,0:T(8,128)(2,1)} %collective-permute-done.17.rest_2_), channel_id=1, source_target_pairs={{0,4},{4,0},{1,5},{5,1},{2,6},{6,2},{3,7},{7,3},{8,12},{12,8},{9,1... | collective-permute-start | bytes 2654216 | tf_op jit(solution)/shard_map/ppermute | solution.py:585
  163.5 21.6 %collective-permute-start.21 = (bf16[288,1536]{1,0:T(8,128)(2,1)S(1)}, bf16[288,1536]{1,0:T(8,128)(2,1)}, u32[]{:S(2)}, u32[]{:S(2)}) collective-permute-start(bf16[288,1536]{1,0:T(8,128)(2,1)S(1)} %constant_dynamic-slice_fusion.4), channel_id=1, source_target_pairs={{0,16},{8,24},{16,0},{24,8},{1,17},{9,25},{17,1},{25,9},{2,18},{10... | collective-permute-start | bytes 2654216 | tf_op jit(solution)/shard_map/ppermute | solution.py:588
  164.9 49.2 %collective-permute-start.28 = (bf16[576,1536]{1,0:T(8,128)(2,1)}, bf16[576,1536]{1,0:T(8,128)(2,1)}, u32[]{:S(2)}, u32[]{:S(2)}) collective-permute-start(bf16[576,1536]{1,0:T(8,128)(2,1)} %pad.33.rest_0_), channel_id=1, source_target_pairs={{0,8},{8,0},{16,24},{24,16},{1,9},{9,1},{17,25},{25,17},{2,10},{10... | collective-permute-start | bytes 5308424 | tf_op jit(solution)/shard_map/ppermute | solution.py:714
  164.9 20.3 %collective-permute-start.24 = (bf16[2,288,640]{2,1,0:T(8,128)(2,1)}, bf16[2,288,640]{2,1,0:T(8,128)(2,1)}, u32[]{:S(2)}, u32[]{:S(2)}) collective-permute-start(bf16[2,288,640]{2,1,0:T(8,128)(2,1)} %collective-permute-done.13.rest_2_), channel_id=1, source_target_pairs={{0,8},{8,0},{16,24},{24,16},{1,9},{9,1},{17,25},{25,17},{2,10},{10... | collective-permute-start | bytes 2211848 | tf_op jit(solution)/shard_map/ppermute | solution.py:596
  185.2 28.4 %collective-permute-start.33 = (bf16[288,1536]{1,0:T(8,128)(2,1)}, bf16[288,1536]{1,0:T(8,128)(2,1)}, u32[]{:S(2)}, u32[]{:S(2)}) collective-permute-start(bf16[288,1536]{1,0:T(8,128)(2,1)} %collective-permute-done.21.rest_8_), channel_id=1, source_target_pairs={{0,4},{4,0},{1,5},{5,1},{2,6},{6,2},{3,7},{7,3},{8,12},{12,8},{9,1... | collective-permute-start | bytes 2654216 | tf_op jit(solution)/shard_map/ppermute | solution.py:585
  186.5 27.7 %collective-permute-start.31 = (bf16[576,1536]{1,0:T(8,128)(2,1)}, bf16[576,1536]{1,0:T(8,128)(2,1)}, u32[]{:S(2)}, u32[]{:S(2)}) collective-permute-start(bf16[576,1536]{1,0:T(8,128)(2,1)} %pad.34.rest_6_), channel_id=1, source_target_pairs={{0,8},{8,0},{16,24},{24,16},{1,9},{9,1},{17,25},{25,17},{2,10},{10... | collective-permute-start | bytes 5308424 | tf_op jit(solution)/shard_map/ppermute | solution.py:714
  193.5 20.8 %collective-permute-start.29 = (bf16[288,1536]{1,0:T(8,128)(2,1)}, bf16[288,1536]{1,0:T(8,128)(2,1)}, u32[]{:S(2)}, u32[]{:S(2)}) collective-permute-start(bf16[288,1536]{1,0:T(8,128)(2,1)} %collective-permute-done.17.rest_2_), channel_id=1, source_target_pairs={{0,8},{8,0},{16,24},{24,16},{1,9},{9,1},{17,25},{25,17},{2,10},{10... | collective-permute-start | bytes 2654216 | tf_op jit(solution)/shard_map/ppermute | solution.py:596
  193.8 20.4 %collective-permute-start.30 = (bf16[288,1536]{1,0:T(8,128)(2,1)}, bf16[288,1536]{1,0:T(8,128)(2,1)}, u32[]{:S(2)}, u32[]{:S(2)}) collective-permute-start(bf16[288,1536]{1,0:T(8,128)(2,1)} %copy-done.103), channel_id=1, source_target_pairs={{0,8},{8,0},{16,24},{24,16},{1,9},{9,1},{17,25},{25,17},{2,10},{10... | collective-permute-start | bytes 2654216 | tf_op jit(solution)/shard_map/ppermute | solution.py:596
  245.3 125.3 %all-gather.8.cloned.1.call-start = ((), (), s32[]{:S(2)}) async-start(), calls=%async_computation.4 | async-start | bytes 3686400 | tf_op jit(solution)/shard_map/all_gather | solution.py:564
  264.4 41.2 %collective-permute-start.36 = (bf16[576,1536]{1,0:T(8,128)(2,1)}, bf16[576,1536]{1,0:T(8,128)(2,1)}, u32[]{:S(2)}, u32[]{:S(2)}) collective-permute-start(bf16[576,1536]{1,0:T(8,128)(2,1)} %shard_map.221), channel_id=1, source_target_pairs={{0,16},{8,24},{16,0},{24,8},{1,17},{9,25},{17,1},{25,9},{2,18},{10... | collective-permute-start | bytes 5308424 | tf_op jit(solution)/shard_map/ppermute | solution.py:619
  293.1 26.7 %collective-permute-start.38 = (bf16[1152,1536]{1,0:T(8,128)(2,1)}, bf16[1152,1536]{1,0:T(8,128)(2,1)}, u32[]{:S(2)}, u32[]{:S(2)}) collective-permute-start(bf16[1152,1536]{1,0:T(8,128)(2,1)} %get-tuple-element.114), channel_id=1, source_target_pairs={{0,8},{8,0},{16,24},{24,16},{1,9},{9,1},{17,25},{25,17},{2,10},{10... | collective-permute-start | bytes 10616840 | tf_op jit(solution)/shard_map/ppermute | solution.py:611
  309.2 124.7 %reduce-scatter.6.cloned.1.call-start = ((), (), s32[]{:S(2)}) async-start(), calls=%async_computation.5 | async-start | bytes 3686400 | tf_op jit(solution)/shard_map/reduce_scatter | solution.py:560
  319.8 47.2 %collective-permute-start.40 = (bf16[1152,1536]{1,0:T(8,128)(2,1)S(1)}, bf16[1152,1536]{1,0:T(8,128)(2,1)S(1)}, u32[]{:S(2)}, u32[]{:S(2)}) collective-permute-start(bf16[1152,1536]{1,0:T(8,128)(2,1)S(1)} %get-tuple-element.121), channel_id=1, source_target_pairs={{0,8},{8,0},{16,24},{24,16},{1,9},{9,1},{17,25},{25,17},{2,10},{10... | collective-permute-start | bytes 10616840 | tf_op jit(solution)/shard_map/ppermute | solution.py:611
  323.9 40.5 %collective-permute-start.39 = (bf16[576,1536]{1,0:T(8,128)(2,1)S(1)}, bf16[576,1536]{1,0:T(8,128)(2,1)S(1)}, u32[]{:S(2)}, u32[]{:S(2)}) collective-permute-start(bf16[576,1536]{1,0:T(8,128)(2,1)S(1)} %shard_map.224), channel_id=1, source_target_pairs={{0,16},{8,24},{16,0},{24,8},{1,17},{9,25},{17,1},{25,9},{2,18},{10... | collective-permute-start | bytes 5308424 | tf_op jit(solution)/shard_map/ppermute | solution.py:619
  327.9 42.7 %collective-permute-start.37 = (bf16[576,1536]{1,0:T(8,128)(2,1)S(1)}, bf16[576,1536]{1,0:T(8,128)(2,1)}, u32[]{:S(2)}, u32[]{:S(2)}) collective-permute-start(bf16[576,1536]{1,0:T(8,128)(2,1)S(1)} %shard_map.223), channel_id=1, source_target_pairs={{0,4},{4,0},{1,5},{5,1},{2,6},{6,2},{3,7},{7,3},{8,12},{12,8},{9,1... | collective-permute-start | bytes 5308424 | tf_op jit(solution)/shard_map/ppermute | solution.py:637
  370.6 126.5 %all-gather.10.cloned.1.call-start = ((), (), s32[]{:S(2)}) async-start(), calls=%async_computation.6 | async-start | bytes 3686400 | tf_op jit(solution)/shard_map/all_gather | solution.py:564
  370.7 40.4 %collective-permute-start.42 = (bf16[576,1536]{1,0:T(8,128)(2,1)}, bf16[576,1536]{1,0:T(8,128)(2,1)S(1)}, u32[]{:S(2)}, u32[]{:S(2)}) collective-permute-start(bf16[576,1536]{1,0:T(8,128)(2,1)} %copy-done.78), channel_id=1, source_target_pairs={{0,16},{8,24},{16,0},{24,8},{1,17},{9,25},{17,1},{25,9},{2,18},{10... | collective-permute-start | bytes 5308424 | tf_op jit(solution)/shard_map/ppermute | solution.py:619
  372.1 41.8 %collective-permute-start.41 = (bf16[576,1536]{1,0:T(8,128)(2,1)}, bf16[576,1536]{1,0:T(8,128)(2,1)S(1)}, u32[]{:S(2)}, u32[]{:S(2)}) collective-permute-start(bf16[576,1536]{1,0:T(8,128)(2,1)} %copy-done.43), channel_id=1, source_target_pairs={{0,4},{4,0},{1,5},{5,1},{2,6},{6,2},{3,7},{7,3},{8,12},{12,8},{9,1... | collective-permute-start | bytes 5308424 | tf_op jit(solution)/shard_map/ppermute | solution.py:637
  399.7 33.1 %collective-permute-start.43 = (bf16[640,640]{1,0:T(8,128)(2,1)S(1)}, bf16[640,640]{1,0:T(8,128)(2,1)S(1)}, u32[]{:S(2)}, u32[]{:S(2)}) collective-permute-start(bf16[640,640]{1,0:T(8,128)(2,1)S(1)} %get-tuple-element.131), channel_id=1, source_target_pairs={{0,4},{4,0},{1,5},{5,1},{2,6},{6,2},{3,7},{7,3},{8,12},{12,8},{9,1... | collective-permute-start | bytes 2457608 | tf_op jit(solution)/shard_map/ppermute | solution.py:695
  436.5 119.4 %reduce-scatter.8.cloned.1.call-start = ((), (), s32[]{:S(2)}) async-start(), calls=%async_computation.7 | async-start | bytes 3686400 | tf_op jit(solution)/shard_map/reduce_scatter | solution.py:560
  443.9 22.1 %collective-permute-start.46 = (bf16[640,640]{1,0:T(8,128)(2,1)S(1)}, bf16[640,640]{1,0:T(8,128)(2,1)S(1)}, u32[]{:S(2)}, u32[]{:S(2)}) collective-permute-start(bf16[640,640]{1,0:T(8,128)(2,1)S(1)} %copy-done.88), channel_id=1, source_target_pairs={{0,4},{4,0},{1,5},{5,1},{2,6},{6,2},{3,7},{7,3},{8,12},{12,8},{9,1... | collective-permute-start | bytes 2457608 | tf_op jit(solution)/shard_map/ppermute | solution.py:695
  497.1 138.1 %all-gather.12.cloned.1.call-start = ((), (), s32[]{:S(2)}) async-start(), calls=%async_computation.8 | async-start | bytes 3686400 | tf_op jit(solution)/shard_map/all_gather | solution.py:564
  511.8 41.1 %collective-permute-start.56 = (bf16[576,1536]{1,0:T(8,128)(2,1)S(1)}, bf16[576,1536]{1,0:T(8,128)(2,1)}, u32[]{:S(2)}, u32[]{:S(2)}) collective-permute-start(bf16[576,1536]{1,0:T(8,128)(2,1)S(1)} %copy-done.46), channel_id=1, source_target_pairs={{0,4},{4,0},{1,5},{5,1},{2,6},{6,2},{3,7},{7,3},{8,12},{12,8},{9,1... | collective-permute-start | bytes 5308424 | tf_op jit(solution)/shard_map/ppermute | solution.py:637
  513.7 19.4 %collective-permute-start.53 = (bf16[576,640]{1,0:T(8,128)(2,1)S(1)}, bf16[576,640]{1,0:T(8,128)(2,1)S(1)}, u32[]{:S(2)}, u32[]{:S(2)}) collective-permute-start(bf16[576,640]{1,0:T(8,128)(2,1)S(1)} %shard_map.240), channel_id=1, source_target_pairs={{0,16},{8,24},{16,0},{24,8},{1,17},{9,25},{17,1},{25,9},{2,18},{10... | collective-permute-start | bytes 2211848 | tf_op jit(solution)/shard_map/ppermute | solution.py:619
  515.5 33.4 %collective-permute-start.51 = (bf16[576,640]{1,0:T(8,128)(2,1)S(1)}, bf16[576,640]{1,0:T(8,128)(2,1)S(1)}, u32[]{:S(2)}, u32[]{:S(2)}) collective-permute-start(bf16[576,640]{1,0:T(8,128)(2,1)S(1)} %shard_map.237), channel_id=1, source_target_pairs={{0,16},{8,24},{16,0},{24,8},{1,17},{9,25},{17,1},{25,9},{2,18},{10... | collective-permute-start | bytes 2211848 | tf_op jit(solution)/shard_map/ppermute | solution.py:619
  517.3 46.7 %collective-permute-start.55 = (bf16[576,640]{1,0:T(8,128)(2,1)S(1)}, bf16[576,640]{1,0:T(8,128)(2,1)S(1)}, u32[]{:S(2)}, u32[]{:S(2)}) collective-permute-start(bf16[576,640]{1,0:T(8,128)(2,1)S(1)} %shard_map.243), channel_id=1, source_target_pairs={{0,16},{8,24},{16,0},{24,8},{1,17},{9,25},{17,1},{25,9},{2,18},{10... | collective-permute-start | bytes 2211848 | tf_op jit(solution)/shard_map/ppermute | solution.py:619
  568.6 19.7 %collective-permute-start.62 = (bf16[576,640]{1,0:T(8,128)(2,1)}, bf16[576,640]{1,0:T(8,128)(2,1)S(1)}, u32[]{:S(2)}, u32[]{:S(2)}) collective-permute-start(bf16[576,640]{1,0:T(8,128)(2,1)} %shard_map.234), channel_id=1, source_target_pairs={{0,4},{4,0},{1,5},{5,1},{2,6},{6,2},{3,7},{7,3},{8,12},{12,8},{9,1... | collective-permute-start | bytes 2211848 | tf_op jit(solution)/shard_map/ppermute | solution.py:637
  569.2 34.9 %collective-permute-start.60 = (bf16[576,640]{1,0:T(8,128)(2,1)}, bf16[576,640]{1,0:T(8,128)(2,1)S(1)}, u32[]{:S(2)}, u32[]{:S(2)}) collective-permute-start(bf16[576,640]{1,0:T(8,128)(2,1)} %shard_map.241), channel_id=1, source_target_pairs={{0,4},{4,0},{1,5},{5,1},{2,6},{6,2},{3,7},{7,3},{8,12},{12,8},{9,1... | collective-permute-start | bytes 2211848 | tf_op jit(solution)/shard_map/ppermute | solution.py:637
  570.7 49.2 %collective-permute-start.59 = (bf16[576,640]{1,0:T(8,128)(2,1)}, bf16[576,640]{1,0:T(8,128)(2,1)S(1)}, u32[]{:S(2)}, u32[]{:S(2)}) collective-permute-start(bf16[576,640]{1,0:T(8,128)(2,1)} %shard_map.238), channel_id=1, source_target_pairs={{0,4},{4,0},{1,5},{5,1},{2,6},{6,2},{3,7},{7,3},{8,12},{12,8},{9,1... | collective-permute-start | bytes 2211848 | tf_op jit(solution)/shard_map/ppermute | solution.py:637
  588.3 45.7 %collective-permute-start.61 = (bf16[576,640]{1,0:T(8,128)(2,1)S(1)}, bf16[576,640]{1,0:T(8,128)(2,1)S(1)}, u32[]{:S(2)}, u32[]{:S(2)}) collective-permute-start(bf16[576,640]{1,0:T(8,128)(2,1)S(1)} %shard_map.244), channel_id=1, source_target_pairs={{0,4},{4,0},{1,5},{5,1},{2,6},{6,2},{3,7},{7,3},{8,12},{12,8},{9,1... | collective-permute-start | bytes 2211848 | tf_op jit(solution)/shard_map/ppermute | solution.py:637
  (129 other events, 815.9 us)
Sparse Core Ops, SparseCore 0:
  16.1 60.5 all-gather.15
  121.3 65.7 all-gather.13
  245.4 58.0 reduce-scatter.3
  309.3 61.0 all-gather.7
  372.7 56.1 reduce-scatter.5
  436.6 60.4 all-gather.9
  500.0 55.8 reduce-scatter.7
  568.7 58.8 all-gather.11

commit v4 on v3

--- a/solution.py
+++ b/solution.py
@@ -136,6 +136,25 @@
         compiler_params=params(20),
         cost_estimate=COST,
     )(offs, a, *shards)
+
+
+def row_kernel(a_ref, w_ref, o_ref):
+    o_ref[...] = dot(a_ref[...], w_ref[...]).astype(bf)
+
+
+def row_matmul(a, weight):
+    rows, depth = a.shape
+    feats = weight.shape[1]
+    step = 128 if rows % 128 == 0 else rows
+    return pl.pallas_call(
+        row_kernel,
+        grid=(rows // step,),
+        out_shape=jax.ShapeDtypeStruct((rows, feats), bf),
+        in_specs=[pl.BlockSpec((step, depth), lambda i: (i, 0)), pl.BlockSpec((depth, feats), lambda i: (0, 0))],
+        out_specs=pl.BlockSpec((step, feats), lambda i: (i, 0)),
+        compiler_params=params(56),
+        cost_estimate=COST,
+    )(a, weight)
 
 
 def qkv_back_kernel(ns, offs, x_ref, scale_ref, *rest):
@@ -353,6 +372,26 @@
     )(*pairs, *others)
 
 
+def assemble_kernel(me_ref, *refs):
+    out, parts = refs[-1], refs[:-1]
+    n, rows = len(parts), parts[0].shape[0]
+    for k, part in enumerate(parts):
+        first = pl.multiple_of((me_ref[0] + n - k) % n * rows, 8)
+        out[pl.ds(first, rows), :] = part[...].astype(f32)
+
+
+def assemble(parts, me):
+    rows, cols = parts[0].shape
+    return pl.pallas_call(
+        assemble_kernel,
+        out_shape=jax.ShapeDtypeStruct((rows * len(parts), cols), f32),
+        in_specs=[SM] + [VM] * len(parts),
+        out_specs=VM,
+        compiler_params=params(24),
+        cost_estimate=COST,
+    )(me[None], *parts)
+
+
 def fill_bias(qseg_ref, qpos_ref, kseg_ref, kpos_ref, bias_ref):
     kseg = kseg_ref[...]
     allowed = ((kseg == qseg_ref[...]) | (kseg == 0)) & (kpos_ref[...] <= qpos_ref[...])
@@ -604,15 +643,21 @@
     def __init__(self, n, n_ctx, offs):
         self.n, self.n_ctx, self.offs = n, n_ctx, offs
 
-    def start(self, left, right):
+    def make(self, left, right):
         if self.n == 4:
-            self.keep, send = weight_grad(left, right, self.offs)
-            self.first = send
-            self.got = lax.ppermute(send, "dp", swap(4, 1))
-            self.far = add_halves((self.keep, self.got), (), 1)
+            self.keep, self.first = weight_grad(left, right, self.offs)
         else:
             self.first = self.far = self.whole = dot(left, right, ((0,), (0,))).astype(bf)
         return self
+
+    def trade(self, *late):
+        if self.n == 4:
+            self.got = lax.ppermute(after(self.first, *late), "dp", swap(4, 1))
+            self.far = add_halves((self.keep, self.got), (), 1)
+        return self
+
+    def start(self, left, right):
+        return self.make(left, right).trade()
 
     def start_x(self):
         if self.n == 4:
@@ -638,6 +683,15 @@
         else:
             self.other = lax.psum(self.total, "ctx")
         return self.other
+
+    def along_y_halves(self, first, *late):
+        if self.n_ctx != 2:
+            return self.along_y()
+        half = self.total.shape[0] // 2
+        parts = [after(self.total[:half], *first), after(self.total[half:], *late)]
+        parts = [lax.ppermute(p, "ctx", swap(2, 1)) for p in parts]
+        self.other = jnp.concatenate(parts)
+        return parts[0]
 
     def finish(self, size, *before):
         other = after(self.other, *before).astype(f32)
@@ -708,7 +762,7 @@
     if n_dp == 4 and n_ctx == 2:
         cut = lambda a: lax.dynamic_slice_in_dim(a, ctx * half, half, a.ndim - 2)
         items = [cut(wide[0]), cut(wo_all[:mid]), cut(wo_all[mid:]), cut(wide[1]), cut(wide[2])]
-    *wq, raw_q = gather_weight(after(q_cast, wv[1][-2] if n_dp == 4 else raw_v), n_dp, offs, early + tuple(wide))
+    *wq, raw_q = gather_weight(after(q_cast, wv[1][-2] if n_dp == 4 else raw_v), n_dp, offs, early + tuple(wide) + tuple(t for m in k_metas for t in m[2:]))
     grad_ffn = (branch_scale * cotangent.astype(f32)).astype(bf)
     if n_dp == 4 and n_ctx == 2:
         near = lambda a: lax.ppermute(a, "dp", swap(4, 1))
@@ -751,9 +805,7 @@
         grad_hidden = wide_matmul(grad_ffn, wd, False, f32)
     att_all = after(lax.all_gather(att, "tensor", axis=0, tiled=False), *late)
     my_in, my_scale = mine(tokens).astype(f32), mine(scale1)
-    att_all = after(att_all, *[t for m in k_metas for t in m[2:]])
     normed2, hidden_in, wo_dev = mix(att_all, tokens, gain2, places, wo_pieces, me)
-    wo = (jnp.zeros((1,), jnp.int32), [wo_dev])
     if n_dp == 4 and n_ctx == 2:
         wu = shards_of(wide[2], firsts[4], after(seconds[4], normed2))
     scale2 = lax.rsqrt(jnp.mean(hidden_in * hidden_in, axis=-1, keepdims=True) + norm_eps)
@@ -779,35 +831,39 @@
     grad_mixed = after(grad_mixed, grad_d.along_y(), grad_g.along_x(), grad_u.far)
     ffn_part = scatter_sum(after(ffn_part, grad_mixed))
 
-    grad_att = wide_matmul(grad_mixed, wo, False, bf)
+    grad_att = row_matmul(grad_mixed, wo_dev)
     back = lambda k, v, m: attention_bwd(query, att, grad_att, lse, k, v, q_meta, m, feats // HEAD)
     if n_ctx == 2:
         grad_q1, grad_k1, grad_v1 = back(keys_all[1:], values_all[1:], k_metas[1:])
-        grad_att = after(grad_att, grad_q1, grad_g.along_y(), grad_u.along_x(grad_q1))
+        grad_o = make().start(after(grad_mixed, grad_q1), att)
+        grad_att = after(grad_att, grad_o.got, grad_u.start_x())
         grad_q0, grad_k0, grad_v0 = back(keys_all[:1], values_all[:1], k_metas[:1])
         grad_q = (grad_q0.astype(f32) + grad_q1.astype(f32)).astype(bf)
         grad_ks, grad_vs = grad_k0 + grad_k1, grad_v0 + grad_v1
     else:
-        grad_g.along_y(), grad_u.along_x()
+        grad_u.start_x()
         grad_q, grad_ks, grad_vs = back(keys_all, values_all, k_metas)
+        grad_o = make().start(grad_mixed, att)
     if n_ctx == 2:
         merge = lambda pair: (pair[0].astype(f32) + trade(pair[1]).astype(f32)).astype(bf)
     else:
         merge = lambda whole: lax.psum_scatter(whole[0], "ctx", scatter_dimension=0, tiled=True)
     grad_k, grad_v = merge(grad_ks), merge(grad_vs)
 
-    grad_o = make().start(grad_mixed, att)
-    worked = (grad_q, grad_k)
-    grad_q = after(grad_q, grad_o.along_x())
-    grad_u.along_y(grad_k, grad_v)
+    output = (hidden_in + branch_scale * after(ffn_part, grad_q)).astype(bf)
+    rounds = [lax.optimization_barrier(output)]
+    total_u, total_o = grad_u.finish_x(grad_q), grad_o.along_x()
     partial1, part_g1 = qkv_back((grad_q, grad_k, grad_v), (wq, wk, wv), tokens, scale1)
-    output = hidden_in + branch_scale * after(ffn_part, *worked)
-    output = gather_rows(lax.optimization_barrier(output.astype(bf)))
+    ring = [(i, (i + 1) % n_tp) for i in range(n_tp)]
+    step = lambda *before: rounds.append(lax.ppermute(after(rounds[-1], *before), "tensor", ring)) or rounds[-1]
+    rest = n_tp - 1
+    grad_norm1 = scatter_sum(after(partial1, *([step()] if rest > 0 else [])))
     grads_a = [make().start(normed1, g) for g in (grad_q, grad_k, grad_v)]
-    gain_sum = sum_all(jnp.concatenate([part_g1, part_g2[None, :]]), (("ctx", n_ctx), ("dp", n_dp)))
     totals = [g.along_x() for g in grads_a[:2]]
-    grad_u.other = after(grad_u.other, *totals)
-    grad_norm1 = after(scatter_sum(after(partial1, output, gain_sum)), *totals, grads_a[2].start_x(), grad_u.other)
+    grad_g.along_y(grad_k, grad_v)
+    part_u = grad_u.along_y_halves((grad_g.other, grads_a[0].raw))
+    beside = [step()] if rest > 1 else []
+    grad_norm1 = after(grad_norm1, *totals, grad_g.other, part_u, *beside)
     grad_o.along_y()
     grad_in = (
         grad_h
@@ -815,18 +871,22 @@
         - my_in * my_scale**3 * jnp.mean(my_in * gain1 * grad_norm1, axis=-1, keepdims=True)
     )
     local_in = lax.optimization_barrier(grad_in.astype(bf))
-    grads_a[2].finish_x(local_in)
+    grads_a[2].along_x(local_in)
     grad_in = gather_rows(local_in).astype(f32)
-    gain_sum = sum_all(after(gain_sum, local_in), (("tensor", n_tp),))
+    while len(rounds) < n_tp:
+        step(local_in)
+    output = assemble(rounds, me)
+    gain_sum = after(jnp.concatenate([part_g1, part_g2[None, :]]), local_in)
+    gain_sum = sum_all(gain_sum, (("tensor", n_tp), ("dp", n_dp), ("ctx", n_ctx)))
     gain_sum = lax.dynamic_slice_in_dim(gain_sum, dp * shard, shard, 1)
 
     for g in grads_a:
         g.along_y()
     sum_wd = grad_d.finish(hidden_dev, local_in).T
     sum_wg, sum_wu = grad_g.finish(hidden_dev, local_in), grad_u.finish(hidden_dev, local_in)
-    sum_wo = grad_o.finish(feats, local_in).T
+    sum_wo = grad_o.finish(feats, local_in, rounds[-1]).T
     sum_wq, sum_wk, sum_wv = [g.finish(feats, local_in) for g in grads_a]
-    return (output.astype(f32), grad_in, gain_sum[0], sum_wq, sum_wk, sum_wv, sum_wo, gain_sum[1], sum_wg, sum_wu, sum_wd)
+    return (output, grad_in, gain_sum[0], sum_wq, sum_wk, sum_wv, sum_wo, gain_sum[1], sum_wg, sum_wu, sum_wd)
 
 
 def solution(mesh):

time: 657 us -> 635 us (0.967)
  the two profiles are of different devices: /device:TPU:0 before, /device:TPU:26 now
where the time goes in v4:
time: 635 us; the launch traced here: 623 us
  Pallas kernels  223 us (35%)
  waiting for transfers between devices  216 us (34%)
  local copies, waits for them, and re-layouts  63.4 us (10%)
  other arithmetic  58.1 us (9%)
  starting transfers between devices  46.2 us (7%)
  between operations  15.9 us (3%)
    ppermute x7, waiting for transfers between devices, start_x(): self.raw = lax.ppermute(self.far, 'dp', swap(4, 2))  59.8 us
    ppermute x6, waiting for transfers between devices, along_y(): self.other = lax.ppermute(after(self.total, *late), 'ctx', swap(2, 1))  48.7 us
    unnamed x232, local copies, waits for them, and re-layouts  42.1 us
    pallas_call x7, Pallas kernels, weight_grad(): pl.pallas_call(grad_kernel, out_shape=(half, half), in_specs=[SM, VM, VM]...  40.2 us
    pallas_call x2, Pallas kernels, attention_bwd(): pl.pallas_call(functools.partial(attn_bwd_kernel, parts, heads), grid=(bl...  33.9 us
    pallas_call x1, Pallas kernels, ffn(): pl.pallas_call(functools.partial(ffn_kernel, ns, width), out_shape=(mid,...  27.3 us
    pallas_call x14, Pallas kernels, add_halves(): pl.pallas_call(add_kernel, grid=(steps,), out_shape=jax.ShapeDtypeStruct(...  25.1 us
    pallas_call x2, Pallas kernels, wide_matmul(): pl.pallas_call(functools.partial(wide_kernel, ns, nt, width), out_shape=j...  20.8 us
  transfers between devices with their start and end apart: 74, of which 32 were waited for; matrix products, arithmetic and copies ran while one was open for 12% of the time, Pallas kernels for 31%

profile of v4, /device:TPU:26, one launch (start us, length us, event | category | flops | bytes accessed | tf_op | source)
XLA Modules:
  0.0 622.9 jit_solution(2562645370263616317)
XLA Ops:
  13.8 3.6 fusion.9
  23.7 7.7 %collective-permute-done.1.rest_2_.rest_9_ = bf16[592,640]{1,0:T(8,128)(2,1)} collective-permute-done((bf16[592,640]{1,0:T(8,128)(2,1)}, bf16[592,640]{1,0:T(8,128)(2,1)}, u32[]{:S(2)}, u32[]{:S(2)}) %collective-permute-start.1) | collective-permute-done | bytes 757792 | tf_op jit(solution)/shard_map/ppermute | solution.py:610
  38.4 5.9 shard_map.212.refs_7_.refs_12_
  45.9 4.8 collective-permute-done.3.rest_2_.rest_13_
  54.2 5.1 shard_map.213.refs_9_.refs_13_
  59.4 5.6 collective-permute-done.8.refs_8_.refs_12_
  66.9 3.0 collective-permute-done.5.rest_2_.rest_5_
  81.2 3.3 collective-permute-done.9.refs_10_.refs_13_
  85.0 2.7 collective-permute-done.10.rest_3_.rest_6_
  87.7 4.9 shard_map.214.refs_6_.refs_8_
  95.0 3.2 fusion.13
  101.1 17.4 %shard_map.215 = (bf16[640,640]{1,0:T(8,128)(2,1)S(1)}, f32[5,8,640]{2,1,0:T(8,128)S(1)}) custom-call(s32[1,640]{1,0:T(1,128)S(1)} %broadcast_in_dim.19.refs_0_, s32[1,640]{1,0:T(1,128)S(1)} %broadcast_in_dim.20.refs_1_, s32[640,1]{1,0:T(8,128)S(1)} %broadcast_in_dim.53.refs_2_.refs_4_, s32[640,1]{1,0:T(8,128)S(1)} %broadcast_in_dim.54.refs_3_.refs_4_, ...), custom_call_target="tpu_custom_call" | custom-call | flops 1024 | bytes 1024 | tf_op jit(solution)/shard_map/pallas_call | solution.py:464
  125.1 14.2 %collective-permute-done.14.rest_6_ = bf16[2,288,640]{2,1,0:T(8,128)(2,1)} collective-permute-done((bf16[2,288,640]{2,1,0:T(8,128)(2,1)S(1)}, bf16[2,288,640]{2,1,0:T(8,128)(2,1)}, u32[]{:S(2)}, u32[]{:S(2)}) %collective-permute-start.14) | collective-permute-done | bytes 737312 | tf_op jit(solution)/shard_map/ppermute | solution.py:627
  145.8 12.1 %shard_map.216.dh_hbm = f32[640,1536]{1,0:T(8,128)S(1)} custom-call(s32[6]{0:T(128)S(1)} %stack.71.offs, bf16[640,2304]{1,0:T(8,128)(2,1)S(1)} %copy-done.4, bf16[576,1536]{1,0:T(8,128)(2,1)} %pad.32.rest_0_, bf16[576,1536]{1,0:T(8,128)(2,1)} %collective-permute-done.18.rest_1_, bf16[288,1536]{1,0:T(8,128)(2,1)} %collective-permute-done.11.rest_2_, ...), custom_call_target="tpu_custom_call" | custom-call | flops 1024 | bytes 1024 | tf_op jit(solution)/shard_map/pallas_call | solution.py:130
  162.8 19.2 %collective-permute-done.22.rest_4_ = bf16[288,1536]{1,0:T(8,128)(2,1)S(1)} collective-permute-done((bf16[288,1536]{1,0:T(8,128)(2,1)}, bf16[288,1536]{1,0:T(8,128)(2,1)S(1)}, u32[]{:S(2)}, u32[]{:S(2)}) %collective-permute-start.22) | collective-permute-done | bytes 884768 | tf_op jit(solution)/shard_map/ppermute | solution.py:624
  186.8 2.8 collective-permute-done.27.rest_9_
  189.7 19.9 %shard_map.217 = (bf16[640,2304]{1,0:T(8,128)(2,1)}, f32[160,2304]{1,0:T(8,128)}, bf16[2304,640]{1,0:T(8,128)(2,1)}) custom-call(s32[1]{0:T(128)} %bitcast.me_ref, s32[10]{0:T(128)} %stack.64.offs, bf16[4,640,640]{2,1,0:T(8,128)(2,1)} %bitcast.26, bf16[640,2304]{1,0:T(8,128)(2,1)} %x_ref.3, f32[1,2304]{1,0:T(1,128)} %get-tuple-element.221.gain_ref, ...), custom_call_target="tpu_custom_call" | custom-call | flops 1024 | bytes 1024 | tf_op jit(solution)/shard_map/pallas_call | solution.py:308
  213.8 27.3 %shard_map.218 = (bf16[640,1536]{1,0:T(8,128)(2,1)}, bf16[640,1536]{1,0:T(8,128)(2,1)}, bf16[640,1536]{1,0:T(8,128)(2,1)}, bf16[640,2304]{1,0:T(8,128)(2,1)}) custom-call(s32[6]{0:T(128)} %copy-done.93, bf16[640,2304]{1,0:T(8,128)(2,1)} %get-tuple-element.117.n_hbm.a_ref, f32[640,1536]{1,0:T(8,128)} %copy-done.12, bf16[576,1536]{1,0:T(8,128)(2,1)} %pad.33.rest_0_, ...), custom_call_target="tpu_custom_call" | custom-call | flops 1024 | bytes 1024 | tf_op jit(solution)/shard_map/pallas_call | solution.py:252
  244.5 7.0 %shard_map.220 = (bf16[1152,1536]{1,0:T(8,128)(2,1)S(1)}, bf16[1152,1536]{1,0:T(8,128)(2,1)S(1)}) custom-call(s32[4]{0:T(128)S(1)} %pad_add_fusion.offs, bf16[640,2304]{1,0:T(8,128)(2,1)S(1)} %copy-done.5, bf16[640,1536]{1,0:T(8,128)(2,1)S(1)} %copy-done.30), custom_call_target="tpu_custom_call" | custom-call | flops 1024 | bytes 1024 | tf_op jit(solution)/shard_map/pallas_call | solution.py:340
  251.9 5.9 collective-permute-done.35.refs_1_
  264.1 8.6 %shard_map.219 = bf16[640,2304]{1,0:T(8,128)(2,1)S(1)} custom-call(s32[6]{0:T(128)S(1)} %copy-done.94, bf16[640,1536]{1,0:T(8,128)(2,1)S(1)} %copy-done.31, bf16[576,1536]{1,0:T(8,128)(2,1)} %pad.32.rest_0_, bf16[576,1536]{1,0:T(8,128)(2,1)} %collective-permute-done.18.rest_1_, bf16[288,1536]{1,0:T(8,128)(2,1)} %collective-permute-done.11.rest_2_, ...), custom_call_target="tpu_custom_call" | custom-call | flops 1024 | bytes 1024 | tf_op jit(solution)/shard_map/pallas_call | solution.py:130
  277.8 8.8 %shard_map.222 = (bf16[1152,1536]{1,0:T(8,128)(2,1)S(1)}, bf16[1152,1536]{1,0:T(8,128)(2,1)}) custom-call(s32[4]{0:T(128)S(1)} %pad_add_fusion.offs, bf16[640,2304]{1,0:T(8,128)(2,1)S(1)} %copy-done.2, bf16[640,1536]{1,0:T(8,128)(2,1)S(1)} %copy-done.85), custom_call_target="tpu_custom_call" | custom-call | flops 1024 | bytes 1024 | tf_op jit(solution)/shard_map/pallas_call | solution.py:340
  288.4 9.8 %reduce-scatter.4.cloned.1.call-done = bf16[160,2304]{1,0:T(8,128)(2,1)} async-done(((bf16[640,2304]{1,0:T(8,128)(2,1)}), bf16[160,2304]{1,0:T(8,128)(2,1)}) %reduce-scatter.4.cloned.1.call-update) | async-done | bytes 737296 | tf_op jit(solution)/shard_map/reduce_scatter | solution.py:599
  302.0 3.0 multiply_convert_fusion.1
  308.8 7.0 %shard_map.226 = (bf16[1152,1536]{1,0:T(8,128)(2,1)S(1)}, bf16[1152,1536]{1,0:T(8,128)(2,1)S(1)}) custom-call(s32[4]{0:T(128)S(1)} %pad_add_fusion.offs, bf16[640,2304]{1,0:T(8,128)(2,1)S(1)} %copy-done.3, bf16[640,1536]{1,0:T(8,128)(2,1)S(1)} %copy-done.84), custom_call_target="tpu_custom_call" | custom-call | flops 1024 | bytes 1024 | tf_op jit(solution)/shard_map/pallas_call | solution.py:340
  315.9 4.0 shard_map.224
  324.8 35.7 %collective-permute-done.39.refs_2_ = bf16[576,1536]{1,0:T(8,128)(2,1)S(1)} collective-permute-done((bf16[576,1536]{1,0:T(8,128)(2,1)S(1)}, bf16[576,1536]{1,0:T(8,128)(2,1)S(1)}, u32[]{:S(2)}, u32[]{:S(2)}) %collective-permute-start.39) | collective-permute-done | bytes 1769504 | tf_op jit(solution)/shard_map/ppermute | solution.py:664
  367.5 7.0 %shard_map.228.refs_10_ = bf16[640,640]{1,0:T(8,128)(2,1)} custom-call(bf16[640,2304]{1,0:T(8,128)(2,1)} %all-gather.7.cloned.1.call-done.a_ref, bf16[2304,640]{1,0:T(8,128)(2,1)} %get-tuple-element.123.w_ref), custom_call_target="tpu_custom_call" | custom-call | flops 1024 | bytes 1024 | tf_op jit(solution)/shard_map/pallas_call | solution.py:149
  375.8 17.2 %shard_map.229 = (bf16[640,640]{1,0:T(8,128)(2,1)S(1)}, bf16[640,640]{1,0:T(8,128)(2,1)}, bf16[640,640]{1,0:T(8,128)(2,1)}) custom-call(s32[1,640]{1,0:T(1,128)S(1)} %broadcast_in_dim.19.refs_0_, s32[1,640]{1,0:T(1,128)S(1)} %broadcast_in_dim.20.refs_1_, f32[640,128]{1,0:T(8,128)S(1)} %pad_maximum_fusion.1.cos_ref.refs_2_.refs_6_, f32[640,128]{1,0:T(8,128)S(1)} %copy-done.9, ...), custom_call_target="tpu_custom_call" | custom-call | flops 1024 | bytes 1024 | tf_op jit(solution)/shard_map/pallas_call | solution.py:553
  393.0 4.1 shard_map.230
  400.3 6.6 %collective-permute-done.42.refs_2_ = bf16[576,1536]{1,0:T(8,128)(2,1)} collective-permute-done((bf16[576,1536]{1,0:T(8,128)(2,1)}, bf16[576,1536]{1,0:T(8,128)(2,1)}, u32[]{:S(2)}, u32[]{:S(2)}) %collective-permute-start.42) | collective-permute-done | bytes 1769504 | tf_op jit(solution)/shard_map/ppermute | solution.py:664
  408.1 16.6 %shard_map.231 = (bf16[640,640]{1,0:T(8,128)(2,1)S(1)}, bf16[640,640]{1,0:T(8,128)(2,1)S(1)}, bf16[640,640]{1,0:T(8,128)(2,1)S(1)}) custom-call(s32[1,640]{1,0:T(1,128)S(1)} %broadcast_in_dim.19.refs_0_, s32[1,640]{1,0:T(1,128)S(1)} %broadcast_in_dim.20.refs_1_, f32[640,128]{1,0:T(8,128)S(1)} %pad_maximum_fusion.1.cos_ref.refs_2_.refs_6_, ...), custom_call_target="tpu_custom_call" | custom-call | flops 1024 | bytes 1024 | tf_op jit(solution)/shard_map/pallas_call | solution.py:553
  433.3 3.5 collective-permute-done.45
  438.2 11.5 %shard_map.232 = (bf16[640,2304]{1,0:T(8,128)(2,1)S(1)}, f32[1,2304]{1,0:T(1,128)S(1)}) custom-call(s32[4]{0:T(128)S(1)} %pad_add_fusion.offs, bf16[640,2304]{1,0:T(8,128)(2,1)S(1)} %copy-done.1, f32[640,1]{1,0:T(8,128)S(1)} %rsqrt.19.scale_ref, bf16[640,640]{1,0:T(8,128)(2,1)S(1)} %copy-done.34, bf16[640,640]{1,0:T(8,128)(2,1)S(1)} %add_convert_fusion.1.rest_1_.b_ref, ...), custom_call_target="tpu_custom_call" | custom-call | flops 1024 | bytes 1024 | tf_op jit(solution)/shard_map/pallas_call | solution.py:183
  452.5 4.1 shard_map.233
  458.3 4.1 shard_map.236
  469.0 28.8 %collective-permute-done.51 = bf16[576,1536]{1,0:T(8,128)(2,1)S(1)} collective-permute-done((bf16[576,1536]{1,0:T(8,128)(2,1)S(1)}, bf16[576,1536]{1,0:T(8,128)(2,1)S(1)}, u32[]{:S(2)}, u32[]{:S(2)}) %collective-permute-start.51) | collective-permute-done | bytes 1769504 | tf_op jit(solution)/shard_map/ppermute | solution.py:682
  501.5 5.2 shard_map.241
  509.7 9.2 %collective-permute-done.50.refs_2_ = bf16[576,640]{1,0:T(8,128)(2,1)S(1)} collective-permute-done((bf16[576,640]{1,0:T(8,128)(2,1)S(1)}, bf16[576,640]{1,0:T(8,128)(2,1)S(1)}, u32[]{:S(2)}, u32[]{:S(2)}) %collective-permute-start.50) | collective-permute-done | bytes 737312 | tf_op jit(solution)/shard_map/ppermute | solution.py:664
  526.9 6.4 %collective-permute-done.64.refs_2_ = bf16[576,640]{1,0:T(8,128)(2,1)} collective-permute-done((bf16[576,640]{1,0:T(8,128)(2,1)}, bf16[576,640]{1,0:T(8,128)(2,1)}, u32[]{:S(2)}, u32[]{:S(2)}) %collective-permute-start.64) | collective-permute-done | bytes 737312 | tf_op jit(solution)/shard_map/ppermute | solution.py:664
  544.7 3.8 add_bitcast_fusion
  556.4 2.9 collective-permute-start.53
  559.3 3.4 shard_map.243
  562.7 8.4 %collective-permute-done.60 = bf16[576,640]{1,0:T(8,128)(2,1)S(1)} collective-permute-done((bf16[576,640]{1,0:T(8,128)(2,1)S(1)}, bf16[576,640]{1,0:T(8,128)(2,1)S(1)}, u32[]{:S(2)}, u32[]{:S(2)}) %collective-permute-start.60) | collective-permute-done | bytes 737312 | tf_op jit(solution)/shard_map/ppermute | solution.py:682
  575.2 11.6 %collective-permute-done.59 = bf16[576,640]{1,0:T(8,128)(2,1)S(1)} collective-permute-done((bf16[576,640]{1,0:T(8,128)(2,1)S(1)}, bf16[576,640]{1,0:T(8,128)(2,1)S(1)}, u32[]{:S(2)}, u32[]{:S(2)}) %collective-permute-start.59) | collective-permute-done | bytes 737312 | tf_op jit(solution)/shard_map/ppermute | solution.py:682
  589.7 12.1 %collective-permute-done.58 = f32[2,2304]{1,0:T(2,128)S(1)} collective-permute-done((f32[2,2304]{1,0:T(2,128)S(1)}, f32[2,2304]{1,0:T(2,128)S(1)}, u32[]{:S(2)}, u32[]{:S(2)}) %collective-permute-start.58) | collective-permute-done | bytes 18464 | tf_op jit(solution)/shard_map/ppermute | solution.py:587
  602.5 4.3 shard_map.240
  610.9 4.9 convert_element_type.202
  (463 shorter events, 179.0 us)
Async XLA Ops:
  7.2 87.9 %all-gather.13.cloned.1.call-start = ((), (), s32[]{:S(2)}) async-start(), calls=%async_computation.9 | async-start | bytes 3686400 | tf_op jit(solution)/shard_map/all_gather | solution.py:718
  11.7 20.3 %collective-permute-start = (bf16[592,640]{1,0:T(8,128)(2,1)}, bf16[592,640]{1,0:T(8,128)(2,1)}, u32[]{:S(2)}, u32[]{:S(2)}) collective-permute-start(bf16[592,640]{1,0:T(8,128)(2,1)} %pad_dynamic-update-slice_fusion.rest_0_.rest_7_), channel_id=1, source_target_pairs={{0,8},{8,0},{16,24},{24,16},{1,9},{9,1},{17,25},{25,17},{2,10},{10... | collective-permute-start | bytes 2273288 | tf_op jit(solution)/shard_map/ppermute | solution.py:612
  11.7 19.7 %collective-permute-start.1 = (bf16[592,640]{1,0:T(8,128)(2,1)}, bf16[592,640]{1,0:T(8,128)(2,1)}, u32[]{:S(2)}, u32[]{:S(2)}) collective-permute-start(bf16[592,640]{1,0:T(8,128)(2,1)} %pad_dynamic-update-slice_fusion.rest_0_.rest_7_), channel_id=1, source_target_pairs={{0,16},{8,24},{16,0},{24,8},{1,17},{9,25},{17,1},{25,9},{2,18},{10... | collective-permute-start | bytes 2273288 | tf_op jit(solution)/shard_map/ppermute | solution.py:610
  13.6 172.9 %all-gather.11.cloned.1.call-start = ((), (), s32[]{:S(2)}) async-start(), calls=%async_computation.8 | async-start | bytes 4096000 | tf_op jit(solution)/shard_map/all_gather | solution.py:806
  44.4 20.7 %collective-permute-start.8 = (bf16[640,640]{1,0:T(8,128)(2,1)}, bf16[640,640]{1,0:T(8,128)(2,1)}, u32[]{:S(2)}, u32[]{:S(2)}) collective-permute-start(bf16[640,640]{1,0:T(8,128)(2,1)} %shard_map.212.refs_7_.refs_12_), channel_id=1, source_target_pairs={{0,4},{4,0},{1,5},{5,1},{2,6},{6,2},{3,7},{7,3},{8,12},{12,8},{9,1... | collective-permute-start | bytes 2457608 | tf_op jit(solution)/shard_map/ppermute | solution.py:749
  65.0 19.5 %collective-permute-start.9 = (bf16[640,640]{1,0:T(8,128)(2,1)S(1)}, bf16[640,640]{1,0:T(8,128)(2,1)S(1)}, u32[]{:S(2)}, u32[]{:S(2)}) collective-permute-start(bf16[640,640]{1,0:T(8,128)(2,1)S(1)} %shard_map.213.refs_9_.refs_13_), channel_id=1, source_target_pairs={{0,4},{4,0},{1,5},{5,1},{2,6},{6,2},{3,7},{7,3},{8,12},{12,8},{9,1... | collective-permute-start | bytes 2457608 | tf_op jit(solution)/shard_map/ppermute | solution.py:749
  69.8 23.7 %collective-permute-start.11 = (bf16[288,1536]{1,0:T(8,128)(2,1)S(1)}, bf16[288,1536]{1,0:T(8,128)(2,1)}, u32[]{:S(2)}, u32[]{:S(2)}) collective-permute-start(bf16[288,1536]{1,0:T(8,128)(2,1)S(1)} %constant_dynamic-slice_fusion.2), channel_id=1, source_target_pairs={{0,16},{8,24},{16,0},{24,8},{1,17},{9,25},{17,1},{25,9},{2,18},{10... | collective-permute-start | bytes 2654216 | tf_op jit(solution)/shard_map/ppermute | solution.py:627
  84.5 56.8 %collective-permute-start.18 = (bf16[576,1536]{1,0:T(8,128)(2,1)}, bf16[576,1536]{1,0:T(8,128)(2,1)}, u32[]{:S(2)}, u32[]{:S(2)}) collective-permute-start(bf16[576,1536]{1,0:T(8,128)(2,1)} %pad.32.rest_0_), channel_id=1, source_target_pairs={{0,8},{8,0},{16,24},{24,16},{1,9},{9,1},{17,25},{25,17},{2,10},{10... | collective-permute-start | bytes 5308424 | tf_op jit(solution)/shard_map/ppermute | solution.py:768
  93.5 27.6 %collective-permute-start.12 = (bf16[288,1536]{1,0:T(8,128)(2,1)}, bf16[288,1536]{1,0:T(8,128)(2,1)}, u32[]{:S(2)}, u32[]{:S(2)}) collective-permute-start(bf16[288,1536]{1,0:T(8,128)(2,1)} %collective-permute-done.11.rest_2_), channel_id=1, source_target_pairs={{0,4},{4,0},{1,5},{5,1},{2,6},{6,2},{3,7},{7,3},{8,12},{12,8},{9,1... | collective-permute-start | bytes 2654216 | tf_op jit(solution)/shard_map/ppermute | solution.py:624
  99.2 22.0 %collective-permute-start.13 = (bf16[2,288,640]{2,1,0:T(8,128)(2,1)}, bf16[2,288,640]{2,1,0:T(8,128)(2,1)}, u32[]{:S(2)}, u32[]{:S(2)}) collective-permute-start(bf16[2,288,640]{2,1,0:T(8,128)(2,1)} %constant_dynamic-slice_fusion.1), channel_id=1, source_target_pairs={{0,16},{8,24},{16,0},{24,8},{1,17},{9,25},{17,1},{25,9},{2,18},{10... | collective-permute-start | bytes 2211848 | tf_op jit(solution)/shard_map/ppermute | solution.py:627
  119.5 178.7 %reduce-scatter.4.cloned.1.call-start = ((), (), s32[]{:S(2)}) async-start(), calls=%async_computation.3 | async-start | bytes 3686400 | tf_op jit(solution)/shard_map/reduce_scatter | solution.py:599
  124.6 19.4 %collective-permute-start.19 = (bf16[288,1536]{1,0:T(8,128)(2,1)}, bf16[288,1536]{1,0:T(8,128)(2,1)}, u32[]{:S(2)}, u32[]{:S(2)}) collective-permute-start(bf16[288,1536]{1,0:T(8,128)(2,1)} %collective-permute-done.11.rest_2_), channel_id=1, source_target_pairs={{0,8},{8,0},{16,24},{24,16},{1,9},{9,1},{17,25},{25,17},{2,10},{10... | collective-permute-start | bytes 2654216 | tf_op jit(solution)/shard_map/ppermute | solution.py:635
  139.9 20.5 %collective-permute-start.17 = (bf16[288,1536]{1,0:T(8,128)(2,1)}, bf16[288,1536]{1,0:T(8,128)(2,1)}, u32[]{:S(2)}, u32[]{:S(2)}) collective-permute-start(bf16[288,1536]{1,0:T(8,128)(2,1)} %constant_dynamic-slice_fusion), channel_id=1, source_target_pairs={{0,16},{8,24},{16,0},{24,8},{1,17},{9,25},{17,1},{25,9},{2,18},{10... | collective-permute-start | bytes 2654216 | tf_op jit(solution)/shard_map/ppermute | solution.py:627
  141.2 45.2 %collective-permute-start.23 = (bf16[4,576,640]{2,1,0:T(8,128)(2,1)}, bf16[4,576,640]{2,1,0:T(8,128)(2,1)}, u32[]{:S(2)}, u32[]{:S(2)}) collective-permute-start(bf16[4,576,640]{2,1,0:T(8,128)(2,1)} %bitcast.14.rest_0_), channel_id=1, source_target_pairs={{0,8},{8,0},{16,24},{24,16},{1,9},{9,1},{17,25},{25,17},{2,10},{10... | collective-permute-start | bytes 8847368 | tf_op jit(solution)/shard_map/ppermute | solution.py:768
  160.5 21.5 %collective-permute-start.22 = (bf16[288,1536]{1,0:T(8,128)(2,1)}, bf16[288,1536]{1,0:T(8,128)(2,1)S(1)}, u32[]{:S(2)}, u32[]{:S(2)}) collective-permute-start(bf16[288,1536]{1,0:T(8,128)(2,1)} %collective-permute-done.17.rest_2_), channel_id=1, source_target_pairs={{0,4},{4,0},{1,5},{5,1},{2,6},{6,2},{3,7},{7,3},{8,12},{12,8},{9,1... | collective-permute-start | bytes 2654216 | tf_op jit(solution)/shard_map/ppermute | solution.py:624
  161.5 21.7 %collective-permute-start.21 = (bf16[288,1536]{1,0:T(8,128)(2,1)S(1)}, bf16[288,1536]{1,0:T(8,128)(2,1)}, u32[]{:S(2)}, u32[]{:S(2)}) collective-permute-start(bf16[288,1536]{1,0:T(8,128)(2,1)S(1)} %constant_dynamic-slice_fusion.4), channel_id=1, source_target_pairs={{0,16},{8,24},{16,0},{24,8},{1,17},{9,25},{17,1},{25,9},{2,18},{10... | collective-permute-start | bytes 2654216 | tf_op jit(solution)/shard_map/ppermute | solution.py:627
  162.3 47.9 %collective-permute-start.28 = (bf16[576,1536]{1,0:T(8,128)(2,1)}, bf16[576,1536]{1,0:T(8,128)(2,1)}, u32[]{:S(2)}, u32[]{:S(2)}) collective-permute-start(bf16[576,1536]{1,0:T(8,128)(2,1)} %pad.33.rest_0_), channel_id=1, source_target_pairs={{0,8},{8,0},{16,24},{24,16},{1,9},{9,1},{17,25},{25,17},{2,10},{10... | collective-permute-start | bytes 5308424 | tf_op jit(solution)/shard_map/ppermute | solution.py:768
  162.3 20.9 %collective-permute-start.24 = (bf16[2,288,640]{2,1,0:T(8,128)(2,1)}, bf16[2,288,640]{2,1,0:T(8,128)(2,1)}, u32[]{:S(2)}, u32[]{:S(2)}) collective-permute-start(bf16[2,288,640]{2,1,0:T(8,128)(2,1)} %collective-permute-done.13.rest_2_), channel_id=1, source_target_pairs={{0,8},{8,0},{16,24},{24,16},{1,9},{9,1},{17,25},{25,17},{2,10},{10... | collective-permute-start | bytes 2211848 | tf_op jit(solution)/shard_map/ppermute | solution.py:635
  183.2 26.5 %collective-permute-start.33 = (bf16[288,1536]{1,0:T(8,128)(2,1)}, bf16[288,1536]{1,0:T(8,128)(2,1)}, u32[]{:S(2)}, u32[]{:S(2)}) collective-permute-start(bf16[288,1536]{1,0:T(8,128)(2,1)} %collective-permute-done.21.rest_8_), channel_id=1, source_target_pairs={{0,4},{4,0},{1,5},{5,1},{2,6},{6,2},{3,7},{7,3},{8,12},{12,8},{9,1... | collective-permute-start | bytes 2654216 | tf_op jit(solution)/shard_map/ppermute | solution.py:624
  184.5 25.8 %collective-permute-start.31 = (bf16[576,1536]{1,0:T(8,128)(2,1)}, bf16[576,1536]{1,0:T(8,128)(2,1)}, u32[]{:S(2)}, u32[]{:S(2)}) collective-permute-start(bf16[576,1536]{1,0:T(8,128)(2,1)} %pad.34.rest_6_), channel_id=1, source_target_pairs={{0,8},{8,0},{16,24},{24,16},{1,9},{9,1},{17,25},{25,17},{2,10},{10... | collective-permute-start | bytes 5308424 | tf_op jit(solution)/shard_map/ppermute | solution.py:768
  186.5 23.8 %collective-permute-start.29 = (bf16[288,1536]{1,0:T(8,128)(2,1)}, bf16[288,1536]{1,0:T(8,128)(2,1)}, u32[]{:S(2)}, u32[]{:S(2)}) collective-permute-start(bf16[288,1536]{1,0:T(8,128)(2,1)} %collective-permute-done.17.rest_2_), channel_id=1, source_target_pairs={{0,8},{8,0},{16,24},{24,16},{1,9},{9,1},{17,25},{25,17},{2,10},{10... | collective-permute-start | bytes 2654216 | tf_op jit(solution)/shard_map/ppermute | solution.py:635
  189.6 20.7 %collective-permute-start.30 = (bf16[288,1536]{1,0:T(8,128)(2,1)}, bf16[288,1536]{1,0:T(8,128)(2,1)}, u32[]{:S(2)}, u32[]{:S(2)}) collective-permute-start(bf16[288,1536]{1,0:T(8,128)(2,1)} %copy-done.112), channel_id=1, source_target_pairs={{0,8},{8,0},{16,24},{24,16},{1,9},{9,1},{17,25},{25,17},{2,10},{10... | collective-permute-start | bytes 2654216 | tf_op jit(solution)/shard_map/ppermute | solution.py:635
  241.1 125.6 %all-gather.7.cloned.1.call-start = ((), (), s32[]{:S(2)}) async-start(), calls=%async_computation.4 | async-start | bytes 3686400 | tf_op jit(solution)/shard_map/all_gather | solution.py:603
  260.2 41.2 %collective-permute-start.36 = (bf16[576,1536]{1,0:T(8,128)(2,1)}, bf16[576,1536]{1,0:T(8,128)(2,1)}, u32[]{:S(2)}, u32[]{:S(2)}) collective-permute-start(bf16[576,1536]{1,0:T(8,128)(2,1)} %shard_map.221), channel_id=1, source_target_pairs={{0,16},{8,24},{16,0},{24,8},{1,17},{9,25},{17,1},{25,9},{2,18},{10... | collective-permute-start | bytes 5308424 | tf_op jit(solution)/shard_map/ppermute | solution.py:664
  288.3 27.6 %collective-permute-start.38 = (bf16[1152,1536]{1,0:T(8,128)(2,1)}, bf16[1152,1536]{1,0:T(8,128)(2,1)}, u32[]{:S(2)}, u32[]{:S(2)}) collective-permute-start(bf16[1152,1536]{1,0:T(8,128)(2,1)} %get-tuple-element.113), channel_id=1, source_target_pairs={{0,8},{8,0},{16,24},{24,16},{1,9},{9,1},{17,25},{25,17},{2,10},{10... | collective-permute-start | bytes 10616840 | tf_op jit(solution)/shard_map/ppermute | solution.py:655
  305.0 122.7 %reduce-scatter.6.cloned.1.call-start = ((), (), s32[]{:S(2)}) async-start(), calls=%async_computation.5 | async-start | bytes 3686400 | tf_op jit(solution)/shard_map/reduce_scatter | solution.py:599
  315.8 47.3 %collective-permute-start.40 = (bf16[1152,1536]{1,0:T(8,128)(2,1)S(1)}, bf16[1152,1536]{1,0:T(8,128)(2,1)S(1)}, u32[]{:S(2)}, u32[]{:S(2)}) collective-permute-start(bf16[1152,1536]{1,0:T(8,128)(2,1)S(1)} %get-tuple-element.120), channel_id=1, source_target_pairs={{0,8},{8,0},{16,24},{24,16},{1,9},{9,1},{17,25},{25,17},{2,10},{10... | collective-permute-start | bytes 10616840 | tf_op jit(solution)/shard_map/ppermute | solution.py:655
  319.9 40.6 %collective-permute-start.39 = (bf16[576,1536]{1,0:T(8,128)(2,1)S(1)}, bf16[576,1536]{1,0:T(8,128)(2,1)S(1)}, u32[]{:S(2)}, u32[]{:S(2)}) collective-permute-start(bf16[576,1536]{1,0:T(8,128)(2,1)S(1)} %shard_map.224), channel_id=1, source_target_pairs={{0,16},{8,24},{16,0},{24,8},{1,17},{9,25},{17,1},{25,9},{2,18},{10... | collective-permute-start | bytes 5308424 | tf_op jit(solution)/shard_map/ppermute | solution.py:664
  323.3 43.4 %collective-permute-start.37 = (bf16[576,1536]{1,0:T(8,128)(2,1)S(1)}, bf16[576,1536]{1,0:T(8,128)(2,1)}, u32[]{:S(2)}, u32[]{:S(2)}) collective-permute-start(bf16[576,1536]{1,0:T(8,128)(2,1)S(1)} %shard_map.223), channel_id=1, source_target_pairs={{0,4},{4,0},{1,5},{5,1},{2,6},{6,2},{3,7},{7,3},{8,12},{12,8},{9,1... | collective-permute-start | bytes 5308424 | tf_op jit(solution)/shard_map/ppermute | solution.py:682
  366.7 153.8 %reduce-scatter.8.cloned.1.call-start = ((), (), s32[]{:S(2)}) async-start(), calls=%async_computation.6 | async-start | bytes 3686400 | tf_op jit(solution)/shard_map/reduce_scatter | solution.py:599
  366.8 40.1 %collective-permute-start.42 = (bf16[576,1536]{1,0:T(8,128)(2,1)}, bf16[576,1536]{1,0:T(8,128)(2,1)}, u32[]{:S(2)}, u32[]{:S(2)}) collective-permute-start(bf16[576,1536]{1,0:T(8,128)(2,1)} %copy-done.86), channel_id=1, source_target_pairs={{0,16},{8,24},{16,0},{24,8},{1,17},{9,25},{17,1},{25,9},{2,18},{10... | collective-permute-start | bytes 5308424 | tf_op jit(solution)/shard_map/ppermute | solution.py:664
  398.2 33.5 %collective-permute-start.46 = (bf16[640,640]{1,0:T(8,128)(2,1)}, bf16[640,640]{1,0:T(8,128)(2,1)}, u32[]{:S(2)}, u32[]{:S(2)}) collective-permute-start(bf16[640,640]{1,0:T(8,128)(2,1)} %get-tuple-element.134), channel_id=1, source_target_pairs={{0,4},{4,0},{1,5},{5,1},{2,6},{6,2},{3,7},{7,3},{8,12},{12,8},{9,1... | collective-permute-start | bytes 2457608 | tf_op jit(solution)/shard_map/ppermute | solution.py:749
  399.7 37.1 %collective-permute-start.45 = (bf16[640,640]{1,0:T(8,128)(2,1)}, bf16[640,640]{1,0:T(8,128)(2,1)}, u32[]{:S(2)}, u32[]{:S(2)}) collective-permute-start(bf16[640,640]{1,0:T(8,128)(2,1)} %get-tuple-element.132), channel_id=1, source_target_pairs={{0,4},{4,0},{1,5},{5,1},{2,6},{6,2},{3,7},{7,3},{8,12},{12,8},{9,1... | collective-permute-start | bytes 2457608 | tf_op jit(solution)/shard_map/ppermute | solution.py:749
  430.7 20.6 %collective-permute-start.43 = (bf16[160,2304]{1,0:T(8,128)(2,1)S(1)}, bf16[160,2304]{1,0:T(8,128)(2,1)}, u32[]{:S(2)}, u32[]{:S(2)}) collective-permute-start(bf16[160,2304]{1,0:T(8,128)(2,1)S(1)} %add_convert_fusion.3.refs_0_), channel_id=1, source_target_pairs={{0,1},{1,2},{2,3},{3,0},{4,5},{5,6},{6,7},{7,4},{8,9},{9,10},{10,1... | collective-permute-start | bytes 2211848 | tf_op jit(solution)/shard_map/ppermute | solution.py:858
  451.3 159.6 %all-gather.9.cloned.1.call-start = ((), (), s32[]{:S(2)}) async-start(), calls=%async_computation.7 | async-start | bytes 3686400 | tf_op jit(solution)/shard_map/all_gather | solution.py:603
  456.7 41.0 %collective-permute-start.51 = (bf16[576,1536]{1,0:T(8,128)(2,1)S(1)}, bf16[576,1536]{1,0:T(8,128)(2,1)S(1)}, u32[]{:S(2)}, u32[]{:S(2)}) collective-permute-start(bf16[576,1536]{1,0:T(8,128)(2,1)S(1)} %copy-done.43), channel_id=1, source_target_pairs={{0,4},{4,0},{1,5},{5,1},{2,6},{6,2},{3,7},{7,3},{8,12},{12,8},{9,1... | collective-permute-start | bytes 5308424 | tf_op jit(solution)/shard_map/ppermute | solution.py:682
  462.4 36.9 %collective-permute-start.49 = (bf16[1152,640]{1,0:T(8,128)(2,1)S(1)}, bf16[1152,640]{1,0:T(8,128)(2,1)S(1)}, u32[]{:S(2)}, u32[]{:S(2)}) collective-permute-start(bf16[1152,640]{1,0:T(8,128)(2,1)S(1)} %get-tuple-element.140), channel_id=1, source_target_pairs={{0,8},{8,0},{16,24},{24,16},{1,9},{9,1},{17,25},{25,17},{2,10},{10... | collective-permute-start | bytes 4423688 | tf_op jit(solution)/shard_map/ppermute | solution.py:655
  462.8 34.9 %collective-permute-start.48 = (bf16[576,640]{1,0:T(8,128)(2,1)S(1)}, bf16[576,640]{1,0:T(8,128)(2,1)S(1)}, u32[]{:S(2)}, u32[]{:S(2)}) collective-permute-start(bf16[576,640]{1,0:T(8,128)(2,1)S(1)} %shard_map.234), channel_id=1, source_target_pairs={{0,16},{8,24},{16,0},{24,8},{1,17},{9,25},{17,1},{25,9},{2,18},{10... | collective-permute-start | bytes 2211848 | tf_op jit(solution)/shard_map/ppermute | solution.py:664
  497.7 24.3 %collective-permute-start.52 = (bf16[288,1536]{1,0:T(8,128)(2,1)}, bf16[288,1536]{1,0:T(8,128)(2,1)}, u32[]{:S(2)}, u32[]{:S(2)}) collective-permute-start(bf16[288,1536]{1,0:T(8,128)(2,1)} %get-tuple-element.143), channel_id=1, source_target_pairs={{0,4},{4,0},{1,5},{5,1},{2,6},{6,2},{3,7},{7,3},{8,12},{12,8},{9,1... | collective-permute-start | bytes 2654216 | tf_op jit(solution)/shard_map/ppermute | solution.py:692
  499.5 19.5 %collective-permute-start.50 = (bf16[576,640]{1,0:T(8,128)(2,1)S(1)}, bf16[576,640]{1,0:T(8,128)(2,1)S(1)}, u32[]{:S(2)}, u32[]{:S(2)}) collective-permute-start(bf16[576,640]{1,0:T(8,128)(2,1)S(1)} %shard_map.237), channel_id=1, source_target_pairs={{0,16},{8,24},{16,0},{24,8},{1,17},{9,25},{17,1},{25,9},{2,18},{10... | collective-permute-start | bytes 2211848 | tf_op jit(solution)/shard_map/ppermute | solution.py:664
  500.9 21.8 %collective-permute-start.44 = (bf16[160,2304]{1,0:T(8,128)(2,1)}, bf16[160,2304]{1,0:T(8,128)(2,1)}, u32[]{:S(2)}, u32[]{:S(2)}) collective-permute-start(bf16[160,2304]{1,0:T(8,128)(2,1)} %collective-permute-done.43.refs_1_), channel_id=1, source_target_pairs={{0,1},{1,2},{2,3},{3,0},{4,5},{5,6},{6,7},{7,4},{8,9},{9,10},{10,1... | collective-permute-start | bytes 2211848 | tf_op jit(solution)/shard_map/ppermute | solution.py:858
  506.7 36.0 %collective-permute-start.66 = (bf16[288,1536]{1,0:T(8,128)(2,1)}, bf16[288,1536]{1,0:T(8,128)(2,1)}, u32[]{:S(2)}, u32[]{:S(2)}) collective-permute-start(bf16[288,1536]{1,0:T(8,128)(2,1)} %get-tuple-element.219), channel_id=1, source_target_pairs={{0,4},{4,0},{1,5},{5,1},{2,6},{6,2},{3,7},{7,3},{8,12},{12,8},{9,1... | collective-permute-start | bytes 2654216 | tf_op jit(solution)/shard_map/ppermute | solution.py:692
  509.0 24.3 %collective-permute-start.64 = (bf16[576,640]{1,0:T(8,128)(2,1)}, bf16[576,640]{1,0:T(8,128)(2,1)}, u32[]{:S(2)}, u32[]{:S(2)}) collective-permute-start(bf16[576,640]{1,0:T(8,128)(2,1)} %shard_map.244), channel_id=1, source_target_pairs={{0,16},{8,24},{16,0},{24,8},{1,17},{9,25},{17,1},{25,9},{2,18},{10... | collective-permute-start | bytes 2211848 | tf_op jit(solution)/shard_map/ppermute | solution.py:664
  535.6 71.2 %collective-permute-start.65 = (bf16[576,640]{1,0:T(8,128)(2,1)S(1)}, bf16[576,640]{1,0:T(8,128)(2,1)S(1)}, u32[]{:S(2)}, u32[]{:S(2)}) collective-permute-start(bf16[576,640]{1,0:T(8,128)(2,1)S(1)} %shard_map.245), channel_id=1, source_target_pairs={{0,4},{4,0},{1,5},{5,1},{2,6},{6,2},{3,7},{7,3},{8,12},{12,8},{9,1... | collective-permute-start | bytes 2211848 | tf_op jit(solution)/shard_map/ppermute | solution.py:682
  540.6 30.5 %collective-permute-start.60 = (bf16[576,640]{1,0:T(8,128)(2,1)S(1)}, bf16[576,640]{1,0:T(8,128)(2,1)S(1)}, u32[]{:S(2)}, u32[]{:S(2)}) collective-permute-start(bf16[576,640]{1,0:T(8,128)(2,1)S(1)} %copy-done.83), channel_id=1, source_target_pairs={{0,4},{4,0},{1,5},{5,1},{2,6},{6,2},{3,7},{7,3},{8,12},{12,8},{9,1... | collective-permute-start | bytes 2211848 | tf_op jit(solution)/shard_map/ppermute | solution.py:682
  541.5 45.4 %collective-permute-start.59 = (bf16[576,640]{1,0:T(8,128)(2,1)S(1)}, bf16[576,640]{1,0:T(8,128)(2,1)S(1)}, u32[]{:S(2)}, u32[]{:S(2)}) collective-permute-start(bf16[576,640]{1,0:T(8,128)(2,1)S(1)} %copy-done.81), channel_id=1, source_target_pairs={{0,4},{4,0},{1,5},{5,1},{2,6},{6,2},{3,7},{7,3},{8,12},{12,8},{9,1... | collective-permute-start | bytes 2211848 | tf_op jit(solution)/shard_map/ppermute | solution.py:682
  556.4 46.1 %collective-permute-start.53 = (bf16[160,2304]{1,0:T(8,128)(2,1)}, bf16[160,2304]{1,0:T(8,128)(2,1)S(1)}, u32[]{:S(2)}, u32[]{:S(2)}) collective-permute-start(bf16[160,2304]{1,0:T(8,128)(2,1)} %collective-permute-done.44.refs_2_), channel_id=1, source_target_pairs={{0,1},{1,2},{2,3},{3,0},{4,5},{5,6},{6,7},{7,4},{8,9},{9,10},{10,1... | collective-permute-start | bytes 2211848 | tf_op jit(solution)/shard_map/ppermute | solution.py:858
  571.1 37.5 %collective-permute-start.63 = (bf16[576,640]{1,0:T(8,128)(2,1)}, bf16[576,640]{1,0:T(8,128)(2,1)S(1)}, u32[]{:S(2)}, u32[]{:S(2)}) collective-permute-start(bf16[576,640]{1,0:T(8,128)(2,1)} %shard_map.243), channel_id=1, source_target_pairs={{0,4},{4,0},{1,5},{5,1},{2,6},{6,2},{3,7},{7,3},{8,12},{12,8},{9,1... | collective-permute-start | bytes 2211848 | tf_op jit(solution)/shard_map/ppermute | solution.py:682
  (141 other events, 999.6 us)
Sparse Core Ops, SparseCore 0:
  13.7 58.8 all-gather.12
  119.6 63.2 all-gather.10
  241.2 56.9 reduce-scatter.3
  305.1 58.7 all-gather.6
  366.8 56.9 reduce-scatter.5
  451.5 60.9 reduce-scatter.7
  527.0 74.5 all-gather.8

commit v5 on v4

--- a/solution.py
+++ b/solution.py
@@ -145,7 +145,7 @@
 def row_matmul(a, weight):
     rows, depth = a.shape
     feats = weight.shape[1]
-    step = 128 if rows % 128 == 0 else rows
+    step = 320 if rows % 320 == 0 else rows
     return pl.pallas_call(
         row_kernel,
         grid=(rows // step,),
@@ -159,17 +159,21 @@
 
 def qkv_back_kernel(ns, offs, x_ref, scale_ref, *rest):
     grads, rest = rest[:3], rest[3:]
-    shards, (o_ref, gain_ref, w_ref, sems) = rest[: 3 * ns], rest[3 * ns :]
-    rows = [fetch(offs, shards[i * ns : (i + 1) * ns], w_ref.at[i], sems.at[i], w_ref.shape[2])[0] for i in range(3)]
-    for row in rows:
-        wait_all(row)
+    shards, (o_ref, gain_ref, w_ref, g_ref, sems) = rest[: 3 * ns], rest[3 * ns :]
+    feats = grads[0].shape[1]
+    copies = []
+    for i in range(3):
+        cols = pl.ds(i * feats, feats)
+        for j, ref in enumerate(shards[i * ns : (i + 1) * ns]):
+            rows = pl.ds(pl.multiple_of(offs[j], 16), w_ref.shape[0] // min(ns, 4))
+            copies.append(pltpu.make_async_copy(ref.at[pl.ds(0, rows.size), :], w_ref.at[rows, cols], sems.at[i, j]))
+            copies[-1].start()
+        g_ref[:, i * feats : (i + 1) * feats] = grads[i][...]
+    wait_all(copies)
     width = 256
     for first in range(0, o_ref.shape[1], width):
         part = slice(first, first + width)
-        total = None
-        for i in range(3):
-            y = dot(grads[i][...], w_ref[i, part, :], ((1,), (1,)))
-            total = y if total is None else total + y
+        total = dot(g_ref[...], w_ref[part, :], ((1,), (1,)))
         o_ref[:, part] = total.astype(bf)
         gain_ref[:, part] = jnp.sum(total * (x_ref[:, part].astype(f32) * scale_ref[...]), axis=0, keepdims=True)
 
@@ -185,8 +189,12 @@
         out_shape=(jax.ShapeDtypeStruct((rows, depth), bf), jax.ShapeDtypeStruct((1, depth), f32)),
         in_specs=[SM] + [VM] * 5 + [HBM] * (3 * ns),
         out_specs=(VM, VM),
-        scratch_shapes=[pltpu.VMEM((3, depth, feats), bf), pltpu.SemaphoreType.DMA((3, 1, ns))],
-        compiler_params=params(28),
+        scratch_shapes=[
+            pltpu.VMEM((depth, 3 * feats), bf),
+            pltpu.VMEM((rows, 3 * feats), bf),
+            pltpu.SemaphoreType.DMA((3, ns)),
+        ],
+        compiler_params=params(32),
         cost_estimate=COST,
     )(offs, tokens, scale, *grads, *shards)
 
@@ -196,7 +204,8 @@
     outs, dn_hbm, rest = rest[:3], rest[3], rest[4:]
     n_ref, dh_ref, wg, wu, mids, dn_ref, w_sems, in_sems, out_sems = rest
     hidden, depth = dh_ref.shape[1], n_ref.shape[1]
-    blocks = [slice(f, min(f + width, hidden)) for f in range(0, hidden, width)]
+    edges = [0] + list(range(width // 2, hidden, width)) + [hidden]
+    blocks = [slice(a, b) for a, b in zip(edges[:-1], edges[1:])]
     span = lambda part: pl.ds(part.start, part.stop - part.start)
 
     def load(b):
@@ -247,7 +256,7 @@
     ns = len(g_shards)
     rows, depth = normed.shape
     hidden = g_shards[0].shape[1]
-    blocks = -(-hidden // width)
+    blocks = -(-hidden // width) + 1
     mid = jax.ShapeDtypeStruct((rows, hidden), bf)
     return pl.pallas_call(
         functools.partial(ffn_kernel, ns, width),
@@ -270,35 +279,49 @@
     )(offs, normed, grad_hidden, *g_shards, *w_up[1])
 
 
-def mix_kernel(spans, me_ref, offs, att_ref, x_ref, gain_ref, *rest):
+def mix_kernel(spans, me_ref, offs, gain_ref, att_hbm, x_hbm, *rest):
     ns = len(spans)
-    shards, (n_ref, own_ref, wo_hbm, w_ref, h_ref, sems) = rest[:ns], rest[ns:]
-    copies = []
-    for j, (ref, (z0, z1)) in enumerate(zip(shards, spans)):
-        rows = pl.ds(pl.multiple_of(offs[j], 16), ref.shape[1])
-        copies.append(pltpu.make_async_copy(ref, w_ref.at[z0:z1, rows, :], sems.at[j]))
-        copies[-1].start()
-    wait_all(copies)
-    keep = pltpu.make_async_copy(w_ref.at[me_ref[0]], wo_hbm, sems.at[ns])
-    keep.start()
-    depth = h_ref.shape[1]
-    width = 768
-    for f in range(0, depth, width):
-        part = slice(f, f + width)
-        total = None
-        for z in range(att_ref.shape[0]):
-            y = dot(att_ref[z], w_ref[z, part, :], ((1,), (1,)))
-            total = y if total is None else total + y
-        h_ref[:, part] = x_ref[:, part].astype(f32) + branch_scale * total
-    step = min(128, h_ref.shape[0])
-    for f in range(0, h_ref.shape[0], step):
+    shards, rest = rest[:ns], rest[ns:]
+    n_hbm, own_ref, wo_hbm, att_ref, x_ref, w_ref, h_ref, n_ref, w_sems, in_sems, out_sems = rest
+    heads, _, feats = att_hbm.shape
+    loads = []
+    for z in range(heads):
+        cols = pl.ds(z * feats, feats)
+        row = [pltpu.make_async_copy(att_hbm.at[z], att_ref.at[:, cols], in_sems.at[z])]
+        for j, (ref, (z0, z1)) in enumerate(zip(shards, spans)):
+            if z0 <= z < z1:
+                rows = pl.ds(pl.multiple_of(offs[j], 16), ref.shape[1])
+                row.append(pltpu.make_async_copy(ref.at[z - z0], w_ref.at[rows, cols], w_sems.at[z, j]))
+        if z == 0:
+            row.append(pltpu.make_async_copy(x_hbm, x_ref, in_sems.at[heads]))
+        for copy in row:
+            copy.start()
+        loads.append(row)
+    depth, width = h_ref.shape[1], 768
+    half = heads // 2
+    for z in range(0, heads, half):
+        for row in loads[z : z + half]:
+            wait_all(row)
+        cols = slice(z * feats, (z + half) * feats)
+        for f in range(0, depth, width):
+            part = slice(f, f + width)
+            y = branch_scale * dot(att_ref[:, cols], w_ref[part, cols], ((1,), (1,)))
+            h_ref[:, part] = (x_ref[:, part].astype(f32) if z == 0 else h_ref[:, part]) + y
+    mine = pl.ds(pl.multiple_of(me_ref[0] * feats, LANES), feats)
+    stores = [pltpu.make_async_copy(w_ref.at[:, mine], wo_hbm, out_sems.at[0])]
+    stores[0].start()
+    rows = h_ref.shape[0]
+    step = 128 if rows % 128 == 0 else rows
+    for k, f in enumerate(range(0, rows, step)):
         part = slice(f, f + step)
         h = h_ref[part, :]
         scale = lax.rsqrt(jnp.mean(h * h, axis=-1, keepdims=True) + norm_eps)
         n_ref[part, :] = (h * scale * gain_ref[...]).astype(bf)
+        stores.append(pltpu.make_async_copy(n_ref.at[pl.ds(f, step), :], n_hbm.at[pl.ds(f, step), :], out_sems.at[k + 1]))
+        stores[-1].start()
     piece = own_ref.shape[0]
     own_ref[...] = h_ref[pl.ds(pl.multiple_of(me_ref[0] * piece, 8), piece), :]
-    keep.wait()
+    wait_all(stores)
 
 
 def mix(att, tokens, gain, offs, pieces, me):
@@ -312,16 +335,21 @@
             jax.ShapeDtypeStruct((rows // n, depth), f32),
             jax.ShapeDtypeStruct((depth, feats), bf),
         ),
-        in_specs=[SM, SM, VM, VM, VM] + [HBM] * len(shards),
-        out_specs=(VM, VM, HBM),
+        in_specs=[SM, SM, VM] + [HBM] * (2 + len(shards)),
+        out_specs=(HBM, VM, HBM),
         scratch_shapes=[
-            pltpu.VMEM((n, depth, feats), bf),
+            pltpu.VMEM((rows, n * feats), bf),
+            pltpu.VMEM((rows, depth), bf),
+            pltpu.VMEM((depth, n * feats), bf),
             pltpu.VMEM((rows, depth), f32),
-            pltpu.SemaphoreType.DMA((len(shards) + 1,)),
+            pltpu.VMEM((rows, depth), bf),
+            pltpu.SemaphoreType.DMA((n, len(shards))),
+            pltpu.SemaphoreType.DMA((n + 1,)),
+            pltpu.SemaphoreType.DMA((1 + -(-rows // 128),)),
         ],
         compiler_params=params(56),
         cost_estimate=COST,
-    )(me[None], offs, att, tokens, gain[None, :], *shards)
+    )(me[None], offs, gain[None, :], att, tokens, *shards)
 
 
 def grad_kernel(offs, a_ref, b_ref, keep_ref, send_ref, at_ref):
@@ -877,7 +905,8 @@
         step(local_in)
     output = assemble(rounds, me)
     gain_sum = after(jnp.concatenate([part_g1, part_g2[None, :]]), local_in)
-    gain_sum = sum_all(gain_sum, (("tensor", n_tp), ("dp", n_dp), ("ctx", n_ctx)))
+    gain_sum = sum_all(gain_sum, (("tensor", n_tp), ("dp", n_dp)))
+    gain_sum = sum_all(after(gain_sum, output), (("ctx", n_ctx),))
     gain_sum = lax.dynamic_slice_in_dim(gain_sum, dp * shard, shard, 1)
 
     for g in grads_a:

time: 635 us -> 634 us (level)
  waiting for transfers between devices: 216 us -> 225 us
    ppermute x5, waiting for transfers between devices: 15.1 us -> 30.6 us  [sum_all(): value = value + lax.ppermute(value, axis, swap(n, bit))]
    ppermute x6, waiting for transfers between devices: 48.7 us -> 38.8 us  [along_y(): self.other = lax.ppermute(after(self.total, *late), 'ctx', swap(2, 1))]
  transfers between devices with their start and end apart: 74 -> 74, of which waited for: 32 -> 31; matrix products, arithmetic and copies ran while one was open for 12% -> 11% of each run, Pallas kernels for 31% -> 31%
where the time goes in v5:
time: 634 us; the launch traced here: 625 us
  waiting for transfers between devices  225 us (35%)
  Pallas kernels  217 us (34%)
  local copies, waits for them, and re-layouts  63.8 us (10%)
  other arithmetic  57.1 us (9%)
  starting transfers between devices  45 us (7%)
  between operations  15.9 us (3%)
    ppermute x7, waiting for transfers between devices, start_x(): self.raw = lax.ppermute(self.far, 'dp', swap(4, 2))  64.4 us
    unnamed x232, local copies, waits for them, and re-layouts  42.5 us
    pallas_call x7, Pallas kernels, weight_grad(): pl.pallas_call(grad_kernel, out_shape=(half, half), in_specs=[SM, VM, VM]...  40.2 us
    ppermute x6, waiting for transfers between devices, along_y(): self.other = lax.ppermute(after(self.total, *late), 'ctx', swap(2, 1))  38.8 us
    pallas_call x2, Pallas kernels, attention_bwd(): pl.pallas_call(functools.partial(attn_bwd_kernel, parts, heads), grid=(bl...  33.9 us
    ppermute x5, waiting for transfers between devices, sum_all(): value = value + lax.ppermute(value, axis, swap(n, bit))  30.6 us
    pallas_call x1, Pallas kernels, ffn(): pl.pallas_call(functools.partial(ffn_kernel, ns, width), out_shape=(mid,...  26.8 us
    pallas_call x14, Pallas kernels, add_halves(): pl.pallas_call(add_kernel, grid=(steps,), out_shape=jax.ShapeDtypeStruct(...  23.9 us
  transfers between devices with their start and end apart: 74, of which 31 were waited for; matrix products, arithmetic and copies ran while one was open for 11% of the time, Pallas kernels for 31%

profile of v5, /device:TPU:26, one launch (start us, length us, event | category | flops | bytes accessed | tf_op | source)
XLA Modules:
  0.0 624.5 jit_solution(1245747317116685146)
XLA Ops:
  13.8 3.6 fusion.9
  23.7 7.7 %collective-permute-done.1.rest_2_.rest_9_ = bf16[592,640]{1,0:T(8,128)(2,1)} collective-permute-done((bf16[592,640]{1,0:T(8,128)(2,1)}, bf16[592,640]{1,0:T(8,128)(2,1)}, u32[]{:S(2)}, u32[]{:S(2)}) %collective-permute-start.1) | collective-permute-done | bytes 757792 | tf_op jit(solution)/shard_map/ppermute | solution.py:638
  35.7 2.7 fusion.2.n_ref.a_ref
  38.4 5.9 shard_map.212.refs_7_.refs_12_
  45.9 4.8 collective-permute-done.3.rest_2_.rest_13_
  54.2 5.1 shard_map.213.refs_9_.refs_13_
  59.4 5.6 collective-permute-done.8.refs_8_.refs_12_
  66.9 3.0 collective-permute-done.5.rest_2_.rest_5_
  81.2 3.3 collective-permute-done.9.refs_10_.refs_13_
  85.0 2.7 collective-permute-done.10.rest_3_.rest_6_
  87.7 4.9 shard_map.214.refs_6_.refs_8_
  95.0 3.2 fusion.13
  101.1 17.4 %shard_map.215 = (bf16[640,640]{1,0:T(8,128)(2,1)S(1)}, f32[5,8,640]{2,1,0:T(8,128)S(1)}) custom-call(s32[1,640]{1,0:T(1,128)S(1)} %broadcast_in_dim.20.refs_0_, s32[1,640]{1,0:T(1,128)S(1)} %broadcast_in_dim.21.refs_1_, s32[640,1]{1,0:T(8,128)S(1)} %broadcast_in_dim.53.refs_2_.refs_4_, s32[640,1]{1,0:T(8,128)S(1)} %broadcast_in_dim.54.refs_3_.refs_4_, ...), custom_call_target="tpu_custom_call" | custom-call | flops 1024 | bytes 1024 | tf_op jit(solution)/shard_map/pallas_call | solution.py:492
  125.1 14.2 %collective-permute-done.14.rest_6_ = bf16[2,288,640]{2,1,0:T(8,128)(2,1)} collective-permute-done((bf16[2,288,640]{2,1,0:T(8,128)(2,1)S(1)}, bf16[2,288,640]{2,1,0:T(8,128)(2,1)}, u32[]{:S(2)}, u32[]{:S(2)}) %collective-permute-start.14) | collective-permute-done | bytes 737312 | tf_op jit(solution)/shard_map/ppermute | solution.py:655
  145.8 12.1 %shard_map.216.dh_hbm = f32[640,1536]{1,0:T(8,128)S(1)} custom-call(s32[6]{0:T(128)S(1)} %stack.71.offs, bf16[640,2304]{1,0:T(8,128)(2,1)S(1)} %copy-done.4, bf16[576,1536]{1,0:T(8,128)(2,1)} %pad.32.rest_0_, bf16[576,1536]{1,0:T(8,128)(2,1)} %collective-permute-done.18.rest_1_, bf16[288,1536]{1,0:T(8,128)(2,1)} %collective-permute-done.11.rest_2_, ...), custom_call_target="tpu_custom_call" | custom-call | flops 1024 | bytes 1024 | tf_op jit(solution)/shard_map/pallas_call | solution.py:130
  162.8 19.2 %collective-permute-done.22.rest_4_ = bf16[288,1536]{1,0:T(8,128)(2,1)S(1)} collective-permute-done((bf16[288,1536]{1,0:T(8,128)(2,1)}, bf16[288,1536]{1,0:T(8,128)(2,1)S(1)}, u32[]{:S(2)}, u32[]{:S(2)}) %collective-permute-start.22) | collective-permute-done | bytes 884768 | tf_op jit(solution)/shard_map/ppermute | solution.py:652
  186.8 2.8 collective-permute-done.27.rest_9_
  189.7 18.7 %shard_map.217 = (bf16[640,2304]{1,0:T(8,128)(2,1)}, f32[160,2304]{1,0:T(8,128)}, bf16[2304,640]{1,0:T(8,128)(2,1)}) custom-call(s32[1]{0:T(128)} %bitcast.me_ref, s32[10]{0:T(128)} %stack.64.offs, f32[1,2304]{1,0:T(1,128)} %get-tuple-element.223.gain_ref, bf16[4,640,640]{2,1,0:T(8,128)(2,1)} %bitcast.26, bf16[640,2304]{1,0:T(8,128)(2,1)} %x_ref.1, ...), custom_call_target="tpu_custom_call" | custom-call | flops 1024 | bytes 1024 | tf_op jit(solution)/shard_map/pallas_call | solution.py:331
  212.6 26.8 %shard_map.218 = (bf16[640,1536]{1,0:T(8,128)(2,1)}, bf16[640,1536]{1,0:T(8,128)(2,1)}, bf16[640,1536]{1,0:T(8,128)(2,1)}, bf16[640,2304]{1,0:T(8,128)(2,1)}) custom-call(s32[6]{0:T(128)} %copy-done.93, bf16[640,2304]{1,0:T(8,128)(2,1)} %get-tuple-element.118.n_hbm.a_ref, f32[640,1536]{1,0:T(8,128)} %copy-done.12, bf16[576,1536]{1,0:T(8,128)(2,1)} %pad.33.rest_0_, ...), custom_call_target="tpu_custom_call" | custom-call | flops 1024 | bytes 1024 | tf_op jit(solution)/shard_map/pallas_call | solution.py:261
  242.8 7.0 %shard_map.220 = (bf16[1152,1536]{1,0:T(8,128)(2,1)S(1)}, bf16[1152,1536]{1,0:T(8,128)(2,1)S(1)}) custom-call(s32[4]{0:T(128)S(1)} %pad_add_fusion.offs, bf16[640,2304]{1,0:T(8,128)(2,1)S(1)} %copy-done.5, bf16[640,1536]{1,0:T(8,128)(2,1)S(1)} %copy-done.30), custom_call_target="tpu_custom_call" | custom-call | flops 1024 | bytes 1024 | tf_op jit(solution)/shard_map/pallas_call | solution.py:368
  250.2 5.9 collective-permute-done.35.refs_1_
  262.4 8.6 %shard_map.219 = bf16[640,2304]{1,0:T(8,128)(2,1)S(1)} custom-call(s32[6]{0:T(128)S(1)} %copy-done.94, bf16[640,1536]{1,0:T(8,128)(2,1)S(1)} %copy-done.31, bf16[576,1536]{1,0:T(8,128)(2,1)} %pad.32.rest_0_, bf16[576,1536]{1,0:T(8,128)(2,1)} %collective-permute-done.18.rest_1_, bf16[288,1536]{1,0:T(8,128)(2,1)} %collective-permute-done.11.rest_2_, ...), custom_call_target="tpu_custom_call" | custom-call | flops 1024 | bytes 1024 | tf_op jit(solution)/shard_map/pallas_call | solution.py:130
  276.1 8.8 %shard_map.222 = (bf16[1152,1536]{1,0:T(8,128)(2,1)S(1)}, bf16[1152,1536]{1,0:T(8,128)(2,1)}) custom-call(s32[4]{0:T(128)S(1)} %pad_add_fusion.offs, bf16[640,2304]{1,0:T(8,128)(2,1)S(1)} %copy-done.2, bf16[640,1536]{1,0:T(8,128)(2,1)S(1)} %copy-done.85), custom_call_target="tpu_custom_call" | custom-call | flops 1024 | bytes 1024 | tf_op jit(solution)/shard_map/pallas_call | solution.py:368
  286.7 9.9 %reduce-scatter.4.cloned.1.call-done = bf16[160,2304]{1,0:T(8,128)(2,1)} async-done(((bf16[640,2304]{1,0:T(8,128)(2,1)}), bf16[160,2304]{1,0:T(8,128)(2,1)}) %reduce-scatter.4.cloned.1.call-update) | async-done | bytes 737296 | tf_op jit(solution)/shard_map/reduce_scatter | solution.py:627
  300.3 3.0 multiply_convert_fusion.1
  307.1 7.0 %shard_map.226 = (bf16[1152,1536]{1,0:T(8,128)(2,1)S(1)}, bf16[1152,1536]{1,0:T(8,128)(2,1)S(1)}) custom-call(s32[4]{0:T(128)S(1)} %pad_add_fusion.offs, bf16[640,2304]{1,0:T(8,128)(2,1)S(1)} %copy-done.3, bf16[640,1536]{1,0:T(8,128)(2,1)S(1)} %copy-done.84), custom_call_target="tpu_custom_call" | custom-call | flops 1024 | bytes 1024 | tf_op jit(solution)/shard_map/pallas_call | solution.py:368
  314.2 4.0 shard_map.224
  323.1 35.6 %collective-permute-done.39.refs_2_ = bf16[576,1536]{1,0:T(8,128)(2,1)S(1)} collective-permute-done((bf16[576,1536]{1,0:T(8,128)(2,1)S(1)}, bf16[576,1536]{1,0:T(8,128)(2,1)S(1)}, u32[]{:S(2)}, u32[]{:S(2)}) %collective-permute-start.39) | collective-permute-done | bytes 1769504 | tf_op jit(solution)/shard_map/ppermute | solution.py:692
  365.8 5.8 shard_map.228.refs_10_
  373.1 17.2 %shard_map.229 = (bf16[640,640]{1,0:T(8,128)(2,1)S(1)}, bf16[640,640]{1,0:T(8,128)(2,1)}, bf16[640,640]{1,0:T(8,128)(2,1)}) custom-call(s32[1,640]{1,0:T(1,128)S(1)} %broadcast_in_dim.20.refs_0_, s32[1,640]{1,0:T(1,128)S(1)} %broadcast_in_dim.21.refs_1_, f32[640,128]{1,0:T(8,128)S(1)} %pad_maximum_fusion.1.cos_ref.refs_2_.refs_6_, f32[640,128]{1,0:T(8,128)S(1)} %copy-done.9, ...), custom_call_target="tpu_custom_call" | custom-call | flops 1024 | bytes 1024 | tf_op jit(solution)/shard_map/pallas_call | solution.py:581
  390.3 4.1 shard_map.230
  397.6 7.6 %collective-permute-done.42.refs_2_ = bf16[576,1536]{1,0:T(8,128)(2,1)} collective-permute-done((bf16[576,1536]{1,0:T(8,128)(2,1)}, bf16[576,1536]{1,0:T(8,128)(2,1)}, u32[]{:S(2)}, u32[]{:S(2)}) %collective-permute-start.42) | collective-permute-done | bytes 1769504 | tf_op jit(solution)/shard_map/ppermute | solution.py:692
  406.4 16.6 %shard_map.231 = (bf16[640,640]{1,0:T(8,128)(2,1)S(1)}, bf16[640,640]{1,0:T(8,128)(2,1)S(1)}, bf16[640,640]{1,0:T(8,128)(2,1)S(1)}) custom-call(s32[1,640]{1,0:T(1,128)S(1)} %broadcast_in_dim.20.refs_0_, s32[1,640]{1,0:T(1,128)S(1)} %broadcast_in_dim.21.refs_1_, f32[640,128]{1,0:T(8,128)S(1)} %pad_maximum_fusion.1.cos_ref.refs_2_.refs_6_, ...), custom_call_target="tpu_custom_call" | custom-call | flops 1024 | bytes 1024 | tf_op jit(solution)/shard_map/pallas_call | solution.py:581
  435.5 9.7 %shard_map.232 = (bf16[640,2304]{1,0:T(8,128)(2,1)S(1)}, f32[1,2304]{1,0:T(1,128)S(1)}) custom-call(s32[4]{0:T(128)S(1)} %pad_add_fusion.offs, bf16[640,2304]{1,0:T(8,128)(2,1)S(1)} %copy-done.1, f32[640,1]{1,0:T(8,128)S(1)} %rsqrt.19.scale_ref, bf16[640,640]{1,0:T(8,128)(2,1)S(1)} %copy-done.34, bf16[640,640]{1,0:T(8,128)(2,1)S(1)} %add_convert_fusion.1.rest_1_.b_ref, ...), custom_call_target="tpu_custom_call" | custom-call | flops 1024 | bytes 1024 | tf_op jit(solution)/shard_map/pallas_call | solution.py:187
  448.1 4.1 shard_map.233
  453.8 4.1 shard_map.236
  460.1 2.6 shard_map.239
  464.5 28.8 %collective-permute-done.51 = bf16[576,1536]{1,0:T(8,128)(2,1)S(1)} collective-permute-done((bf16[576,1536]{1,0:T(8,128)(2,1)S(1)}, bf16[576,1536]{1,0:T(8,128)(2,1)S(1)}, u32[]{:S(2)}, u32[]{:S(2)}) %collective-permute-start.51) | collective-permute-done | bytes 1769504 | tf_op jit(solution)/shard_map/ppermute | solution.py:710
  497.8 5.2 shard_map.241
  507.0 7.5 %collective-permute-done.50.refs_2_ = bf16[576,640]{1,0:T(8,128)(2,1)S(1)} collective-permute-done((bf16[576,640]{1,0:T(8,128)(2,1)S(1)}, bf16[576,640]{1,0:T(8,128)(2,1)S(1)}, u32[]{:S(2)}, u32[]{:S(2)}) %collective-permute-start.50) | collective-permute-done | bytes 737312 | tf_op jit(solution)/shard_map/ppermute | solution.py:692
  519.8 2.7 fusion.5
  522.5 6.4 %collective-permute-done.64.refs_2_ = bf16[576,640]{1,0:T(8,128)(2,1)} collective-permute-done((bf16[576,640]{1,0:T(8,128)(2,1)}, bf16[576,640]{1,0:T(8,128)(2,1)}, u32[]{:S(2)}, u32[]{:S(2)}) %collective-permute-start.64) | collective-permute-done | bytes 737312 | tf_op jit(solution)/shard_map/ppermute | solution.py:692
  539.6 3.9 add_bitcast_fusion
  546.3 5.4 collective-permute-done.62.refs_2_
  556.6 10.1 %collective-permute-done.60 = bf16[576,640]{1,0:T(8,128)(2,1)S(1)} collective-permute-done((bf16[576,640]{1,0:T(8,128)(2,1)S(1)}, bf16[576,640]{1,0:T(8,128)(2,1)S(1)}, u32[]{:S(2)}, u32[]{:S(2)}) %collective-permute-start.60) | collective-permute-done | bytes 737312 | tf_op jit(solution)/shard_map/ppermute | solution.py:710
  569.3 28.5 %collective-permute-done.55 = f32[2,2304]{1,0:T(2,128)S(1)} collective-permute-done((f32[2,2304]{1,0:T(2,128)S(1)}, f32[2,2304]{1,0:T(2,128)S(1)}, u32[]{:S(2)}, u32[]{:S(2)}) %collective-permute-start.55) | collective-permute-done | bytes 18464 | tf_op jit(solution)/shard_map/ppermute | solution.py:615
  603.1 4.3 shard_map.240
  612.6 4.9 convert_element_type.202
  (463 shorter events, 175.7 us)
Async XLA Ops:
  7.2 87.9 %all-gather.13.cloned.1.call-start = ((), (), s32[]{:S(2)}) async-start(), calls=%async_computation.9 | async-start | bytes 3686400 | tf_op jit(solution)/shard_map/all_gather | solution.py:746
  11.7 20.3 %collective-permute-start = (bf16[592,640]{1,0:T(8,128)(2,1)}, bf16[592,640]{1,0:T(8,128)(2,1)}, u32[]{:S(2)}, u32[]{:S(2)}) collective-permute-start(bf16[592,640]{1,0:T(8,128)(2,1)} %pad_dynamic-update-slice_fusion.rest_0_.rest_7_), channel_id=1, source_target_pairs={{0,8},{8,0},{16,24},{24,16},{1,9},{9,1},{17,25},{25,17},{2,10},{10... | collective-permute-start | bytes 2273288 | tf_op jit(solution)/shard_map/ppermute | solution.py:640
  11.7 19.7 %collective-permute-start.1 = (bf16[592,640]{1,0:T(8,128)(2,1)}, bf16[592,640]{1,0:T(8,128)(2,1)}, u32[]{:S(2)}, u32[]{:S(2)}) collective-permute-start(bf16[592,640]{1,0:T(8,128)(2,1)} %pad_dynamic-update-slice_fusion.rest_0_.rest_7_), channel_id=1, source_target_pairs={{0,16},{8,24},{16,0},{24,8},{1,17},{9,25},{17,1},{25,9},{2,18},{10... | collective-permute-start | bytes 2273288 | tf_op jit(solution)/shard_map/ppermute | solution.py:638
  13.6 172.9 %all-gather.11.cloned.1.call-start = ((), (), s32[]{:S(2)}) async-start(), calls=%async_computation.8 | async-start | bytes 4096000 | tf_op jit(solution)/shard_map/all_gather | solution.py:834
  44.4 20.7 %collective-permute-start.8 = (bf16[640,640]{1,0:T(8,128)(2,1)}, bf16[640,640]{1,0:T(8,128)(2,1)}, u32[]{:S(2)}, u32[]{:S(2)}) collective-permute-start(bf16[640,640]{1,0:T(8,128)(2,1)} %shard_map.212.refs_7_.refs_12_), channel_id=1, source_target_pairs={{0,4},{4,0},{1,5},{5,1},{2,6},{6,2},{3,7},{7,3},{8,12},{12,8},{9,1... | collective-permute-start | bytes 2457608 | tf_op jit(solution)/shard_map/ppermute | solution.py:777
  65.0 19.5 %collective-permute-start.9 = (bf16[640,640]{1,0:T(8,128)(2,1)S(1)}, bf16[640,640]{1,0:T(8,128)(2,1)S(1)}, u32[]{:S(2)}, u32[]{:S(2)}) collective-permute-start(bf16[640,640]{1,0:T(8,128)(2,1)S(1)} %shard_map.213.refs_9_.refs_13_), channel_id=1, source_target_pairs={{0,4},{4,0},{1,5},{5,1},{2,6},{6,2},{3,7},{7,3},{8,12},{12,8},{9,1... | collective-permute-start | bytes 2457608 | tf_op jit(solution)/shard_map/ppermute | solution.py:777
  69.8 23.7 %collective-permute-start.11 = (bf16[288,1536]{1,0:T(8,128)(2,1)S(1)}, bf16[288,1536]{1,0:T(8,128)(2,1)}, u32[]{:S(2)}, u32[]{:S(2)}) collective-permute-start(bf16[288,1536]{1,0:T(8,128)(2,1)S(1)} %constant_dynamic-slice_fusion.2), channel_id=1, source_target_pairs={{0,16},{8,24},{16,0},{24,8},{1,17},{9,25},{17,1},{25,9},{2,18},{10... | collective-permute-start | bytes 2654216 | tf_op jit(solution)/shard_map/ppermute | solution.py:655
  84.5 56.8 %collective-permute-start.18 = (bf16[576,1536]{1,0:T(8,128)(2,1)}, bf16[576,1536]{1,0:T(8,128)(2,1)}, u32[]{:S(2)}, u32[]{:S(2)}) collective-permute-start(bf16[576,1536]{1,0:T(8,128)(2,1)} %pad.32.rest_0_), channel_id=1, source_target_pairs={{0,8},{8,0},{16,24},{24,16},{1,9},{9,1},{17,25},{25,17},{2,10},{10... | collective-permute-start | bytes 5308424 | tf_op jit(solution)/shard_map/ppermute | solution.py:796
  93.5 27.6 %collective-permute-start.12 = (bf16[288,1536]{1,0:T(8,128)(2,1)}, bf16[288,1536]{1,0:T(8,128)(2,1)}, u32[]{:S(2)}, u32[]{:S(2)}) collective-permute-start(bf16[288,1536]{1,0:T(8,128)(2,1)} %collective-permute-done.11.rest_2_), channel_id=1, source_target_pairs={{0,4},{4,0},{1,5},{5,1},{2,6},{6,2},{3,7},{7,3},{8,12},{12,8},{9,1... | collective-permute-start | bytes 2654216 | tf_op jit(solution)/shard_map/ppermute | solution.py:652
  99.2 22.0 %collective-permute-start.13 = (bf16[2,288,640]{2,1,0:T(8,128)(2,1)}, bf16[2,288,640]{2,1,0:T(8,128)(2,1)}, u32[]{:S(2)}, u32[]{:S(2)}) collective-permute-start(bf16[2,288,640]{2,1,0:T(8,128)(2,1)} %constant_dynamic-slice_fusion.1), channel_id=1, source_target_pairs={{0,16},{8,24},{16,0},{24,8},{1,17},{9,25},{17,1},{25,9},{2,18},{10... | collective-permute-start | bytes 2211848 | tf_op jit(solution)/shard_map/ppermute | solution.py:655
  119.5 177.1 %reduce-scatter.4.cloned.1.call-start = ((), (), s32[]{:S(2)}) async-start(), calls=%async_computation.3 | async-start | bytes 3686400 | tf_op jit(solution)/shard_map/reduce_scatter | solution.py:627
  124.6 19.4 %collective-permute-start.19 = (bf16[288,1536]{1,0:T(8,128)(2,1)}, bf16[288,1536]{1,0:T(8,128)(2,1)}, u32[]{:S(2)}, u32[]{:S(2)}) collective-permute-start(bf16[288,1536]{1,0:T(8,128)(2,1)} %collective-permute-done.11.rest_2_), channel_id=1, source_target_pairs={{0,8},{8,0},{16,24},{24,16},{1,9},{9,1},{17,25},{25,17},{2,10},{10... | collective-permute-start | bytes 2654216 | tf_op jit(solution)/shard_map/ppermute | solution.py:663
  139.9 20.5 %collective-permute-start.17 = (bf16[288,1536]{1,0:T(8,128)(2,1)}, bf16[288,1536]{1,0:T(8,128)(2,1)}, u32[]{:S(2)}, u32[]{:S(2)}) collective-permute-start(bf16[288,1536]{1,0:T(8,128)(2,1)} %constant_dynamic-slice_fusion), channel_id=1, source_target_pairs={{0,16},{8,24},{16,0},{24,8},{1,17},{9,25},{17,1},{25,9},{2,18},{10... | collective-permute-start | bytes 2654216 | tf_op jit(solution)/shard_map/ppermute | solution.py:655
  141.2 45.2 %collective-permute-start.23 = (bf16[4,576,640]{2,1,0:T(8,128)(2,1)}, bf16[4,576,640]{2,1,0:T(8,128)(2,1)}, u32[]{:S(2)}, u32[]{:S(2)}) collective-permute-start(bf16[4,576,640]{2,1,0:T(8,128)(2,1)} %bitcast.14.rest_0_), channel_id=1, source_target_pairs={{0,8},{8,0},{16,24},{24,16},{1,9},{9,1},{17,25},{25,17},{2,10},{10... | collective-permute-start | bytes 8847368 | tf_op jit(solution)/shard_map/ppermute | solution.py:796
  160.5 21.5 %collective-permute-start.22 = (bf16[288,1536]{1,0:T(8,128)(2,1)}, bf16[288,1536]{1,0:T(8,128)(2,1)S(1)}, u32[]{:S(2)}, u32[]{:S(2)}) collective-permute-start(bf16[288,1536]{1,0:T(8,128)(2,1)} %collective-permute-done.17.rest_2_), channel_id=1, source_target_pairs={{0,4},{4,0},{1,5},{5,1},{2,6},{6,2},{3,7},{7,3},{8,12},{12,8},{9,1... | collective-permute-start | bytes 2654216 | tf_op jit(solution)/shard_map/ppermute | solution.py:652
  161.5 21.7 %collective-permute-start.21 = (bf16[288,1536]{1,0:T(8,128)(2,1)S(1)}, bf16[288,1536]{1,0:T(8,128)(2,1)}, u32[]{:S(2)}, u32[]{:S(2)}) collective-permute-start(bf16[288,1536]{1,0:T(8,128)(2,1)S(1)} %constant_dynamic-slice_fusion.4), channel_id=1, source_target_pairs={{0,16},{8,24},{16,0},{24,8},{1,17},{9,25},{17,1},{25,9},{2,18},{10... | collective-permute-start | bytes 2654216 | tf_op jit(solution)/shard_map/ppermute | solution.py:655
  162.3 46.7 %collective-permute-start.28 = (bf16[576,1536]{1,0:T(8,128)(2,1)}, bf16[576,1536]{1,0:T(8,128)(2,1)}, u32[]{:S(2)}, u32[]{:S(2)}) collective-permute-start(bf16[576,1536]{1,0:T(8,128)(2,1)} %pad.33.rest_0_), channel_id=1, source_target_pairs={{0,8},{8,0},{16,24},{24,16},{1,9},{9,1},{17,25},{25,17},{2,10},{10... | collective-permute-start | bytes 5308424 | tf_op jit(solution)/shard_map/ppermute | solution.py:796
  162.3 20.9 %collective-permute-start.24 = (bf16[2,288,640]{2,1,0:T(8,128)(2,1)}, bf16[2,288,640]{2,1,0:T(8,128)(2,1)}, u32[]{:S(2)}, u32[]{:S(2)}) collective-permute-start(bf16[2,288,640]{2,1,0:T(8,128)(2,1)} %collective-permute-done.13.rest_2_), channel_id=1, source_target_pairs={{0,8},{8,0},{16,24},{24,16},{1,9},{9,1},{17,25},{25,17},{2,10},{10... | collective-permute-start | bytes 2211848 | tf_op jit(solution)/shard_map/ppermute | solution.py:663
  183.2 25.3 %collective-permute-start.33 = (bf16[288,1536]{1,0:T(8,128)(2,1)}, bf16[288,1536]{1,0:T(8,128)(2,1)}, u32[]{:S(2)}, u32[]{:S(2)}) collective-permute-start(bf16[288,1536]{1,0:T(8,128)(2,1)} %collective-permute-done.21.rest_8_), channel_id=1, source_target_pairs={{0,4},{4,0},{1,5},{5,1},{2,6},{6,2},{3,7},{7,3},{8,12},{12,8},{9,1... | collective-permute-start | bytes 2654216 | tf_op jit(solution)/shard_map/ppermute | solution.py:652
  184.5 24.5 %collective-permute-start.31 = (bf16[576,1536]{1,0:T(8,128)(2,1)}, bf16[576,1536]{1,0:T(8,128)(2,1)}, u32[]{:S(2)}, u32[]{:S(2)}) collective-permute-start(bf16[576,1536]{1,0:T(8,128)(2,1)} %pad.34.rest_6_), channel_id=1, source_target_pairs={{0,8},{8,0},{16,24},{24,16},{1,9},{9,1},{17,25},{25,17},{2,10},{10... | collective-permute-start | bytes 5308424 | tf_op jit(solution)/shard_map/ppermute | solution.py:796
  186.5 22.6 %collective-permute-start.29 = (bf16[288,1536]{1,0:T(8,128)(2,1)}, bf16[288,1536]{1,0:T(8,128)(2,1)}, u32[]{:S(2)}, u32[]{:S(2)}) collective-permute-start(bf16[288,1536]{1,0:T(8,128)(2,1)} %collective-permute-done.17.rest_2_), channel_id=1, source_target_pairs={{0,8},{8,0},{16,24},{24,16},{1,9},{9,1},{17,25},{25,17},{2,10},{10... | collective-permute-start | bytes 2654216 | tf_op jit(solution)/shard_map/ppermute | solution.py:663
  189.6 19.5 %collective-permute-start.30 = (bf16[288,1536]{1,0:T(8,128)(2,1)}, bf16[288,1536]{1,0:T(8,128)(2,1)}, u32[]{:S(2)}, u32[]{:S(2)}) collective-permute-start(bf16[288,1536]{1,0:T(8,128)(2,1)} %copy-done.112), channel_id=1, source_target_pairs={{0,8},{8,0},{16,24},{24,16},{1,9},{9,1},{17,25},{25,17},{2,10},{10... | collective-permute-start | bytes 2654216 | tf_op jit(solution)/shard_map/ppermute | solution.py:663
  239.4 125.6 %all-gather.7.cloned.1.call-start = ((), (), s32[]{:S(2)}) async-start(), calls=%async_computation.4 | async-start | bytes 3686400 | tf_op jit(solution)/shard_map/all_gather | solution.py:631
  258.5 41.2 %collective-permute-start.36 = (bf16[576,1536]{1,0:T(8,128)(2,1)}, bf16[576,1536]{1,0:T(8,128)(2,1)}, u32[]{:S(2)}, u32[]{:S(2)}) collective-permute-start(bf16[576,1536]{1,0:T(8,128)(2,1)} %shard_map.221), channel_id=1, source_target_pairs={{0,16},{8,24},{16,0},{24,8},{1,17},{9,25},{17,1},{25,9},{2,18},{10... | collective-permute-start | bytes 5308424 | tf_op jit(solution)/shard_map/ppermute | solution.py:692
  286.6 27.6 %collective-permute-start.38 = (bf16[1152,1536]{1,0:T(8,128)(2,1)}, bf16[1152,1536]{1,0:T(8,128)(2,1)}, u32[]{:S(2)}, u32[]{:S(2)}) collective-permute-start(bf16[1152,1536]{1,0:T(8,128)(2,1)} %get-tuple-element.114), channel_id=1, source_target_pairs={{0,8},{8,0},{16,24},{24,16},{1,9},{9,1},{17,25},{25,17},{2,10},{10... | collective-permute-start | bytes 10616840 | tf_op jit(solution)/shard_map/ppermute | solution.py:683
  303.3 122.7 %reduce-scatter.6.cloned.1.call-start = ((), (), s32[]{:S(2)}) async-start(), calls=%async_computation.5 | async-start | bytes 3686400 | tf_op jit(solution)/shard_map/reduce_scatter | solution.py:627
  314.1 47.3 %collective-permute-start.40 = (bf16[1152,1536]{1,0:T(8,128)(2,1)S(1)}, bf16[1152,1536]{1,0:T(8,128)(2,1)S(1)}, u32[]{:S(2)}, u32[]{:S(2)}) collective-permute-start(bf16[1152,1536]{1,0:T(8,128)(2,1)S(1)} %get-tuple-element.121), channel_id=1, source_target_pairs={{0,8},{8,0},{16,24},{24,16},{1,9},{9,1},{17,25},{25,17},{2,10},{10... | collective-permute-start | bytes 10616840 | tf_op jit(solution)/shard_map/ppermute | solution.py:683
  318.2 40.6 %collective-permute-start.39 = (bf16[576,1536]{1,0:T(8,128)(2,1)S(1)}, bf16[576,1536]{1,0:T(8,128)(2,1)S(1)}, u32[]{:S(2)}, u32[]{:S(2)}) collective-permute-start(bf16[576,1536]{1,0:T(8,128)(2,1)S(1)} %shard_map.224), channel_id=1, source_target_pairs={{0,16},{8,24},{16,0},{24,8},{1,17},{9,25},{17,1},{25,9},{2,18},{10... | collective-permute-start | bytes 5308424 | tf_op jit(solution)/shard_map/ppermute | solution.py:692
  321.6 43.4 %collective-permute-start.37 = (bf16[576,1536]{1,0:T(8,128)(2,1)S(1)}, bf16[576,1536]{1,0:T(8,128)(2,1)}, u32[]{:S(2)}, u32[]{:S(2)}) collective-permute-start(bf16[576,1536]{1,0:T(8,128)(2,1)S(1)} %shard_map.223), channel_id=1, source_target_pairs={{0,4},{4,0},{1,5},{5,1},{2,6},{6,2},{3,7},{7,3},{8,12},{12,8},{9,1... | collective-permute-start | bytes 5308424 | tf_op jit(solution)/shard_map/ppermute | solution.py:710
  365.0 151.1 %reduce-scatter.8.cloned.1.call-start = ((), (), s32[]{:S(2)}) async-start(), calls=%async_computation.6 | async-start | bytes 3686400 | tf_op jit(solution)/shard_map/reduce_scatter | solution.py:627
  365.1 40.1 %collective-permute-start.42 = (bf16[576,1536]{1,0:T(8,128)(2,1)}, bf16[576,1536]{1,0:T(8,128)(2,1)}, u32[]{:S(2)}, u32[]{:S(2)}) collective-permute-start(bf16[576,1536]{1,0:T(8,128)(2,1)} %copy-done.86), channel_id=1, source_target_pairs={{0,16},{8,24},{16,0},{24,8},{1,17},{9,25},{17,1},{25,9},{2,18},{10... | collective-permute-start | bytes 5308424 | tf_op jit(solution)/shard_map/ppermute | solution.py:692
  395.6 34.5 %collective-permute-start.46 = (bf16[640,640]{1,0:T(8,128)(2,1)}, bf16[640,640]{1,0:T(8,128)(2,1)}, u32[]{:S(2)}, u32[]{:S(2)}) collective-permute-start(bf16[640,640]{1,0:T(8,128)(2,1)} %get-tuple-element.135), channel_id=1, source_target_pairs={{0,4},{4,0},{1,5},{5,1},{2,6},{6,2},{3,7},{7,3},{8,12},{12,8},{9,1... | collective-permute-start | bytes 2457608 | tf_op jit(solution)/shard_map/ppermute | solution.py:777
  397.0 37.1 %collective-permute-start.45 = (bf16[640,640]{1,0:T(8,128)(2,1)}, bf16[640,640]{1,0:T(8,128)(2,1)}, u32[]{:S(2)}, u32[]{:S(2)}) collective-permute-start(bf16[640,640]{1,0:T(8,128)(2,1)} %get-tuple-element.133), channel_id=1, source_target_pairs={{0,4},{4,0},{1,5},{5,1},{2,6},{6,2},{3,7},{7,3},{8,12},{12,8},{9,1... | collective-permute-start | bytes 2457608 | tf_op jit(solution)/shard_map/ppermute | solution.py:777
  446.9 165.7 %all-gather.9.cloned.1.call-start = ((), (), s32[]{:S(2)}) async-start(), calls=%async_computation.7 | async-start | bytes 3686400 | tf_op jit(solution)/shard_map/all_gather | solution.py:631
  452.3 41.0 %collective-permute-start.51 = (bf16[576,1536]{1,0:T(8,128)(2,1)S(1)}, bf16[576,1536]{1,0:T(8,128)(2,1)S(1)}, u32[]{:S(2)}, u32[]{:S(2)}) collective-permute-start(bf16[576,1536]{1,0:T(8,128)(2,1)S(1)} %copy-done.43), channel_id=1, source_target_pairs={{0,4},{4,0},{1,5},{5,1},{2,6},{6,2},{3,7},{7,3},{8,12},{12,8},{9,1... | collective-permute-start | bytes 5308424 | tf_op jit(solution)/shard_map/ppermute | solution.py:710
  457.9 36.9 %collective-permute-start.49 = (bf16[1152,640]{1,0:T(8,128)(2,1)S(1)}, bf16[1152,640]{1,0:T(8,128)(2,1)S(1)}, u32[]{:S(2)}, u32[]{:S(2)}) collective-permute-start(bf16[1152,640]{1,0:T(8,128)(2,1)S(1)} %get-tuple-element.141), channel_id=1, source_target_pairs={{0,8},{8,0},{16,24},{24,16},{1,9},{9,1},{17,25},{25,17},{2,10},{10... | collective-permute-start | bytes 4423688 | tf_op jit(solution)/shard_map/ppermute | solution.py:683
  458.4 34.9 %collective-permute-start.48 = (bf16[576,640]{1,0:T(8,128)(2,1)S(1)}, bf16[576,640]{1,0:T(8,128)(2,1)S(1)}, u32[]{:S(2)}, u32[]{:S(2)}) collective-permute-start(bf16[576,640]{1,0:T(8,128)(2,1)S(1)} %shard_map.234), channel_id=1, source_target_pairs={{0,16},{8,24},{16,0},{24,8},{1,17},{9,25},{17,1},{25,9},{2,18},{10... | collective-permute-start | bytes 2211848 | tf_op jit(solution)/shard_map/ppermute | solution.py:692
  493.3 24.3 %collective-permute-start.52 = (bf16[288,1536]{1,0:T(8,128)(2,1)}, bf16[288,1536]{1,0:T(8,128)(2,1)}, u32[]{:S(2)}, u32[]{:S(2)}) collective-permute-start(bf16[288,1536]{1,0:T(8,128)(2,1)} %get-tuple-element.144), channel_id=1, source_target_pairs={{0,4},{4,0},{1,5},{5,1},{2,6},{6,2},{3,7},{7,3},{8,12},{12,8},{9,1... | collective-permute-start | bytes 2654216 | tf_op jit(solution)/shard_map/ppermute | solution.py:720
  495.0 19.5 %collective-permute-start.50 = (bf16[576,640]{1,0:T(8,128)(2,1)S(1)}, bf16[576,640]{1,0:T(8,128)(2,1)S(1)}, u32[]{:S(2)}, u32[]{:S(2)}) collective-permute-start(bf16[576,640]{1,0:T(8,128)(2,1)S(1)} %shard_map.237), channel_id=1, source_target_pairs={{0,16},{8,24},{16,0},{24,8},{1,17},{9,25},{17,1},{25,9},{2,18},{10... | collective-permute-start | bytes 2211848 | tf_op jit(solution)/shard_map/ppermute | solution.py:692
  496.3 22.0 %collective-permute-start.44 = (bf16[160,2304]{1,0:T(8,128)(2,1)}, bf16[160,2304]{1,0:T(8,128)(2,1)}, u32[]{:S(2)}, u32[]{:S(2)}) collective-permute-start(bf16[160,2304]{1,0:T(8,128)(2,1)} %collective-permute-done.43.refs_1_), channel_id=1, source_target_pairs={{0,1},{1,2},{2,3},{3,0},{4,5},{5,6},{6,7},{7,4},{8,9},{9,10},{10,1... | collective-permute-start | bytes 2211848 | tf_op jit(solution)/shard_map/ppermute | solution.py:886
  503.0 34.9 %collective-permute-start.66 = (bf16[288,1536]{1,0:T(8,128)(2,1)}, bf16[288,1536]{1,0:T(8,128)(2,1)}, u32[]{:S(2)}, u32[]{:S(2)}) collective-permute-start(bf16[288,1536]{1,0:T(8,128)(2,1)} %get-tuple-element.221), channel_id=1, source_target_pairs={{0,4},{4,0},{1,5},{5,1},{2,6},{6,2},{3,7},{7,3},{8,12},{12,8},{9,1... | collective-permute-start | bytes 2654216 | tf_op jit(solution)/shard_map/ppermute | solution.py:720
  505.4 23.4 %collective-permute-start.64 = (bf16[576,640]{1,0:T(8,128)(2,1)}, bf16[576,640]{1,0:T(8,128)(2,1)}, u32[]{:S(2)}, u32[]{:S(2)}) collective-permute-start(bf16[576,640]{1,0:T(8,128)(2,1)} %shard_map.244), channel_id=1, source_target_pairs={{0,16},{8,24},{16,0},{24,8},{1,17},{9,25},{17,1},{25,9},{2,18},{10... | collective-permute-start | bytes 2211848 | tf_op jit(solution)/shard_map/ppermute | solution.py:692
  531.2 76.2 %collective-permute-start.65 = (bf16[576,640]{1,0:T(8,128)(2,1)S(1)}, bf16[576,640]{1,0:T(8,128)(2,1)S(1)}, u32[]{:S(2)}, u32[]{:S(2)}) collective-permute-start(bf16[576,640]{1,0:T(8,128)(2,1)S(1)} %shard_map.245), channel_id=1, source_target_pairs={{0,4},{4,0},{1,5},{5,1},{2,6},{6,2},{3,7},{7,3},{8,12},{12,8},{9,1... | collective-permute-start | bytes 2211848 | tf_op jit(solution)/shard_map/ppermute | solution.py:710
  536.0 30.7 %collective-permute-start.60 = (bf16[576,640]{1,0:T(8,128)(2,1)S(1)}, bf16[576,640]{1,0:T(8,128)(2,1)S(1)}, u32[]{:S(2)}, u32[]{:S(2)}) collective-permute-start(bf16[576,640]{1,0:T(8,128)(2,1)S(1)} %copy-done.83), channel_id=1, source_target_pairs={{0,4},{4,0},{1,5},{5,1},{2,6},{6,2},{3,7},{7,3},{8,12},{12,8},{9,1... | collective-permute-start | bytes 2211848 | tf_op jit(solution)/shard_map/ppermute | solution.py:710
  536.8 62.3 %collective-permute-start.59 = (bf16[576,640]{1,0:T(8,128)(2,1)S(1)}, bf16[576,640]{1,0:T(8,128)(2,1)S(1)}, u32[]{:S(2)}, u32[]{:S(2)}) collective-permute-start(bf16[576,640]{1,0:T(8,128)(2,1)S(1)} %copy-done.81), channel_id=1, source_target_pairs={{0,4},{4,0},{1,5},{5,1},{2,6},{6,2},{3,7},{7,3},{8,12},{12,8},{9,1... | collective-permute-start | bytes 2211848 | tf_op jit(solution)/shard_map/ppermute | solution.py:710
  551.7 51.3 %collective-permute-start.53 = (bf16[160,2304]{1,0:T(8,128)(2,1)}, bf16[160,2304]{1,0:T(8,128)(2,1)S(1)}, u32[]{:S(2)}, u32[]{:S(2)}) collective-permute-start(bf16[160,2304]{1,0:T(8,128)(2,1)} %collective-permute-done.44.refs_2_), channel_id=1, source_target_pairs={{0,1},{1,2},{2,3},{3,0},{4,5},{5,6},{6,7},{7,4},{8,9},{9,10},{10,1... | collective-permute-start | bytes 2211848 | tf_op jit(solution)/shard_map/ppermute | solution.py:886
  555.9 51.5 %collective-permute-start.63 = (bf16[576,640]{1,0:T(8,128)(2,1)S(1)}, bf16[576,640]{1,0:T(8,128)(2,1)S(1)}, u32[]{:S(2)}, u32[]{:S(2)}) collective-permute-start(bf16[576,640]{1,0:T(8,128)(2,1)S(1)} %shard_map.243), channel_id=1, source_target_pairs={{0,4},{4,0},{1,5},{5,1},{2,6},{6,2},{3,7},{7,3},{8,12},{12,8},{9,1... | collective-permute-start | bytes 2211848 | tf_op jit(solution)/shard_map/ppermute | solution.py:710
  566.6 31.2 %collective-permute-start.55 = (f32[2,2304]{1,0:T(2,128)S(1)}, f32[2,2304]{1,0:T(2,128)S(1)}, u32[]{:S(2)}, u32[]{:S(2)}) collective-permute-start(f32[2,2304]{1,0:T(2,128)S(1)} %add.185), channel_id=1, source_target_pairs={{0,2},{1,3},{2,0},{3,1},{4,6},{5,7},{6,4},{7,5},{8,10},{9,11},{10,... | collective-permute-start | bytes 55304 | tf_op jit(solution)/shard_map/ppermute | solution.py:615
  (141 other events, 969.5 us)
Sparse Core Ops, SparseCore 0:
  13.7 58.8 all-gather.12
  119.6 63.2 all-gather.10
  239.5 56.9 reduce-scatter.3
  303.4 58.7 all-gather.6
  365.1 56.9 reduce-scatter.5
  447.0 60.8 reduce-scatter.7
  522.6 74.4 all-gather.8

commit v6 on v5

--- a/solution.py
+++ b/solution.py
@@ -400,6 +400,25 @@
     )(*pairs, *others)
 
 
+def widen_kernel(a_ref, o_ref):
+    o_ref[...] = a_ref[...].astype(f32)
+
+
+def widen(a):
+    rows, cols = a.shape
+    step = 128 if rows % 128 == 0 else rows
+    block = pl.BlockSpec((step, cols), lambda i: (i, 0))
+    return pl.pallas_call(
+        widen_kernel,
+        grid=(rows // step,),
+        out_shape=jax.ShapeDtypeStruct((rows, cols), f32),
+        in_specs=[block],
+        out_specs=block,
+        compiler_params=params(24),
+        cost_estimate=COST,
+    )(a)
+
+
 def assemble_kernel(me_ref, *refs):
     out, parts = refs[-1], refs[:-1]
     n, rows = len(parts), parts[0].shape[0]
@@ -900,7 +919,7 @@
     )
     local_in = lax.optimization_barrier(grad_in.astype(bf))
     grads_a[2].along_x(local_in)
-    grad_in = gather_rows(local_in).astype(f32)
+    grad_in = widen(gather_rows(local_in))
     while len(rounds) < n_tp:
         step(local_in)
     output = assemble(rounds, me)

time: 634 us -> 635 us (level)
    unnamed x232 -> x234, local copies, waits for them, and re-layouts: 42.5 us -> 44.3 us
where the time goes in v6:
time: 635 us; the launch traced here: 625 us
  waiting for transfers between devices  225 us (35%)
  Pallas kernels  221 us (35%)
  local copies, waits for them, and re-layouts  65.6 us (10%)
  other arithmetic  52.3 us (8%)
  starting transfers between devices  45 us (7%)
  between operations  15.9 us (3%)
    ppermute x7, waiting for transfers between devices, start_x(): self.raw = lax.ppermute(self.far, 'dp', swap(4, 2))  64.5 us
    unnamed x234, local copies, waits for them, and re-layouts  44.3 us
    pallas_call x7, Pallas kernels, weight_grad(): pl.pallas_call(grad_kernel, out_shape=(half, half), in_specs=[SM, VM, VM]...  40.2 us
    ppermute x6, waiting for transfers between devices, along_y(): self.other = lax.ppermute(after(self.total, *late), 'ctx', swap(2, 1))  38.8 us
    pallas_call x2, Pallas kernels, attention_bwd(): pl.pallas_call(functools.partial(attn_bwd_kernel, parts, heads), grid=(bl...  33.9 us
    ppermute x5, waiting for transfers between devices, sum_all(): value = value + lax.ppermute(value, axis, swap(n, bit))  30.6 us
    pallas_call x1, Pallas kernels, ffn(): pl.pallas_call(functools.partial(ffn_kernel, ns, width), out_shape=(mid,...  26.8 us
    pallas_call x14, Pallas kernels, add_halves(): pl.pallas_call(add_kernel, grid=(steps,), out_shape=jax.ShapeDtypeStruct(...  23.9 us
  transfers between devices with their start and end apart: 74, of which 31 were waited for; matrix products, arithmetic and copies ran while one was open for 11% of the time, Pallas kernels for 31%

profile of v6, /device:TPU:26, one launch (start us, length us, event | category | flops | bytes accessed | tf_op | source)
XLA Modules:
  0.0 624.8 jit_solution(13517810383272516126)
XLA Ops:
  13.8 3.6 fusion.9
  23.7 7.7 %collective-permute-done.1.rest_2_.rest_9_ = bf16[592,640]{1,0:T(8,128)(2,1)} collective-permute-done((bf16[592,640]{1,0:T(8,128)(2,1)}, bf16[592,640]{1,0:T(8,128)(2,1)}, u32[]{:S(2)}, u32[]{:S(2)}) %collective-permute-start.1) | collective-permute-done | bytes 757792 | tf_op jit(solution)/shard_map/ppermute | solution.py:657
  35.7 2.7 fusion.2.n_ref.a_ref
  38.4 5.9 shard_map.212.refs_7_.refs_12_
  46.0 4.8 collective-permute-done.3.rest_2_.rest_13_
  54.3 5.1 shard_map.213.refs_9_.refs_13_
  59.4 5.7 collective-permute-done.8.refs_8_.refs_12_
  66.9 3.0 collective-permute-done.5.rest_2_.rest_5_
  81.2 3.3 collective-permute-done.9.refs_10_.refs_13_
  85.0 2.7 collective-permute-done.10.rest_3_.rest_6_
  87.7 4.9 shard_map.214.refs_6_.refs_8_
  95.1 3.2 fusion.13
  101.2 17.4 %shard_map.215 = (bf16[640,640]{1,0:T(8,128)(2,1)S(1)}, f32[5,8,640]{2,1,0:T(8,128)S(1)}) custom-call(s32[1,640]{1,0:T(1,128)S(1)} %broadcast_in_dim.20.refs_0_, s32[1,640]{1,0:T(1,128)S(1)} %broadcast_in_dim.21.refs_1_, s32[640,1]{1,0:T(8,128)S(1)} %broadcast_in_dim.53.refs_2_.refs_4_, s32[640,1]{1,0:T(8,128)S(1)} %broadcast_in_dim.54.refs_3_.refs_4_, ...), custom_call_target="tpu_custom_call" | custom-call | flops 1024 | bytes 1024 | tf_op jit(solution)/shard_map/pallas_call | solution.py:511
  125.1 14.2 %collective-permute-done.14.rest_6_ = bf16[2,288,640]{2,1,0:T(8,128)(2,1)} collective-permute-done((bf16[2,288,640]{2,1,0:T(8,128)(2,1)S(1)}, bf16[2,288,640]{2,1,0:T(8,128)(2,1)}, u32[]{:S(2)}, u32[]{:S(2)}) %collective-permute-start.14) | collective-permute-done | bytes 737312 | tf_op jit(solution)/shard_map/ppermute | solution.py:674
  145.8 12.1 %shard_map.216.dh_hbm = f32[640,1536]{1,0:T(8,128)S(1)} custom-call(s32[6]{0:T(128)S(1)} %stack.71.offs, bf16[640,2304]{1,0:T(8,128)(2,1)S(1)} %copy-done.4, bf16[576,1536]{1,0:T(8,128)(2,1)} %pad.32.rest_0_, bf16[576,1536]{1,0:T(8,128)(2,1)} %collective-permute-done.18.rest_1_, bf16[288,1536]{1,0:T(8,128)(2,1)} %collective-permute-done.11.rest_2_, ...), custom_call_target="tpu_custom_call" | custom-call | flops 1024 | bytes 1024 | tf_op jit(solution)/shard_map/pallas_call | solution.py:130
  162.8 19.2 %collective-permute-done.22.rest_4_ = bf16[288,1536]{1,0:T(8,128)(2,1)S(1)} collective-permute-done((bf16[288,1536]{1,0:T(8,128)(2,1)}, bf16[288,1536]{1,0:T(8,128)(2,1)S(1)}, u32[]{:S(2)}, u32[]{:S(2)}) %collective-permute-start.22) | collective-permute-done | bytes 884768 | tf_op jit(solution)/shard_map/ppermute | solution.py:671
  186.9 2.8 collective-permute-done.27.rest_9_
  189.8 18.7 %shard_map.217 = (bf16[640,2304]{1,0:T(8,128)(2,1)}, f32[160,2304]{1,0:T(8,128)}, bf16[2304,640]{1,0:T(8,128)(2,1)}) custom-call(s32[1]{0:T(128)} %bitcast.me_ref, s32[10]{0:T(128)} %stack.64.offs, f32[1,2304]{1,0:T(1,128)} %get-tuple-element.223.gain_ref, bf16[4,640,640]{2,1,0:T(8,128)(2,1)} %bitcast.26, bf16[640,2304]{1,0:T(8,128)(2,1)} %x_ref.1, ...), custom_call_target="tpu_custom_call" | custom-call | flops 1024 | bytes 1024 | tf_op jit(solution)/shard_map/pallas_call | solution.py:331
  212.6 26.8 %shard_map.218 = (bf16[640,1536]{1,0:T(8,128)(2,1)}, bf16[640,1536]{1,0:T(8,128)(2,1)}, bf16[640,1536]{1,0:T(8,128)(2,1)}, bf16[640,2304]{1,0:T(8,128)(2,1)}) custom-call(s32[6]{0:T(128)} %copy-done.94, bf16[640,2304]{1,0:T(8,128)(2,1)} %get-tuple-element.118.n_hbm.a_ref, f32[640,1536]{1,0:T(8,128)} %copy-done.12, bf16[576,1536]{1,0:T(8,128)(2,1)} %pad.33.rest_0_, ...), custom_call_target="tpu_custom_call" | custom-call | flops 1024 | bytes 1024 | tf_op jit(solution)/shard_map/pallas_call | solution.py:261
  242.8 7.0 %shard_map.220 = (bf16[1152,1536]{1,0:T(8,128)(2,1)S(1)}, bf16[1152,1536]{1,0:T(8,128)(2,1)S(1)}) custom-call(s32[4]{0:T(128)S(1)} %pad_add_fusion.offs, bf16[640,2304]{1,0:T(8,128)(2,1)S(1)} %copy-done.5, bf16[640,1536]{1,0:T(8,128)(2,1)S(1)} %copy-done.30), custom_call_target="tpu_custom_call" | custom-call | flops 1024 | bytes 1024 | tf_op jit(solution)/shard_map/pallas_call | solution.py:368
  250.3 5.8 collective-permute-done.35.refs_1_
  262.4 8.6 %shard_map.219 = bf16[640,2304]{1,0:T(8,128)(2,1)S(1)} custom-call(s32[6]{0:T(128)S(1)} %copy-done.95, bf16[640,1536]{1,0:T(8,128)(2,1)S(1)} %copy-done.31, bf16[576,1536]{1,0:T(8,128)(2,1)} %pad.32.rest_0_, bf16[576,1536]{1,0:T(8,128)(2,1)} %collective-permute-done.18.rest_1_, bf16[288,1536]{1,0:T(8,128)(2,1)} %collective-permute-done.11.rest_2_, ...), custom_call_target="tpu_custom_call" | custom-call | flops 1024 | bytes 1024 | tf_op jit(solution)/shard_map/pallas_call | solution.py:130
  276.0 8.8 %shard_map.222 = (bf16[1152,1536]{1,0:T(8,128)(2,1)S(1)}, bf16[1152,1536]{1,0:T(8,128)(2,1)}) custom-call(s32[4]{0:T(128)S(1)} %pad_add_fusion.offs, bf16[640,2304]{1,0:T(8,128)(2,1)S(1)} %copy-done.2, bf16[640,1536]{1,0:T(8,128)(2,1)S(1)} %copy-done.86), custom_call_target="tpu_custom_call" | custom-call | flops 1024 | bytes 1024 | tf_op jit(solution)/shard_map/pallas_call | solution.py:368
  286.7 9.9 %reduce-scatter.4.cloned.1.call-done = bf16[160,2304]{1,0:T(8,128)(2,1)} async-done(((bf16[640,2304]{1,0:T(8,128)(2,1)}), bf16[160,2304]{1,0:T(8,128)(2,1)}) %reduce-scatter.4.cloned.1.call-update) | async-done | bytes 737296 | tf_op jit(solution)/shard_map/reduce_scatter | solution.py:646
  300.3 3.0 multiply_convert_fusion.1
  307.1 7.0 %shard_map.226 = (bf16[1152,1536]{1,0:T(8,128)(2,1)S(1)}, bf16[1152,1536]{1,0:T(8,128)(2,1)S(1)}) custom-call(s32[4]{0:T(128)S(1)} %pad_add_fusion.offs, bf16[640,2304]{1,0:T(8,128)(2,1)S(1)} %copy-done.3, bf16[640,1536]{1,0:T(8,128)(2,1)S(1)} %copy-done.85), custom_call_target="tpu_custom_call" | custom-call | flops 1024 | bytes 1024 | tf_op jit(solution)/shard_map/pallas_call | solution.py:368
  314.3 4.0 shard_map.224
  319.0 2.6 shard_map.223
  323.1 35.7 %collective-permute-done.39.refs_2_ = bf16[576,1536]{1,0:T(8,128)(2,1)S(1)} collective-permute-done((bf16[576,1536]{1,0:T(8,128)(2,1)S(1)}, bf16[576,1536]{1,0:T(8,128)(2,1)S(1)}, u32[]{:S(2)}, u32[]{:S(2)}) %collective-permute-start.39) | collective-permute-done | bytes 1769504 | tf_op jit(solution)/shard_map/ppermute | solution.py:711
  365.8 5.8 shard_map.228.refs_10_
  373.1 17.2 %shard_map.229 = (bf16[640,640]{1,0:T(8,128)(2,1)S(1)}, bf16[640,640]{1,0:T(8,128)(2,1)}, bf16[640,640]{1,0:T(8,128)(2,1)}) custom-call(s32[1,640]{1,0:T(1,128)S(1)} %broadcast_in_dim.20.refs_0_, s32[1,640]{1,0:T(1,128)S(1)} %broadcast_in_dim.21.refs_1_, f32[640,128]{1,0:T(8,128)S(1)} %pad_maximum_fusion.1.cos_ref.refs_2_.refs_6_, f32[640,128]{1,0:T(8,128)S(1)} %copy-done.9, ...), custom_call_target="tpu_custom_call" | custom-call | flops 1024 | bytes 1024 | tf_op jit(solution)/shard_map/pallas_call | solution.py:600
  390.3 4.1 shard_map.230
  397.6 7.6 %collective-permute-done.42.refs_2_ = bf16[576,1536]{1,0:T(8,128)(2,1)} collective-permute-done((bf16[576,1536]{1,0:T(8,128)(2,1)}, bf16[576,1536]{1,0:T(8,128)(2,1)}, u32[]{:S(2)}, u32[]{:S(2)}) %collective-permute-start.42) | collective-permute-done | bytes 1769504 | tf_op jit(solution)/shard_map/ppermute | solution.py:711
  406.4 16.6 %shard_map.231 = (bf16[640,640]{1,0:T(8,128)(2,1)S(1)}, bf16[640,640]{1,0:T(8,128)(2,1)S(1)}, bf16[640,640]{1,0:T(8,128)(2,1)S(1)}) custom-call(s32[1,640]{1,0:T(1,128)S(1)} %broadcast_in_dim.20.refs_0_, s32[1,640]{1,0:T(1,128)S(1)} %broadcast_in_dim.21.refs_1_, f32[640,128]{1,0:T(8,128)S(1)} %pad_maximum_fusion.1.cos_ref.refs_2_.refs_6_, ...), custom_call_target="tpu_custom_call" | custom-call | flops 1024 | bytes 1024 | tf_op jit(solution)/shard_map/pallas_call | solution.py:600
  435.5 9.7 %shard_map.232 = (bf16[640,2304]{1,0:T(8,128)(2,1)S(1)}, f32[1,2304]{1,0:T(1,128)S(1)}) custom-call(s32[4]{0:T(128)S(1)} %pad_add_fusion.offs, bf16[640,2304]{1,0:T(8,128)(2,1)S(1)} %copy-done.1, f32[640,1]{1,0:T(8,128)S(1)} %rsqrt.19.scale_ref, bf16[640,640]{1,0:T(8,128)(2,1)S(1)} %copy-done.34, bf16[640,640]{1,0:T(8,128)(2,1)S(1)} %add_convert_fusion.1.rest_1_.b_ref, ...), custom_call_target="tpu_custom_call" | custom-call | flops 1024 | bytes 1024 | tf_op jit(solution)/shard_map/pallas_call | solution.py:187
  448.1 4.1 shard_map.233
  453.8 4.1 shard_map.236
  464.5 28.8 %collective-permute-done.51 = bf16[576,1536]{1,0:T(8,128)(2,1)S(1)} collective-permute-done((bf16[576,1536]{1,0:T(8,128)(2,1)S(1)}, bf16[576,1536]{1,0:T(8,128)(2,1)S(1)}, u32[]{:S(2)}, u32[]{:S(2)}) %collective-permute-start.51) | collective-permute-done | bytes 1769504 | tf_op jit(solution)/shard_map/ppermute | solution.py:729
  497.8 5.2 shard_map.242
  507.0 7.5 %collective-permute-done.50.refs_2_ = bf16[576,640]{1,0:T(8,128)(2,1)S(1)} collective-permute-done((bf16[576,640]{1,0:T(8,128)(2,1)S(1)}, bf16[576,640]{1,0:T(8,128)(2,1)S(1)}, u32[]{:S(2)}, u32[]{:S(2)}) %collective-permute-start.50) | collective-permute-done | bytes 737312 | tf_op jit(solution)/shard_map/ppermute | solution.py:711
  519.8 2.7 fusion.5
  522.5 6.4 %collective-permute-done.64.refs_2_ = bf16[576,640]{1,0:T(8,128)(2,1)} collective-permute-done((bf16[576,640]{1,0:T(8,128)(2,1)}, bf16[576,640]{1,0:T(8,128)(2,1)}, u32[]{:S(2)}, u32[]{:S(2)}) %collective-permute-start.64) | collective-permute-done | bytes 737312 | tf_op jit(solution)/shard_map/ppermute | solution.py:711
  539.6 3.9 add_bitcast_fusion
  546.3 5.4 collective-permute-done.62.refs_2_
  556.6 10.1 %collective-permute-done.60 = bf16[576,640]{1,0:T(8,128)(2,1)S(1)} collective-permute-done((bf16[576,640]{1,0:T(8,128)(2,1)S(1)}, bf16[576,640]{1,0:T(8,128)(2,1)S(1)}, u32[]{:S(2)}, u32[]{:S(2)}) %collective-permute-start.60) | collective-permute-done | bytes 737312 | tf_op jit(solution)/shard_map/ppermute | solution.py:729
  569.3 28.6 %collective-permute-done.55 = f32[2,2304]{1,0:T(2,128)S(1)} collective-permute-done((f32[2,2304]{1,0:T(2,128)S(1)}, f32[2,2304]{1,0:T(2,128)S(1)}, u32[]{:S(2)}, u32[]{:S(2)}) %collective-permute-start.55) | collective-permute-done | bytes 18464 | tf_op jit(solution)/shard_map/ppermute | solution.py:634
  603.1 4.3 shard_map.240
  614.4 3.3 shard_map.241
  (465 shorter events, 177.6 us)
Async XLA Ops:
  7.2 87.9 %all-gather.13.cloned.1.call-start = ((), (), s32[]{:S(2)}) async-start(), calls=%async_computation.9 | async-start | bytes 3686400 | tf_op jit(solution)/shard_map/all_gather | solution.py:765
  11.8 20.3 %collective-permute-start = (bf16[592,640]{1,0:T(8,128)(2,1)}, bf16[592,640]{1,0:T(8,128)(2,1)}, u32[]{:S(2)}, u32[]{:S(2)}) collective-permute-start(bf16[592,640]{1,0:T(8,128)(2,1)} %pad_dynamic-update-slice_fusion.rest_0_.rest_7_), channel_id=1, source_target_pairs={{0,8},{8,0},{16,24},{24,16},{1,9},{9,1},{17,25},{25,17},{2,10},{10... | collective-permute-start | bytes 2273288 | tf_op jit(solution)/shard_map/ppermute | solution.py:659
  11.8 19.7 %collective-permute-start.1 = (bf16[592,640]{1,0:T(8,128)(2,1)}, bf16[592,640]{1,0:T(8,128)(2,1)}, u32[]{:S(2)}, u32[]{:S(2)}) collective-permute-start(bf16[592,640]{1,0:T(8,128)(2,1)} %pad_dynamic-update-slice_fusion.rest_0_.rest_7_), channel_id=1, source_target_pairs={{0,16},{8,24},{16,0},{24,8},{1,17},{9,25},{17,1},{25,9},{2,18},{10... | collective-permute-start | bytes 2273288 | tf_op jit(solution)/shard_map/ppermute | solution.py:657
  13.6 172.9 %all-gather.11.cloned.1.call-start = ((), (), s32[]{:S(2)}) async-start(), calls=%async_computation.8 | async-start | bytes 4096000 | tf_op jit(solution)/shard_map/all_gather | solution.py:853
  44.4 20.7 %collective-permute-start.8 = (bf16[640,640]{1,0:T(8,128)(2,1)}, bf16[640,640]{1,0:T(8,128)(2,1)}, u32[]{:S(2)}, u32[]{:S(2)}) collective-permute-start(bf16[640,640]{1,0:T(8,128)(2,1)} %shard_map.212.refs_7_.refs_12_), channel_id=1, source_target_pairs={{0,4},{4,0},{1,5},{5,1},{2,6},{6,2},{3,7},{7,3},{8,12},{12,8},{9,1... | collective-permute-start | bytes 2457608 | tf_op jit(solution)/shard_map/ppermute | solution.py:796
  65.0 19.5 %collective-permute-start.9 = (bf16[640,640]{1,0:T(8,128)(2,1)S(1)}, bf16[640,640]{1,0:T(8,128)(2,1)S(1)}, u32[]{:S(2)}, u32[]{:S(2)}) collective-permute-start(bf16[640,640]{1,0:T(8,128)(2,1)S(1)} %shard_map.213.refs_9_.refs_13_), channel_id=1, source_target_pairs={{0,4},{4,0},{1,5},{5,1},{2,6},{6,2},{3,7},{7,3},{8,12},{12,8},{9,1... | collective-permute-start | bytes 2457608 | tf_op jit(solution)/shard_map/ppermute | solution.py:796
  69.8 23.7 %collective-permute-start.11 = (bf16[288,1536]{1,0:T(8,128)(2,1)S(1)}, bf16[288,1536]{1,0:T(8,128)(2,1)}, u32[]{:S(2)}, u32[]{:S(2)}) collective-permute-start(bf16[288,1536]{1,0:T(8,128)(2,1)S(1)} %constant_dynamic-slice_fusion.2), channel_id=1, source_target_pairs={{0,16},{8,24},{16,0},{24,8},{1,17},{9,25},{17,1},{25,9},{2,18},{10... | collective-permute-start | bytes 2654216 | tf_op jit(solution)/shard_map/ppermute | solution.py:674
  84.5 56.8 %collective-permute-start.18 = (bf16[576,1536]{1,0:T(8,128)(2,1)}, bf16[576,1536]{1,0:T(8,128)(2,1)}, u32[]{:S(2)}, u32[]{:S(2)}) collective-permute-start(bf16[576,1536]{1,0:T(8,128)(2,1)} %pad.32.rest_0_), channel_id=1, source_target_pairs={{0,8},{8,0},{16,24},{24,16},{1,9},{9,1},{17,25},{25,17},{2,10},{10... | collective-permute-start | bytes 5308424 | tf_op jit(solution)/shard_map/ppermute | solution.py:815
  93.5 27.6 %collective-permute-start.12 = (bf16[288,1536]{1,0:T(8,128)(2,1)}, bf16[288,1536]{1,0:T(8,128)(2,1)}, u32[]{:S(2)}, u32[]{:S(2)}) collective-permute-start(bf16[288,1536]{1,0:T(8,128)(2,1)} %collective-permute-done.11.rest_2_), channel_id=1, source_target_pairs={{0,4},{4,0},{1,5},{5,1},{2,6},{6,2},{3,7},{7,3},{8,12},{12,8},{9,1... | collective-permute-start | bytes 2654216 | tf_op jit(solution)/shard_map/ppermute | solution.py:671
  99.2 22.0 %collective-permute-start.13 = (bf16[2,288,640]{2,1,0:T(8,128)(2,1)}, bf16[2,288,640]{2,1,0:T(8,128)(2,1)}, u32[]{:S(2)}, u32[]{:S(2)}) collective-permute-start(bf16[2,288,640]{2,1,0:T(8,128)(2,1)} %constant_dynamic-slice_fusion.1), channel_id=1, source_target_pairs={{0,16},{8,24},{16,0},{24,8},{1,17},{9,25},{17,1},{25,9},{2,18},{10... | collective-permute-start | bytes 2211848 | tf_op jit(solution)/shard_map/ppermute | solution.py:674
  119.5 177.0 %reduce-scatter.4.cloned.1.call-start = ((), (), s32[]{:S(2)}) async-start(), calls=%async_computation.3 | async-start | bytes 3686400 | tf_op jit(solution)/shard_map/reduce_scatter | solution.py:646
  124.6 19.4 %collective-permute-start.19 = (bf16[288,1536]{1,0:T(8,128)(2,1)}, bf16[288,1536]{1,0:T(8,128)(2,1)}, u32[]{:S(2)}, u32[]{:S(2)}) collective-permute-start(bf16[288,1536]{1,0:T(8,128)(2,1)} %collective-permute-done.11.rest_2_), channel_id=1, source_target_pairs={{0,8},{8,0},{16,24},{24,16},{1,9},{9,1},{17,25},{25,17},{2,10},{10... | collective-permute-start | bytes 2654216 | tf_op jit(solution)/shard_map/ppermute | solution.py:682
  139.9 20.6 %collective-permute-start.17 = (bf16[288,1536]{1,0:T(8,128)(2,1)}, bf16[288,1536]{1,0:T(8,128)(2,1)}, u32[]{:S(2)}, u32[]{:S(2)}) collective-permute-start(bf16[288,1536]{1,0:T(8,128)(2,1)} %constant_dynamic-slice_fusion), channel_id=1, source_target_pairs={{0,16},{8,24},{16,0},{24,8},{1,17},{9,25},{17,1},{25,9},{2,18},{10... | collective-permute-start | bytes 2654216 | tf_op jit(solution)/shard_map/ppermute | solution.py:674
  141.2 45.2 %collective-permute-start.23 = (bf16[4,576,640]{2,1,0:T(8,128)(2,1)}, bf16[4,576,640]{2,1,0:T(8,128)(2,1)}, u32[]{:S(2)}, u32[]{:S(2)}) collective-permute-start(bf16[4,576,640]{2,1,0:T(8,128)(2,1)} %bitcast.14.rest_0_), channel_id=1, source_target_pairs={{0,8},{8,0},{16,24},{24,16},{1,9},{9,1},{17,25},{25,17},{2,10},{10... | collective-permute-start | bytes 8847368 | tf_op jit(solution)/shard_map/ppermute | solution.py:815
  160.5 21.5 %collective-permute-start.22 = (bf16[288,1536]{1,0:T(8,128)(2,1)}, bf16[288,1536]{1,0:T(8,128)(2,1)S(1)}, u32[]{:S(2)}, u32[]{:S(2)}) collective-permute-start(bf16[288,1536]{1,0:T(8,128)(2,1)} %collective-permute-done.17.rest_2_), channel_id=1, source_target_pairs={{0,4},{4,0},{1,5},{5,1},{2,6},{6,2},{3,7},{7,3},{8,12},{12,8},{9,1... | collective-permute-start | bytes 2654216 | tf_op jit(solution)/shard_map/ppermute | solution.py:671
  161.5 21.7 %collective-permute-start.21 = (bf16[288,1536]{1,0:T(8,128)(2,1)S(1)}, bf16[288,1536]{1,0:T(8,128)(2,1)}, u32[]{:S(2)}, u32[]{:S(2)}) collective-permute-start(bf16[288,1536]{1,0:T(8,128)(2,1)S(1)} %constant_dynamic-slice_fusion.4), channel_id=1, source_target_pairs={{0,16},{8,24},{16,0},{24,8},{1,17},{9,25},{17,1},{25,9},{2,18},{10... | collective-permute-start | bytes 2654216 | tf_op jit(solution)/shard_map/ppermute | solution.py:674
  162.3 46.7 %collective-permute-start.28 = (bf16[576,1536]{1,0:T(8,128)(2,1)}, bf16[576,1536]{1,0:T(8,128)(2,1)}, u32[]{:S(2)}, u32[]{:S(2)}) collective-permute-start(bf16[576,1536]{1,0:T(8,128)(2,1)} %pad.33.rest_0_), channel_id=1, source_target_pairs={{0,8},{8,0},{16,24},{24,16},{1,9},{9,1},{17,25},{25,17},{2,10},{10... | collective-permute-start | bytes 5308424 | tf_op jit(solution)/shard_map/ppermute | solution.py:815
  162.3 20.9 %collective-permute-start.24 = (bf16[2,288,640]{2,1,0:T(8,128)(2,1)}, bf16[2,288,640]{2,1,0:T(8,128)(2,1)}, u32[]{:S(2)}, u32[]{:S(2)}) collective-permute-start(bf16[2,288,640]{2,1,0:T(8,128)(2,1)} %collective-permute-done.13.rest_2_), channel_id=1, source_target_pairs={{0,8},{8,0},{16,24},{24,16},{1,9},{9,1},{17,25},{25,17},{2,10},{10... | collective-permute-start | bytes 2211848 | tf_op jit(solution)/shard_map/ppermute | solution.py:682
  183.2 25.3 %collective-permute-start.33 = (bf16[288,1536]{1,0:T(8,128)(2,1)}, bf16[288,1536]{1,0:T(8,128)(2,1)}, u32[]{:S(2)}, u32[]{:S(2)}) collective-permute-start(bf16[288,1536]{1,0:T(8,128)(2,1)} %collective-permute-done.21.rest_8_), channel_id=1, source_target_pairs={{0,4},{4,0},{1,5},{5,1},{2,6},{6,2},{3,7},{7,3},{8,12},{12,8},{9,1... | collective-permute-start | bytes 2654216 | tf_op jit(solution)/shard_map/ppermute | solution.py:671
  184.5 24.5 %collective-permute-start.31 = (bf16[576,1536]{1,0:T(8,128)(2,1)}, bf16[576,1536]{1,0:T(8,128)(2,1)}, u32[]{:S(2)}, u32[]{:S(2)}) collective-permute-start(bf16[576,1536]{1,0:T(8,128)(2,1)} %pad.34.rest_6_), channel_id=1, source_target_pairs={{0,8},{8,0},{16,24},{24,16},{1,9},{9,1},{17,25},{25,17},{2,10},{10... | collective-permute-start | bytes 5308424 | tf_op jit(solution)/shard_map/ppermute | solution.py:815
  186.5 22.6 %collective-permute-start.29 = (bf16[288,1536]{1,0:T(8,128)(2,1)}, bf16[288,1536]{1,0:T(8,128)(2,1)}, u32[]{:S(2)}, u32[]{:S(2)}) collective-permute-start(bf16[288,1536]{1,0:T(8,128)(2,1)} %collective-permute-done.17.rest_2_), channel_id=1, source_target_pairs={{0,8},{8,0},{16,24},{24,16},{1,9},{9,1},{17,25},{25,17},{2,10},{10... | collective-permute-start | bytes 2654216 | tf_op jit(solution)/shard_map/ppermute | solution.py:682
  189.6 19.5 %collective-permute-start.30 = (bf16[288,1536]{1,0:T(8,128)(2,1)}, bf16[288,1536]{1,0:T(8,128)(2,1)}, u32[]{:S(2)}, u32[]{:S(2)}) collective-permute-start(bf16[288,1536]{1,0:T(8,128)(2,1)} %copy-done.113), channel_id=1, source_target_pairs={{0,8},{8,0},{16,24},{24,16},{1,9},{9,1},{17,25},{25,17},{2,10},{10... | collective-permute-start | bytes 2654216 | tf_op jit(solution)/shard_map/ppermute | solution.py:682
  239.4 125.6 %all-gather.7.cloned.1.call-start = ((), (), s32[]{:S(2)}) async-start(), calls=%async_computation.4 | async-start | bytes 3686400 | tf_op jit(solution)/shard_map/all_gather | solution.py:650
  258.5 41.2 %collective-permute-start.36 = (bf16[576,1536]{1,0:T(8,128)(2,1)}, bf16[576,1536]{1,0:T(8,128)(2,1)}, u32[]{:S(2)}, u32[]{:S(2)}) collective-permute-start(bf16[576,1536]{1,0:T(8,128)(2,1)} %shard_map.221), channel_id=1, source_target_pairs={{0,16},{8,24},{16,0},{24,8},{1,17},{9,25},{17,1},{25,9},{2,18},{10... | collective-permute-start | bytes 5308424 | tf_op jit(solution)/shard_map/ppermute | solution.py:711
  286.6 27.6 %collective-permute-start.38 = (bf16[1152,1536]{1,0:T(8,128)(2,1)}, bf16[1152,1536]{1,0:T(8,128)(2,1)}, u32[]{:S(2)}, u32[]{:S(2)}) collective-permute-start(bf16[1152,1536]{1,0:T(8,128)(2,1)} %get-tuple-element.114), channel_id=1, source_target_pairs={{0,8},{8,0},{16,24},{24,16},{1,9},{9,1},{17,25},{25,17},{2,10},{10... | collective-permute-start | bytes 10616840 | tf_op jit(solution)/shard_map/ppermute | solution.py:702
  303.3 122.7 %reduce-scatter.6.cloned.1.call-start = ((), (), s32[]{:S(2)}) async-start(), calls=%async_computation.5 | async-start | bytes 3686400 | tf_op jit(solution)/shard_map/reduce_scatter | solution.py:646
  314.1 47.3 %collective-permute-start.40 = (bf16[1152,1536]{1,0:T(8,128)(2,1)S(1)}, bf16[1152,1536]{1,0:T(8,128)(2,1)S(1)}, u32[]{:S(2)}, u32[]{:S(2)}) collective-permute-start(bf16[1152,1536]{1,0:T(8,128)(2,1)S(1)} %get-tuple-element.121), channel_id=1, source_target_pairs={{0,8},{8,0},{16,24},{24,16},{1,9},{9,1},{17,25},{25,17},{2,10},{10... | collective-permute-start | bytes 10616840 | tf_op jit(solution)/shard_map/ppermute | solution.py:702
  318.3 40.6 %collective-permute-start.39 = (bf16[576,1536]{1,0:T(8,128)(2,1)S(1)}, bf16[576,1536]{1,0:T(8,128)(2,1)S(1)}, u32[]{:S(2)}, u32[]{:S(2)}) collective-permute-start(bf16[576,1536]{1,0:T(8,128)(2,1)S(1)} %shard_map.224), channel_id=1, source_target_pairs={{0,16},{8,24},{16,0},{24,8},{1,17},{9,25},{17,1},{25,9},{2,18},{10... | collective-permute-start | bytes 5308424 | tf_op jit(solution)/shard_map/ppermute | solution.py:711
  321.6 43.4 %collective-permute-start.37 = (bf16[576,1536]{1,0:T(8,128)(2,1)S(1)}, bf16[576,1536]{1,0:T(8,128)(2,1)}, u32[]{:S(2)}, u32[]{:S(2)}) collective-permute-start(bf16[576,1536]{1,0:T(8,128)(2,1)S(1)} %shard_map.223), channel_id=1, source_target_pairs={{0,4},{4,0},{1,5},{5,1},{2,6},{6,2},{3,7},{7,3},{8,12},{12,8},{9,1... | collective-permute-start | bytes 5308424 | tf_op jit(solution)/shard_map/ppermute | solution.py:729
  365.0 151.1 %reduce-scatter.8.cloned.1.call-start = ((), (), s32[]{:S(2)}) async-start(), calls=%async_computation.6 | async-start | bytes 3686400 | tf_op jit(solution)/shard_map/reduce_scatter | solution.py:646
  365.1 40.1 %collective-permute-start.42 = (bf16[576,1536]{1,0:T(8,128)(2,1)}, bf16[576,1536]{1,0:T(8,128)(2,1)}, u32[]{:S(2)}, u32[]{:S(2)}) collective-permute-start(bf16[576,1536]{1,0:T(8,128)(2,1)} %copy-done.87), channel_id=1, source_target_pairs={{0,16},{8,24},{16,0},{24,8},{1,17},{9,25},{17,1},{25,9},{2,18},{10... | collective-permute-start | bytes 5308424 | tf_op jit(solution)/shard_map/ppermute | solution.py:711
  395.6 34.5 %collective-permute-start.46 = (bf16[640,640]{1,0:T(8,128)(2,1)}, bf16[640,640]{1,0:T(8,128)(2,1)}, u32[]{:S(2)}, u32[]{:S(2)}) collective-permute-start(bf16[640,640]{1,0:T(8,128)(2,1)} %get-tuple-element.135), channel_id=1, source_target_pairs={{0,4},{4,0},{1,5},{5,1},{2,6},{6,2},{3,7},{7,3},{8,12},{12,8},{9,1... | collective-permute-start | bytes 2457608 | tf_op jit(solution)/shard_map/ppermute | solution.py:796
  397.0 37.1 %collective-permute-start.45 = (bf16[640,640]{1,0:T(8,128)(2,1)}, bf16[640,640]{1,0:T(8,128)(2,1)}, u32[]{:S(2)}, u32[]{:S(2)}) collective-permute-start(bf16[640,640]{1,0:T(8,128)(2,1)} %get-tuple-element.133), channel_id=1, source_target_pairs={{0,4},{4,0},{1,5},{5,1},{2,6},{6,2},{3,7},{7,3},{8,12},{12,8},{9,1... | collective-permute-start | bytes 2457608 | tf_op jit(solution)/shard_map/ppermute | solution.py:796
  446.9 165.7 %all-gather.9.cloned.1.call-start = ((), (), s32[]{:S(2)}) async-start(), calls=%async_computation.7 | async-start | bytes 3686400 | tf_op jit(solution)/shard_map/all_gather | solution.py:650
  452.3 41.0 %collective-permute-start.51 = (bf16[576,1536]{1,0:T(8,128)(2,1)S(1)}, bf16[576,1536]{1,0:T(8,128)(2,1)S(1)}, u32[]{:S(2)}, u32[]{:S(2)}) collective-permute-start(bf16[576,1536]{1,0:T(8,128)(2,1)S(1)} %copy-done.43), channel_id=1, source_target_pairs={{0,4},{4,0},{1,5},{5,1},{2,6},{6,2},{3,7},{7,3},{8,12},{12,8},{9,1... | collective-permute-start | bytes 5308424 | tf_op jit(solution)/shard_map/ppermute | solution.py:729
  457.9 36.9 %collective-permute-start.49 = (bf16[1152,640]{1,0:T(8,128)(2,1)S(1)}, bf16[1152,640]{1,0:T(8,128)(2,1)S(1)}, u32[]{:S(2)}, u32[]{:S(2)}) collective-permute-start(bf16[1152,640]{1,0:T(8,128)(2,1)S(1)} %get-tuple-element.141), channel_id=1, source_target_pairs={{0,8},{8,0},{16,24},{24,16},{1,9},{9,1},{17,25},{25,17},{2,10},{10... | collective-permute-start | bytes 4423688 | tf_op jit(solution)/shard_map/ppermute | solution.py:702
  458.4 34.9 %collective-permute-start.48 = (bf16[576,640]{1,0:T(8,128)(2,1)S(1)}, bf16[576,640]{1,0:T(8,128)(2,1)S(1)}, u32[]{:S(2)}, u32[]{:S(2)}) collective-permute-start(bf16[576,640]{1,0:T(8,128)(2,1)S(1)} %shard_map.234), channel_id=1, source_target_pairs={{0,16},{8,24},{16,0},{24,8},{1,17},{9,25},{17,1},{25,9},{2,18},{10... | collective-permute-start | bytes 2211848 | tf_op jit(solution)/shard_map/ppermute | solution.py:711
  493.3 24.3 %collective-permute-start.52 = (bf16[288,1536]{1,0:T(8,128)(2,1)}, bf16[288,1536]{1,0:T(8,128)(2,1)}, u32[]{:S(2)}, u32[]{:S(2)}) collective-permute-start(bf16[288,1536]{1,0:T(8,128)(2,1)} %get-tuple-element.144), channel_id=1, source_target_pairs={{0,4},{4,0},{1,5},{5,1},{2,6},{6,2},{3,7},{7,3},{8,12},{12,8},{9,1... | collective-permute-start | bytes 2654216 | tf_op jit(solution)/shard_map/ppermute | solution.py:739
  495.0 19.5 %collective-permute-start.50 = (bf16[576,640]{1,0:T(8,128)(2,1)S(1)}, bf16[576,640]{1,0:T(8,128)(2,1)S(1)}, u32[]{:S(2)}, u32[]{:S(2)}) collective-permute-start(bf16[576,640]{1,0:T(8,128)(2,1)S(1)} %shard_map.237), channel_id=1, source_target_pairs={{0,16},{8,24},{16,0},{24,8},{1,17},{9,25},{17,1},{25,9},{2,18},{10... | collective-permute-start | bytes 2211848 | tf_op jit(solution)/shard_map/ppermute | solution.py:711
  496.3 22.0 %collective-permute-start.44 = (bf16[160,2304]{1,0:T(8,128)(2,1)}, bf16[160,2304]{1,0:T(8,128)(2,1)}, u32[]{:S(2)}, u32[]{:S(2)}) collective-permute-start(bf16[160,2304]{1,0:T(8,128)(2,1)} %collective-permute-done.43.refs_1_), channel_id=1, source_target_pairs={{0,1},{1,2},{2,3},{3,0},{4,5},{5,6},{6,7},{7,4},{8,9},{9,10},{10,1... | collective-permute-start | bytes 2211848 | tf_op jit(solution)/shard_map/ppermute | solution.py:905
  503.0 35.0 %collective-permute-start.66 = (bf16[288,1536]{1,0:T(8,128)(2,1)}, bf16[288,1536]{1,0:T(8,128)(2,1)}, u32[]{:S(2)}, u32[]{:S(2)}) collective-permute-start(bf16[288,1536]{1,0:T(8,128)(2,1)} %get-tuple-element.221), channel_id=1, source_target_pairs={{0,4},{4,0},{1,5},{5,1},{2,6},{6,2},{3,7},{7,3},{8,12},{12,8},{9,1... | collective-permute-start | bytes 2654216 | tf_op jit(solution)/shard_map/ppermute | solution.py:739
  505.4 23.5 %collective-permute-start.64 = (bf16[576,640]{1,0:T(8,128)(2,1)}, bf16[576,640]{1,0:T(8,128)(2,1)}, u32[]{:S(2)}, u32[]{:S(2)}) collective-permute-start(bf16[576,640]{1,0:T(8,128)(2,1)} %shard_map.245), channel_id=1, source_target_pairs={{0,16},{8,24},{16,0},{24,8},{1,17},{9,25},{17,1},{25,9},{2,18},{10... | collective-permute-start | bytes 2211848 | tf_op jit(solution)/shard_map/ppermute | solution.py:711
  531.2 76.2 %collective-permute-start.65 = (bf16[576,640]{1,0:T(8,128)(2,1)S(1)}, bf16[576,640]{1,0:T(8,128)(2,1)S(1)}, u32[]{:S(2)}, u32[]{:S(2)}) collective-permute-start(bf16[576,640]{1,0:T(8,128)(2,1)S(1)} %shard_map.246), channel_id=1, source_target_pairs={{0,4},{4,0},{1,5},{5,1},{2,6},{6,2},{3,7},{7,3},{8,12},{12,8},{9,1... | collective-permute-start | bytes 2211848 | tf_op jit(solution)/shard_map/ppermute | solution.py:729
  536.0 30.7 %collective-permute-start.60 = (bf16[576,640]{1,0:T(8,128)(2,1)S(1)}, bf16[576,640]{1,0:T(8,128)(2,1)S(1)}, u32[]{:S(2)}, u32[]{:S(2)}) collective-permute-start(bf16[576,640]{1,0:T(8,128)(2,1)S(1)} %copy-done.84), channel_id=1, source_target_pairs={{0,4},{4,0},{1,5},{5,1},{2,6},{6,2},{3,7},{7,3},{8,12},{12,8},{9,1... | collective-permute-start | bytes 2211848 | tf_op jit(solution)/shard_map/ppermute | solution.py:729
  536.8 62.3 %collective-permute-start.59 = (bf16[576,640]{1,0:T(8,128)(2,1)S(1)}, bf16[576,640]{1,0:T(8,128)(2,1)S(1)}, u32[]{:S(2)}, u32[]{:S(2)}) collective-permute-start(bf16[576,640]{1,0:T(8,128)(2,1)S(1)} %copy-done.82), channel_id=1, source_target_pairs={{0,4},{4,0},{1,5},{5,1},{2,6},{6,2},{3,7},{7,3},{8,12},{12,8},{9,1... | collective-permute-start | bytes 2211848 | tf_op jit(solution)/shard_map/ppermute | solution.py:729
  551.7 51.3 %collective-permute-start.53 = (bf16[160,2304]{1,0:T(8,128)(2,1)}, bf16[160,2304]{1,0:T(8,128)(2,1)S(1)}, u32[]{:S(2)}, u32[]{:S(2)}) collective-permute-start(bf16[160,2304]{1,0:T(8,128)(2,1)} %collective-permute-done.44.refs_2_), channel_id=1, source_target_pairs={{0,1},{1,2},{2,3},{3,0},{4,5},{5,6},{6,7},{7,4},{8,9},{9,10},{10,1... | collective-permute-start | bytes 2211848 | tf_op jit(solution)/shard_map/ppermute | solution.py:905
  555.9 51.5 %collective-permute-start.63 = (bf16[576,640]{1,0:T(8,128)(2,1)S(1)}, bf16[576,640]{1,0:T(8,128)(2,1)S(1)}, u32[]{:S(2)}, u32[]{:S(2)}) collective-permute-start(bf16[576,640]{1,0:T(8,128)(2,1)S(1)} %shard_map.244), channel_id=1, source_target_pairs={{0,4},{4,0},{1,5},{5,1},{2,6},{6,2},{3,7},{7,3},{8,12},{12,8},{9,1... | collective-permute-start | bytes 2211848 | tf_op jit(solution)/shard_map/ppermute | solution.py:729
  566.6 31.2 %collective-permute-start.55 = (f32[2,2304]{1,0:T(2,128)S(1)}, f32[2,2304]{1,0:T(2,128)S(1)}, u32[]{:S(2)}, u32[]{:S(2)}) collective-permute-start(f32[2,2304]{1,0:T(2,128)S(1)} %add.185), channel_id=1, source_target_pairs={{0,2},{1,3},{2,0},{3,1},{4,6},{5,7},{6,4},{7,5},{8,10},{9,11},{10,... | collective-permute-start | bytes 55304 | tf_op jit(solution)/shard_map/ppermute | solution.py:634
  (142 other events, 971.4 us)
Sparse Core Ops, SparseCore 0:
  13.7 58.8 all-gather.12
  119.6 63.2 all-gather.10
  239.5 56.9 reduce-scatter.3
  303.4 58.7 all-gather.6
  365.1 56.9 reduce-scatter.5
  447.0 60.8 reduce-scatter.7
  522.6 74.4 all-gather.8
